TPU v7x, 256 devices: a whole 4x4x8 slice. The times are simulated.
256 devices in a mesh: tp: 8 (over y_hi, x), cp: 32 (over y_lo, z, core).
Axes of the slice: x: 4, y: 4 (y_hi: 2, y_lo: 2; y = y_hi * 2 + y_lo), z: 8, core: 2. Of those that a mesh axis runs over, the one named last changes fastest.
Arguments:
- inputs: bfloat16 [4096, 4096], P(None, 'cp'), may hold values from -6 to 6
- projected: bfloat16 [3, 4096, 4096], P(None, 'tp', 'cp'), may hold values from -6 to 6
- filters: float32 [4096, 4096], P(('tp', 'cp')), may hold values from -4.5 to 4.5
- grad_out: bfloat16 [4096, 4096], P('tp', 'cp'), may hold values from -6 to 6
Outputs:
- proj_grad: bfloat16 [3, 4096, 4096], P(None, 'tp', 'cp')
- weight_grad: float32 [4096, 3, 4096], P('cp', None, 'tp')
- filter_grad: float32 [4096, 4096], P(('tp', 'cp'))
All inputs are finite; a program needn't handle non-finite values.
Results may differ from a plain program's by a relative error of at most 0.013.
Values may be sent and summed in bfloat16 or wider, within the bound.
No kernel may reach another device: no remote copies, remote signals or barrier semaphores. Data moves between devices by JAX's collectives and lax.ppermute only.
A program may use at most 128 MiB of HBM per device.

v0:
```python
import math

import jax
import jax.numpy as jnp
from jax import lax
from jax.sharding import PartitionSpec as P

EXACT = lax.Precision.HIGHEST


def split_length(full_size):
    lead_size = 2
    while lead_size * lead_size < full_size or full_size % lead_size != 0:
        lead_size = lead_size + 2
    return lead_size


def angle_table(count_rows, count_cols, modulus):
    row_ids = jnp.arange(count_rows, dtype=jnp.int32)[:, None]
    col_ids = jnp.arange(count_cols, dtype=jnp.int32)[None, :]
    phase = (row_ids * col_ids % modulus).astype(jnp.float32) * (2.0 * math.pi / modulus)
    return (jnp.cos(phase), -jnp.sin(phase))


def fourier_tables(lead_size, tail_size):
    lead_cos, lead_sin = angle_table(lead_size, lead_size, lead_size)
    tail_cos, tail_sin = angle_table(tail_size, tail_size, tail_size)
    twid_cos, twid_sin = angle_table(lead_size, tail_size, lead_size * tail_size)
    return (lead_cos, lead_sin, tail_cos, tail_sin, twid_cos, twid_sin)


def forward_transform(signal, tables):
    lead_cos, lead_sin, tail_cos, tail_sin, twid_cos, twid_sin = tables
    half_rows = lead_cos.shape[0] // 2
    grid_rows = signal.reshape(signal.shape[0], half_rows, tail_cos.shape[0])
    first_real = jnp.einsum("kn,bnm->bkm", lead_cos[:, :half_rows], grid_rows, precision=EXACT)
    first_imag = jnp.einsum("kn,bnm->bkm", lead_sin[:, :half_rows], grid_rows, precision=EXACT)
    turned_real = first_real * twid_cos - first_imag * twid_sin
    turned_imag = first_real * twid_sin + first_imag * twid_cos
    spec_real = jnp.einsum("bkm,mj->bkj", turned_real, tail_cos, precision=EXACT) - jnp.einsum(
        "bkm,mj->bkj", turned_imag, tail_sin, precision=EXACT
    )
    spec_imag = jnp.einsum("bkm,mj->bkj", turned_real, tail_sin, precision=EXACT) + jnp.einsum(
        "bkm,mj->bkj", turned_imag, tail_cos, precision=EXACT
    )
    return (spec_real, spec_imag)


def inverse_transform(spec_real, spec_imag, tables):
    lead_cos, lead_sin, tail_cos, tail_sin, twid_cos, twid_sin = tables
    half_rows = lead_cos.shape[0] // 2
    full_size = lead_cos.shape[0] * tail_cos.shape[0]
    mid_real = jnp.einsum("bkj,jm->bkm", spec_real, tail_cos, precision=EXACT) + jnp.einsum(
        "bkj,jm->bkm", spec_imag, tail_sin, precision=EXACT
    )
    mid_imag = jnp.einsum("bkj,jm->bkm", spec_imag, tail_cos, precision=EXACT) - jnp.einsum(
        "bkj,jm->bkm", spec_real, tail_sin, precision=EXACT
    )
    turned_real = mid_real * twid_cos + mid_imag * twid_sin
    turned_imag = mid_imag * twid_cos - mid_real * twid_sin
    signal = jnp.einsum(
        "nk,bkm->bnm", lead_cos[:half_rows, :], turned_real, precision=EXACT
    ) + jnp.einsum("nk,bkm->bnm", lead_sin[:half_rows, :], turned_imag, precision=EXACT)
    return signal.reshape(signal.shape[0], -1) / full_size


def make_term(inputs, flat_grad, stream_count, chan_width, count):
    return lax.dot_general(
        inputs, flat_grad, (((1,), (1,)), ((), ())), preferred_element_type=jnp.float32
    ).reshape(count, stream_count, chan_width)


def local(inputs, projected, filters, grad_out):
    query_rows = projected[0].astype(jnp.float32)
    key_rows = projected[1].astype(jnp.float32)
    value_rows = projected[2].astype(jnp.float32)
    out_rows = grad_out.astype(jnp.float32)
    gated = (key_rows * value_rows).astype(jnp.bfloat16)
    carried = (out_rows * query_rows).astype(jnp.bfloat16)
    carried_chan, gated_chan = (
        lax.all_to_all(carried, "cp", split_axis=0, concat_axis=1, tiled=True),
        lax.all_to_all(gated, "cp", split_axis=0, concat_axis=1, tiled=True),
    )
    length = filters.shape[1]
    lead_size = split_length(2 * length)
    tables = fourier_tables(lead_size, 2 * length // lead_size)
    filt_real, filt_imag = forward_transform(filters, tables)
    gate_real, gate_imag = forward_transform(gated_chan.astype(jnp.float32), tables)
    carr_real, carr_imag = forward_transform(carried_chan.astype(jnp.float32), tables)
    conv_chan = inverse_transform(
        filt_real * gate_real - filt_imag * gate_imag,
        filt_real * gate_imag + filt_imag * gate_real,
        tables,
    ).astype(jnp.bfloat16)
    back_chan = inverse_transform(
        filt_real * carr_real + filt_imag * carr_imag,
        filt_real * carr_imag - filt_imag * carr_real,
        tables,
    ).astype(jnp.bfloat16)
    filter_grad = inverse_transform(
        carr_real * gate_real + carr_imag * gate_imag,
        carr_imag * gate_real - carr_real * gate_imag,
        tables,
    )
    chan_width = grad_out.shape[0]
    tok_width = grad_out.shape[1]
    row_count = inputs.shape[0] // lax.axis_size("cp")
    conv_seq, back_seq = (
        lax.all_to_all(conv_chan, "cp", split_axis=1, concat_axis=0, tiled=True),
        lax.all_to_all(back_chan, "cp", split_axis=1, concat_axis=0, tiled=True),
    )
    conv_seq = conv_seq.astype(jnp.float32)
    back_seq = back_seq.astype(jnp.float32)
    proj_grad = jnp.stack([out_rows * conv_seq, back_seq * value_rows, back_seq * key_rows]).astype(
        jnp.bfloat16
    )
    flat_grad = proj_grad.reshape(3 * chan_width, tok_width)
    weight_grad = lax.psum_scatter(
        make_term(inputs, flat_grad, 3, chan_width, lax.axis_size("cp") * row_count),
        "cp",
        scatter_dimension=0,
        tiled=True,
    )
    return (proj_grad, weight_grad, filter_grad)


def solution(mesh):
    in_specs = (P(None, "cp"), P(None, "tp", "cp"), P(("tp", "cp"), None), P("tp", "cp"))
    out_specs = (P(None, "tp", "cp"), P("cp", None, "tp"), P(("tp", "cp"), None))
    return jax.shard_map(local, mesh=mesh, in_specs=in_specs, out_specs=out_specs, check_vma=False)
```

profile of v0, /device:TPU:1, one launch (start us, length us, event | category | flops | bytes accessed | tf_op | source)
XLA Modules:
  0.0 292.0 jit_solution(15836650522964716547)
XLA Ops:
  7.2 1.7 fusion.37
  8.9 11.1 %all-to-all-start = ((bf16[32,16,128]{2,1,0:T(8,128)(2,1)}), bf16[32,16,128]{2,1,0:T(8,128)(2,1)S(1)}, u32[]{:S(2)}, u32[]{:S(2)}) async-start(bf16[32,16,128]{2,1,0:T(8,128)(2,1)} %bitcast.10), calls=%async_computation | async-start | bytes 262144 | tf_op jit(solution)/shard_map/all_to_all | solution.py:82
  20.1 0.3 fusion.104
  20.3 0.3 sine_negate_fusion
  20.6 0.1 sine_negate_fusion.2
  20.8 1.1 reshape.108
  21.9 0.2 copy.54
  22.1 0.6 fusion.109
  22.7 0.6 fusion.113
  23.2 0.8 fusion.10
  24.0 0.8 fusion.12
  24.9 1.6 convolution_add_fusion.8
  26.4 1.6 convolution_subtract_fusion.5
  28.0 1.7 fusion.36
  29.7 8.5 %all-to-all-start.2 = ((bf16[32,16,128]{2,1,0:T(8,128)(2,1)}), bf16[32,16,128]{2,1,0:T(8,128)(2,1)S(1)}, u32[]{:S(2)}, u32[]{:S(2)}) async-start(bf16[32,16,128]{2,1,0:T(8,128)(2,1)} %bitcast.23), calls=%async_computation.2 | async-start | bytes 262144 | tf_op jit(solution)/shard_map/all_to_all | solution.py:81
  38.2 0.1 reshape.109
  38.4 0.4 convolution_bitcast_fusion.2
  38.8 0.4 convolution_bitcast_fusion.3
  39.3 7.8 %all-to-all-done.2 = bf16[32,16,128]{2,1,0:T(8,128)(2,1)S(1)} async-done(((bf16[32,16,128]{2,1,0:T(8,128)(2,1)}), bf16[32,16,128]{2,1,0:T(8,128)(2,1)S(1)}, u32[]{:S(2)}, u32[]{:S(2)}) %all-to-all-start.2) | async-done | bytes 131104 | tf_op jit(solution)/shard_map/all_to_all | solution.py:81
  47.3 0.4 convolution_bitcast_fusion
  47.7 0.4 convolution_bitcast_fusion.1
  48.1 0.8 fusion.52
  48.9 0.8 fusion.53
  49.7 0.8 fusion.50
  50.5 0.8 fusion.51
  51.3 0.8 convolution_subtract_fusion.2
  52.1 0.8 convolution_add_fusion.7
  52.9 0.8 convolution_subtract_fusion.4
  53.7 2.4 multiply_add_fusion
  56.1 0.7 fusion.92
  56.8 0.7 fusion.94
  57.6 0.7 convolution_subtract_fusion.3
  58.3 0.7 convolution_add_fusion.6
  59.0 0.6 fusion.31
  59.6 1.5 fusion.7
  61.1 1.8 copy.61
  62.9 1.8 convert_element_type.226
  64.7 1.6 copy.62
  66.3 5.8 %all-to-all-start.1 = ((bf16[16,32,128]{2,0,1:T(8,128)(2,1)}), bf16[16,32,128]{2,0,1:T(8,128)(2,1)}, u32[]{:S(2)}, u32[]{:S(2)}) async-start(bf16[16,32,128]{2,0,1:T(8,128)(2,1)} %copy.62), calls=%async_computation.1 | async-start | bytes 262144 | tf_op jit(solution)/shard_map/all_to_all | solution.py:109
  72.1 0.7 fusion.86
  72.9 0.7 fusion.88
  73.6 0.7 convolution_subtract_fusion.1
  74.4 0.7 convolution_add_fusion.3
  75.1 0.6 fusion.24
  75.7 0.6 fusion.6
  76.3 0.2 copy.68
  76.5 0.1 convert_element_type.235
  76.6 0.7 copy.69
  77.3 4.0 %all-to-all-done.1 = bf16[16,32,128]{2,0,1:T(8,128)(2,1)} async-done(((bf16[16,32,128]{2,0,1:T(8,128)(2,1)}), bf16[16,32,128]{2,0,1:T(8,128)(2,1)}, u32[]{:S(2)}, u32[]{:S(2)}) %all-to-all-start.1) | async-done | bytes 131104 | tf_op jit(solution)/shard_map/all_to_all | solution.py:109
  81.3 5.1 %all-to-all-start.3 = ((bf16[16,32,128]{2,0,1:T(8,128)(2,1)}), bf16[16,32,128]{2,0,1:T(8,128)(2,1)S(1)}, u32[]{:S(2)}, u32[]{:S(2)}) async-start(bf16[16,32,128]{2,0,1:T(8,128)(2,1)} %copy.69), calls=%async_computation.3 | async-start | bytes 262144 | tf_op jit(solution)/shard_map/all_to_all | solution.py:110
  86.6 0.9 fusion.35
  87.5 8.2 %all-to-all-done.3 = bf16[16,32,128]{2,0,1:T(8,128)(2,1)S(1)} async-done(((bf16[16,32,128]{2,0,1:T(8,128)(2,1)}), bf16[16,32,128]{2,0,1:T(8,128)(2,1)S(1)}, u32[]{:S(2)}, u32[]{:S(2)}) %all-to-all-start.3) | async-done | bytes 131104 | tf_op jit(solution)/shard_map/all_to_all | solution.py:110
  95.7 1.0 convert_multiply_fusion
  96.8 10.4 %fusion.225 = f32[1536,4096]{1,0:T(8,128)} fusion(bf16[1536,128]{1,0:T(8,128)(2,1)S(1)} %bitcast.160, bf16[4096,128]{1,0:T(8,128)(2,1)S(1)} %copy-done), kind=kOutput, calls=%fused_computation.264 | convolution fusion | flops 1610612736 | bytes 26607616 | tf_op jit(solution)/shard_map/dot_general | solution.py:68
  107.2 24.8 %copy.70 = f32[4096,3,512]{2,0,1:T(8,128)} copy(f32[4096,3,512]{0,2,1:T(8,128)} %bitcast.149) | data formatting | bytes 50331648 | tf_op jit(solution)/shard_map/reshape | solution.py:70
  132.0 0.7 fusion.84
  132.7 0.7 fusion.82
  133.4 0.7 convolution_add_fusion.1
  134.2 0.7 convolution_subtract_fusion
  134.9 0.6 fusion.17
  135.5 0.6 fusion.1
  136.1 0.2 copy.73
  136.3 0.9 div.17
  137.2 147.9 %reduce-scatter.2.cloned.1.call-done = f32[128,3,512]{2,0,1:T(8,128)} async-done(((f32[4096,3,512]{2,0,1:T(8,128)}), f32[128,3,512]{2,0,1:T(8,128)}) %reduce-scatter.2.cloned.1.call-update) | async-done | bytes 786448 | tf_op jit(solution)/shard_map/reduce_scatter | solution.py:118
  (15 shorter events, 0.3 us)
Async XLA Ops:
  7.2 89.6 %copy-start = (bf16[4096,128]{1,0:T(8,128)(2,1)S(1)}, bf16[4096,128]{1,0:T(8,128)(2,1)}, u32[]{:S(2)}) copy-start(bf16[4096,128]{1,0:T(8,128)(2,1)} %param.4) | copy-start | bytes 3145732
  8.9 20.8 %all-to-all-start = ((bf16[32,16,128]{2,1,0:T(8,128)(2,1)}), bf16[32,16,128]{2,1,0:T(8,128)(2,1)S(1)}, u32[]{:S(2)}, u32[]{:S(2)}) async-start(bf16[32,16,128]{2,1,0:T(8,128)(2,1)} %bitcast.10), calls=%async_computation | async-start | bytes 262144 | tf_op jit(solution)/shard_map/all_to_all | solution.py:82
  24.8 61.7 %copy-start.3 = (bf16[512,128]{1,0:T(8,128)(2,1)S(1)}, bf16[512,128]{1,0:T(8,128)(2,1)}, u32[]{:S(2)}) copy-start(bf16[512,128]{1,0:T(8,128)(2,1)} %param.7) | copy-start | bytes 393220
  29.7 17.4 %all-to-all-start.2 = ((bf16[32,16,128]{2,1,0:T(8,128)(2,1)}), bf16[32,16,128]{2,1,0:T(8,128)(2,1)S(1)}, u32[]{:S(2)}, u32[]{:S(2)}) async-start(bf16[32,16,128]{2,1,0:T(8,128)(2,1)} %bitcast.23), calls=%async_computation.2 | async-start | bytes 262144 | tf_op jit(solution)/shard_map/all_to_all | solution.py:81
  66.3 15.0 %all-to-all-start.1 = ((bf16[16,32,128]{2,0,1:T(8,128)(2,1)}), bf16[16,32,128]{2,0,1:T(8,128)(2,1)}, u32[]{:S(2)}, u32[]{:S(2)}) async-start(bf16[16,32,128]{2,0,1:T(8,128)(2,1)} %copy.62), calls=%async_computation.1 | async-start | bytes 262144 | tf_op jit(solution)/shard_map/all_to_all | solution.py:109
  81.3 14.3 %all-to-all-start.3 = ((bf16[16,32,128]{2,0,1:T(8,128)(2,1)}), bf16[16,32,128]{2,0,1:T(8,128)(2,1)S(1)}, u32[]{:S(2)}, u32[]{:S(2)}) async-start(bf16[16,32,128]{2,0,1:T(8,128)(2,1)} %copy.69), calls=%async_computation.3 | async-start | bytes 262144 | tf_op jit(solution)/shard_map/all_to_all | solution.py:110
  86.5 198.6 %reduce-scatter.2.cloned.1.call-start = ((), (), s32[]{:S(2)}) async-start(), calls=%async_computation.5 | async-start | bytes 25952256 | tf_op jit(solution)/shard_map/reduce_scatter | solution.py:118
  96.8 35.2 %copy-start.2 = (bf16[3,512,128]{2,1,0:T(8,128)(2,1)}, bf16[3,512,128]{2,1,0:T(8,128)(2,1)S(1)}, u32[]{:S(2)}) copy-start(bf16[3,512,128]{2,1,0:T(8,128)(2,1)S(1)} %maximum_convert_fusion) | copy-start | bytes 1179652
  107.1 178.0 %copy-start.1 = (bf16[4096,128]{1,0:T(8,128)(2,1)S(1)}, bf16[4096,128]{1,0:T(8,128)(2,1)}, u32[]{:S(2)}) copy-start(bf16[4096,128]{1,0:T(8,128)(2,1)} %param.4) | copy-start | bytes 3145732
Sparse Core Ops, SparseCore 0:
  132.1 152.9 reduce-scatter.1
where the time goes:
time: 295 us; the launch traced here: 292 us
  waiting for transfers between devices  168 us (57%)
  matrix products  39 us (13%)
  local copies, waits for them, and re-layouts  33.8 us (11%)
  starting transfers between devices  30.6 us (10%)
  between operations  14.5 us (5%)
  other arithmetic  6.09 us (2%)
    reduce_scatter x1, waiting for transfers between devices, local(): lax.psum_scatter(make_term(inputs, flat_grad, 3, chan_width, lax.axis_siz...  148 us
    reshape x1, local copies, waits for them, and re-layouts, make_term(): return lax.dot_general(inputs, flat_grad, (((1,), (1,)), ((), ())), prefe...  24.8 us
    all_to_all x1, starting transfers between devices, local(): lax.all_to_all(gated, 'cp', split_axis=0, concat_axis=1, tiled=True)  11.1 us
    dot_general x1, matrix products, make_term(): lax.dot_general(inputs, flat_grad, (((1,), (1,)), ((), ())), preferred_el...  10.4 us
    all_to_all x1, starting transfers between devices, local(): lax.all_to_all(carried, 'cp', split_axis=0, concat_axis=1, tiled=True)  8.49 us
    all_to_all x1, waiting for transfers between devices, local(): lax.all_to_all(back_chan, 'cp', split_axis=1, concat_axis=0, tiled=True)  8.15 us
    all_to_all x1, waiting for transfers between devices, local(): lax.all_to_all(carried, 'cp', split_axis=0, concat_axis=1, tiled=True)  7.83 us
  transfers between devices with their start and end apart: 5, of which 4 were waited for; matrix products, arithmetic and copies ran while one was open for 7% of the time, Pallas kernels for 0%

commit v1 on v0

v1 whole, which is shorter than its diff:
```python
import functools
import math

import jax
import jax.numpy as jnp
import ml_dtypes
import numpy as np
from jax import lax
from jax.experimental import pallas as pl
from jax.experimental.pallas import tpu as pltpu
from jax.sharding import Mesh
from jax.sharding import PartitionSpec as P

SEQ = ("ylo", "z", "core")

def halves(table):
    high = table.astype(np.float32).astype(ml_dtypes.bfloat16)
    low = (table - high.astype(np.float64)).astype(np.float32).astype(ml_dtypes.bfloat16)
    return high, low


def tables(blocks, width):
    lead = 2 * blocks
    size = lead * width
    rows = -(-(blocks + 1) // 8) * 8
    k = np.arange(rows, dtype=np.float64)
    live = (k <= blocks).astype(np.float64)
    i = np.arange(blocks, dtype=np.float64)
    j = np.arange(width, dtype=np.float64)
    turn = 2.0 * math.pi * np.outer(k, i) / lead
    lead_fwd = np.concatenate([np.cos(turn) * live[:, None], -np.sin(turn) * live[:, None]], 0)
    weight = np.where((k == 0) | (k == blocks), 1.0, 2.0) * live / size
    lead_inv = np.concatenate([np.cos(turn).T * weight, -np.sin(turn).T * weight], 1)
    twist = 2.0 * math.pi * np.outer(k, j) / size
    tail = 2.0 * math.pi * np.outer(j, j) / width
    cos, sin = np.cos(tail), np.sin(tail)
    tail_fwd = np.block([[cos, -sin], [sin, cos]])
    fh, fl = halves(lead_fwd)
    ih, il = halves(lead_inv)
    th, tl = halves(tail_fwd)
    uh, ul = halves(tail_fwd.T.copy())
    return (
        np.concatenate([fh, fl, fh], 1),
        np.concatenate([ih, il, ih], 1),
        np.cos(twist).astype(np.float32),
        np.sin(twist).astype(np.float32),
        th,
        tl,
        uh,
        ul,
    )


def dot(a, b):
    return jnp.dot(a, b, preferred_element_type=jnp.float32)


def split(x):
    high = x.astype(jnp.bfloat16)
    return high, (x - high.astype(jnp.float32)).astype(jnp.bfloat16)


def kernel(
    chans, width, blocks, pair_ref, filt_ref, lf_ref, li_ref, tc_ref, ts_ref, th_ref, tl_ref, uh_ref, ul_ref, out_ref, grad_ref
):
    rows = tc_ref.shape[0]
    tc, ts = tc_ref[...], ts_ref[...]
    th, tl, uh, ul = th_ref[...], tl_ref[...], uh_ref[...], ul_ref[...]
    lf, li = lf_ref[...], li_ref[...]
    def flat(x):
        return pltpu.einshape("icj->i(cj)", x)
    def forward(high, low):
        if low is None:
            a = dot(lf[:, : 2 * blocks], jnp.concatenate([high, high], 0))
        else:
            a = dot(lf, jnp.concatenate([high, high, low], 0))
        parts = []
        for c in range(chans):
            ar = a[:rows, c * width : (c + 1) * width]
            ai = a[rows:, c * width : (c + 1) * width]
            parts.append(jnp.concatenate([ar * tc + ai * ts, ai * tc - ar * ts], 1))
        high, low = split(jnp.concatenate(parts, 0))
        x = dot(high, th) + dot(low, th) + dot(high, tl)
        return x[:, :width], x[:, width:]
    def inverse(re, im):
        high, low = split(jnp.concatenate([re, im], 1))
        b = dot(high, uh) + dot(low, uh) + dot(high, ul)
        parts = []
        for c in range(chans):
            br = b[c * rows : (c + 1) * rows, :width]
            bi = b[c * rows : (c + 1) * rows, width:]
            parts.append(jnp.concatenate([br * tc - bi * ts, br * ts + bi * tc], 0))
        high, low = split(jnp.concatenate(parts, 1))
        y = dot(li, jnp.concatenate([high, high, low], 0))
        return pltpu.einshape("i(cj)->icj", y, c=chans)
    pair = pair_ref[...]
    gate = flat(pair[:, :chans].astype(jnp.float32)).astype(jnp.bfloat16)
    carr = flat(pair[:, chans:].astype(jnp.float32)).astype(jnp.bfloat16)
    filt = jnp.stack([filt_ref[:, i * width : (i + 1) * width] for i in range(blocks)], 0)
    fr, fi = forward(*split(flat(filt)))
    gr, gi = forward(gate, None)
    cr, ci = forward(carr, None)
    out_ref[:, :chans] = inverse(fr * gr - fi * gi, fr * gi + fi * gr).astype(jnp.bfloat16)
    out_ref[:, chans:] = inverse(fr * cr + fi * ci, fr * ci - fi * cr).astype(jnp.bfloat16)
    taps = inverse(cr * gr + ci * gi, ci * gr - cr * gi)
    for i in range(blocks):
        grad_ref[:, i * width : (i + 1) * width] = taps[i]


def spectral(pair, filters):
    blocks, twice, width = pair.shape
    chans = twice // 2
    return pl.pallas_call(
        functools.partial(kernel, chans, width, blocks),
        out_shape=(jax.ShapeDtypeStruct(pair.shape, jnp.bfloat16), jax.ShapeDtypeStruct(filters.shape, jnp.float32)),
        in_specs=[pl.BlockSpec(memory_space=pltpu.VMEM)] * 10,
        out_specs=[pl.BlockSpec(memory_space=pltpu.VMEM)] * 2,
        compiler_params=pltpu.CompilerParams(vmem_limit_bytes=48 * 1024 * 1024),
    )(pair, filters, *tables(blocks, width))


def swap(x, axis):
    return lax.ppermute(x, axis, [(0, 1), (1, 0)])


def pick(x, index, axis):
    return lax.dynamic_index_in_dim(x, index, axis, keepdims=False)


def exchange_rows(inputs, count_z):
    width = inputs.shape[1]
    y, c = lax.axis_index("ylo"), lax.axis_index("core")
    rows = inputs.shape[0] // (4 * count_z)
    grid = inputs.reshape(2, count_z, 2, rows, width)
    got = swap(pick(grid, 1 - c, 2), "core")
    grid = jnp.concatenate([pick(grid, c, 2), got], -1)
    got = swap(pick(grid, 1 - y, 0), "ylo")
    return jnp.concatenate([pick(grid, y, 0), got], -1)


def gather_near(x):
    x = jnp.concatenate([x, swap(x, "core")], -1)
    return jnp.concatenate([x, swap(x, "ylo")], -1)


def ring_sum(rows, cols, ahead, behind):
    n = rows.shape[0]
    z = lax.axis_index("z")

    def part(k):
        return lax.dot_general(
            pick(rows, lax.rem(k + n, n), 0), cols, (((1,), (1,)), ((), ())), preferred_element_type=jnp.float32
        )

    def arm(hops, way):
        perm = [(i, (i + way) % n) for i in range(n)]
        got = None
        for hop in range(hops, 0, -1):
            total = part(z + way * hop)
            if got is not None:
                total = total + got.astype(jnp.float32)
            got = lax.ppermute(total.astype(jnp.bfloat16), "z", perm)
        return got.astype(jnp.float32)

    up = arm(ahead, 1)
    down = arm(behind, -1)
    return part(z) + up + down


def local(inputs, projected, filters, grad_out):
    chan_width, tok_width = grad_out.shape
    chans = filters.shape[0]
    owners = chan_width // chans
    count_z = lax.axis_size("z")
    query = projected[0].astype(jnp.float32)
    key = projected[1].astype(jnp.float32)
    value = projected[2].astype(jnp.float32)
    out_grad = grad_out.astype(jnp.float32)
    gated = (key * value).astype(jnp.bfloat16).reshape(owners, chans, tok_width)
    carried = (out_grad * query).astype(jnp.bfloat16).reshape(owners, chans, tok_width)
    pair = jnp.concatenate([gated, carried], 1)
    pair = lax.all_to_all(pair, SEQ, split_axis=0, concat_axis=0, tiled=True)
    rows = exchange_rows(inputs, count_z)
    pair, filter_grad = spectral(pair, filters)
    pair = lax.all_to_all(pair, SEQ, split_axis=0, concat_axis=0, tiled=True)
    conv = pair[:, :chans].reshape(chan_width, tok_width).astype(jnp.float32)
    back = pair[:, chans:].reshape(chan_width, tok_width).astype(jnp.float32)
    proj_grad = jnp.stack([out_grad * conv, back * value, back * key]).astype(jnp.bfloat16)
    half = chan_width // 2
    sums = []
    for part in range(2):
        cols = proj_grad[:, part * half : (part + 1) * half].reshape(3 * half, tok_width)
        total = ring_sum(rows, gather_near(cols), count_z // 2 - part, count_z // 2 - 1 + part)
        sums.append(total.reshape(-1, 3, half))
    return proj_grad, jnp.concatenate(sums, 2), filter_grad


def solution(mesh):
    fine = Mesh(mesh.devices.reshape(2, 4, 2, 8, 2), ("yhi", "x", "ylo", "z", "core"))
    tp = ("yhi", "x")
    in_specs = (P(None, SEQ), P(None, tp, SEQ), P(tp + SEQ, None), P(tp, SEQ))
    out_specs = (P(None, tp, SEQ), P(SEQ, None, tp), P(tp + SEQ, None))
    return jax.shard_map(local, mesh=fine, in_specs=in_specs, out_specs=out_specs, check_vma=False)
```

time: 295 us -> 119 us (0.40)
  the two profiles are of different devices: /device:TPU:1 before, /device:TPU:6 now
where the time goes in v1:
time: 119 us
  waiting for transfers between devices  37.4 us (31%)
  starting transfers between devices  30.9 us (26%)
  blocking collectives  23 us (19%)
  matrix products  16.8 us (14%)
  Pallas kernels  4.14 us (3%)
  other arithmetic  3.51 us (3%)
  local copies, waits for them, and re-layouts  2.12 us (2%)
    ppermute x14, starting transfers between devices, arm(): got = lax.ppermute(total.astype(jnp.bfloat16), 'z', perm)  24.1 us
    all_to_all x1, blocking collectives, local(): pair = lax.all_to_all(pair, SEQ, split_axis=0, concat_axis=0, tiled=True)  23 us
    ppermute x6, waiting for transfers between devices, swap(): return lax.ppermute(x, axis, [(0, 1), (1, 0)])  21 us
    dot_general x16, matrix products, part(): lax.dot_general(pick(rows, lax.rem(k + n, n), 0), cols, (((1,), (1,)), ((...  16.8 us
    all_to_all x1, waiting for transfers between devices, local(): pair = lax.all_to_all(pair, SEQ, split_axis=0, concat_axis=0, tiled=True)  12.8 us
    pallas_call x1, Pallas kernels, spectral(): pl.pallas_call(functools.partial(kernel, chans, width, blocks), out_shape...  4.14 us
    all_to_all x1, starting transfers between devices, local(): pair = lax.all_to_all(pair, SEQ, split_axis=0, concat_axis=0, tiled=True)  3.87 us
    ppermute x14, waiting for transfers between devices, arm(): got = lax.ppermute(total.astype(jnp.bfloat16), 'z', perm)  3.58 us
  transfers between devices with their start and end apart: 21, of which 8 were waited for; matrix products, arithmetic and copies ran while one was open for 14% of the time, Pallas kernels for 0%

profile of v1, /device:TPU:6, one launch (start us, length us, event | category | flops | bytes accessed | tf_op | source)
XLA Modules:
  0.0 118.9 jit_solution(3969987828046429940)
XLA Ops:
  0.6 0.0 copy-start.5
  0.6 0.0 copy-start.8
  0.7 0.0 copy-start.6
  0.7 0.0 copy-start.7
  0.7 0.0 copy-start.1
  0.7 0.0 copy-start.2
  0.7 0.0 copy-start.3
  0.7 0.0 copy-start.4
  0.7 1.1 fusion.18
  1.8 1.0 fusion.16
  2.9 23.0 %all_to_all.10.pair_ref = bf16[32,32,128]{2,1,0:T(8,128)(2,1)S(1)} all-to-all(bf16[32,32,128]{2,1,0:T(8,128)(2,1)S(1)} %pad_maximum_fusion.6), channel_id=1, replica_groups=mesh['yhi'=2,'x'=4,'ylo'=2,'z'=8,'core'=2] {'ylo','z','core'}, dimensions={0} | all-to-all | bytes 524288 | tf_op jit(solution)/shard_map/all_to_all | solution.py:182
  25.9 4.1 %shard_map.139 = (bf16[32,32,128]{2,1,0:T(8,128)(2,1)}, f32[16,4096]{1,0:T(8,128)}) custom-call(bf16[32,32,128]{2,1,0:T(8,128)(2,1)S(1)} %all_to_all.10.pair_ref, f32[16,4096]{1,0:T(8,128)S(1)} %copy-done, bf16[80,96]{1,0:T(8,128)(2,1)S(1)} %copy-done.5, bf16[32,240]{1,0:T(8,128)(2,1)S(1)} %copy-done.8, f32[40,128]{1,0:T(8,128)S(1)} %copy-done.6, ...), custom_call_target="tpu_custom_call" | custom-call | tf_op jit(solution)/shard_map/pallas_call | solution.py:113
  30.1 3.9 %all-to-all-start.1 = ((bf16[32,32,128]{2,1,0:T(8,128)(2,1)}), bf16[32,32,128]{2,1,0:T(8,128)(2,1)S(1)}, u32[]{:S(2)}, u32[]{:S(2)}) async-start(bf16[32,32,128]{2,1,0:T(8,128)(2,1)} %get-tuple-element.5), calls=%async_computation.1 | async-start | bytes 524288 | tf_op jit(solution)/shard_map/all_to_all | solution.py:185
  34.0 0.1 dynamic-slice_bitcast_fusion
  34.1 0.2 collective-permute-start
  34.4 12.8 %all-to-all-done.1 = bf16[32,32,128]{2,1,0:T(8,128)(2,1)S(1)} async-done(((bf16[32,32,128]{2,1,0:T(8,128)(2,1)}), bf16[32,32,128]{2,1,0:T(8,128)(2,1)S(1)}, u32[]{:S(2)}, u32[]{:S(2)}) %all-to-all-start.1) | async-done | bytes 262176 | tf_op jit(solution)/shard_map/all_to_all | solution.py:185
  47.2 0.1 fusion.19
  47.4 0.1 collective-permute-start.2
  47.5 0.1 fusion.13
  47.7 0.4 copy-done.9
  48.1 0.3 collective-permute-start.1
  48.5 0.6 collective-permute-done.2
  49.1 1.0 pad_maximum_fusion.4
  50.1 1.2 collective-permute-start.3
  51.3 1.0 collective-permute-start.12
  52.3 10.6 %collective-permute-done.1 = bf16[8,128,256]{2,1,0:T(8,128)(2,1)S(1)} collective-permute-done((bf16[8,128,256]{2,1,0:T(8,128)(2,1)S(1)}, bf16[8,128,256]{2,1,0:T(8,128)(2,1)S(1)}, u32[]{:S(2)}, u32[]{:S(2)}) %collective-permute-start.1) | collective-permute-done | bytes 524320 | tf_op jit(solution)/shard_map/ppermute | solution.py:123
  62.9 8.5 %collective-permute-done.3 = bf16[768,256]{1,0:T(8,128)(2,1)} collective-permute-done((bf16[768,256]{1,0:T(8,128)(2,1)S(1)}, bf16[768,256]{1,0:T(8,128)(2,1)}, u32[]{:S(2)}, u32[]{:S(2)}) %collective-permute-start.3) | collective-permute-done | bytes 393248 | tf_op jit(solution)/shard_map/ppermute | solution.py:123
  71.4 1.4 %convolution_convert_fusion.3 = bf16[128,768]{1,0:T(8,128)(2,1)S(1)} fusion(s32[]{:T(128)S(6)} %select_n.57, bf16[8,128,256]{2,1,0:T(8,128)(2,1)S(1)} %get-tuple-element.11, bf16[8,128,256]{2,1,0:T(8,128)(2,1)S(1)} %collective-permute-done.1, bf16[768,256]{1,0:T(8,128)(2,1)} %collective-permute-done.3, bf16[768,128]{1,0:T(8,128)(2,1)} %collective-permute-done.2, ...), kind=kOutput, calls=%fused_computation.49 | convolution fusion | flops 103383040 | bytes 2031620 | tf_op jit(solution)/shard_map/dot_general | solution.py:151
  72.9 0.8 collective-permute-start.4
  73.7 1.4 %convolution_convert_fusion.2 = bf16[128,768]{1,0:T(8,128)(2,1)S(1)} fusion(s32[]{:T(128)S(6)} %select_n.60, bf16[8,128,256]{2,1,0:T(8,128)(2,1)S(1)} %get-tuple-element.11, bf16[8,128,256]{2,1,0:T(8,128)(2,1)S(1)} %collective-permute-done.1, bf16[768,256]{1,0:T(8,128)(2,1)} %collective-permute-done.3, bf16[768,128]{1,0:T(8,128)(2,1)} %collective-permute-done.2, ...), kind=kOutput, calls=%fused_computation.48 | convolution fusion | flops 103383040 | bytes 2031620 | tf_op jit(solution)/shard_map/dot_general | solution.py:151
  75.1 2.6 %collective-permute-start.8 = (bf16[128,768]{1,0:T(8,128)(2,1)S(1)}, bf16[128,768]{1,0:T(8,128)(2,1)S(1)}, u32[]{:S(2)}, u32[]{:S(2)}) collective-permute-start(bf16[128,768]{1,0:T(8,128)(2,1)S(1)} %convolution_convert_fusion.2), channel_id=1, source_target_pairs={{0,14},{2,0},{4,2},{6,4},{8,6},{10,8},{12,10},{14,12},{1,15},{3,1}... | collective-permute-start | bytes 589832 | tf_op jit(solution)/shard_map/ppermute | solution.py:162
  77.7 1.3 %collective-permute-done.12 = bf16[768,256]{1,0:T(8,128)(2,1)S(1)} collective-permute-done((bf16[768,256]{1,0:T(8,128)(2,1)S(1)}, bf16[768,256]{1,0:T(8,128)(2,1)S(1)}, u32[]{:S(2)}, u32[]{:S(2)}) %collective-permute-start.12) | collective-permute-done | bytes 393248 | tf_op jit(solution)/shard_map/ppermute | solution.py:123
  78.9 0.4 convolution_convert_fusion.1
  79.3 0.8 collective-permute-start.13
  80.2 0.4 convolution_convert_fusion
  80.6 2.6 %collective-permute-start.16 = (bf16[128,768]{1,0:T(8,128)(2,1)S(1)}, bf16[128,768]{1,0:T(8,128)(2,1)S(1)}, u32[]{:S(2)}, u32[]{:S(2)}) collective-permute-start(bf16[128,768]{1,0:T(8,128)(2,1)S(1)} %convolution_convert_fusion), channel_id=1, source_target_pairs={{0,14},{2,0},{4,2},{6,4},{8,6},{10,8},{12,10},{14,12},{1,15},{3,1}... | collective-permute-start | bytes 589832 | tf_op jit(solution)/shard_map/ppermute | solution.py:162
  83.1 1.4 %fusion.4 = bf16[128,768]{1,0:T(8,128)(2,1)S(1)} fusion(bf16[128,768]{1,0:T(8,128)(2,1)S(1)} %collective-permute-done.4, s32[]{:T(128)S(6)} %select_n.56, bf16[8,128,256]{2,1,0:T(8,128)(2,1)S(1)} %get-tuple-element.11, bf16[8,128,256]{2,1,0:T(8,128)(2,1)S(1)} %collective-permute-done.1, bf16[768,256]{1,0:T(8,128)(2,1)} %collective-permute-done.3, ...), kind=kOutput, calls=%fused_computation.38 | convolution fusion | flops 103579648 | bytes 2228228 | tf_op jit(solution)/shard_map/dot_general | solution.py:151
  84.5 0.3 collective-permute-start.5
  84.8 1.4 %fusion.6 = bf16[128,768]{1,0:T(8,128)(2,1)S(1)} fusion(bf16[128,768]{1,0:T(8,128)(2,1)S(1)} %collective-permute-done.8, s32[]{:T(128)S(6)} %select_n.59, bf16[8,128,256]{2,1,0:T(8,128)(2,1)S(1)} %get-tuple-element.11, bf16[8,128,256]{2,1,0:T(8,128)(2,1)S(1)} %collective-permute-done.1, bf16[768,256]{1,0:T(8,128)(2,1)} %collective-permute-done.3, ...), kind=kOutput, calls=%fused_computation.40 | convolution fusion | flops 103579648 | bytes 2228228 | tf_op jit(solution)/shard_map/dot_general | solution.py:151
  86.3 3.3 %collective-permute-start.9 = (bf16[128,768]{1,0:T(8,128)(2,1)S(1)}, bf16[128,768]{1,0:T(8,128)(2,1)S(1)}, u32[]{:S(2)}, u32[]{:S(2)}) collective-permute-start(bf16[128,768]{1,0:T(8,128)(2,1)S(1)} %fusion.6), channel_id=1, source_target_pairs={{0,14},{2,0},{4,2},{6,4},{8,6},{10,8},{12,10},{14,12},{1,15},{3,1}... | collective-permute-start | bytes 589832 | tf_op jit(solution)/shard_map/ppermute | solution.py:162
  89.6 0.4 fusion.8
  89.9 0.1 collective-permute-start.14
  90.0 0.4 fusion.11
  90.4 3.3 %collective-permute-start.17 = (bf16[128,768]{1,0:T(8,128)(2,1)S(1)}, bf16[128,768]{1,0:T(8,128)(2,1)S(1)}, u32[]{:S(2)}, u32[]{:S(2)}) collective-permute-start(bf16[128,768]{1,0:T(8,128)(2,1)S(1)} %fusion.11), channel_id=1, source_target_pairs={{0,14},{2,0},{4,2},{6,4},{8,6},{10,8},{12,10},{14,12},{1,15},{3,1}... | collective-permute-start | bytes 589832 | tf_op jit(solution)/shard_map/ppermute | solution.py:162
  93.7 1.4 %fusion.3 = bf16[128,768]{1,0:T(8,128)(2,1)S(1)} fusion(bf16[128,768]{1,0:T(8,128)(2,1)S(1)} %collective-permute-done.5, s32[]{:T(128)S(6)} %select_n.55, bf16[8,128,256]{2,1,0:T(8,128)(2,1)S(1)} %get-tuple-element.11, bf16[8,128,256]{2,1,0:T(8,128)(2,1)S(1)} %collective-permute-done.1, bf16[768,256]{1,0:T(8,128)(2,1)} %collective-permute-done.3, ...), kind=kOutput, calls=%fused_computation.37 | convolution fusion | flops 103579648 | bytes 2228228 | tf_op jit(solution)/shard_map/dot_general | solution.py:151
  95.2 0.1 collective-permute-start.6
  95.3 1.4 %fusion.5 = bf16[128,768]{1,0:T(8,128)(2,1)S(1)} fusion(bf16[128,768]{1,0:T(8,128)(2,1)S(1)} %collective-permute-done.9, s32[]{:T(128)S(6)} %select_n.58, bf16[8,128,256]{2,1,0:T(8,128)(2,1)S(1)} %get-tuple-element.11, bf16[8,128,256]{2,1,0:T(8,128)(2,1)S(1)} %collective-permute-done.1, bf16[768,256]{1,0:T(8,128)(2,1)} %collective-permute-done.3, ...), kind=kOutput, calls=%fused_computation.39 | convolution fusion | flops 103579648 | bytes 2228228 | tf_op jit(solution)/shard_map/dot_general | solution.py:151
  96.7 3.3 %collective-permute-start.10 = (bf16[128,768]{1,0:T(8,128)(2,1)S(1)}, bf16[128,768]{1,0:T(8,128)(2,1)S(1)}, u32[]{:S(2)}, u32[]{:S(2)}) collective-permute-start(bf16[128,768]{1,0:T(8,128)(2,1)S(1)} %fusion.5), channel_id=1, source_target_pairs={{0,14},{2,0},{4,2},{6,4},{8,6},{10,8},{12,10},{14,12},{1,15},{3,1}... | collective-permute-start | bytes 589832 | tf_op jit(solution)/shard_map/ppermute | solution.py:162
  100.0 1.1 fusion.7
  101.1 0.4 fusion.10
  101.5 3.3 %collective-permute-start.18 = (bf16[128,768]{1,0:T(8,128)(2,1)S(1)}, bf16[128,768]{1,0:T(8,128)(2,1)S(1)}, u32[]{:S(2)}, u32[]{:S(2)}) collective-permute-start(bf16[128,768]{1,0:T(8,128)(2,1)S(1)} %fusion.10), channel_id=1, source_target_pairs={{0,14},{2,0},{4,2},{6,4},{8,6},{10,8},{12,10},{14,12},{1,15},{3,1}... | collective-permute-start | bytes 589832 | tf_op jit(solution)/shard_map/ppermute | solution.py:162
  104.8 1.4 %fusion.2 = bf16[128,768]{1,0:T(8,128)(2,1)S(1)} fusion(bf16[128,768]{1,0:T(8,128)(2,1)S(1)} %collective-permute-done.6, s32[]{:T(128)S(6)} %select_n.54, bf16[8,128,256]{2,1,0:T(8,128)(2,1)S(1)} %get-tuple-element.11, bf16[8,128,256]{2,1,0:T(8,128)(2,1)S(1)} %collective-permute-done.1, bf16[768,256]{1,0:T(8,128)(2,1)} %collective-permute-done.3, ...), kind=kOutput, calls=%fused_computation.36 | convolution fusion | flops 103579648 | bytes 2228228 | tf_op jit(solution)/shard_map/dot_general | solution.py:151
  106.2 0.1 collective-permute-start.7
  106.3 1.7 %collective-permute-done.18 = bf16[128,768]{1,0:T(8,128)(2,1)S(1)} collective-permute-done((bf16[128,768]{1,0:T(8,128)(2,1)S(1)}, bf16[128,768]{1,0:T(8,128)(2,1)S(1)}, u32[]{:S(2)}, u32[]{:S(2)}) %collective-permute-start.18) | collective-permute-done | bytes 196640 | tf_op jit(solution)/shard_map/ppermute | solution.py:162
  108.0 1.1 fusion.9
  109.0 3.7 %collective-permute-start.19 = (bf16[128,768]{1,0:T(8,128)(2,1)}, bf16[128,768]{1,0:T(8,128)(2,1)}, u32[]{:S(2)}, u32[]{:S(2)}) collective-permute-start(bf16[128,768]{1,0:T(8,128)(2,1)} %fusion.9), channel_id=1, source_target_pairs={{0,14},{2,0},{4,2},{6,4},{8,6},{10,8},{12,10},{14,12},{1,15},{3,1}... | collective-permute-start | bytes 589832 | tf_op jit(solution)/shard_map/ppermute | solution.py:162
  112.7 0.4 collective-permute-done.7
  113.2 1.4 %fusion.1 = f32[128,768]{1,0:T(8,128)S(1)} fusion(bf16[128,768]{1,0:T(8,128)(2,1)S(1)} %collective-permute-done.10, bf16[128,768]{1,0:T(8,128)(2,1)S(1)} %collective-permute-done.7, s32[]{:T(128)S(6)} %select_n.53, bf16[8,128,256]{2,1,0:T(8,128)(2,1)S(1)} %get-tuple-element.11, bf16[8,128,256]{2,1,0:T(8,128)(2,1)S(1)} %collective-permute-done.1, ...), kind=kOutput, calls=%fused_computation.31 | convolution fusion | flops 103677952 | bytes 2621444 | tf_op jit(solution)/shard_map/dot_general | solution.py:151
  114.6 0.2 copy.17
  114.8 1.4 %collective-permute-done.19 = bf16[128,768]{1,0:T(8,128)(2,1)} collective-permute-done((bf16[128,768]{1,0:T(8,128)(2,1)}, bf16[128,768]{1,0:T(8,128)(2,1)}, u32[]{:S(2)}, u32[]{:S(2)}) %collective-permute-start.19) | collective-permute-done | bytes 196640 | tf_op jit(solution)/shard_map/ppermute | solution.py:162
  116.2 1.3 %fusion = f32[128,768]{1,0:T(8,128)S(1)} fusion(bf16[128,768]{1,0:T(8,128)(2,1)} %collective-permute-done.19, bf16[128,768]{1,0:T(8,128)(2,1)S(1)} %collective-permute-done.15, s32[]{:T(128)S(6)} %select_n.53, bf16[8,128,256]{2,1,0:T(8,128)(2,1)S(1)} %get-tuple-element.11, bf16[8,128,256]{2,1,0:T(8,128)(2,1)S(1)} %collective-permute-done.1, ...), kind=kOutput, calls=%fused_computation.24 | convolution fusion | flops 103677952 | bytes 2621444 | tf_op jit(solution)/shard_map/dot_general | solution.py:151
  117.5 0.2 copy.18
  117.7 0.1 pad_maximum_fusion.2
  117.8 1.1 copy.19
  (38 shorter events, 0.3 us)
Async XLA Ops:
  0.6 25.2 %copy-start.5 = (bf16[80,96]{1,0:T(8,128)(2,1)S(1)}, bf16[80,96]{1,0:T(8,128)(2,1)}, u32[]{:S(2)}) copy-start(bf16[80,96]{1,0:T(8,128)(2,1)} %constant.124.clone.lf_ref) | copy-start | bytes 46084
  0.6 25.2 %copy-start.8 = (bf16[32,240]{1,0:T(8,128)(2,1)S(1)}, bf16[32,240]{1,0:T(8,128)(2,1)}, u32[]{:S(2)}) copy-start(bf16[32,240]{1,0:T(8,128)(2,1)} %constant.125.clone.li_ref) | copy-start | bytes 46084
  0.7 25.2 %copy-start.6 = (f32[40,128]{1,0:T(8,128)S(1)}, f32[40,128]{1,0:T(8,128)}, u32[]{:S(2)}) copy-start(f32[40,128]{1,0:T(8,128)} %constant.126.clone.tc_ref) | copy-start | bytes 61444
  0.7 25.2 %copy-start.7 = (f32[40,128]{1,0:T(8,128)S(1)}, f32[40,128]{1,0:T(8,128)}, u32[]{:S(2)}) copy-start(f32[40,128]{1,0:T(8,128)} %constant.127.clone.ts_ref) | copy-start | bytes 61444
  0.7 25.2 %copy-start.1 = (bf16[256,256]{1,0:T(8,128)(2,1)S(1)}, bf16[256,256]{1,0:T(8,128)(2,1)}, u32[]{:S(2)}) copy-start(bf16[256,256]{1,0:T(8,128)(2,1)} %constant.128.clone.th_ref) | copy-start | bytes 393220
  0.7 25.2 %copy-start.2 = (bf16[256,256]{1,0:T(8,128)(2,1)S(1)}, bf16[256,256]{1,0:T(8,128)(2,1)}, u32[]{:S(2)}) copy-start(bf16[256,256]{1,0:T(8,128)(2,1)} %constant.129.clone.tl_ref) | copy-start | bytes 393220
  0.7 25.2 %copy-start.3 = (bf16[256,256]{1,0:T(8,128)(2,1)S(1)}, bf16[256,256]{1,0:T(8,128)(2,1)}, u32[]{:S(2)}) copy-start(bf16[256,256]{1,0:T(8,128)(2,1)} %constant.130.clone.uh_ref) | copy-start | bytes 393220
  0.7 25.2 %copy-start.4 = (bf16[256,256]{1,0:T(8,128)(2,1)S(1)}, bf16[256,256]{1,0:T(8,128)(2,1)}, u32[]{:S(2)}) copy-start(bf16[256,256]{1,0:T(8,128)(2,1)} %constant.131.clone.ul_ref) | copy-start | bytes 393220
  0.7 25.2 %copy-start = (f32[16,4096]{1,0:T(8,128)S(1)}, f32[16,4096]{1,0:T(8,128)}, u32[]{:S(2)}) copy-start(f32[16,4096]{1,0:T(8,128)} %filt_ref.1) | copy-start | bytes 786436
  2.9 31.1 %copy-start.11 = (bf16[4096,128]{1,0:T(8,128)(2,1)S(1)}, bf16[4096,128]{1,0:T(8,128)(2,1)}, u32[]{:S(2)}) copy-start(bf16[4096,128]{1,0:T(8,128)(2,1)} %param.12) | copy-start | bytes 3145732
  30.1 17.1 %all-to-all-start.1 = ((bf16[32,32,128]{2,1,0:T(8,128)(2,1)}), bf16[32,32,128]{2,1,0:T(8,128)(2,1)S(1)}, u32[]{:S(2)}, u32[]{:S(2)}) async-start(bf16[32,32,128]{2,1,0:T(8,128)(2,1)} %get-tuple-element.5), calls=%async_computation.1 | async-start | bytes 524288 | tf_op jit(solution)/shard_map/all_to_all | solution.py:185
  34.0 13.2 %copy-start.10 = (bf16[3,512,128]{2,1,0:T(8,128)(2,1)S(1)}, bf16[3,512,128]{2,1,0:T(8,128)(2,1)}, u32[]{:S(2)}) copy-start(bf16[3,512,128]{2,1,0:T(8,128)(2,1)} %param.13) | copy-start | bytes 1179652
  34.1 13.1 %copy-start.12 = (bf16[512,128]{1,0:T(8,128)(2,1)S(1)}, bf16[512,128]{1,0:T(8,128)(2,1)}, u32[]{:S(2)}) copy-start(bf16[512,128]{1,0:T(8,128)(2,1)} %param.15) | copy-start | bytes 393220
  34.1 13.4 %collective-permute-start = (bf16[2,8,128,128]{3,2,1,0:T(8,128)(2,1)S(1)}, bf16[2,8,128,128]{3,2,1,0:T(8,128)(2,1)S(1)}, u32[]{:S(2)}, u32[]{:S(2)}) collective-permute-start(bf16[2,8,128,128]{3,2,1,0:T(8,128)(2,1)S(1)} %get-tuple-element.12), channel_id=1, source_target_pairs={{0,1},{1,0},{2,3},{3,2},{4,5},{5,4},{6,7},{7,6},{8,9},{9,8},{10,11... | collective-permute-start | bytes 1572872 | tf_op jit(solution)/shard_map/ppermute | solution.py:123
  47.4 0.7 copy-start.9
  47.4 1.7 %collective-permute-start.2 = (bf16[768,128]{1,0:T(8,128)(2,1)S(1)}, bf16[768,128]{1,0:T(8,128)(2,1)}, u32[]{:S(2)}, u32[]{:S(2)}) collective-permute-start(bf16[768,128]{1,0:T(8,128)(2,1)S(1)} %bitcast.82), channel_id=1, source_target_pairs={{0,1},{1,0},{2,3},{3,2},{4,5},{5,4},{6,7},{7,6},{8,9},{9,8},{10,11... | collective-permute-start | bytes 589832 | tf_op jit(solution)/shard_map/ppermute | solution.py:123
  48.1 14.8 %collective-permute-start.1 = (bf16[8,128,256]{2,1,0:T(8,128)(2,1)S(1)}, bf16[8,128,256]{2,1,0:T(8,128)(2,1)S(1)}, u32[]{:S(2)}, u32[]{:S(2)}) collective-permute-start(bf16[8,128,256]{2,1,0:T(8,128)(2,1)S(1)} %get-tuple-element.10), channel_id=1, source_target_pairs={{0,16},{16,0},{1,17},{17,1},{2,18},{18,2},{3,19},{19,3},{4,20},{20... | collective-permute-start | bytes 1572872 | tf_op jit(solution)/shard_map/ppermute | solution.py:123
  48.5 2.8 %collective-permute-start.11 = (bf16[768,128]{1,0:T(8,128)(2,1)S(1)}, bf16[768,128]{1,0:T(8,128)(2,1)S(1)}, u32[]{:S(2)}, u32[]{:S(2)}) collective-permute-start(bf16[768,128]{1,0:T(8,128)(2,1)S(1)} %bitcast.72), channel_id=1, source_target_pairs={{0,1},{1,0},{2,3},{3,2},{4,5},{5,4},{6,7},{7,6},{8,9},{9,8},{10,11... | collective-permute-start | bytes 589832 | tf_op jit(solution)/shard_map/ppermute | solution.py:123
  50.1 21.4 %collective-permute-start.3 = (bf16[768,256]{1,0:T(8,128)(2,1)S(1)}, bf16[768,256]{1,0:T(8,128)(2,1)}, u32[]{:S(2)}, u32[]{:S(2)}) collective-permute-start(bf16[768,256]{1,0:T(8,128)(2,1)S(1)} %pad_maximum_fusion.4), channel_id=1, source_target_pairs={{0,16},{16,0},{1,17},{17,1},{2,18},{18,2},{3,19},{19,3},{4,20},{20... | collective-permute-start | bytes 1179656 | tf_op jit(solution)/shard_map/ppermute | solution.py:123
  51.3 27.7 %collective-permute-start.12 = (bf16[768,256]{1,0:T(8,128)(2,1)S(1)}, bf16[768,256]{1,0:T(8,128)(2,1)S(1)}, u32[]{:S(2)}, u32[]{:S(2)}) collective-permute-start(bf16[768,256]{1,0:T(8,128)(2,1)S(1)} %pad_maximum_fusion.5), channel_id=1, source_target_pairs={{0,16},{16,0},{1,17},{17,1},{2,18},{18,2},{3,19},{19,3},{4,20},{20... | collective-permute-start | bytes 1179656 | tf_op jit(solution)/shard_map/ppermute | solution.py:123
  72.9 10.3 %collective-permute-start.4 = (bf16[128,768]{1,0:T(8,128)(2,1)S(1)}, bf16[128,768]{1,0:T(8,128)(2,1)S(1)}, u32[]{:S(2)}, u32[]{:S(2)}) collective-permute-start(bf16[128,768]{1,0:T(8,128)(2,1)S(1)} %convolution_convert_fusion.3), channel_id=1, source_target_pairs={{0,2},{2,4},{4,6},{6,8},{8,10},{10,12},{12,14},{14,0},{1,3},{3,5},... | collective-permute-start | bytes 589832 | tf_op jit(solution)/shard_map/ppermute | solution.py:162
  75.1 9.7 %collective-permute-start.8 = (bf16[128,768]{1,0:T(8,128)(2,1)S(1)}, bf16[128,768]{1,0:T(8,128)(2,1)S(1)}, u32[]{:S(2)}, u32[]{:S(2)}) collective-permute-start(bf16[128,768]{1,0:T(8,128)(2,1)S(1)} %convolution_convert_fusion.2), channel_id=1, source_target_pairs={{0,14},{2,0},{4,2},{6,4},{8,6},{10,8},{12,10},{14,12},{1,15},{3,1}... | collective-permute-start | bytes 589832 | tf_op jit(solution)/shard_map/ppermute | solution.py:162
  79.3 10.2 %collective-permute-start.13 = (bf16[128,768]{1,0:T(8,128)(2,1)S(1)}, bf16[128,768]{1,0:T(8,128)(2,1)S(1)}, u32[]{:S(2)}, u32[]{:S(2)}) collective-permute-start(bf16[128,768]{1,0:T(8,128)(2,1)S(1)} %convolution_convert_fusion.1), channel_id=1, source_target_pairs={{0,2},{2,4},{4,6},{6,8},{8,10},{10,12},{12,14},{14,0},{1,3},{3,5},... | collective-permute-start | bytes 589832 | tf_op jit(solution)/shard_map/ppermute | solution.py:162
  80.6 9.5 %collective-permute-start.16 = (bf16[128,768]{1,0:T(8,128)(2,1)S(1)}, bf16[128,768]{1,0:T(8,128)(2,1)S(1)}, u32[]{:S(2)}, u32[]{:S(2)}) collective-permute-start(bf16[128,768]{1,0:T(8,128)(2,1)S(1)} %convolution_convert_fusion), channel_id=1, source_target_pairs={{0,14},{2,0},{4,2},{6,4},{8,6},{10,8},{12,10},{14,12},{1,15},{3,1}... | collective-permute-start | bytes 589832 | tf_op jit(solution)/shard_map/ppermute | solution.py:162
  84.5 9.2 %collective-permute-start.5 = (bf16[128,768]{1,0:T(8,128)(2,1)S(1)}, bf16[128,768]{1,0:T(8,128)(2,1)S(1)}, u32[]{:S(2)}, u32[]{:S(2)}) collective-permute-start(bf16[128,768]{1,0:T(8,128)(2,1)S(1)} %fusion.4), channel_id=1, source_target_pairs={{0,2},{2,4},{4,6},{6,8},{8,10},{10,12},{12,14},{14,0},{1,3},{3,5},... | collective-permute-start | bytes 589832 | tf_op jit(solution)/shard_map/ppermute | solution.py:162
  86.3 9.0 %collective-permute-start.9 = (bf16[128,768]{1,0:T(8,128)(2,1)S(1)}, bf16[128,768]{1,0:T(8,128)(2,1)S(1)}, u32[]{:S(2)}, u32[]{:S(2)}) collective-permute-start(bf16[128,768]{1,0:T(8,128)(2,1)S(1)} %fusion.6), channel_id=1, source_target_pairs={{0,14},{2,0},{4,2},{6,4},{8,6},{10,8},{12,10},{14,12},{1,15},{3,1}... | collective-permute-start | bytes 589832 | tf_op jit(solution)/shard_map/ppermute | solution.py:162
  89.9 10.1 %collective-permute-start.14 = (bf16[128,768]{1,0:T(8,128)(2,1)S(1)}, bf16[128,768]{1,0:T(8,128)(2,1)S(1)}, u32[]{:S(2)}, u32[]{:S(2)}) collective-permute-start(bf16[128,768]{1,0:T(8,128)(2,1)S(1)} %fusion.8), channel_id=1, source_target_pairs={{0,2},{2,4},{4,6},{6,8},{8,10},{10,12},{12,14},{14,0},{1,3},{3,5},... | collective-permute-start | bytes 589832 | tf_op jit(solution)/shard_map/ppermute | solution.py:162
  90.4 10.6 %collective-permute-start.17 = (bf16[128,768]{1,0:T(8,128)(2,1)S(1)}, bf16[128,768]{1,0:T(8,128)(2,1)S(1)}, u32[]{:S(2)}, u32[]{:S(2)}) collective-permute-start(bf16[128,768]{1,0:T(8,128)(2,1)S(1)} %fusion.11), channel_id=1, source_target_pairs={{0,14},{2,0},{4,2},{6,4},{8,6},{10,8},{12,10},{14,12},{1,15},{3,1}... | collective-permute-start | bytes 589832 | tf_op jit(solution)/shard_map/ppermute | solution.py:162
  95.2 9.6 %collective-permute-start.6 = (bf16[128,768]{1,0:T(8,128)(2,1)S(1)}, bf16[128,768]{1,0:T(8,128)(2,1)S(1)}, u32[]{:S(2)}, u32[]{:S(2)}) collective-permute-start(bf16[128,768]{1,0:T(8,128)(2,1)S(1)} %fusion.3), channel_id=1, source_target_pairs={{0,2},{2,4},{4,6},{6,8},{8,10},{10,12},{12,14},{14,0},{1,3},{3,5},... | collective-permute-start | bytes 589832 | tf_op jit(solution)/shard_map/ppermute | solution.py:162
  96.7 16.0 %collective-permute-start.10 = (bf16[128,768]{1,0:T(8,128)(2,1)S(1)}, bf16[128,768]{1,0:T(8,128)(2,1)S(1)}, u32[]{:S(2)}, u32[]{:S(2)}) collective-permute-start(bf16[128,768]{1,0:T(8,128)(2,1)S(1)} %fusion.5), channel_id=1, source_target_pairs={{0,14},{2,0},{4,2},{6,4},{8,6},{10,8},{12,10},{14,12},{1,15},{3,1}... | collective-permute-start | bytes 589832 | tf_op jit(solution)/shard_map/ppermute | solution.py:162
  101.1 13.7 %collective-permute-start.15 = (bf16[128,768]{1,0:T(8,128)(2,1)}, bf16[128,768]{1,0:T(8,128)(2,1)S(1)}, u32[]{:S(2)}, u32[]{:S(2)}) collective-permute-start(bf16[128,768]{1,0:T(8,128)(2,1)} %fusion.7), channel_id=1, source_target_pairs={{0,2},{2,4},{4,6},{6,8},{8,10},{10,12},{12,14},{14,0},{1,3},{3,5},... | collective-permute-start | bytes 589832 | tf_op jit(solution)/shard_map/ppermute | solution.py:162
  101.5 6.5 %collective-permute-start.18 = (bf16[128,768]{1,0:T(8,128)(2,1)S(1)}, bf16[128,768]{1,0:T(8,128)(2,1)S(1)}, u32[]{:S(2)}, u32[]{:S(2)}) collective-permute-start(bf16[128,768]{1,0:T(8,128)(2,1)S(1)} %fusion.10), channel_id=1, source_target_pairs={{0,14},{2,0},{4,2},{6,4},{8,6},{10,8},{12,10},{14,12},{1,15},{3,1}... | collective-permute-start | bytes 589832 | tf_op jit(solution)/shard_map/ppermute | solution.py:162
  106.2 7.0 %collective-permute-start.7 = (bf16[128,768]{1,0:T(8,128)(2,1)S(1)}, bf16[128,768]{1,0:T(8,128)(2,1)S(1)}, u32[]{:S(2)}, u32[]{:S(2)}) collective-permute-start(bf16[128,768]{1,0:T(8,128)(2,1)S(1)} %fusion.2), channel_id=1, source_target_pairs={{0,2},{2,4},{4,6},{6,8},{8,10},{10,12},{12,14},{14,0},{1,3},{3,5},... | collective-permute-start | bytes 589832 | tf_op jit(solution)/shard_map/ppermute | solution.py:162
  109.0 7.2 %collective-permute-start.19 = (bf16[128,768]{1,0:T(8,128)(2,1)}, bf16[128,768]{1,0:T(8,128)(2,1)}, u32[]{:S(2)}, u32[]{:S(2)}) collective-permute-start(bf16[128,768]{1,0:T(8,128)(2,1)} %fusion.9), channel_id=1, source_target_pairs={{0,14},{2,0},{4,2},{6,4},{8,6},{10,8},{12,10},{14,12},{1,15},{3,1}... | collective-permute-start | bytes 589832 | tf_op jit(solution)/shard_map/ppermute | solution.py:162

commit v2 on v1

--- a/solution.py
+++ b/solution.py
@@ -119,6 +119,58 @@
     )(pair, filters, *tables(blocks, width))
 
 
+def vmem_call(body, outs, *args):
+    return pl.pallas_call(
+        body,
+        out_shape=tuple(jax.ShapeDtypeStruct(shape, dtype) for shape, dtype in outs),
+        in_specs=[pl.BlockSpec(memory_space=pltpu.VMEM)] * len(args),
+        out_specs=tuple(pl.BlockSpec(memory_space=pltpu.VMEM) for _ in outs),
+        compiler_params=pltpu.CompilerParams(vmem_limit_bytes=48 * 1024 * 1024),
+    )(*args)
+
+
+def gate_kernel(owners, chans, projected_ref, grad_ref, pair_ref):
+    width = grad_ref.shape[1]
+    query, key, value = (projected_ref[s].astype(jnp.float32) for s in range(3))
+    gated = (key * value).astype(jnp.bfloat16)
+    carried = (grad_ref[...].astype(jnp.float32) * query).astype(jnp.bfloat16)
+    pair_ref[:, :chans] = gated.reshape(owners, chans, width)
+    pair_ref[:, chans:] = carried.reshape(owners, chans, width)
+
+
+def grad_kernel(chans, pair_ref, projected_ref, grad_ref, out_ref, low_ref, high_ref):
+    count, width = grad_ref.shape
+    conv = pair_ref[:, :chans].reshape(count, width).astype(jnp.float32)
+    back = pair_ref[:, chans:].reshape(count, width).astype(jnp.float32)
+    first = (grad_ref[...].astype(jnp.float32) * conv).astype(jnp.bfloat16)
+    second = (back * projected_ref[2].astype(jnp.float32)).astype(jnp.bfloat16)
+    third = (back * projected_ref[1].astype(jnp.float32)).astype(jnp.bfloat16)
+    out_ref[0] = first
+    out_ref[1] = second
+    out_ref[2] = third
+    low_ref[:count] = first
+    low_ref[count:] = second[: count // 2]
+    high_ref[: count // 2] = second[count // 2 :]
+    high_ref[count // 2 :] = third
+
+
+def product_kernel(rows_ref, a_ref, b_ref, c_ref, d_ref, out_ref):
+    cols = jnp.concatenate([a_ref[...], b_ref[...], c_ref[...], d_ref[...]], 1)
+    out_ref[...] = lax.dot_general(
+        rows_ref[...], cols, (((1,), (1,)), ((), ())), preferred_element_type=jnp.float32
+    ).astype(jnp.bfloat16)
+
+
+def finish_kernel(count, *refs):
+    sums = [sum(ref[...].astype(jnp.float32) for ref in refs[3 * k : 3 * k + 3]) for k in range(2)]
+    out_ref = refs[6]
+    half = count // 2
+    out_ref[0] = sums[0][:, :count]
+    out_ref[1, :, :half] = sums[0][:, count:]
+    out_ref[1, :, half:] = sums[1][:, :half]
+    out_ref[2] = sums[1][:, half:]
+
+
 def swap(x, axis):
     return lax.ppermute(x, axis, [(0, 1), (1, 0)])
 
@@ -127,72 +179,84 @@
     return lax.dynamic_index_in_dim(x, index, axis, keepdims=False)
 
 
-def exchange_rows(inputs, count_z):
-    width = inputs.shape[1]
+def after(x, *others):
+    return lax.optimization_barrier((x, *others))[0]
+
+
+def near_blocks(x):
+    beside = swap(x, "ylo")
+    return x, beside, swap(x, "core"), swap(beside, "core")
+
+
+def add(x, y):
+    return (x.astype(jnp.float32) + y.astype(jnp.float32)).astype(jnp.bfloat16)
+
+
+def ring_sums(owns, n):
+    z = lax.axis_index("z")
+    ways = (1, -1)
+    hops = [[n // 2 - (k % 2), n // 2 - 1 + (k % 2)] for k in range(len(owns))]
+    got = [[None, None] for _ in owns]
+    last = None
+    for turn in range(n // 2):
+        for k, own in enumerate(owns):
+            totals = []
+            for w, way in enumerate(ways):
+                hop = hops[k][w] - turn
+                if hop < 1:
+                    continue
+                total = pick(own, lax.rem(z + way * hop + n, n), 0)
+                if got[k][w] is not None:
+                    total = add(total, got[k][w])
+                totals.append((w, total))
+            if last is not None:
+                fixed = lax.optimization_barrier((*[t for _, t in totals], last))
+                totals = [(w, fixed[m]) for m, (w, _) in enumerate(totals)]
+            last = totals[0][1]
+            for w, total in totals:
+                perm = [(i, (i + ways[w]) % n) for i in range(n)]
+                got[k][w] = lax.ppermute(total, "z", perm)
+    return [x for k, own in enumerate(owns) for x in (pick(own, z, 0), *got[k])]
+
+
+def local(inputs, projected, filters, grad_out):
+    count, width = grad_out.shape
+    chans = filters.shape[0]
+    owners = count // chans
+    n = lax.axis_size("z")
     y, c = lax.axis_index("ylo"), lax.axis_index("core")
-    rows = inputs.shape[0] // (4 * count_z)
-    grid = inputs.reshape(2, count_z, 2, rows, width)
-    got = swap(pick(grid, 1 - c, 2), "core")
-    grid = jnp.concatenate([pick(grid, c, 2), got], -1)
-    got = swap(pick(grid, 1 - y, 0), "ylo")
-    return jnp.concatenate([pick(grid, y, 0), got], -1)
-
-
-def gather_near(x):
-    x = jnp.concatenate([x, swap(x, "core")], -1)
-    return jnp.concatenate([x, swap(x, "ylo")], -1)
-
-
-def ring_sum(rows, cols, ahead, behind):
-    n = rows.shape[0]
-    z = lax.axis_index("z")
-
-    def part(k):
-        return lax.dot_general(
-            pick(rows, lax.rem(k + n, n), 0), cols, (((1,), (1,)), ((), ())), preferred_element_type=jnp.float32
-        )
-
-    def arm(hops, way):
-        perm = [(i, (i + way) % n) for i in range(n)]
-        got = None
-        for hop in range(hops, 0, -1):
-            total = part(z + way * hop)
-            if got is not None:
-                total = total + got.astype(jnp.float32)
-            got = lax.ppermute(total.astype(jnp.bfloat16), "z", perm)
-        return got.astype(jnp.float32)
-
-    up = arm(ahead, 1)
-    down = arm(behind, -1)
-    return part(z) + up + down
-
-
-def local(inputs, projected, filters, grad_out):
-    chan_width, tok_width = grad_out.shape
-    chans = filters.shape[0]
-    owners = chan_width // chans
-    count_z = lax.axis_size("z")
-    query = projected[0].astype(jnp.float32)
-    key = projected[1].astype(jnp.float32)
-    value = projected[2].astype(jnp.float32)
-    out_grad = grad_out.astype(jnp.float32)
-    gated = (key * value).astype(jnp.bfloat16).reshape(owners, chans, tok_width)
-    carried = (out_grad * query).astype(jnp.bfloat16).reshape(owners, chans, tok_width)
-    pair = jnp.concatenate([gated, carried], 1)
+    bf16 = jnp.bfloat16
+
+    rows = inputs.shape[0] // (4 * n)
+    grid = inputs.reshape(2, n, 2, rows, width)
+    beside = swap(pick(grid, 1 - y, 0), "ylo")
+    (pair,) = vmem_call(
+        functools.partial(gate_kernel, owners, chans), [((owners, 2 * chans, width), bf16)], projected, grad_out
+    )
     pair = lax.all_to_all(pair, SEQ, split_axis=0, concat_axis=0, tiled=True)
-    rows = exchange_rows(inputs, count_z)
+    pair, beside = lax.optimization_barrier((pair, beside))
+    grid = jnp.concatenate([pick(grid, y, 0), beside], -1)
+    far = swap(pick(grid, 1 - c, 1), "core")
     pair, filter_grad = spectral(pair, filters)
+    rows_near = jnp.concatenate([pick(grid, c, 1), far], -1).reshape(n * rows, 4 * width)
+
     pair = lax.all_to_all(pair, SEQ, split_axis=0, concat_axis=0, tiled=True)
-    conv = pair[:, :chans].reshape(chan_width, tok_width).astype(jnp.float32)
-    back = pair[:, chans:].reshape(chan_width, tok_width).astype(jnp.float32)
-    proj_grad = jnp.stack([out_grad * conv, back * value, back * key]).astype(jnp.bfloat16)
-    half = chan_width // 2
-    sums = []
-    for part in range(2):
-        cols = proj_grad[:, part * half : (part + 1) * half].reshape(3 * half, tok_width)
-        total = ring_sum(rows, gather_near(cols), count_z // 2 - part, count_z // 2 - 1 + part)
-        sums.append(total.reshape(-1, 3, half))
-    return proj_grad, jnp.concatenate(sums, 2), filter_grad
+    half = 3 * count // 2
+    proj_grad, low, high = vmem_call(
+        functools.partial(grad_kernel, chans),
+        [((3, count, width), bf16), ((half, width), bf16), ((half, width), bf16)],
+        pair,
+        projected,
+        grad_out,
+    )
+    owns = []
+    for cols in (low, high):
+        (own,) = vmem_call(product_kernel, [((n * rows, half), bf16)], rows_near, *near_blocks(cols))
+        owns.append(own.reshape(n, rows, half))
+    (weight_grad,) = vmem_call(
+        functools.partial(finish_kernel, count), [((3, rows, count), jnp.float32)], *ring_sums(owns, n)
+    )
+    return proj_grad, weight_grad.transpose(1, 0, 2), filter_grad
 
 
 def solution(mesh):

time: 119 us -> 106 us (0.89)
  the two profiles are of different devices: /device:TPU:6 before, /device:TPU:4 now
where the time goes in v2:
time: 106 us
  waiting for transfers between devices  41.6 us (39%)
  starting transfers between devices  22.4 us (21%)
  blocking collectives  21.8 us (21%)
  Pallas kernels  8.97 us (8%)
  local copies, waits for them, and re-layouts  6.5 us (6%)
  other arithmetic  3.58 us (3%)
    ppermute x14, waiting for transfers between devices, ring_sums(): got[k][w] = lax.ppermute(total, 'z', perm)  22 us
    all_to_all x1, blocking collectives, local(): pair = lax.all_to_all(pair, SEQ, split_axis=0, concat_axis=0, tiled=True)  21.8 us
    ppermute x14, starting transfers between devices, ring_sums(): got[k][w] = lax.ppermute(total, 'z', perm)  14.2 us
    all_to_all x1, waiting for transfers between devices, local(): pair = lax.all_to_all(pair, SEQ, split_axis=0, concat_axis=0, tiled=True)  12 us
    ppermute x8, waiting for transfers between devices, swap(): return lax.ppermute(x, axis, [(0, 1), (1, 0)])  7.51 us
    pallas_call x5, Pallas kernels, vmem_call(): pl.pallas_call(body, out_shape=tuple((jax.ShapeDtypeStruct(shape, dtype)...  4.86 us
    ppermute x8, starting transfers between devices, swap(): return lax.ppermute(x, axis, [(0, 1), (1, 0)])  4.37 us
    unnamed x34, local copies, waits for them, and re-layouts  4.22 us
  transfers between devices with their start and end apart: 23, of which 15 were waited for; matrix products, arithmetic and copies ran while one was open for 4% of the time, Pallas kernels for 4%

profile of v2, /device:TPU:4, one launch (start us, length us, event | category | flops | bytes accessed | tf_op | source)
XLA Modules:
  0.0 105.8 jit_solution(10993641200632965434)
XLA Ops:
  0.7 1.3 %constant_dynamic-slice_fusion = (bf16[1,8,2,128,128]{4,3,2,1,0:T(8,128)(2,1)S(1)}, bf16[1,8,2,128,128]{4,3,2,1,0:T(8,128)(2,1)S(1)}) fusion(bf16[2,8,2,128,128]{4,3,2,1,0:T(8,128)(2,1)} %bitcast.66, s32[]{:T(128)S(6)} %select_n.50, s32[]{:T(128)S(6)} %select_n.49), kind=kLoop, calls=%fused_computation.36 | loop fusion | bytes 2097160 | tf_op jit(solution)/shard_map/jit(dynamic_index_in_dim)/dynamic_slice | solution.py:179
  2.0 0.0 copy-start.9
  2.0 0.0 copy-start.10
  2.0 0.0 copy-start.12
  2.1 0.0 copy-start.13
  2.1 0.0 copy-start.14
  2.1 0.0 copy-start.15
  2.2 1.7 %collective-permute-start = (bf16[8,2,128,128]{3,2,0,1:T(8,128)(2,1)S(1)}, bf16[8,2,128,128]{3,2,0,1:T(8,128)(2,1)S(1)}, u32[]{:S(2)}, u32[]{:S(2)}) collective-permute-start(bf16[8,2,128,128]{3,2,0,1:T(8,128)(2,1)S(1)} %bitcast.68), channel_id=1, source_target_pairs={{0,16},{16,0},{1,17},{17,1},{2,18},{18,2},{3,19},{19,3},{4,20},{20... | collective-permute-start | bytes 1572872 | tf_op jit(solution)/shard_map/ppermute | solution.py:175
  3.8 0.1 shard_map.139
  3.9 21.8 %all_to_all.10.pair_ref = bf16[32,32,128]{2,1,0:T(8,128)(2,1)S(1)} all-to-all(bf16[32,32,128]{2,1,0:T(8,128)(2,1)S(1)} %shard_map.139), channel_id=1, replica_groups=mesh['yhi'=2,'x'=4,'ylo'=2,'z'=8,'core'=2] {'ylo','z','core'}, dimensions={0} | all-to-all | bytes 524288 | tf_op jit(solution)/shard_map/all_to_all | solution.py:236
  25.8 4.1 %shard_map.140 = (bf16[32,32,128]{2,1,0:T(8,128)(2,1)}, f32[16,4096]{1,0:T(8,128)}) custom-call(bf16[32,32,128]{2,1,0:T(8,128)(2,1)S(1)} %all_to_all.10.pair_ref, f32[16,4096]{1,0:T(8,128)S(1)} %copy-done.2, bf16[80,96]{1,0:T(8,128)(2,1)S(1)} %copy-done.15, bf16[32,240]{1,0:T(8,128)(2,1)S(1)} %copy-done.16, f32[40,128]{1,0:T(8,128)S(1)} %copy-done.14, ...), custom_call_target="tpu_custom_call" | custom-call | tf_op jit(solution)/shard_map/pallas_call | solution.py:113
  29.9 3.9 %all-to-all-start.1 = ((bf16[32,32,128]{2,1,0:T(8,128)(2,1)}), bf16[32,32,128]{2,1,0:T(8,128)(2,1)S(1)}, u32[]{:S(2)}, u32[]{:S(2)}) async-start(bf16[32,32,128]{2,1,0:T(8,128)(2,1)} %get-tuple-element.23), calls=%async_computation.1 | async-start | bytes 524288 | tf_op jit(solution)/shard_map/all_to_all | solution.py:243
  33.9 0.9 fusion.2
  34.8 0.2 collective-permute-start.1
  35.0 12.0 %all-to-all-done.1.pair_ref = bf16[32,32,128]{2,1,0:T(8,128)(2,1)S(1)} async-done(((bf16[32,32,128]{2,1,0:T(8,128)(2,1)}), bf16[32,32,128]{2,1,0:T(8,128)(2,1)S(1)}, u32[]{:S(2)}, u32[]{:S(2)}) %all-to-all-start.1) | async-done | bytes 262176 | tf_op jit(solution)/shard_map/all_to_all | solution.py:243
  47.0 0.8 shard_map.141
  47.8 0.3 collective-permute-start.2
  48.2 1.7 %collective-permute-start.7 = (bf16[768,128]{1,0:T(8,128)(2,1)S(1)}, bf16[768,128]{1,0:T(8,128)(2,1)S(1)}, u32[]{:S(2)}, u32[]{:S(2)}) collective-permute-start(bf16[768,128]{1,0:T(8,128)(2,1)S(1)} %get-tuple-element.27.a_ref), channel_id=1, source_target_pairs={{0,16},{16,0},{1,17},{17,1},{2,18},{18,2},{3,19},{19,3},{4,20},{20... | collective-permute-start | bytes 589832 | tf_op jit(solution)/shard_map/ppermute | solution.py:175
  49.8 5.8 %collective-permute-done.2.b_ref = bf16[768,128]{1,0:T(8,128)(2,1)S(1)} collective-permute-done((bf16[768,128]{1,0:T(8,128)(2,1)S(1)}, bf16[768,128]{1,0:T(8,128)(2,1)S(1)}, u32[]{:S(2)}, u32[]{:S(2)}) %collective-permute-start.2) | collective-permute-done | bytes 196640 | tf_op jit(solution)/shard_map/ppermute | solution.py:175
  55.7 0.5 collective-permute-start.8
  56.2 1.7 %collective-permute-done.7.b_ref = bf16[768,128]{1,0:T(8,128)(2,1)S(1)} collective-permute-done((bf16[768,128]{1,0:T(8,128)(2,1)S(1)}, bf16[768,128]{1,0:T(8,128)(2,1)S(1)}, u32[]{:S(2)}, u32[]{:S(2)}) %collective-permute-start.7) | collective-permute-done | bytes 196640 | tf_op jit(solution)/shard_map/ppermute | solution.py:175
  57.9 1.1 %pad_maximum_fusion.rows_ref = bf16[1024,512]{1,0:T(8,128)(2,1)S(1)} fusion(bf16[1024,256]{1,0:T(8,128)(2,1)} %bitcast.5, bf16[1024,256]{1,0:T(8,128)(2,1)S(1)} %bitcast.65), kind=kLoop, calls=%fused_computation.4 | loop fusion | flops 2097152 | bytes 2097152 | tf_op jit(solution)/shard_map/concatenate | solution.py:241
  59.0 0.7 copy-done.5
  59.7 0.7 copy-done.7
  60.4 0.9 copy-done.4
  61.3 0.9 copy-done.6
  62.2 0.9 copy-done.8
  63.2 1.0 shard_map.142
  64.2 0.8 dynamic-slice_bitcast_fusion.3
  65.0 0.1 collective-permute-start.6
  65.1 2.0 %collective-permute-start.5 = (bf16[128,768]{1,0:T(8,128)(2,1)}, bf16[128,768]{1,0:T(8,128)(2,1)}, u32[]{:S(2)}, u32[]{:S(2)}) collective-permute-start(bf16[128,768]{1,0:T(8,128)(2,1)} %get-tuple-element.53), channel_id=1, source_target_pairs={{0,2},{2,4},{4,6},{6,8},{8,10},{10,12},{12,14},{14,0},{1,3},{3,5},... | collective-permute-start | bytes 589832 | tf_op jit(solution)/shard_map/ppermute | solution.py:218
  67.0 1.9 %shard_map.143 = bf16[1024,768]{1,0:T(8,128)(2,1)S(1)} custom-call(bf16[1024,512]{1,0:T(8,128)(2,1)S(1)} %pad_maximum_fusion.rows_ref, bf16[768,128]{1,0:T(8,128)(2,1)S(1)} %get-tuple-element.27.a_ref, bf16[768,128]{1,0:T(8,128)(2,1)S(1)} %collective-permute-done.7.b_ref, bf16[768,128]{1,0:T(8,128)(2,1)S(1)} %collective-permute-done.8.c_ref, ...), custom_call_target="tpu_custom_call" | custom-call | tf_op jit(solution)/shard_map/pallas_call | solution.py:123
  69.0 0.1 dynamic-slice_bitcast_fusion
  69.0 1.5 %collective-permute-start.13 = (bf16[128,768]{1,0:T(8,128)(2,1)S(1)}, bf16[128,768]{1,0:T(8,128)(2,1)S(1)}, u32[]{:S(2)}, u32[]{:S(2)}) collective-permute-start(bf16[128,768]{1,0:T(8,128)(2,1)S(1)} %get-tuple-element.31), channel_id=1, source_target_pairs={{0,14},{2,0},{4,2},{6,4},{8,6},{10,8},{12,10},{14,12},{1,15},{3,1}... | collective-permute-start | bytes 589832 | tf_op jit(solution)/shard_map/ppermute | solution.py:218
  70.6 0.8 collective-permute-start.12
  71.3 1.7 %collective-permute-done.6 = bf16[128,768]{1,0:T(8,128)(2,1)} collective-permute-done((bf16[128,768]{1,0:T(8,128)(2,1)}, bf16[128,768]{1,0:T(8,128)(2,1)}, u32[]{:S(2)}, u32[]{:S(2)}) %collective-permute-start.6) | collective-permute-done | bytes 196640 | tf_op jit(solution)/shard_map/ppermute | solution.py:218
  73.0 0.8 collective-permute-done.5
  73.8 1.1 %fusion.9 = (bf16[128,768]{1,0:T(8,128)(2,1)S(1)}, bf16[128,768]{1,0:T(8,128)(2,1)S(1)}) fusion(bf16[128,768]{1,0:T(8,128)(2,1)} %collective-permute-done.6, bf16[8,128,768]{2,1,0:T(8,128)(2,1)S(1)} %bitcast.61, s32[]{:T(128)S(6)} %select_n.58, bf16[128,768]{1,0:T(8,128)(2,1)} %collective-permute-done.5, s32[]{:T(128)S(6)} %select_n.56), kind=kLoop, calls=%fused_computation.23 | loop fusion | flops 786432 | bytes 1179656 | tf_op jit(solution)/shard_map/convert_element_type | solution.py:192
  75.0 1.2 %collective-permute-start.11 = (bf16[128,768]{1,0:T(8,128)(2,1)S(1)}, bf16[128,768]{1,0:T(8,128)(2,1)S(1)}, u32[]{:S(2)}, u32[]{:S(2)}) collective-permute-start(bf16[128,768]{1,0:T(8,128)(2,1)S(1)} %get-tuple-element.30), channel_id=1, source_target_pairs={{0,14},{2,0},{4,2},{6,4},{8,6},{10,8},{12,10},{14,12},{1,15},{3,1}... | collective-permute-start | bytes 589832 | tf_op jit(solution)/shard_map/ppermute | solution.py:218
  76.2 0.9 collective-permute-start.10
  77.1 1.4 %collective-permute-done.12 = bf16[128,768]{1,0:T(8,128)(2,1)S(1)} collective-permute-done((bf16[128,768]{1,0:T(8,128)(2,1)S(1)}, bf16[128,768]{1,0:T(8,128)(2,1)S(1)}, u32[]{:S(2)}, u32[]{:S(2)}) %collective-permute-start.12) | collective-permute-done | bytes 196640 | tf_op jit(solution)/shard_map/ppermute | solution.py:218
  78.5 0.1 fusion.6
  78.6 1.0 collective-permute-start.16
  79.6 1.1 %collective-permute-start.15 = (bf16[128,768]{1,0:T(8,128)(2,1)S(1)}, bf16[128,768]{1,0:T(8,128)(2,1)S(1)}, u32[]{:S(2)}, u32[]{:S(2)}) collective-permute-start(bf16[128,768]{1,0:T(8,128)(2,1)S(1)} %get-tuple-element.32), channel_id=1, source_target_pairs={{0,2},{2,4},{4,6},{6,8},{8,10},{10,12},{12,14},{14,0},{1,3},{3,5},... | collective-permute-start | bytes 589832 | tf_op jit(solution)/shard_map/ppermute | solution.py:218
  80.7 2.0 %collective-permute-done.11 = bf16[128,768]{1,0:T(8,128)(2,1)S(1)} collective-permute-done((bf16[128,768]{1,0:T(8,128)(2,1)S(1)}, bf16[128,768]{1,0:T(8,128)(2,1)S(1)}, u32[]{:S(2)}, u32[]{:S(2)}) %collective-permute-start.11) | collective-permute-done | bytes 196640 | tf_op jit(solution)/shard_map/ppermute | solution.py:218
  82.7 1.7 %collective-permute-done.10 = bf16[128,768]{1,0:T(8,128)(2,1)S(1)} collective-permute-done((bf16[128,768]{1,0:T(8,128)(2,1)S(1)}, bf16[128,768]{1,0:T(8,128)(2,1)S(1)}, u32[]{:S(2)}, u32[]{:S(2)}) %collective-permute-start.10) | collective-permute-done | bytes 196640 | tf_op jit(solution)/shard_map/ppermute | solution.py:218
  84.4 0.1 fusion.8
  84.5 0.1 collective-permute-start.14
  84.6 1.1 %collective-permute-done.16 = bf16[128,768]{1,0:T(8,128)(2,1)S(1)} collective-permute-done((bf16[128,768]{1,0:T(8,128)(2,1)S(1)}, bf16[128,768]{1,0:T(8,128)(2,1)S(1)}, u32[]{:S(2)}, u32[]{:S(2)}) %collective-permute-start.16) | collective-permute-done | bytes 196640 | tf_op jit(solution)/shard_map/ppermute | solution.py:218
  85.7 2.9 %collective-permute-done.15 = bf16[128,768]{1,0:T(8,128)(2,1)S(1)} collective-permute-done((bf16[128,768]{1,0:T(8,128)(2,1)S(1)}, bf16[128,768]{1,0:T(8,128)(2,1)S(1)}, u32[]{:S(2)}, u32[]{:S(2)}) %collective-permute-start.15) | collective-permute-done | bytes 196640 | tf_op jit(solution)/shard_map/ppermute | solution.py:218
  88.7 0.1 fusion.4
  88.8 0.1 collective-permute-start.20
  88.9 2.0 %collective-permute-start.19 = (bf16[128,768]{1,0:T(8,128)(2,1)S(1)}, bf16[128,768]{1,0:T(8,128)(2,1)S(1)}, u32[]{:S(2)}, u32[]{:S(2)}) collective-permute-start(bf16[128,768]{1,0:T(8,128)(2,1)S(1)} %get-tuple-element.35), channel_id=1, source_target_pairs={{0,2},{2,4},{4,6},{6,8},{8,10},{10,12},{12,14},{14,0},{1,3},{3,5},... | collective-permute-start | bytes 589832 | tf_op jit(solution)/shard_map/ppermute | solution.py:218
  90.9 1.3 %collective-permute-start.18 = (bf16[128,768]{1,0:T(8,128)(2,1)S(1)}, bf16[128,768]{1,0:T(8,128)(2,1)S(1)}, u32[]{:S(2)}, u32[]{:S(2)}) collective-permute-start(bf16[128,768]{1,0:T(8,128)(2,1)S(1)} %get-tuple-element.37), channel_id=1, source_target_pairs={{0,14},{2,0},{4,2},{6,4},{8,6},{10,8},{12,10},{14,12},{1,15},{3,1}... | collective-permute-start | bytes 589832 | tf_op jit(solution)/shard_map/ppermute | solution.py:218
  92.2 0.8 collective-permute-done.14
  92.9 0.1 fusion.12
  93.0 3.4 %collective-permute-done.20 = bf16[128,768]{1,0:T(8,128)(2,1)S(1)} collective-permute-done((bf16[128,768]{1,0:T(8,128)(2,1)S(1)}, bf16[128,768]{1,0:T(8,128)(2,1)S(1)}, u32[]{:S(2)}, u32[]{:S(2)}) %collective-permute-start.20) | collective-permute-done | bytes 196640 | tf_op jit(solution)/shard_map/ppermute | solution.py:218
  96.4 0.1 fusion.3
  96.5 1.4 %collective-permute-start.21 = (bf16[128,768]{1,0:T(8,128)(2,1)S(1)}, bf16[128,768]{1,0:T(8,128)(2,1)S(1)}, u32[]{:S(2)}, u32[]{:S(2)}) collective-permute-start(bf16[128,768]{1,0:T(8,128)(2,1)S(1)} %fusion.3), channel_id=1, source_target_pairs={{0,14},{2,0},{4,2},{6,4},{8,6},{10,8},{12,10},{14,12},{1,15},{3,1}... | collective-permute-start | bytes 589832 | tf_op jit(solution)/shard_map/ppermute | solution.py:218
  97.9 0.7 collective-permute-start.17
  98.6 0.7 collective-permute-done.18.refs_2_
  99.3 2.9 %collective-permute-done.21.refs_5_ = bf16[128,768]{1,0:T(8,128)(2,1)S(1)} collective-permute-done((bf16[128,768]{1,0:T(8,128)(2,1)S(1)}, bf16[128,768]{1,0:T(8,128)(2,1)S(1)}, u32[]{:S(2)}, u32[]{:S(2)}) %collective-permute-start.21) | collective-permute-done | bytes 196640 | tf_op jit(solution)/shard_map/ppermute | solution.py:218
  102.2 2.6 %collective-permute-done.17.refs_1_ = bf16[128,768]{1,0:T(8,128)(2,1)S(1)} collective-permute-done((bf16[128,768]{1,0:T(8,128)(2,1)S(1)}, bf16[128,768]{1,0:T(8,128)(2,1)S(1)}, u32[]{:S(2)}, u32[]{:S(2)}) %collective-permute-start.17) | collective-permute-done | bytes 196640 | tf_op jit(solution)/shard_map/ppermute | solution.py:218
  104.8 1.0 shard_map.144
  (36 shorter events, 0.2 us)
Async XLA Ops:
  0.6 3.2 %copy-start = (bf16[3,512,128]{2,1,0:T(8,128)(2,1)S(1)}, bf16[3,512,128]{2,1,0:T(8,128)(2,1)}, u32[]{:S(2)}) copy-start(bf16[3,512,128]{2,1,0:T(8,128)(2,1)} %projected_ref.3) | copy-start | bytes 1179652
  0.6 3.2 %copy-start.1 = (bf16[512,128]{1,0:T(8,128)(2,1)S(1)}, bf16[512,128]{1,0:T(8,128)(2,1)}, u32[]{:S(2)}) copy-start(bf16[512,128]{1,0:T(8,128)(2,1)} %grad_ref.3) | copy-start | bytes 393220
  2.0 23.7 %copy-start.2 = (f32[16,4096]{1,0:T(8,128)S(1)}, f32[16,4096]{1,0:T(8,128)}, u32[]{:S(2)}) copy-start(f32[16,4096]{1,0:T(8,128)} %filt_ref.1) | copy-start | bytes 786436
  2.0 23.7 %copy-start.9 = (bf16[256,256]{1,0:T(8,128)(2,1)S(1)}, bf16[256,256]{1,0:T(8,128)(2,1)}, u32[]{:S(2)}) copy-start(bf16[256,256]{1,0:T(8,128)(2,1)} %constant.129.clone.ul_ref) | copy-start | bytes 393220
  2.0 23.7 %copy-start.10 = (bf16[256,256]{1,0:T(8,128)(2,1)S(1)}, bf16[256,256]{1,0:T(8,128)(2,1)}, u32[]{:S(2)}) copy-start(bf16[256,256]{1,0:T(8,128)(2,1)} %constant.128.clone.uh_ref) | copy-start | bytes 393220
  2.0 23.7 %copy-start.11 = (bf16[256,256]{1,0:T(8,128)(2,1)S(1)}, bf16[256,256]{1,0:T(8,128)(2,1)}, u32[]{:S(2)}) copy-start(bf16[256,256]{1,0:T(8,128)(2,1)} %constant.127.clone.tl_ref) | copy-start | bytes 393220
  2.0 23.7 %copy-start.12 = (bf16[256,256]{1,0:T(8,128)(2,1)S(1)}, bf16[256,256]{1,0:T(8,128)(2,1)}, u32[]{:S(2)}) copy-start(bf16[256,256]{1,0:T(8,128)(2,1)} %constant.126.clone.th_ref) | copy-start | bytes 393220
  2.1 23.7 %copy-start.13 = (f32[40,128]{1,0:T(8,128)S(1)}, f32[40,128]{1,0:T(8,128)}, u32[]{:S(2)}) copy-start(f32[40,128]{1,0:T(8,128)} %constant.125.clone.ts_ref) | copy-start | bytes 61444
  2.1 23.7 %copy-start.14 = (f32[40,128]{1,0:T(8,128)S(1)}, f32[40,128]{1,0:T(8,128)}, u32[]{:S(2)}) copy-start(f32[40,128]{1,0:T(8,128)} %constant.124.clone.tc_ref) | copy-start | bytes 61444
  2.1 23.7 %copy-start.15 = (bf16[80,96]{1,0:T(8,128)(2,1)S(1)}, bf16[80,96]{1,0:T(8,128)(2,1)}, u32[]{:S(2)}) copy-start(bf16[80,96]{1,0:T(8,128)(2,1)} %constant.122.clone.lf_ref) | copy-start | bytes 46084
  2.1 23.7 %copy-start.16 = (bf16[32,240]{1,0:T(8,128)(2,1)S(1)}, bf16[32,240]{1,0:T(8,128)(2,1)}, u32[]{:S(2)}) copy-start(bf16[32,240]{1,0:T(8,128)(2,1)} %constant.123.clone.li_ref) | copy-start | bytes 46084
  2.2 23.6 %collective-permute-start = (bf16[8,2,128,128]{3,2,0,1:T(8,128)(2,1)S(1)}, bf16[8,2,128,128]{3,2,0,1:T(8,128)(2,1)S(1)}, u32[]{:S(2)}, u32[]{:S(2)}) collective-permute-start(bf16[8,2,128,128]{3,2,0,1:T(8,128)(2,1)S(1)} %bitcast.68), channel_id=1, source_target_pairs={{0,16},{16,0},{1,17},{17,1},{2,18},{18,2},{3,19},{19,3},{4,20},{20... | collective-permute-start | bytes 1572872 | tf_op jit(solution)/shard_map/ppermute | solution.py:175
  29.9 17.1 %all-to-all-start.1 = ((bf16[32,32,128]{2,1,0:T(8,128)(2,1)}), bf16[32,32,128]{2,1,0:T(8,128)(2,1)S(1)}, u32[]{:S(2)}, u32[]{:S(2)}) async-start(bf16[32,32,128]{2,1,0:T(8,128)(2,1)} %get-tuple-element.23), calls=%async_computation.1 | async-start | bytes 524288 | tf_op jit(solution)/shard_map/all_to_all | solution.py:243
  34.8 23.1 %collective-permute-start.1 = (bf16[8,128,256]{2,1,0:T(8,128)(2,1)}, bf16[8,128,256]{2,1,0:T(8,128)(2,1)}, u32[]{:S(2)}, u32[]{:S(2)}) collective-permute-start(bf16[8,128,256]{2,1,0:T(8,128)(2,1)} %get-tuple-element.56), channel_id=1, source_target_pairs={{0,1},{1,0},{2,3},{3,2},{4,5},{5,4},{6,7},{7,6},{8,9},{9,8},{10,11... | collective-permute-start | bytes 1572872 | tf_op jit(solution)/shard_map/ppermute | solution.py:175
  47.8 7.8 %collective-permute-start.2 = (bf16[768,128]{1,0:T(8,128)(2,1)S(1)}, bf16[768,128]{1,0:T(8,128)(2,1)S(1)}, u32[]{:S(2)}, u32[]{:S(2)}) collective-permute-start(bf16[768,128]{1,0:T(8,128)(2,1)S(1)} %get-tuple-element.26.a_ref), channel_id=1, source_target_pairs={{0,16},{16,0},{1,17},{17,1},{2,18},{18,2},{3,19},{19,3},{4,20},{20... | collective-permute-start | bytes 589832 | tf_op jit(solution)/shard_map/ppermute | solution.py:175
  48.2 9.7 %collective-permute-start.7 = (bf16[768,128]{1,0:T(8,128)(2,1)S(1)}, bf16[768,128]{1,0:T(8,128)(2,1)S(1)}, u32[]{:S(2)}, u32[]{:S(2)}) collective-permute-start(bf16[768,128]{1,0:T(8,128)(2,1)S(1)} %get-tuple-element.27.a_ref), channel_id=1, source_target_pairs={{0,16},{16,0},{1,17},{17,1},{2,18},{18,2},{3,19},{19,3},{4,20},{20... | collective-permute-start | bytes 589832 | tf_op jit(solution)/shard_map/ppermute | solution.py:175
  49.8 9.1 %collective-permute-start.3 = (bf16[768,128]{1,0:T(8,128)(2,1)S(1)}, bf16[768,128]{1,0:T(8,128)(2,1)S(1)}, u32[]{:S(2)}, u32[]{:S(2)}) collective-permute-start(bf16[768,128]{1,0:T(8,128)(2,1)S(1)} %get-tuple-element.26.a_ref), channel_id=1, source_target_pairs={{0,1},{1,0},{2,3},{3,2},{4,5},{5,4},{6,7},{7,6},{8,9},{9,8},{10,11... | collective-permute-start | bytes 589832 | tf_op jit(solution)/shard_map/ppermute | solution.py:175
  55.7 3.3 %copy-start.3 = (bf16[768,128]{1,0:T(8,128)(2,1)}, bf16[768,128]{1,0:T(8,128)(2,1)S(1)}, u32[]{:S(2)}) copy-start(bf16[768,128]{1,0:T(8,128)(2,1)S(1)} %collective-permute-done.2.b_ref) | copy-start | bytes 589828
  55.7 4.0 %collective-permute-start.4 = (bf16[768,128]{1,0:T(8,128)(2,1)S(1)}, bf16[768,128]{1,0:T(8,128)(2,1)S(1)}, u32[]{:S(2)}, u32[]{:S(2)}) collective-permute-start(bf16[768,128]{1,0:T(8,128)(2,1)S(1)} %collective-permute-done.2.b_ref), channel_id=1, source_target_pairs={{0,1},{1,0},{2,3},{3,2},{4,5},{5,4},{6,7},{7,6},{8,9},{9,8},{10,11... | collective-permute-start | bytes 589832 | tf_op jit(solution)/shard_map/ppermute | solution.py:175
  55.7 11.4 %collective-permute-start.8 = (bf16[768,128]{1,0:T(8,128)(2,1)S(1)}, bf16[768,128]{1,0:T(8,128)(2,1)S(1)}, u32[]{:S(2)}, u32[]{:S(2)}) collective-permute-start(bf16[768,128]{1,0:T(8,128)(2,1)S(1)} %get-tuple-element.27.a_ref), channel_id=1, source_target_pairs={{0,1},{1,0},{2,3},{3,2},{4,5},{5,4},{6,7},{7,6},{8,9},{9,8},{10,11... | collective-permute-start | bytes 589832 | tf_op jit(solution)/shard_map/ppermute | solution.py:175
  57.9 9.2 %collective-permute-start.9 = (bf16[768,128]{1,0:T(8,128)(2,1)S(1)}, bf16[768,128]{1,0:T(8,128)(2,1)}, u32[]{:S(2)}, u32[]{:S(2)}) collective-permute-start(bf16[768,128]{1,0:T(8,128)(2,1)S(1)} %collective-permute-done.7.b_ref), channel_id=1, source_target_pairs={{0,1},{1,0},{2,3},{3,2},{4,5},{5,4},{6,7},{7,6},{8,9},{9,8},{10,11... | collective-permute-start | bytes 589832 | tf_op jit(solution)/shard_map/ppermute | solution.py:175
  59.0 0.7 copy-start.5
  59.7 0.7 copy-start.7
  60.4 0.9 copy-start.4
  61.3 0.9 copy-start.6
  62.2 0.9 copy-start.8
  65.0 8.0 %collective-permute-start.6 = (bf16[128,768]{1,0:T(8,128)(2,1)}, bf16[128,768]{1,0:T(8,128)(2,1)}, u32[]{:S(2)}, u32[]{:S(2)}) collective-permute-start(bf16[128,768]{1,0:T(8,128)(2,1)} %get-tuple-element.52), channel_id=1, source_target_pairs={{0,14},{2,0},{4,2},{6,4},{8,6},{10,8},{12,10},{14,12},{1,15},{3,1}... | collective-permute-start | bytes 589832 | tf_op jit(solution)/shard_map/ppermute | solution.py:218
  65.1 8.8 %collective-permute-start.5 = (bf16[128,768]{1,0:T(8,128)(2,1)}, bf16[128,768]{1,0:T(8,128)(2,1)}, u32[]{:S(2)}, u32[]{:S(2)}) collective-permute-start(bf16[128,768]{1,0:T(8,128)(2,1)} %get-tuple-element.53), channel_id=1, source_target_pairs={{0,2},{2,4},{4,6},{6,8},{8,10},{10,12},{12,14},{14,0},{1,3},{3,5},... | collective-permute-start | bytes 589832 | tf_op jit(solution)/shard_map/ppermute | solution.py:218
  69.0 8.0 %collective-permute-start.13 = (bf16[128,768]{1,0:T(8,128)(2,1)S(1)}, bf16[128,768]{1,0:T(8,128)(2,1)S(1)}, u32[]{:S(2)}, u32[]{:S(2)}) collective-permute-start(bf16[128,768]{1,0:T(8,128)(2,1)S(1)} %get-tuple-element.31), channel_id=1, source_target_pairs={{0,14},{2,0},{4,2},{6,4},{8,6},{10,8},{12,10},{14,12},{1,15},{3,1}... | collective-permute-start | bytes 589832 | tf_op jit(solution)/shard_map/ppermute | solution.py:218
  70.6 7.9 %collective-permute-start.12 = (bf16[128,768]{1,0:T(8,128)(2,1)S(1)}, bf16[128,768]{1,0:T(8,128)(2,1)S(1)}, u32[]{:S(2)}, u32[]{:S(2)}) collective-permute-start(bf16[128,768]{1,0:T(8,128)(2,1)S(1)} %get-tuple-element.28), channel_id=1, source_target_pairs={{0,2},{2,4},{4,6},{6,8},{8,10},{10,12},{12,14},{14,0},{1,3},{3,5},... | collective-permute-start | bytes 589832 | tf_op jit(solution)/shard_map/ppermute | solution.py:218
  75.0 7.7 %collective-permute-start.11 = (bf16[128,768]{1,0:T(8,128)(2,1)S(1)}, bf16[128,768]{1,0:T(8,128)(2,1)S(1)}, u32[]{:S(2)}, u32[]{:S(2)}) collective-permute-start(bf16[128,768]{1,0:T(8,128)(2,1)S(1)} %get-tuple-element.30), channel_id=1, source_target_pairs={{0,14},{2,0},{4,2},{6,4},{8,6},{10,8},{12,10},{14,12},{1,15},{3,1}... | collective-permute-start | bytes 589832 | tf_op jit(solution)/shard_map/ppermute | solution.py:218
  76.2 8.2 %collective-permute-start.10 = (bf16[128,768]{1,0:T(8,128)(2,1)S(1)}, bf16[128,768]{1,0:T(8,128)(2,1)S(1)}, u32[]{:S(2)}, u32[]{:S(2)}) collective-permute-start(bf16[128,768]{1,0:T(8,128)(2,1)S(1)} %get-tuple-element.29), channel_id=1, source_target_pairs={{0,2},{2,4},{4,6},{6,8},{8,10},{10,12},{12,14},{14,0},{1,3},{3,5},... | collective-permute-start | bytes 589832 | tf_op jit(solution)/shard_map/ppermute | solution.py:218
  78.6 7.1 %collective-permute-start.16 = (bf16[128,768]{1,0:T(8,128)(2,1)S(1)}, bf16[128,768]{1,0:T(8,128)(2,1)S(1)}, u32[]{:S(2)}, u32[]{:S(2)}) collective-permute-start(bf16[128,768]{1,0:T(8,128)(2,1)S(1)} %get-tuple-element.34), channel_id=1, source_target_pairs={{0,14},{2,0},{4,2},{6,4},{8,6},{10,8},{12,10},{14,12},{1,15},{3,1}... | collective-permute-start | bytes 589832 | tf_op jit(solution)/shard_map/ppermute | solution.py:218
  79.6 9.0 %collective-permute-start.15 = (bf16[128,768]{1,0:T(8,128)(2,1)S(1)}, bf16[128,768]{1,0:T(8,128)(2,1)S(1)}, u32[]{:S(2)}, u32[]{:S(2)}) collective-permute-start(bf16[128,768]{1,0:T(8,128)(2,1)S(1)} %get-tuple-element.32), channel_id=1, source_target_pairs={{0,2},{2,4},{4,6},{6,8},{8,10},{10,12},{12,14},{14,0},{1,3},{3,5},... | collective-permute-start | bytes 589832 | tf_op jit(solution)/shard_map/ppermute | solution.py:218
  84.5 8.5 %collective-permute-start.14 = (bf16[128,768]{1,0:T(8,128)(2,1)S(1)}, bf16[128,768]{1,0:T(8,128)(2,1)S(1)}, u32[]{:S(2)}, u32[]{:S(2)}) collective-permute-start(bf16[128,768]{1,0:T(8,128)(2,1)S(1)} %get-tuple-element.33), channel_id=1, source_target_pairs={{0,2},{2,4},{4,6},{6,8},{8,10},{10,12},{12,14},{14,0},{1,3},{3,5},... | collective-permute-start | bytes 589832 | tf_op jit(solution)/shard_map/ppermute | solution.py:218
  88.8 7.7 %collective-permute-start.20 = (bf16[128,768]{1,0:T(8,128)(2,1)S(1)}, bf16[128,768]{1,0:T(8,128)(2,1)S(1)}, u32[]{:S(2)}, u32[]{:S(2)}) collective-permute-start(bf16[128,768]{1,0:T(8,128)(2,1)S(1)} %get-tuple-element.38), channel_id=1, source_target_pairs={{0,14},{2,0},{4,2},{6,4},{8,6},{10,8},{12,10},{14,12},{1,15},{3,1}... | collective-permute-start | bytes 589832 | tf_op jit(solution)/shard_map/ppermute | solution.py:218
  88.9 9.7 %collective-permute-start.19 = (bf16[128,768]{1,0:T(8,128)(2,1)S(1)}, bf16[128,768]{1,0:T(8,128)(2,1)S(1)}, u32[]{:S(2)}, u32[]{:S(2)}) collective-permute-start(bf16[128,768]{1,0:T(8,128)(2,1)S(1)} %get-tuple-element.35), channel_id=1, source_target_pairs={{0,2},{2,4},{4,6},{6,8},{8,10},{10,12},{12,14},{14,0},{1,3},{3,5},... | collective-permute-start | bytes 589832 | tf_op jit(solution)/shard_map/ppermute | solution.py:218
  90.9 8.4 %collective-permute-start.18 = (bf16[128,768]{1,0:T(8,128)(2,1)S(1)}, bf16[128,768]{1,0:T(8,128)(2,1)S(1)}, u32[]{:S(2)}, u32[]{:S(2)}) collective-permute-start(bf16[128,768]{1,0:T(8,128)(2,1)S(1)} %get-tuple-element.37), channel_id=1, source_target_pairs={{0,14},{2,0},{4,2},{6,4},{8,6},{10,8},{12,10},{14,12},{1,15},{3,1}... | collective-permute-start | bytes 589832 | tf_op jit(solution)/shard_map/ppermute | solution.py:218
  96.5 5.7 %collective-permute-start.21 = (bf16[128,768]{1,0:T(8,128)(2,1)S(1)}, bf16[128,768]{1,0:T(8,128)(2,1)S(1)}, u32[]{:S(2)}, u32[]{:S(2)}) collective-permute-start(bf16[128,768]{1,0:T(8,128)(2,1)S(1)} %fusion.3), channel_id=1, source_target_pairs={{0,14},{2,0},{4,2},{6,4},{8,6},{10,8},{12,10},{14,12},{1,15},{3,1}... | collective-permute-start | bytes 589832 | tf_op jit(solution)/shard_map/ppermute | solution.py:218
  97.9 6.9 %collective-permute-start.17 = (bf16[128,768]{1,0:T(8,128)(2,1)S(1)}, bf16[128,768]{1,0:T(8,128)(2,1)S(1)}, u32[]{:S(2)}, u32[]{:S(2)}) collective-permute-start(bf16[128,768]{1,0:T(8,128)(2,1)S(1)} %fusion.12), channel_id=1, source_target_pairs={{0,2},{2,4},{4,6},{6,8},{8,10},{10,12},{12,14},{14,0},{1,3},{3,5},... | collective-permute-start | bytes 589832 | tf_op jit(solution)/shard_map/ppermute | solution.py:218

commit v3 on v1

v3 whole, which is shorter than its diff:
```python
import functools
import math

import jax
import jax.numpy as jnp
import ml_dtypes
import numpy as np
from jax import lax
from jax.experimental import pallas as pl
from jax.experimental.pallas import tpu as pltpu
from jax.sharding import Mesh
from jax.sharding import PartitionSpec as P

SEQ = ("ylo", "z", "core")

def halves(table):
    high = table.astype(np.float32).astype(ml_dtypes.bfloat16)
    low = (table - high.astype(np.float64)).astype(np.float32).astype(ml_dtypes.bfloat16)
    return high, low


def tables(blocks, width):
    lead = 2 * blocks
    size = lead * width
    rows = -(-(blocks + 1) // 8) * 8
    k = np.arange(rows, dtype=np.float64)
    live = (k <= blocks).astype(np.float64)
    i = np.arange(blocks, dtype=np.float64)
    j = np.arange(width, dtype=np.float64)
    turn = 2.0 * math.pi * np.outer(k, i) / lead
    lead_fwd = np.concatenate([np.cos(turn) * live[:, None], -np.sin(turn) * live[:, None]], 0)
    weight = np.where((k == 0) | (k == blocks), 1.0, 2.0) * live / size
    lead_inv = np.concatenate([np.cos(turn).T * weight, -np.sin(turn).T * weight], 1)
    twist = 2.0 * math.pi * np.outer(k, j) / size
    tail = 2.0 * math.pi * np.outer(j, j) / width
    cos, sin = np.cos(tail), np.sin(tail)
    tail_fwd = np.block([[cos, -sin], [sin, cos]])
    fh, fl = halves(lead_fwd)
    ih, il = halves(lead_inv)
    th, tl = halves(tail_fwd)
    uh, ul = halves(tail_fwd.T.copy())
    return (
        np.concatenate([fh, fl, fh], 1),
        np.concatenate([ih, il, ih], 1),
        np.cos(twist).astype(np.float32),
        np.sin(twist).astype(np.float32),
        th,
        tl,
        uh,
        ul,
    )


def dot(a, b):
    return jnp.dot(a, b, preferred_element_type=jnp.float32)


def split(x):
    high = x.astype(jnp.bfloat16)
    return high, (x - high.astype(jnp.float32)).astype(jnp.bfloat16)


def kernel(
    chans, width, blocks, sent_ref, filt_ref, lf_ref, li_ref, tc_ref, ts_ref, th_ref, tl_ref, uh_ref, ul_ref, out_ref, taps_ref
):
    rows = tc_ref.shape[0]
    tc, ts = tc_ref[...], ts_ref[...]
    th, tl, uh, ul = th_ref[...], tl_ref[...], uh_ref[...], ul_ref[...]
    lf, li = lf_ref[...], li_ref[...]

    def flat(x):
        return pltpu.einshape("icj->i(cj)", x)

    def forward(high, low):
        if low is None:
            a = dot(lf[:, : 2 * blocks], jnp.concatenate([high, high], 0))
        else:
            a = dot(lf, jnp.concatenate([high, high, low], 0))
        parts = []
        for c in range(chans):
            ar = a[:rows, c * width : (c + 1) * width]
            ai = a[rows:, c * width : (c + 1) * width]
            parts.append(jnp.concatenate([ar * tc + ai * ts, ai * tc - ar * ts], 1))
        high, low = split(jnp.concatenate(parts, 0))
        x = dot(high, th) + dot(low, th) + dot(high, tl)
        return x[:, :width], x[:, width:]

    def inverse(re, im):
        high, low = split(jnp.concatenate([re, im], 1))
        b = dot(high, uh) + dot(low, uh) + dot(high, ul)
        parts = []
        for c in range(chans):
            br = b[c * rows : (c + 1) * rows, :width]
            bi = b[c * rows : (c + 1) * rows, width:]
            parts.append(jnp.concatenate([br * tc - bi * ts, br * ts + bi * tc], 0))
        high, low = split(jnp.concatenate(parts, 1))
        y = dot(li, jnp.concatenate([high, high, low], 0))
        return pltpu.einshape("i(cj)->icj", y, c=chans)

    def stream(s):
        return sent_ref[:, s * chans : (s + 1) * chans].astype(jnp.float32)

    def put(s, x):
        half = blocks // 2
        for i in range(blocks):
            at = i % half
            out_ref[i // half, s * chans : (s + 1) * chans, at * width : (at + 1) * width] = x[i].astype(jnp.bfloat16)

    gate = flat((stream(1) * stream(2)).astype(jnp.bfloat16).astype(jnp.float32)).astype(jnp.bfloat16)
    carr = flat((stream(3) * stream(0)).astype(jnp.bfloat16).astype(jnp.float32)).astype(jnp.bfloat16)
    filt = jnp.stack([filt_ref[:, i * width : (i + 1) * width] for i in range(blocks)], 0)
    fr, fi = forward(*split(flat(filt)))
    gr, gi = forward(gate, None)
    cr, ci = forward(carr, None)
    conv = inverse(fr * gr - fi * gi, fr * gi + fi * gr).astype(jnp.bfloat16).astype(jnp.float32)
    put(0, stream(3) * conv)
    back = inverse(fr * cr + fi * ci, fr * ci - fi * cr).astype(jnp.bfloat16).astype(jnp.float32)
    put(1, back * stream(2))
    put(2, back * stream(1))
    taps = inverse(cr * gr + ci * gi, ci * gr - cr * gi)
    for i in range(blocks):
        taps_ref[:, i * width : (i + 1) * width] = taps[i]


def vmem_call(body, outs, *args, scratch=(), place=None):
    specs = [pl.BlockSpec(memory_space=pltpu.VMEM)] * len(args)
    if place is not None:
        specs = [pl.BlockSpec(memory_space=pltpu.SMEM)] + specs
        args = (place,) + args
    return pl.pallas_call(
        body,
        out_shape=tuple(jax.ShapeDtypeStruct(shape, dtype) for shape, dtype in outs),
        in_specs=specs,
        out_specs=tuple(pl.BlockSpec(memory_space=pltpu.VMEM) for _ in outs),
        scratch_shapes=scratch,
        compiler_params=pltpu.CompilerParams(vmem_limit_bytes=48 * 1024 * 1024),
    )(*args)


def spectral(sent, filters):
    blocks, _, width = sent.shape
    chans = filters.shape[0]
    return vmem_call(
        functools.partial(kernel, chans, width, blocks),
        [((2, 3 * chans, blocks * width // 2), jnp.bfloat16), (filters.shape, jnp.float32)],
        sent,
        filters,
        *tables(blocks, width),
    )


def pack_kernel(chans, place_ref, inputs_ref, projected_ref, grad_ref, out_ref):
    owners, _, rows, width = inputs_ref.shape
    for s in range(3):
        out_ref[:, s * chans : (s + 1) * chans] = projected_ref[s].reshape(owners, chans, width)
    out_ref[:, 3 * chans : 4 * chans] = grad_ref[...].reshape(owners, chans, width)
    out_ref[:, 4 * chans :] = inputs_ref[:, place_ref[3]]


def rows_kernel(place_ref, *refs):
    x = place_ref[3]
    for refs, out_ref in ((refs[:5], refs[10]), (refs[5:10], refs[11])):
        own_ref, up_ref, down_ref, first_ref, second_ref = refs
        _, blocks, rows, width = own_ref.shape
        count = out_ref.shape[1] // rows
        for shift, parts in (
            (0, (own_ref[0], own_ref[1])),
            (count - 1, (up_ref[0], up_ref[1])),
            (1, (down_ref[0], down_ref[1])),
            (2, (first_ref[...], second_ref[...])),
        ):
            at = pl.multiple_of(lax.rem(x + shift, count) * rows, rows)
            for y in range(2):
                for i in range(blocks):
                    out_ref[y, pl.ds(at, rows), i * width : (i + 1) * width] = parts[y][i]


def product_kernel(split_last, place_ref, near_ref, far_ref, *refs):
    blocks, outs = refs[:-4], refs[-4:]
    y, z, c = place_ref[0], place_ref[1], place_ref[2]
    if split_last:
        halves = [[r[h] for r in blocks[:-2]] + [blocks[-2 + h][...]] for h in range(2)]
    else:
        halves = [[r[h] for r in blocks] for h in range(2)]
    halves = [jnp.concatenate(h, 0) for h in halves]
    length = halves[0].shape[1]
    rows = halves[0].shape[0]
    width = near_ref.shape[1]
    whole = blocks[:-2] if split_last else blocks
    count = rows // (len(whole) + (1 if split_last else 0))
    for rc, ref in enumerate((near_ref, far_ref)):
        total = None
        for h in range(2):
            x = jnp.concatenate([ref[0, :, h * length : (h + 1) * length], ref[1, :, h * length : (h + 1) * length]], 0)
            part = lax.dot_general(halves[h], x, (((1,), (1,)), ((), ())), preferred_element_type=jnp.float32)
            total = part if total is None else total + part
        total = total.astype(jnp.bfloat16)
        for ry in range(2):
            out_ref = outs[2 * ry + rc]
            out_ref[:rows] = total[:, ry * width : (ry + 1) * width]
            half = lax.rem(y + ry, 2)
            at = pl.multiple_of((2 * z + lax.rem(c + rc, 2)) * width, width)
            for k, ref_k in enumerate(whole):
                out_ref[rows + k * count : rows + (k + 1) * count] = ref_k[half, :, pl.ds(at, width)]
            if split_last:

                @pl.when(half == 0)
                def _():
                    out_ref[2 * rows - count :] = blocks[-2][:, pl.ds(at, width)]

                @pl.when(half == 1)
                def _():
                    out_ref[2 * rows - count :] = blocks[-1][:, pl.ds(at, width)]


def finish_kernel(chans, n, shifts, place_ref, *refs):
    groups, (proj_ref, weight_ref, turned_ref) = refs[:-3], refs[-3:]
    y, z, c = place_ref[0], place_ref[1], place_ref[2]
    for g, shift_list in enumerate(shifts):
        rows = 3 * chans * len(shift_list)
        for near in range(4):
            ref = groups[4 * g + near]
            there = lax.rem(y + near // 2, 2) * 2 * n + lax.rem(c + near % 2, 2)
            for m, shift in enumerate(shift_list):
                at = pl.multiple_of((there + 2 * lax.rem(z + shift, n)) * chans, chans)
                for s in range(3):
                    row = (3 * m + s) * chans
                    turned_ref[s, pl.ds(at, chans), :] = ref[row : row + chans, :].astype(jnp.float32)
                    proj_ref[s, pl.ds(at, chans), :] = ref[rows + row : rows + row + chans, :]
    for s in range(3):
        weight_ref[s] = turned_ref[s].T


def shift_by(x, axis, way):
    n = lax.axis_size(axis)
    return lax.ppermute(x, axis, [(i, (i + way) % n) for i in range(n)])


def swap(x, axis):
    return lax.ppermute(x, axis, [(0, 1), (1, 0)])


def after(x, *others):
    return lax.optimization_barrier((x, *others))[0]


def trade(parts):
    across = lax.ppermute(parts[3], ("ylo", "core"), [(0, 3), (1, 2), (2, 1), (3, 0)])
    return parts[0], swap(parts[1], "core"), swap(parts[2], "ylo"), across


def local(inputs, projected, filters, grad_out):
    count, width = grad_out.shape
    chans = filters.shape[0]
    owners = count // chans
    n = lax.axis_size("z")
    n_x = lax.axis_size("x")
    bf16 = jnp.bfloat16
    place = jnp.stack([lax.axis_index(a) for a in ("ylo", "z", "core", "x")]).astype(jnp.int32)
    rows = inputs.shape[0] // (owners * n_x)

    (sent,) = vmem_call(
        functools.partial(pack_kernel, chans),
        [((owners, 4 * chans + rows, width), bf16)],
        inputs.reshape(owners, n_x, rows, width),
        projected,
        grad_out,
        place=place,
    )
    sent = lax.all_to_all(sent, SEQ, split_axis=0, concat_axis=0, tiled=True)
    own_rows = sent[:, 4 * chans :]
    both_rows = jnp.stack([own_rows, swap(own_rows, "ylo")])

    block, filter_grad = spectral(sent, filters)
    up1, down1 = shift_by(block, "z", 1), shift_by(block, "z", -1)
    both_rows = after(both_rows, block)
    x_up, x_down = shift_by(both_rows, "x", 1), shift_by(both_rows, "x", -1)
    up1, down1, both_rows = lax.optimization_barrier((up1, down1, both_rows))
    up2, down2 = shift_by(up1, "z", 1), shift_by(down1, "z", -1)
    x_up, x_down, up1, down1 = lax.optimization_barrier((x_up, x_down, up1, down1))
    x_first, x_second = shift_by(x_up[0], "x", 1), shift_by(x_down[1], "x", -1)
    up2, down2, x_up, x_down = lax.optimization_barrier((up2, down2, x_up, x_down))
    up3, down3 = shift_by(up2, "z", 1), shift_by(down2, "z", -1)
    pieces = (both_rows, x_up, x_down, x_first, x_second)
    pieces = (*pieces, *(swap(p, "core") for p in pieces))
    near_rows, far_rows = vmem_call(
        rows_kernel, [((2, n_x * rows, owners * width), bf16)] * 2, *pieces, place=place
    )
    near_rows, far_rows, up3, down3 = lax.optimization_barrier((near_rows, far_rows, up3, down3))
    up4, down4 = shift_by(up3[0], "z", 1), shift_by(down3[1], "z", -1)

    shifts = ((0, n - 1, 1, n - 2, 2), (n - 3, 3, n // 2))
    groups = []
    for k, blocks in enumerate(((block, up1, down1, up2, down2), (up3, down3, up4, down4))):
        if groups:
            blocks = lax.optimization_barrier((*blocks, *groups[:1]))[:-1]
        size = 6 * chans * len(shifts[k])
        parts = vmem_call(
            functools.partial(product_kernel, k == 1),
            [((size, width), bf16)] * 4,
            near_rows,
            far_rows,
            *blocks,
            place=place,
        )
        groups += trade(parts)
    proj_grad, weight_grad = vmem_call(
        functools.partial(finish_kernel, chans, n, shifts),
        [((3, count, width), bf16), ((3, n_x * rows, count), jnp.float32)],
        *groups,
        scratch=[pltpu.VMEM((3, count, width), jnp.float32)],
        place=place,
    )
    return proj_grad, weight_grad.transpose(1, 0, 2), filter_grad


def solution(mesh):
    fine = Mesh(mesh.devices.reshape(2, 4, 2, 8, 2), ("yhi", "x", "ylo", "z", "core"))
    tp = ("yhi", "x")
    in_specs = (P(None, SEQ), P(None, tp, SEQ), P(tp + SEQ, None), P(tp, SEQ))
    out_specs = (P(None, tp, SEQ), P(SEQ, None, tp), P(tp + SEQ, None))
    return jax.shard_map(local, mesh=fine, in_specs=in_specs, out_specs=out_specs, check_vma=False)
```

time: 119 us -> 109 us (0.916)
  the two profiles are of different devices: /device:TPU:6 before, /device:TPU:1 now
where the time goes in v3:
time: 109 us; the launch traced here: 108 us
  blocking collectives  32.2 us (30%)
  starting transfers between devices  31 us (28%)
  waiting for transfers between devices  23.5 us (22%)
  Pallas kernels  16 us (15%)
  local copies, waits for them, and re-layouts  4.9 us (4%)
    all_to_all x1, blocking collectives, local(): sent = lax.all_to_all(sent, SEQ, split_axis=0, concat_axis=0, tiled=True)  32.2 us
    ppermute x12, waiting for transfers between devices, shift_by(): return lax.ppermute(x, axis, [(i, (i + way) % n) for i in range(n)])  18.5 us
    ppermute x12, starting transfers between devices, shift_by(): return lax.ppermute(x, axis, [(i, (i + way) % n) for i in range(n)])  18 us
    pallas_call x6, Pallas kernels, vmem_call(): pl.pallas_call(body, out_shape=tuple((jax.ShapeDtypeStruct(shape, dtype)...  16 us
    ppermute x10, starting transfers between devices, swap(): return lax.ppermute(x, axis, [(0, 1), (1, 0)])  9.78 us
    unnamed x28, local copies, waits for them, and re-layouts  4.77 us
    ppermute x2, starting transfers between devices, trade(): lax.ppermute(parts[3], ('ylo', 'core'), [(0, 3), (1, 2), (2, 1), (3, 0)])  3.22 us
    ppermute x2, waiting for transfers between devices, trade(): lax.ppermute(parts[3], ('ylo', 'core'), [(0, 3), (1, 2), (2, 1), (3, 0)])  2.62 us
  transfers between devices with their start and end apart: 24, of which 8 were waited for; matrix products, arithmetic and copies ran while one was open for 0% of the time, Pallas kernels for 13%

profile of v3, /device:TPU:1, one launch (start us, length us, event | category | flops | bytes accessed | tf_op | source)
XLA Modules:
  0.0 108.5 jit_solution(12234760330184778255)
XLA Ops:
  0.6 0.1 pad_add_fusion.place_ref
  0.7 1.2 %copy-done.2 = bf16[4096,128]{1,0:T(8,128)(2,1)S(1)} copy-done((bf16[4096,128]{1,0:T(8,128)(2,1)S(1)}, bf16[4096,128]{1,0:T(8,128)(2,1)}, u32[]{:S(2)}) %copy-start.2) | copy-done | bytes 1048600
  1.9 1.0 copy-done.3
  2.9 0.9 copy-done.5
  3.9 0.0 copy-start.9
  3.9 0.0 copy-start.10
  3.9 0.0 copy-start.11
  3.9 0.0 copy-start.12
  3.9 0.0 copy-start.13
  3.9 0.6 shard_map.139
  4.5 32.2 %all_to_all.5.sent_ref = bf16[32,96,128]{2,1,0:T(8,128)(2,1)S(1)} all-to-all(bf16[32,96,128]{2,1,0:T(8,128)(2,1)S(1)} %shard_map.139), channel_id=1, replica_groups=mesh['yhi'=2,'x'=4,'ylo'=2,'z'=8,'core'=2] {'ylo','z','core'}, dimensions={0} | all-to-all | bytes 1572864 | tf_op jit(solution)/shard_map/all_to_all | solution.py:270
  36.7 0.1 slice_bitcast_fusion.4
  36.8 1.3 %collective-permute-start.2 = (bf16[32,32,128]{2,1,0:T(8,128)(2,1)S(1)}, bf16[32,32,128]{2,1,0:T(8,128)(2,1)S(1)}, u32[]{:S(2)}, u32[]{:S(2)}) collective-permute-start(bf16[32,32,128]{2,1,0:T(8,128)(2,1)S(1)} %get-tuple-element.72), channel_id=1, source_target_pairs={{0,16},{16,0},{1,17},{17,1},{2,18},{18,2},{3,19},{19,3},{4,20},{20... | collective-permute-start | bytes 786440 | tf_op jit(solution)/shard_map/ppermute | solution.py:240
  38.1 4.2 %shard_map.140 = (bf16[2,48,2048]{2,1,0:T(8,128)(2,1)S(1)}, f32[16,4096]{1,0:T(8,128)}) custom-call(bf16[32,96,128]{2,1,0:T(8,128)(2,1)S(1)} %all_to_all.5.sent_ref, f32[16,4096]{1,0:T(8,128)S(1)} %copy-done.4, bf16[80,96]{1,0:T(8,128)(2,1)S(1)} %copy-done.10, bf16[32,240]{1,0:T(8,128)(2,1)S(1)} %copy-done.13, f32[40,128]{1,0:T(8,128)S(1)} %copy-done.11, ...), custom_call_target="tpu_custom_call" | custom-call | tf_op jit(solution)/shard_map/pallas_call | solution.py:130
  42.3 0.0 collective-permute-done.2
  42.3 0.1 pad_maximum_fusion.refs_0_
  42.3 1.3 %collective-permute-start.5 = (bf16[2,32,32,128]{3,2,1,0:T(8,128)(2,1)S(1)}, bf16[2,32,32,128]{3,2,1,0:T(8,128)(2,1)S(1)}, u32[]{:S(2)}, u32[]{:S(2)}) collective-permute-start(bf16[2,32,32,128]{3,2,1,0:T(8,128)(2,1)S(1)} %pad_maximum_fusion.refs_0_), channel_id=1, source_target_pairs={{0,32},{32,64},{64,96},{96,0},{1,33},{33,65},{65,97},{97,1},{2,34}... | collective-permute-start | bytes 1572872 | tf_op jit(solution)/shard_map/ppermute | solution.py:236
  43.6 1.5 %collective-permute-start.6 = (bf16[2,32,32,128]{3,2,1,0:T(8,128)(2,1)S(1)}, bf16[2,32,32,128]{3,2,1,0:T(8,128)(2,1)S(1)}, u32[]{:S(2)}, u32[]{:S(2)}) collective-permute-start(bf16[2,32,32,128]{3,2,1,0:T(8,128)(2,1)S(1)} %pad_maximum_fusion.refs_0_), channel_id=1, source_target_pairs={{0,96},{32,0},{64,32},{96,64},{1,97},{33,1},{65,33},{97,65},{2,98}... | collective-permute-start | bytes 1572872 | tf_op jit(solution)/shard_map/ppermute | solution.py:236
  45.1 4.2 %collective-permute-start = (bf16[2,48,2048]{2,1,0:T(8,128)(2,1)S(1)}, bf16[2,48,2048]{2,1,0:T(8,128)(2,1)S(1)}, u32[]{:S(2)}, u32[]{:S(2)}) collective-permute-start(bf16[2,48,2048]{2,1,0:T(8,128)(2,1)S(1)} %get-tuple-element.37.refs_0_), channel_id=1, source_target_pairs={{0,2},{2,4},{4,6},{6,8},{8,10},{10,12},{12,14},{14,0},{1,3},{3,5},... | collective-permute-start | bytes 1179656 | tf_op jit(solution)/shard_map/ppermute | solution.py:236
  49.3 0.0 collective-permute-start.1
  49.3 5.9 %collective-permute-done.refs_1_ = bf16[2,48,2048]{2,1,0:T(8,128)(2,1)S(1)} collective-permute-done((bf16[2,48,2048]{2,1,0:T(8,128)(2,1)S(1)}, bf16[2,48,2048]{2,1,0:T(8,128)(2,1)S(1)}, u32[]{:S(2)}, u32[]{:S(2)}) %collective-permute-start) | collective-permute-done | bytes 393248 | tf_op jit(solution)/shard_map/ppermute | solution.py:236
  55.3 1.9 %collective-permute-done.1.refs_2_ = bf16[2,48,2048]{2,1,0:T(8,128)(2,1)S(1)} collective-permute-done((bf16[2,48,2048]{2,1,0:T(8,128)(2,1)S(1)}, bf16[2,48,2048]{2,1,0:T(8,128)(2,1)S(1)}, u32[]{:S(2)}, u32[]{:S(2)}) %collective-permute-start.1) | collective-permute-done | bytes 393248 | tf_op jit(solution)/shard_map/ppermute | solution.py:236
  57.2 0.3 collective-permute-start.3
  57.5 2.4 %collective-permute-start.4 = (bf16[2,48,2048]{2,1,0:T(8,128)(2,1)S(1)}, bf16[2,48,2048]{2,1,0:T(8,128)(2,1)S(1)}, u32[]{:S(2)}, u32[]{:S(2)}) collective-permute-start(bf16[2,48,2048]{2,1,0:T(8,128)(2,1)S(1)} %collective-permute-done.1.refs_2_), channel_id=1, source_target_pairs={{0,14},{2,0},{4,2},{6,4},{8,6},{10,8},{12,10},{14,12},{1,15},{3,1}... | collective-permute-start | bytes 1179656 | tf_op jit(solution)/shard_map/ppermute | solution.py:236
  59.9 4.5 %collective-permute-start.9 = (bf16[2,32,32,128]{3,2,1,0:T(8,128)(2,1)S(1)}, bf16[2,32,32,128]{3,2,1,0:T(8,128)(2,1)S(1)}, u32[]{:S(2)}, u32[]{:S(2)}) collective-permute-start(bf16[2,32,32,128]{3,2,1,0:T(8,128)(2,1)S(1)} %pad_maximum_fusion.refs_0_), channel_id=1, source_target_pairs={{0,1},{1,0},{2,3},{3,2},{4,5},{5,4},{6,7},{7,6},{8,9},{9,8},{10,11... | collective-permute-start | bytes 1572872 | tf_op jit(solution)/shard_map/ppermute | solution.py:240
  64.3 0.0 collective-permute-done.5.refs_1_
  64.3 0.0 collective-permute-done.6.refs_2_
  64.4 0.1 collective-permute-start.7
  64.5 2.7 %collective-permute-start.8 = (bf16[32,32,128]{2,1,0:T(8,128)(2,1)S(1)}, bf16[32,32,128]{2,1,0:T(8,128)(2,1)S(1)}, u32[]{:S(2)}, u32[]{:S(2)}) collective-permute-start(bf16[32,32,128]{2,1,0:T(8,128)(2,1)S(1)} %slice_bitcast_fusion), channel_id=1, source_target_pairs={{0,96},{32,0},{64,32},{96,64},{1,97},{33,1},{65,33},{97,65},{2,98}... | collective-permute-start | bytes 786440 | tf_op jit(solution)/shard_map/ppermute | solution.py:236
  67.2 0.0 collective-permute-done.3.refs_3_
  67.2 0.0 collective-permute-done.4.refs_4_
  67.2 6.4 %collective-permute-done.7.refs_3_ = bf16[32,32,128]{2,1,0:T(8,128)(2,1)S(1)} collective-permute-done((bf16[32,32,128]{2,1,0:T(8,128)(2,1)S(1)}, bf16[32,32,128]{2,1,0:T(8,128)(2,1)S(1)}, u32[]{:S(2)}, u32[]{:S(2)}) %collective-permute-start.7) | collective-permute-done | bytes 262176 | tf_op jit(solution)/shard_map/ppermute | solution.py:236
  73.6 0.8 collective-permute-start.12
  74.4 0.0 collective-permute-start.10
  74.4 0.5 collective-permute-start.11
  74.9 0.0 collective-permute-done.9.refs_5_
  74.9 0.0 collective-permute-start.14
  74.9 0.0 collective-permute-done.8.refs_4_
  74.9 2.7 %collective-permute-start.15 = (bf16[2,48,2048]{2,1,0:T(8,128)(2,1)S(1)}, bf16[2,48,2048]{2,1,0:T(8,128)(2,1)S(1)}, u32[]{:S(2)}, u32[]{:S(2)}) collective-permute-start(bf16[2,48,2048]{2,1,0:T(8,128)(2,1)S(1)} %collective-permute-done.4.refs_4_), channel_id=1, source_target_pairs={{0,14},{2,0},{4,2},{6,4},{8,6},{10,8},{12,10},{14,12},{1,15},{3,1}... | collective-permute-start | bytes 1179656 | tf_op jit(solution)/shard_map/ppermute | solution.py:236
  77.6 0.0 collective-permute-done.12.refs_8_
  77.6 0.6 collective-permute-start.13
  78.1 1.2 %collective-permute-done.13.refs_9_ = bf16[32,32,128]{2,1,0:T(8,128)(2,1)S(1)} collective-permute-done((bf16[32,32,128]{2,1,0:T(8,128)(2,1)S(1)}, bf16[32,32,128]{2,1,0:T(8,128)(2,1)S(1)}, u32[]{:S(2)}, u32[]{:S(2)}) %collective-permute-start.13) | collective-permute-done | bytes 262176 | tf_op jit(solution)/shard_map/ppermute | solution.py:240
  79.3 0.0 collective-permute-done.10.refs_6_
  79.3 0.0 collective-permute-done.11.refs_7_
  79.3 3.2 %shard_map.141 = (bf16[2,128,4096]{2,1,0:T(8,128)(2,1)}, bf16[2,128,4096]{2,1,0:T(8,128)(2,1)}) custom-call(s32[4]{0:T(128)S(1)} %pad_add_fusion.place_ref, bf16[2,32,32,128]{3,2,1,0:T(8,128)(2,1)S(1)} %pad_maximum_fusion.refs_0_, bf16[2,32,32,128]{3,2,1,0:T(8,128)(2,1)S(1)} %collective-permute-done.5.refs_1_, ...), custom_call_target="tpu_custom_call" | custom-call | tf_op jit(solution)/shard_map/pallas_call | solution.py:130
  82.5 4.3 %collective-permute-done.14.refs_0_ = bf16[2,48,2048]{2,1,0:T(8,128)(2,1)S(1)} collective-permute-done((bf16[2,48,2048]{2,1,0:T(8,128)(2,1)S(1)}, bf16[2,48,2048]{2,1,0:T(8,128)(2,1)S(1)}, u32[]{:S(2)}, u32[]{:S(2)}) %collective-permute-start.14) | collective-permute-done | bytes 393248 | tf_op jit(solution)/shard_map/ppermute | solution.py:236
  86.8 0.0 collective-permute-done.15.refs_1_
  86.9 0.1 collective-permute-start.19
  87.0 2.7 %collective-permute-start.20 = (bf16[48,2048]{1,0:T(8,128)(2,1)S(1)}, bf16[48,2048]{1,0:T(8,128)(2,1)S(1)}, u32[]{:S(2)}, u32[]{:S(2)}) collective-permute-start(bf16[48,2048]{1,0:T(8,128)(2,1)S(1)} %slice_bitcast_fusion.2), channel_id=1, source_target_pairs={{0,14},{2,0},{4,2},{6,4},{8,6},{10,8},{12,10},{14,12},{1,15},{3,1}... | collective-permute-start | bytes 589832 | tf_op jit(solution)/shard_map/ppermute | solution.py:236
  89.7 1.6 %copy-done = bf16[2,128,4096]{2,1,0:T(8,128)(2,1)S(1)} copy-done((bf16[2,128,4096]{2,1,0:T(8,128)(2,1)S(1)}, bf16[2,128,4096]{2,1,0:T(8,128)(2,1)}, u32[]{:S(2)}) %copy-start) | copy-done | bytes 2097176
  91.3 3.0 %shard_map.142 = (bf16[480,128]{1,0:T(8,128)(2,1)S(1)}, bf16[480,128]{1,0:T(8,128)(2,1)S(1)}, bf16[480,128]{1,0:T(8,128)(2,1)S(1)}, bf16[480,128]{1,0:T(8,128)(2,1)S(1)}) custom-call(s32[4]{0:T(128)S(1)} %pad_add_fusion.place_ref, bf16[2,128,4096]{2,1,0:T(8,128)(2,1)S(1)} %copy-done, bf16[2,128,4096]{2,1,0:T(8,128)(2,1)} %get-tuple-element.51.far_ref, ...), custom_call_target="tpu_custom_call" | custom-call | tf_op jit(solution)/shard_map/pallas_call | solution.py:130
  94.4 1.4 %collective-permute-start.16 = (bf16[480,128]{1,0:T(8,128)(2,1)S(1)}, bf16[480,128]{1,0:T(8,128)(2,1)S(1)}, u32[]{:S(2)}, u32[]{:S(2)}) collective-permute-start(bf16[480,128]{1,0:T(8,128)(2,1)S(1)} %get-tuple-element.55), channel_id=1, source_target_pairs={{0,1},{1,0},{2,3},{3,2},{4,5},{5,4},{6,7},{7,6},{8,9},{9,8},{10,11... | collective-permute-start | bytes 368648 | tf_op jit(solution)/shard_map/ppermute | solution.py:240
  95.8 0.3 collective-permute-start.17
  96.1 1.5 %collective-permute-start.18 = (bf16[480,128]{1,0:T(8,128)(2,1)S(1)}, bf16[480,128]{1,0:T(8,128)(2,1)S(1)}, u32[]{:S(2)}, u32[]{:S(2)}) collective-permute-start(bf16[480,128]{1,0:T(8,128)(2,1)S(1)} %get-tuple-element.57), channel_id=1, source_target_pairs={{0,17},{1,16},{16,1},{17,0},{2,19},{3,18},{18,3},{19,2},{4,21},{5,... | collective-permute-start | bytes 368648 | tf_op jit(solution)/shard_map/ppermute | solution.py:248
  97.5 0.0 collective-permute-done.20.refs_3_
  97.5 3.1 %shard_map.143 = (bf16[288,128]{1,0:T(8,128)(2,1)S(1)}, bf16[288,128]{1,0:T(8,128)(2,1)S(1)}, bf16[288,128]{1,0:T(8,128)(2,1)S(1)}, bf16[288,128]{1,0:T(8,128)(2,1)S(1)}) custom-call(s32[4]{0:T(128)S(1)} %pad_add_fusion.place_ref, bf16[2,128,4096]{2,1,0:T(8,128)(2,1)S(1)} %copy-done, bf16[2,128,4096]{2,1,0:T(8,128)(2,1)S(1)} %copy-done.1, ...), custom_call_target="tpu_custom_call" | custom-call | tf_op jit(solution)/shard_map/pallas_call | solution.py:130
  100.7 0.2 collective-permute-start.21
  100.9 0.2 collective-permute-start.22
  101.1 0.0 collective-permute-done.16.refs_1_
  101.1 1.7 %collective-permute-start.23 = (bf16[288,128]{1,0:T(8,128)(2,1)S(1)}, bf16[288,128]{1,0:T(8,128)(2,1)S(1)}, u32[]{:S(2)}, u32[]{:S(2)}) collective-permute-start(bf16[288,128]{1,0:T(8,128)(2,1)S(1)} %get-tuple-element.67), channel_id=1, source_target_pairs={{0,17},{1,16},{16,1},{17,0},{2,19},{3,18},{18,3},{19,2},{4,21},{5,... | collective-permute-start | bytes 221192 | tf_op jit(solution)/shard_map/ppermute | solution.py:248
  102.9 0.7 collective-permute-done.18.refs_3_
  103.6 1.1 %collective-permute-done.22.refs_6_ = bf16[288,128]{1,0:T(8,128)(2,1)S(1)} collective-permute-done((bf16[288,128]{1,0:T(8,128)(2,1)S(1)}, bf16[288,128]{1,0:T(8,128)(2,1)S(1)}, u32[]{:S(2)}, u32[]{:S(2)}) %collective-permute-start.22) | collective-permute-done | bytes 73760 | tf_op jit(solution)/shard_map/ppermute | solution.py:240
  104.8 1.9 %collective-permute-done.23.refs_7_ = bf16[288,128]{1,0:T(8,128)(2,1)S(1)} collective-permute-done((bf16[288,128]{1,0:T(8,128)(2,1)S(1)}, bf16[288,128]{1,0:T(8,128)(2,1)S(1)}, u32[]{:S(2)}, u32[]{:S(2)}) %collective-permute-start.23) | collective-permute-done | bytes 73760 | tf_op jit(solution)/shard_map/ppermute | solution.py:248
  106.7 1.8 %shard_map.144 = (bf16[3,512,128]{2,1,0:T(8,128)(2,1)}, f32[3,128,512]{2,1,0:T(8,128)}) custom-call(s32[4]{0:T(128)S(1)} %pad_add_fusion.place_ref, bf16[480,128]{1,0:T(8,128)(2,1)S(1)} %get-tuple-element.54.refs_0_, bf16[480,128]{1,0:T(8,128)(2,1)S(1)} %collective-permute-done.16.refs_1_, bf16[480,128]{1,0:T(8,128)(2,1)S(1)} %collective-permute-done.17.refs_2_, ...), custom_call_target="tpu_custom_call" | custom-call | tf_op jit(solution)/shard_map/pallas_call | solution.py:130
  (26 shorter events, 0.1 us)
Async XLA Ops:
  0.7 1.2 %copy-start.2 = (bf16[4096,128]{1,0:T(8,128)(2,1)S(1)}, bf16[4096,128]{1,0:T(8,128)(2,1)}, u32[]{:S(2)}) copy-start(bf16[4096,128]{1,0:T(8,128)(2,1)} %param.12) | copy-start | bytes 3145732
  1.9 1.0 copy-start.3
  2.9 0.9 copy-start.5
  3.8 34.2 %copy-start.4 = (f32[16,4096]{1,0:T(8,128)S(1)}, f32[16,4096]{1,0:T(8,128)}, u32[]{:S(2)}) copy-start(f32[16,4096]{1,0:T(8,128)} %filt_ref.1) | copy-start | bytes 786436
  3.8 34.2 %copy-start.6 = (bf16[256,256]{1,0:T(8,128)(2,1)S(1)}, bf16[256,256]{1,0:T(8,128)(2,1)}, u32[]{:S(2)}) copy-start(bf16[256,256]{1,0:T(8,128)(2,1)} %constant.38.clone.th_ref) | copy-start | bytes 393220
  3.8 34.2 %copy-start.7 = (bf16[256,256]{1,0:T(8,128)(2,1)S(1)}, bf16[256,256]{1,0:T(8,128)(2,1)}, u32[]{:S(2)}) copy-start(bf16[256,256]{1,0:T(8,128)(2,1)} %constant.39.clone.tl_ref) | copy-start | bytes 393220
  3.8 34.2 %copy-start.8 = (bf16[256,256]{1,0:T(8,128)(2,1)S(1)}, bf16[256,256]{1,0:T(8,128)(2,1)}, u32[]{:S(2)}) copy-start(bf16[256,256]{1,0:T(8,128)(2,1)} %constant.40.clone.uh_ref) | copy-start | bytes 393220
  3.9 34.2 %copy-start.9 = (bf16[256,256]{1,0:T(8,128)(2,1)S(1)}, bf16[256,256]{1,0:T(8,128)(2,1)}, u32[]{:S(2)}) copy-start(bf16[256,256]{1,0:T(8,128)(2,1)} %constant.41.clone.ul_ref) | copy-start | bytes 393220
  3.9 34.2 %copy-start.10 = (bf16[80,96]{1,0:T(8,128)(2,1)S(1)}, bf16[80,96]{1,0:T(8,128)(2,1)}, u32[]{:S(2)}) copy-start(bf16[80,96]{1,0:T(8,128)(2,1)} %constant.34.clone.lf_ref) | copy-start | bytes 46084
  3.9 34.2 %copy-start.11 = (f32[40,128]{1,0:T(8,128)S(1)}, f32[40,128]{1,0:T(8,128)}, u32[]{:S(2)}) copy-start(f32[40,128]{1,0:T(8,128)} %constant.36.clone.tc_ref) | copy-start | bytes 61444
  3.9 34.2 %copy-start.12 = (f32[40,128]{1,0:T(8,128)S(1)}, f32[40,128]{1,0:T(8,128)}, u32[]{:S(2)}) copy-start(f32[40,128]{1,0:T(8,128)} %constant.37.clone.ts_ref) | copy-start | bytes 61444
  3.9 34.2 %copy-start.13 = (bf16[32,240]{1,0:T(8,128)(2,1)S(1)}, bf16[32,240]{1,0:T(8,128)(2,1)}, u32[]{:S(2)}) copy-start(bf16[32,240]{1,0:T(8,128)(2,1)} %constant.35.clone.li_ref) | copy-start | bytes 46084
  36.8 5.5 %collective-permute-start.2 = (bf16[32,32,128]{2,1,0:T(8,128)(2,1)S(1)}, bf16[32,32,128]{2,1,0:T(8,128)(2,1)S(1)}, u32[]{:S(2)}, u32[]{:S(2)}) collective-permute-start(bf16[32,32,128]{2,1,0:T(8,128)(2,1)S(1)} %get-tuple-element.72), channel_id=1, source_target_pairs={{0,16},{16,0},{1,17},{17,1},{2,18},{18,2},{3,19},{19,3},{4,20},{20... | collective-permute-start | bytes 786440 | tf_op jit(solution)/shard_map/ppermute | solution.py:240
  42.3 22.0 %collective-permute-start.5 = (bf16[2,32,32,128]{3,2,1,0:T(8,128)(2,1)S(1)}, bf16[2,32,32,128]{3,2,1,0:T(8,128)(2,1)S(1)}, u32[]{:S(2)}, u32[]{:S(2)}) collective-permute-start(bf16[2,32,32,128]{3,2,1,0:T(8,128)(2,1)S(1)} %pad_maximum_fusion.refs_0_), channel_id=1, source_target_pairs={{0,32},{32,64},{64,96},{96,0},{1,33},{33,65},{65,97},{97,1},{2,34}... | collective-permute-start | bytes 1572872 | tf_op jit(solution)/shard_map/ppermute | solution.py:236
  43.6 20.7 %collective-permute-start.6 = (bf16[2,32,32,128]{3,2,1,0:T(8,128)(2,1)S(1)}, bf16[2,32,32,128]{3,2,1,0:T(8,128)(2,1)S(1)}, u32[]{:S(2)}, u32[]{:S(2)}) collective-permute-start(bf16[2,32,32,128]{3,2,1,0:T(8,128)(2,1)S(1)} %pad_maximum_fusion.refs_0_), channel_id=1, source_target_pairs={{0,96},{32,0},{64,32},{96,64},{1,97},{33,1},{65,33},{97,65},{2,98}... | collective-permute-start | bytes 1572872 | tf_op jit(solution)/shard_map/ppermute | solution.py:236
  45.1 10.2 %collective-permute-start = (bf16[2,48,2048]{2,1,0:T(8,128)(2,1)S(1)}, bf16[2,48,2048]{2,1,0:T(8,128)(2,1)S(1)}, u32[]{:S(2)}, u32[]{:S(2)}) collective-permute-start(bf16[2,48,2048]{2,1,0:T(8,128)(2,1)S(1)} %get-tuple-element.37.refs_0_), channel_id=1, source_target_pairs={{0,2},{2,4},{4,6},{6,8},{8,10},{10,12},{12,14},{14,0},{1,3},{3,5},... | collective-permute-start | bytes 1179656 | tf_op jit(solution)/shard_map/ppermute | solution.py:236
  49.3 7.8 %collective-permute-start.1 = (bf16[2,48,2048]{2,1,0:T(8,128)(2,1)S(1)}, bf16[2,48,2048]{2,1,0:T(8,128)(2,1)S(1)}, u32[]{:S(2)}, u32[]{:S(2)}) collective-permute-start(bf16[2,48,2048]{2,1,0:T(8,128)(2,1)S(1)} %get-tuple-element.37.refs_0_), channel_id=1, source_target_pairs={{0,14},{2,0},{4,2},{6,4},{8,6},{10,8},{12,10},{14,12},{1,15},{3,1}... | collective-permute-start | bytes 1179656 | tf_op jit(solution)/shard_map/ppermute | solution.py:236
  57.2 10.0 %collective-permute-start.3 = (bf16[2,48,2048]{2,1,0:T(8,128)(2,1)S(1)}, bf16[2,48,2048]{2,1,0:T(8,128)(2,1)S(1)}, u32[]{:S(2)}, u32[]{:S(2)}) collective-permute-start(bf16[2,48,2048]{2,1,0:T(8,128)(2,1)S(1)} %collective-permute-done.refs_1_), channel_id=1, source_target_pairs={{0,2},{2,4},{4,6},{6,8},{8,10},{10,12},{12,14},{14,0},{1,3},{3,5},... | collective-permute-start | bytes 1179656 | tf_op jit(solution)/shard_map/ppermute | solution.py:236
  57.5 9.7 %collective-permute-start.4 = (bf16[2,48,2048]{2,1,0:T(8,128)(2,1)S(1)}, bf16[2,48,2048]{2,1,0:T(8,128)(2,1)S(1)}, u32[]{:S(2)}, u32[]{:S(2)}) collective-permute-start(bf16[2,48,2048]{2,1,0:T(8,128)(2,1)S(1)} %collective-permute-done.1.refs_2_), channel_id=1, source_target_pairs={{0,14},{2,0},{4,2},{6,4},{8,6},{10,8},{12,10},{14,12},{1,15},{3,1}... | collective-permute-start | bytes 1179656 | tf_op jit(solution)/shard_map/ppermute | solution.py:236
  59.9 15.0 %collective-permute-start.9 = (bf16[2,32,32,128]{3,2,1,0:T(8,128)(2,1)S(1)}, bf16[2,32,32,128]{3,2,1,0:T(8,128)(2,1)S(1)}, u32[]{:S(2)}, u32[]{:S(2)}) collective-permute-start(bf16[2,32,32,128]{3,2,1,0:T(8,128)(2,1)S(1)} %pad_maximum_fusion.refs_0_), channel_id=1, source_target_pairs={{0,1},{1,0},{2,3},{3,2},{4,5},{5,4},{6,7},{7,6},{8,9},{9,8},{10,11... | collective-permute-start | bytes 1572872 | tf_op jit(solution)/shard_map/ppermute | solution.py:240
  64.4 9.2 %collective-permute-start.7 = (bf16[32,32,128]{2,1,0:T(8,128)(2,1)S(1)}, bf16[32,32,128]{2,1,0:T(8,128)(2,1)S(1)}, u32[]{:S(2)}, u32[]{:S(2)}) collective-permute-start(bf16[32,32,128]{2,1,0:T(8,128)(2,1)S(1)} %slice_bitcast_fusion.1), channel_id=1, source_target_pairs={{0,32},{32,64},{64,96},{96,0},{1,33},{33,65},{65,97},{97,1},{2,34}... | collective-permute-start | bytes 786440 | tf_op jit(solution)/shard_map/ppermute | solution.py:236
  64.5 10.4 %collective-permute-start.8 = (bf16[32,32,128]{2,1,0:T(8,128)(2,1)S(1)}, bf16[32,32,128]{2,1,0:T(8,128)(2,1)S(1)}, u32[]{:S(2)}, u32[]{:S(2)}) collective-permute-start(bf16[32,32,128]{2,1,0:T(8,128)(2,1)S(1)} %slice_bitcast_fusion), channel_id=1, source_target_pairs={{0,96},{32,0},{64,32},{96,64},{1,97},{33,1},{65,33},{97,65},{2,98}... | collective-permute-start | bytes 786440 | tf_op jit(solution)/shard_map/ppermute | solution.py:236
  73.6 4.0 %collective-permute-start.12 = (bf16[32,32,128]{2,1,0:T(8,128)(2,1)S(1)}, bf16[32,32,128]{2,1,0:T(8,128)(2,1)S(1)}, u32[]{:S(2)}, u32[]{:S(2)}) collective-permute-start(bf16[32,32,128]{2,1,0:T(8,128)(2,1)S(1)} %collective-permute-done.7.refs_3_), channel_id=1, source_target_pairs={{0,1},{1,0},{2,3},{3,2},{4,5},{5,4},{6,7},{7,6},{8,9},{9,8},{10,11... | collective-permute-start | bytes 786440 | tf_op jit(solution)/shard_map/ppermute | solution.py:240
  74.4 4.9 %collective-permute-start.10 = (bf16[2,32,32,128]{3,2,1,0:T(8,128)(2,1)S(1)}, bf16[2,32,32,128]{3,2,1,0:T(8,128)(2,1)S(1)}, u32[]{:S(2)}, u32[]{:S(2)}) collective-permute-start(bf16[2,32,32,128]{3,2,1,0:T(8,128)(2,1)S(1)} %collective-permute-done.5.refs_1_), channel_id=1, source_target_pairs={{0,1},{1,0},{2,3},{3,2},{4,5},{5,4},{6,7},{7,6},{8,9},{9,8},{10,11... | collective-permute-start | bytes 1572872 | tf_op jit(solution)/shard_map/ppermute | solution.py:240
  74.4 4.9 %collective-permute-start.11 = (bf16[2,32,32,128]{3,2,1,0:T(8,128)(2,1)S(1)}, bf16[2,32,32,128]{3,2,1,0:T(8,128)(2,1)S(1)}, u32[]{:S(2)}, u32[]{:S(2)}) collective-permute-start(bf16[2,32,32,128]{3,2,1,0:T(8,128)(2,1)S(1)} %collective-permute-done.6.refs_2_), channel_id=1, source_target_pairs={{0,1},{1,0},{2,3},{3,2},{4,5},{5,4},{6,7},{7,6},{8,9},{9,8},{10,11... | collective-permute-start | bytes 1572872 | tf_op jit(solution)/shard_map/ppermute | solution.py:240
  74.9 12.0 %collective-permute-start.14 = (bf16[2,48,2048]{2,1,0:T(8,128)(2,1)S(1)}, bf16[2,48,2048]{2,1,0:T(8,128)(2,1)S(1)}, u32[]{:S(2)}, u32[]{:S(2)}) collective-permute-start(bf16[2,48,2048]{2,1,0:T(8,128)(2,1)S(1)} %collective-permute-done.3.refs_3_), channel_id=1, source_target_pairs={{0,2},{2,4},{4,6},{6,8},{8,10},{10,12},{12,14},{14,0},{1,3},{3,5},... | collective-permute-start | bytes 1179656 | tf_op jit(solution)/shard_map/ppermute | solution.py:236
  74.9 12.0 %collective-permute-start.15 = (bf16[2,48,2048]{2,1,0:T(8,128)(2,1)S(1)}, bf16[2,48,2048]{2,1,0:T(8,128)(2,1)S(1)}, u32[]{:S(2)}, u32[]{:S(2)}) collective-permute-start(bf16[2,48,2048]{2,1,0:T(8,128)(2,1)S(1)} %collective-permute-done.4.refs_4_), channel_id=1, source_target_pairs={{0,14},{2,0},{4,2},{6,4},{8,6},{10,8},{12,10},{14,12},{1,15},{3,1}... | collective-permute-start | bytes 1179656 | tf_op jit(solution)/shard_map/ppermute | solution.py:236
  77.6 1.7 %collective-permute-start.13 = (bf16[32,32,128]{2,1,0:T(8,128)(2,1)S(1)}, bf16[32,32,128]{2,1,0:T(8,128)(2,1)S(1)}, u32[]{:S(2)}, u32[]{:S(2)}) collective-permute-start(bf16[32,32,128]{2,1,0:T(8,128)(2,1)S(1)} %collective-permute-done.8.refs_4_), channel_id=1, source_target_pairs={{0,1},{1,0},{2,3},{3,2},{4,5},{5,4},{6,7},{7,6},{8,9},{9,8},{10,11... | collective-permute-start | bytes 786440 | tf_op jit(solution)/shard_map/ppermute | solution.py:240
  86.9 10.7 %collective-permute-start.19 = (bf16[48,2048]{1,0:T(8,128)(2,1)S(1)}, bf16[48,2048]{1,0:T(8,128)(2,1)S(1)}, u32[]{:S(2)}, u32[]{:S(2)}) collective-permute-start(bf16[48,2048]{1,0:T(8,128)(2,1)S(1)} %slice_bitcast_fusion.3), channel_id=1, source_target_pairs={{0,2},{2,4},{4,6},{6,8},{8,10},{10,12},{12,14},{14,0},{1,3},{3,5},... | collective-permute-start | bytes 589832 | tf_op jit(solution)/shard_map/ppermute | solution.py:236
  87.0 10.6 %collective-permute-start.20 = (bf16[48,2048]{1,0:T(8,128)(2,1)S(1)}, bf16[48,2048]{1,0:T(8,128)(2,1)S(1)}, u32[]{:S(2)}, u32[]{:S(2)}) collective-permute-start(bf16[48,2048]{1,0:T(8,128)(2,1)S(1)} %slice_bitcast_fusion.2), channel_id=1, source_target_pairs={{0,14},{2,0},{4,2},{6,4},{8,6},{10,8},{12,10},{14,12},{1,15},{3,1}... | collective-permute-start | bytes 589832 | tf_op jit(solution)/shard_map/ppermute | solution.py:236
  89.7 1.6 %copy-start = (bf16[2,128,4096]{2,1,0:T(8,128)(2,1)S(1)}, bf16[2,128,4096]{2,1,0:T(8,128)(2,1)}, u32[]{:S(2)}) copy-start(bf16[2,128,4096]{2,1,0:T(8,128)(2,1)} %get-tuple-element.50.near_ref) | copy-start | bytes 6291460
  91.3 6.2 %copy-start.1 = (bf16[2,128,4096]{2,1,0:T(8,128)(2,1)S(1)}, bf16[2,128,4096]{2,1,0:T(8,128)(2,1)}, u32[]{:S(2)}) copy-start(bf16[2,128,4096]{2,1,0:T(8,128)(2,1)} %get-tuple-element.51.far_ref) | copy-start | bytes 6291460
  94.4 6.8 %collective-permute-start.16 = (bf16[480,128]{1,0:T(8,128)(2,1)S(1)}, bf16[480,128]{1,0:T(8,128)(2,1)S(1)}, u32[]{:S(2)}, u32[]{:S(2)}) collective-permute-start(bf16[480,128]{1,0:T(8,128)(2,1)S(1)} %get-tuple-element.55), channel_id=1, source_target_pairs={{0,1},{1,0},{2,3},{3,2},{4,5},{5,4},{6,7},{7,6},{8,9},{9,8},{10,11... | collective-permute-start | bytes 368648 | tf_op jit(solution)/shard_map/ppermute | solution.py:240
  95.8 7.1 %collective-permute-start.17 = (bf16[480,128]{1,0:T(8,128)(2,1)S(1)}, bf16[480,128]{1,0:T(8,128)(2,1)S(1)}, u32[]{:S(2)}, u32[]{:S(2)}) collective-permute-start(bf16[480,128]{1,0:T(8,128)(2,1)S(1)} %get-tuple-element.56), channel_id=1, source_target_pairs={{0,16},{16,0},{1,17},{17,1},{2,18},{18,2},{3,19},{19,3},{4,20},{20... | collective-permute-start | bytes 368648 | tf_op jit(solution)/shard_map/ppermute | solution.py:240
  96.1 7.6 %collective-permute-start.18 = (bf16[480,128]{1,0:T(8,128)(2,1)S(1)}, bf16[480,128]{1,0:T(8,128)(2,1)S(1)}, u32[]{:S(2)}, u32[]{:S(2)}) collective-permute-start(bf16[480,128]{1,0:T(8,128)(2,1)S(1)} %get-tuple-element.57), channel_id=1, source_target_pairs={{0,17},{1,16},{16,1},{17,0},{2,19},{3,18},{18,3},{19,2},{4,21},{5,... | collective-permute-start | bytes 368648 | tf_op jit(solution)/shard_map/ppermute | solution.py:248
  100.7 3.0 %collective-permute-start.21 = (bf16[288,128]{1,0:T(8,128)(2,1)S(1)}, bf16[288,128]{1,0:T(8,128)(2,1)S(1)}, u32[]{:S(2)}, u32[]{:S(2)}) collective-permute-start(bf16[288,128]{1,0:T(8,128)(2,1)S(1)} %get-tuple-element.65), channel_id=1, source_target_pairs={{0,1},{1,0},{2,3},{3,2},{4,5},{5,4},{6,7},{7,6},{8,9},{9,8},{10,11... | collective-permute-start | bytes 221192 | tf_op jit(solution)/shard_map/ppermute | solution.py:240
  100.9 3.9 %collective-permute-start.22 = (bf16[288,128]{1,0:T(8,128)(2,1)S(1)}, bf16[288,128]{1,0:T(8,128)(2,1)S(1)}, u32[]{:S(2)}, u32[]{:S(2)}) collective-permute-start(bf16[288,128]{1,0:T(8,128)(2,1)S(1)} %get-tuple-element.66), channel_id=1, source_target_pairs={{0,16},{16,0},{1,17},{17,1},{2,18},{18,2},{3,19},{19,3},{4,20},{20... | collective-permute-start | bytes 221192 | tf_op jit(solution)/shard_map/ppermute | solution.py:240
  101.1 5.5 %collective-permute-start.23 = (bf16[288,128]{1,0:T(8,128)(2,1)S(1)}, bf16[288,128]{1,0:T(8,128)(2,1)S(1)}, u32[]{:S(2)}, u32[]{:S(2)}) collective-permute-start(bf16[288,128]{1,0:T(8,128)(2,1)S(1)} %get-tuple-element.67), channel_id=1, source_target_pairs={{0,17},{1,16},{16,1},{17,0},{2,19},{3,18},{18,3},{19,2},{4,21},{5,... | collective-permute-start | bytes 221192 | tf_op jit(solution)/shard_map/ppermute | solution.py:248

commit v4 on v3

--- a/solution.py
+++ b/solution.py
@@ -133,7 +133,7 @@
         in_specs=specs,
         out_specs=tuple(pl.BlockSpec(memory_space=pltpu.VMEM) for _ in outs),
         scratch_shapes=scratch,
-        compiler_params=pltpu.CompilerParams(vmem_limit_bytes=48 * 1024 * 1024),
+        compiler_params=pltpu.CompilerParams(vmem_limit_bytes=24 * 1024 * 1024),
     )(*args)
 
 
@@ -149,91 +149,87 @@
     )
 
 
-def pack_kernel(chans, place_ref, inputs_ref, projected_ref, grad_ref, out_ref):
-    owners, _, rows, width = inputs_ref.shape
-    for s in range(3):
-        out_ref[:, s * chans : (s + 1) * chans] = projected_ref[s].reshape(owners, chans, width)
-    out_ref[:, 3 * chans : 4 * chans] = grad_ref[...].reshape(owners, chans, width)
-    out_ref[:, 4 * chans :] = inputs_ref[:, place_ref[3]]
-
-
-def rows_kernel(place_ref, *refs):
-    x = place_ref[3]
-    for refs, out_ref in ((refs[:5], refs[10]), (refs[5:10], refs[11])):
-        own_ref, up_ref, down_ref, first_ref, second_ref = refs
-        _, blocks, rows, width = own_ref.shape
-        count = out_ref.shape[1] // rows
-        for shift, parts in (
-            (0, (own_ref[0], own_ref[1])),
-            (count - 1, (up_ref[0], up_ref[1])),
-            (1, (down_ref[0], down_ref[1])),
-            (2, (first_ref[...], second_ref[...])),
-        ):
-            at = pl.multiple_of(lax.rem(x + shift, count) * rows, rows)
-            for y in range(2):
-                for i in range(blocks):
-                    out_ref[y, pl.ds(at, rows), i * width : (i + 1) * width] = parts[y][i]
-
-
-def product_kernel(split_last, place_ref, near_ref, far_ref, *refs):
+def pack_kernel(chans, inputs_ref, projected_ref, grad_ref, out_ref, sems):
+    copies = [
+        pltpu.make_async_copy(projected_ref.at[s], out_ref.at[:, s * chans : (s + 1) * chans], sems.at[s])
+        for s in range(3)
+    ]
+    copies.append(pltpu.make_async_copy(grad_ref, out_ref.at[:, 3 * chans : 4 * chans], sems.at[3]))
+    copies.append(pltpu.make_async_copy(inputs_ref.at[:, lax.axis_index("x")], out_ref.at[:, 4 * chans :], sems.at[4]))
+    for copy in copies:
+        copy.start()
+    for copy in copies:
+        copy.wait()
+
+
+def chunk(place_ref, blocks, ry, rc):
+    y, z, c = place_ref[0], place_ref[1], place_ref[2]
+    half = lax.rem(y + ry, 2)
+    at = pl.multiple_of((2 * z + lax.rem(c + rc, 2)) * 128, 128)
+    return jnp.concatenate([block[half, :, pl.ds(at, 128)] for block in blocks], 0)
+
+
+def chunk_kernel(place_ref, *refs):
     blocks, outs = refs[:-4], refs[-4:]
-    y, z, c = place_ref[0], place_ref[1], place_ref[2]
-    if split_last:
-        halves = [[r[h] for r in blocks[:-2]] + [blocks[-2 + h][...]] for h in range(2)]
-    else:
-        halves = [[r[h] for r in blocks] for h in range(2)]
-    halves = [jnp.concatenate(h, 0) for h in halves]
-    length = halves[0].shape[1]
-    rows = halves[0].shape[0]
-    width = near_ref.shape[1]
-    whole = blocks[:-2] if split_last else blocks
-    count = rows // (len(whole) + (1 if split_last else 0))
-    for rc, ref in enumerate((near_ref, far_ref)):
+    for near, out_ref in enumerate(outs):
+        out_ref[...] = chunk(place_ref, blocks, near // 2, near % 2)
+
+
+def product_kernel(with_chunks, place_ref, *refs):
+    own, first, second, third, other, other_first, other_second, other_third = refs[:8]
+    blocks, outs = refs[8:-4], refs[-4:]
+    halves = [jnp.concatenate([block[h] for block in blocks], 0) for h in range(2)]
+    rows, length = halves[0].shape
+    _, steps, part, width = own.shape
+    size = 4 * part
+    for rc, pieces in enumerate(((own, first, third, other_second), (other, second, other_third, other_first))):
         total = None
         for h in range(2):
-            x = jnp.concatenate([ref[0, :, h * length : (h + 1) * length], ref[1, :, h * length : (h + 1) * length]], 0)
-            part = lax.dot_general(halves[h], x, (((1,), (1,)), ((), ())), preferred_element_type=jnp.float32)
-            total = part if total is None else total + part
-        total = total.astype(jnp.bfloat16)
+            span = range(h * steps // 2, (h + 1) * steps // 2)
+            x = jnp.concatenate(
+                [jnp.concatenate([ref[y, i] for i in span], 1) for y in range(2) for ref in pieces], 0
+            )
+            got = lax.dot_general(halves[h], x, (((1,), (1,)), ((), ())), preferred_element_type=jnp.float32)
+            total = got if total is None else total + got
         for ry in range(2):
+            t = total[:, ry * size : (ry + 1) * size]
+            u = jnp.concatenate([t[:, :part], t[:, 3 * part :], t[:, 2 * part : 3 * part], t[:, part : 2 * part]], 1)
             out_ref = outs[2 * ry + rc]
-            out_ref[:rows] = total[:, ry * width : (ry + 1) * width]
-            half = lax.rem(y + ry, 2)
-            at = pl.multiple_of((2 * z + lax.rem(c + rc, 2)) * width, width)
-            for k, ref_k in enumerate(whole):
-                out_ref[rows + k * count : rows + (k + 1) * count] = ref_k[half, :, pl.ds(at, width)]
-            if split_last:
-
-                @pl.when(half == 0)
-                def _():
-                    out_ref[2 * rows - count :] = blocks[-2][:, pl.ds(at, width)]
-
-                @pl.when(half == 1)
-                def _():
-                    out_ref[2 * rows - count :] = blocks[-1][:, pl.ds(at, width)]
-
-
-def finish_kernel(chans, n, shifts, place_ref, *refs):
+            out_ref[:rows] = jnp.where(place_ref[2] == 0, u, t).astype(jnp.bfloat16)
+            if with_chunks:
+                out_ref[rows:] = chunk(place_ref, blocks, ry, rc)
+
+
+def finish_kernel(chans, n, slots, place_ref, *refs):
     groups, (proj_ref, weight_ref, turned_ref) = refs[:-3], refs[-3:]
-    y, z, c = place_ref[0], place_ref[1], place_ref[2]
-    for g, shift_list in enumerate(shifts):
-        rows = 3 * chans * len(shift_list)
+    y, z, c, x = (place_ref[k] for k in range(4))
+    for g, slot_list in enumerate(slots):
+        rows = 3 * chans * len(slot_list)
         for near in range(4):
-            ref = groups[4 * g + near]
-            there = lax.rem(y + near // 2, 2) * 2 * n + lax.rem(c + near % 2, 2)
-            for m, shift in enumerate(shift_list):
-                at = pl.multiple_of((there + 2 * lax.rem(z + shift, n)) * chans, chans)
+            weights = groups[8 * g + near]
+            chunks, base = (groups[4 + near], 0) if g == 0 else (weights, rows)
+            core = lax.rem(c + near % 2, 2)
+            row_y = lax.rem(y + near // 2, 2) * 2 * n
+            for m, (hops, turned) in enumerate(slot_list):
+                owner = row_y + 2 * lax.rem(z + n - hops + 2 * hops * core, n) + (1 - core if turned else core)
+                at = pl.multiple_of(owner * chans, chans)
                 for s in range(3):
                     row = (3 * m + s) * chans
-                    turned_ref[s, pl.ds(at, chans), :] = ref[row : row + chans, :].astype(jnp.float32)
-                    proj_ref[s, pl.ds(at, chans), :] = ref[rows + row : rows + row + chans, :]
+                    turned_ref[s, pl.ds(at, chans), :] = weights[row : row + chans, :].astype(jnp.float32)
+                    proj_ref[s, pl.ds(at, chans), :] = chunks[base + row : base + row + chans, :]
+    n_x = 4
+    part = weight_ref.shape[1] // n_x
     for s in range(3):
-        weight_ref[s] = turned_ref[s].T
-
-
-def shift_by(x, axis, way):
+        rows = turned_ref[s].T
+        for k in range(n_x):
+            at = pl.multiple_of(lax.rem(x + k, n_x) * part, part)
+            weight_ref[s, pl.ds(at, part), :] = rows[k * part : (k + 1) * part]
+
+
+def spread(x, axis):
     n = lax.axis_size(axis)
-    return lax.ppermute(x, axis, [(i, (i + way) % n) for i in range(n)])
+    perm = [(2 * i, 2 * ((i + 1) % n)) for i in range(n)] + [(2 * i + 1, 2 * ((i + n - 1) % n) + 1) for i in range(n)]
+    return lax.ppermute(x, (axis, "core"), perm)
 
 
 def swap(x, axis):
@@ -259,53 +255,60 @@
     place = jnp.stack([lax.axis_index(a) for a in ("ylo", "z", "core", "x")]).astype(jnp.int32)
     rows = inputs.shape[0] // (owners * n_x)
 
-    (sent,) = vmem_call(
+    sent = pl.pallas_call(
         functools.partial(pack_kernel, chans),
-        [((owners, 4 * chans + rows, width), bf16)],
+        out_shape=jax.ShapeDtypeStruct((owners, 4 * chans + rows, width), bf16),
+        in_specs=[pl.BlockSpec(memory_space=pl.ANY)] * 3,
+        out_specs=pl.BlockSpec(memory_space=pltpu.VMEM),
+        scratch_shapes=[pltpu.SemaphoreType.DMA((5,))],
+    )(
         inputs.reshape(owners, n_x, rows, width),
-        projected,
-        grad_out,
-        place=place,
+        projected.reshape(3, owners, chans, width),
+        grad_out.reshape(owners, chans, width),
     )
     sent = lax.all_to_all(sent, SEQ, split_axis=0, concat_axis=0, tiled=True)
     own_rows = sent[:, 4 * chans :]
     both_rows = jnp.stack([own_rows, swap(own_rows, "ylo")])
 
     block, filter_grad = spectral(sent, filters)
-    up1, down1 = shift_by(block, "z", 1), shift_by(block, "z", -1)
-    both_rows = after(both_rows, block)
-    x_up, x_down = shift_by(both_rows, "x", 1), shift_by(both_rows, "x", -1)
-    up1, down1, both_rows = lax.optimization_barrier((up1, down1, both_rows))
-    up2, down2 = shift_by(up1, "z", 1), shift_by(down1, "z", -1)
-    x_up, x_down, up1, down1 = lax.optimization_barrier((x_up, x_down, up1, down1))
-    x_first, x_second = shift_by(x_up[0], "x", 1), shift_by(x_down[1], "x", -1)
-    up2, down2, x_up, x_down = lax.optimization_barrier((up2, down2, x_up, x_down))
-    up3, down3 = shift_by(up2, "z", 1), shift_by(down2, "z", -1)
-    pieces = (both_rows, x_up, x_down, x_first, x_second)
-    pieces = (*pieces, *(swap(p, "core") for p in pieces))
-    near_rows, far_rows = vmem_call(
-        rows_kernel, [((2, n_x * rows, owners * width), bf16)] * 2, *pieces, place=place
-    )
-    near_rows, far_rows, up3, down3 = lax.optimization_barrier((near_rows, far_rows, up3, down3))
-    up4, down4 = shift_by(up3[0], "z", 1), shift_by(down3[1], "z", -1)
-
-    shifts = ((0, n - 1, 1, n - 2, 2), (n - 3, 3, n // 2))
-    groups = []
-    for k, blocks in enumerate(((block, up1, down1, up2, down2), (up3, down3, up4, down4))):
-        if groups:
-            blocks = lax.optimization_barrier((*blocks, *groups[:1]))[:-1]
-        size = 6 * chans * len(shifts[k])
-        parts = vmem_call(
-            functools.partial(product_kernel, k == 1),
-            [((size, width), bf16)] * 4,
-            near_rows,
-            far_rows,
-            *blocks,
-            place=place,
-        )
-        groups += trade(parts)
+    a1 = spread(block, "z")
+    turned = after(swap(block, "core"), block)
+    b1 = spread(turned, "z")
+    a1 = after(a1, turned)
+    a2 = spread(a1, "z")
+    both_rows = after(both_rows, a1)
+    other_rows = swap(both_rows, "core")
+    xa1 = spread(both_rows, "x")
+    b1 = after(b1, a1)
+    b2 = spread(b1, "z")
+    other_rows = after(other_rows, b1)
+    xb1 = spread(other_rows, "x")
+    a2 = after(a2, b1)
+    a3 = spread(a2, "z")
+    b2 = after(b2, a2)
+    b3 = spread(b2, "z")
+    xa1 = after(xa1, b1)
+    xa2 = spread(xa1, "x")
+    a3 = after(a3, b2)
+    a4 = spread(a3, "z")
+
+    slots = (((0, 0), (1, 0), (1, 1), (2, 0), (2, 1)), ((3, 0), (3, 1), (4, 0)))
+    first, last = (block, a1, b1, a2, b2), (a3, b3, a4)
+    size = 3 * chans
+    chunks = trade(vmem_call(chunk_kernel, [((size * len(first), width), bf16)] * 4, *first, place=place))
+    far = [swap(after(xa1, a3), "core"), swap(after(xb1, a3), "core"), swap(after(xa2, b3), "core")]
+    pieces = (both_rows, xa1, xb1, xa2, other_rows, *far)
+    parts = vmem_call(
+        functools.partial(product_kernel, False), [((size * len(first), width), bf16)] * 4, *pieces, *first, place=place
+    )
+    early = trade(parts)
+    last = lax.optimization_barrier((*last, parts[0]))[:-1]
+    parts = vmem_call(
+        functools.partial(product_kernel, True), [((2 * size * len(last), width), bf16)] * 4, *pieces, *last, place=place
+    )
+    groups = (*early, *chunks, *trade(parts))
     proj_grad, weight_grad = vmem_call(
-        functools.partial(finish_kernel, chans, n, shifts),
+        functools.partial(finish_kernel, chans, n, slots),
         [((3, count, width), bf16), ((3, n_x * rows, count), jnp.float32)],
         *groups,
         scratch=[pltpu.VMEM((3, count, width), jnp.float32)],

time: 109 us -> 102 us (0.936)
  starting transfers between devices: 31 us -> 26.1 us
  waiting for transfers between devices: 23.5 us -> 19.9 us
  local copies, waits for them, and re-layouts: 4.9 us -> 7.88 us
  Pallas kernels: 16 us -> 14.3 us
    ppermute x12 -> x10, waiting for transfers between devices: 18.5 us -> 8.62 us  [spread(): return lax.ppermute(x, (axis, 'core'), perm)]
    ppermute x10 -> x12, waiting for transfers between devices: 2.33 us -> 9.8 us  [swap(): return lax.ppermute(x, axis, [(0, 1), (1, 0)])]
    ppermute x12 -> x10, starting transfers between devices: 18 us -> 13.1 us  [spread(): return lax.ppermute(x, (axis, 'core'), perm)]
    pallas_call x6 -> x5, Pallas kernels: 16 us -> 12.2 us  [vmem_call(): pl.pallas_call(body, out_shape=tuple((jax.ShapeDtypeStruct(shape, dtype)...]
    unnamed x28 -> x38, local copies, waits for them, and re-layouts: 4.77 us -> 7.81 us
    pallas_call x0 -> x1, Pallas kernels: none -> 2.13 us  [local(): pl.pallas_call(functools.partial(pack_kernel, chans), out_shape=jax.Shape...]
    ppermute x2 -> x3, waiting for transfers between devices: 2.62 us -> 1.5 us  [trade(): lax.ppermute(parts[3], ('ylo', 'core'), [(0, 3), (1, 2), (2, 1), (3, 0)])]
    ppermute x2 -> x3, starting transfers between devices: 3.22 us -> 3.86 us  [trade(): lax.ppermute(parts[3], ('ylo', 'core'), [(0, 3), (1, 2), (2, 1), (3, 0)])]
  transfers between devices with their start and end apart: 24 -> 25, of which waited for: 8 -> 7; matrix products, arithmetic and copies ran while one was open for 0% -> 0% of each run, Pallas kernels for 13% -> 6%
where the time goes in v4:
time: 102 us
  blocking collectives  32.5 us (32%)
  starting transfers between devices  26.1 us (26%)
  waiting for transfers between devices  19.9 us (20%)
  Pallas kernels  14.3 us (14%)
  local copies, waits for them, and re-layouts  7.88 us (8%)
    all_to_all x1, blocking collectives, local(): sent = lax.all_to_all(sent, SEQ, split_axis=0, concat_axis=0, tiled=True)  32.5 us
    ppermute x10, starting transfers between devices, spread(): return lax.ppermute(x, (axis, 'core'), perm)  13.1 us
    pallas_call x5, Pallas kernels, vmem_call(): pl.pallas_call(body, out_shape=tuple((jax.ShapeDtypeStruct(shape, dtype)...  12.2 us
    ppermute x12, waiting for transfers between devices, swap(): return lax.ppermute(x, axis, [(0, 1), (1, 0)])  9.8 us
    ppermute x12, starting transfers between devices, swap(): return lax.ppermute(x, axis, [(0, 1), (1, 0)])  9.14 us
    ppermute x10, waiting for transfers between devices, spread(): return lax.ppermute(x, (axis, 'core'), perm)  8.62 us
    unnamed x38, local copies, waits for them, and re-layouts  7.81 us
    ppermute x3, starting transfers between devices, trade(): lax.ppermute(parts[3], ('ylo', 'core'), [(0, 3), (1, 2), (2, 1), (3, 0)])  3.86 us
  transfers between devices with their start and end apart: 25, of which 7 were waited for; matrix products, arithmetic and copies ran while one was open for 0% of the time, Pallas kernels for 6%

profile of v4, /device:TPU:1, one launch (start us, length us, event | category | flops | bytes accessed | tf_op | source)
XLA Modules:
  0.0 101.7 jit_solution(5286921363318813772)
XLA Ops:
  0.6 2.1 %shard_map.139 = bf16[32,96,128]{2,1,0:T(8,128)(2,1)} custom-call(bf16[32,4,32,128]{3,2,1,0:T(8,128)(2,1)} %bitcast.11, bf16[3,32,16,128]{3,2,1,0:T(8,128)(2,1)} %bitcast.12, bf16[32,16,128]{2,1,0:T(8,128)(2,1)} %bitcast.14), custom_call_target="tpu_custom_call" | custom-call | tf_op jit(solution)/shard_map/pallas_call | solution.py:258
  2.8 0.0 copy-start.10
  2.8 0.0 copy-start.11
  2.8 0.0 copy-start.12
  2.8 0.0 copy-start.13
  2.8 0.0 copy-start.14
  2.8 0.0 copy-start.15
  2.8 0.0 copy-start.16
  2.9 0.0 copy-start.17
  2.9 0.0 copy-start.18
  2.9 32.5 %all_to_all.5.sent_ref = bf16[32,96,128]{2,1,0:T(8,128)(2,1)S(1)} all-to-all(bf16[32,96,128]{2,1,0:T(8,128)(2,1)} %shard_map.139), channel_id=1, replica_groups=mesh['yhi'=2,'x'=4,'ylo'=2,'z'=8,'core'=2] {'ylo','z','core'}, dimensions={0} | all-to-all | bytes 1572864 | tf_op jit(solution)/shard_map/all_to_all | solution.py:269
  35.5 4.1 %shard_map.140 = (bf16[2,48,2048]{2,1,0:T(8,128)(2,1)S(1)}, f32[16,4096]{1,0:T(8,128)}) custom-call(bf16[32,96,128]{2,1,0:T(8,128)(2,1)S(1)} %all_to_all.5.sent_ref, f32[16,4096]{1,0:T(8,128)S(1)} %copy-done.10, bf16[80,96]{1,0:T(8,128)(2,1)S(1)} %copy-done.15, bf16[32,240]{1,0:T(8,128)(2,1)S(1)} %copy-done.18, f32[40,128]{1,0:T(8,128)S(1)} %copy-done.16, ...), custom_call_target="tpu_custom_call" | custom-call | tf_op jit(solution)/shard_map/pallas_call | solution.py:130
  39.6 0.4 collective-permute-start.1
  40.0 3.8 %collective-permute-start.2 = (bf16[2,48,2048]{2,1,0:T(8,128)(2,1)S(1)}, bf16[2,48,2048]{2,1,0:T(8,128)(2,1)S(1)}, u32[]{:S(2)}, u32[]{:S(2)}) collective-permute-start(bf16[2,48,2048]{2,1,0:T(8,128)(2,1)S(1)} %get-tuple-element.34.refs_8_.refs_0_), channel_id=1, source_target_pairs={{0,1},{1,0},{2,3},{3,2},{4,5},{5,4},{6,7},{7,6},{8,9},{9,8},{10,11... | collective-permute-start | bytes 1179656 | tf_op jit(solution)/shard_map/ppermute | solution.py:236
  43.8 0.1 slice_bitcast_fusion
  43.8 0.3 collective-permute-start
  44.2 1.0 collective-permute-done.2
  45.1 1.1 %collective-permute-start.4 = (bf16[2,48,2048]{2,1,0:T(8,128)(2,1)S(1)}, bf16[2,48,2048]{2,1,0:T(8,128)(2,1)S(1)}, u32[]{:S(2)}, u32[]{:S(2)}) collective-permute-start(bf16[2,48,2048]{2,1,0:T(8,128)(2,1)S(1)} %collective-permute-done.2), channel_id=1, source_target_pairs={{0,2},{2,4},{4,6},{6,8},{8,10},{10,12},{12,14},{14,0},{1,15},{3,1}... | collective-permute-start | bytes 1179656 | tf_op jit(solution)/shard_map/ppermute | solution.py:232
  46.2 5.6 %collective-permute-done = bf16[32,32,128]{2,1,0:T(8,128)(2,1)S(1)} collective-permute-done((bf16[32,32,128]{2,1,0:T(8,128)(2,1)S(1)}, bf16[32,32,128]{2,1,0:T(8,128)(2,1)S(1)}, u32[]{:S(2)}, u32[]{:S(2)}) %collective-permute-start) | collective-permute-done | bytes 262176 | tf_op jit(solution)/shard_map/ppermute | solution.py:236
  51.9 0.1 pad_maximum_fusion.refs_0_
  51.9 0.0 collective-permute-done.1.refs_9_.refs_1_
  51.9 0.9 collective-permute-start.5
  52.8 2.5 %collective-permute-start.3 = (bf16[2,32,32,128]{3,2,1,0:T(8,128)(2,1)S(1)}, bf16[2,32,32,128]{3,2,1,0:T(8,128)(2,1)S(1)}, u32[]{:S(2)}, u32[]{:S(2)}) collective-permute-start(bf16[2,32,32,128]{3,2,1,0:T(8,128)(2,1)S(1)} %pad_maximum_fusion.refs_0_), channel_id=1, source_target_pairs={{0,32},{32,64},{64,96},{96,0},{1,97},{33,1},{65,33},{97,65},{2,34}... | collective-permute-start | bytes 1572872 | tf_op jit(solution)/shard_map/ppermute | solution.py:232
  55.3 1.1 %collective-permute-start.8 = (bf16[2,48,2048]{2,1,0:T(8,128)(2,1)S(1)}, bf16[2,48,2048]{2,1,0:T(8,128)(2,1)S(1)}, u32[]{:S(2)}, u32[]{:S(2)}) collective-permute-start(bf16[2,48,2048]{2,1,0:T(8,128)(2,1)S(1)} %collective-permute-done.1.refs_9_.refs_1_), channel_id=1, source_target_pairs={{0,2},{2,4},{4,6},{6,8},{8,10},{10,12},{12,14},{14,0},{1,15},{3,1}... | collective-permute-start | bytes 1179656 | tf_op jit(solution)/shard_map/ppermute | solution.py:232
  56.4 0.7 copy-done
  57.1 0.0 collective-permute-done.4.refs_10_.refs_2_
  57.1 0.0 collective-permute-start.10
  57.2 0.7 copy-done.2
  57.9 0.0 collective-permute-done.5.refs_4_
  57.9 0.5 collective-permute-start.6
  58.4 3.0 %collective-permute-done.3.refs_1_ = bf16[2,32,32,128]{3,2,1,0:T(8,128)(2,1)S(1)} collective-permute-done((bf16[2,32,32,128]{3,2,1,0:T(8,128)(2,1)S(1)}, bf16[2,32,32,128]{3,2,1,0:T(8,128)(2,1)S(1)}, u32[]{:S(2)}, u32[]{:S(2)}) %collective-permute-start.3) | collective-permute-done | bytes 524320 | tf_op jit(solution)/shard_map/ppermute | solution.py:232
  61.4 3.4 %collective-permute-start.7 = (bf16[2,32,32,128]{3,2,1,0:T(8,128)(2,1)S(1)}, bf16[2,32,32,128]{3,2,1,0:T(8,128)(2,1)S(1)}, u32[]{:S(2)}, u32[]{:S(2)}) collective-permute-start(bf16[2,32,32,128]{3,2,1,0:T(8,128)(2,1)S(1)} %collective-permute-done.3.refs_1_), channel_id=1, source_target_pairs={{0,32},{32,64},{64,96},{96,0},{1,97},{33,1},{65,33},{97,65},{2,34}... | collective-permute-start | bytes 1572872 | tf_op jit(solution)/shard_map/ppermute | solution.py:232
  64.8 0.8 collective-permute-start.9
  65.6 0.7 copy-done.4
  66.4 0.0 collective-permute-done.10.refs_12_.refs_4_
  66.4 2.3 %collective-permute-start.13 = (bf16[2,48,2048]{2,1,0:T(8,128)(2,1)S(1)}, bf16[2,48,2048]{2,1,0:T(8,128)(2,1)S(1)}, u32[]{:S(2)}, u32[]{:S(2)}) collective-permute-start(bf16[2,48,2048]{2,1,0:T(8,128)(2,1)S(1)} %collective-permute-done.10.refs_12_.refs_4_), channel_id=1, source_target_pairs={{0,2},{2,4},{4,6},{6,8},{8,10},{10,12},{12,14},{14,0},{1,15},{3,1}... | collective-permute-start | bytes 1179656 | tf_op jit(solution)/shard_map/ppermute | solution.py:232
  68.7 0.8 copy-done.6
  69.5 2.3 %collective-permute-done.9.refs_8_ = bf16[2,48,2048]{2,1,0:T(8,128)(2,1)} collective-permute-done((bf16[2,48,2048]{2,1,0:T(8,128)(2,1)S(1)}, bf16[2,48,2048]{2,1,0:T(8,128)(2,1)}, u32[]{:S(2)}, u32[]{:S(2)}) %collective-permute-start.9) | collective-permute-done | bytes 393248 | tf_op jit(solution)/shard_map/ppermute | solution.py:232
  71.8 0.8 collective-permute-start.11
  72.7 0.0 collective-permute-start.12
  72.7 3.3 %collective-permute-done.13.refs_9_ = bf16[2,48,2048]{2,1,0:T(8,128)(2,1)S(1)} collective-permute-done((bf16[2,48,2048]{2,1,0:T(8,128)(2,1)S(1)}, bf16[2,48,2048]{2,1,0:T(8,128)(2,1)S(1)}, u32[]{:S(2)}, u32[]{:S(2)}) %collective-permute-start.13) | collective-permute-done | bytes 393248 | tf_op jit(solution)/shard_map/ppermute | solution.py:232
  76.0 0.8 copy-done.8
  76.7 0.8 collective-permute-start.14
  77.5 0.9 collective-permute-start.21
  78.5 0.1 pad_add_fusion.place_ref
  78.5 1.0 copy-done.1
  79.5 1.0 copy-done.3
  80.5 1.0 copy-done.5
  81.5 1.0 copy-done.7
  82.5 0.6 shard_map.142
  83.1 0.1 collective-permute-start.18
  83.2 0.7 collective-permute-start.19
  83.9 1.5 %collective-permute-start.20 = (bf16[240,128]{1,0:T(8,128)(2,1)S(1)}, bf16[240,128]{1,0:T(8,128)(2,1)S(1)}, u32[]{:S(2)}, u32[]{:S(2)}) collective-permute-start(bf16[240,128]{1,0:T(8,128)(2,1)S(1)} %get-tuple-element.54), channel_id=1, source_target_pairs={{0,17},{1,16},{16,1},{17,0},{2,19},{3,18},{18,3},{19,2},{4,21},{5,... | collective-permute-start | bytes 184328 | tf_op jit(solution)/shard_map/ppermute | solution.py:244
  85.4 2.6 %shard_map.141 = (bf16[240,128]{1,0:T(8,128)(2,1)S(1)}, bf16[240,128]{1,0:T(8,128)(2,1)S(1)}, bf16[240,128]{1,0:T(8,128)(2,1)S(1)}, bf16[240,128]{1,0:T(8,128)(2,1)S(1)}) custom-call(s32[4]{0:T(128)S(1)} %pad_add_fusion.place_ref, bf16[2,32,32,128]{3,2,1,0:T(8,128)(2,1)S(1)} %pad_maximum_fusion.refs_0_, ...), custom_call_target="tpu_custom_call" | custom-call | tf_op jit(solution)/shard_map/pallas_call | solution.py:130
  88.0 0.1 collective-permute-start.15
  88.1 3.0 %shard_map.143 = (bf16[288,128]{1,0:T(8,128)(2,1)S(1)}, bf16[288,128]{1,0:T(8,128)(2,1)S(1)}, bf16[288,128]{1,0:T(8,128)(2,1)S(1)}, bf16[288,128]{1,0:T(8,128)(2,1)S(1)}) custom-call(s32[4]{0:T(128)S(1)} %pad_add_fusion.place_ref, bf16[2,32,32,128]{3,2,1,0:T(8,128)(2,1)S(1)} %pad_maximum_fusion.refs_0_, ...), custom_call_target="tpu_custom_call" | custom-call | tf_op jit(solution)/shard_map/pallas_call | solution.py:130
  91.1 0.6 collective-permute-start.22
  91.7 0.6 collective-permute-start.23
  92.3 1.2 %collective-permute-start.24 = (bf16[288,128]{1,0:T(8,128)(2,1)S(1)}, bf16[288,128]{1,0:T(8,128)(2,1)S(1)}, u32[]{:S(2)}, u32[]{:S(2)}) collective-permute-start(bf16[288,128]{1,0:T(8,128)(2,1)S(1)} %get-tuple-element.61), channel_id=1, source_target_pairs={{0,17},{1,16},{16,1},{17,0},{2,19},{3,18},{18,3},{19,2},{4,21},{5,... | collective-permute-start | bytes 221192 | tf_op jit(solution)/shard_map/ppermute | solution.py:244
  93.4 0.6 collective-permute-start.16
  94.0 1.2 %collective-permute-start.17 = (bf16[240,128]{1,0:T(8,128)(2,1)S(1)}, bf16[240,128]{1,0:T(8,128)(2,1)S(1)}, u32[]{:S(2)}, u32[]{:S(2)}) collective-permute-start(bf16[240,128]{1,0:T(8,128)(2,1)S(1)} %get-tuple-element.50), channel_id=1, source_target_pairs={{0,17},{1,16},{16,1},{17,0},{2,19},{3,18},{18,3},{19,2},{4,21},{5,... | collective-permute-start | bytes 184328 | tf_op jit(solution)/shard_map/ppermute | solution.py:244
  95.2 3.2 %collective-permute-done.16.refs_2_ = bf16[240,128]{1,0:T(8,128)(2,1)S(1)} collective-permute-done((bf16[240,128]{1,0:T(8,128)(2,1)S(1)}, bf16[240,128]{1,0:T(8,128)(2,1)S(1)}, u32[]{:S(2)}, u32[]{:S(2)}) %collective-permute-start.16) | collective-permute-done | bytes 61472 | tf_op jit(solution)/shard_map/ppermute | solution.py:236
  98.4 1.5 %collective-permute-done.17.refs_3_ = bf16[240,128]{1,0:T(8,128)(2,1)S(1)} collective-permute-done((bf16[240,128]{1,0:T(8,128)(2,1)S(1)}, bf16[240,128]{1,0:T(8,128)(2,1)S(1)}, u32[]{:S(2)}, u32[]{:S(2)}) %collective-permute-start.17) | collective-permute-done | bytes 61472 | tf_op jit(solution)/shard_map/ppermute | solution.py:244
  99.9 1.8 %shard_map.144 = (bf16[3,512,128]{2,1,0:T(8,128)(2,1)}, f32[3,128,512]{2,1,0:T(8,128)}) custom-call(s32[4]{0:T(128)S(1)} %pad_add_fusion.place_ref, bf16[240,128]{1,0:T(8,128)(2,1)S(1)} %get-tuple-element.47.refs_0_, bf16[240,128]{1,0:T(8,128)(2,1)S(1)} %collective-permute-done.15.refs_1_, bf16[240,128]{1,0:T(8,128)(2,1)S(1)} %collective-permute-done.16.refs_2_, ...), custom_call_target="tpu_custom_call" | custom-call | tf_op jit(solution)/shard_map/pallas_call | solution.py:130
  (34 shorter events, 0.1 us)
Async XLA Ops:
  2.8 32.6 %copy-start.10 = (f32[16,4096]{1,0:T(8,128)S(1)}, f32[16,4096]{1,0:T(8,128)}, u32[]{:S(2)}) copy-start(f32[16,4096]{1,0:T(8,128)} %filt_ref.1) | copy-start | bytes 786436
  2.8 32.6 %copy-start.11 = (bf16[256,256]{1,0:T(8,128)(2,1)S(1)}, bf16[256,256]{1,0:T(8,128)(2,1)}, u32[]{:S(2)}) copy-start(bf16[256,256]{1,0:T(8,128)(2,1)} %constant.38.clone.th_ref) | copy-start | bytes 393220
  2.8 32.6 %copy-start.12 = (bf16[256,256]{1,0:T(8,128)(2,1)S(1)}, bf16[256,256]{1,0:T(8,128)(2,1)}, u32[]{:S(2)}) copy-start(bf16[256,256]{1,0:T(8,128)(2,1)} %constant.39.clone.tl_ref) | copy-start | bytes 393220
  2.8 32.6 %copy-start.13 = (bf16[256,256]{1,0:T(8,128)(2,1)S(1)}, bf16[256,256]{1,0:T(8,128)(2,1)}, u32[]{:S(2)}) copy-start(bf16[256,256]{1,0:T(8,128)(2,1)} %constant.40.clone.uh_ref) | copy-start | bytes 393220
  2.8 32.6 %copy-start.14 = (bf16[256,256]{1,0:T(8,128)(2,1)S(1)}, bf16[256,256]{1,0:T(8,128)(2,1)}, u32[]{:S(2)}) copy-start(bf16[256,256]{1,0:T(8,128)(2,1)} %constant.41.clone.ul_ref) | copy-start | bytes 393220
  2.8 32.6 %copy-start.15 = (bf16[80,96]{1,0:T(8,128)(2,1)S(1)}, bf16[80,96]{1,0:T(8,128)(2,1)}, u32[]{:S(2)}) copy-start(bf16[80,96]{1,0:T(8,128)(2,1)} %constant.34.clone.lf_ref) | copy-start | bytes 46084
  2.8 32.6 %copy-start.16 = (f32[40,128]{1,0:T(8,128)S(1)}, f32[40,128]{1,0:T(8,128)}, u32[]{:S(2)}) copy-start(f32[40,128]{1,0:T(8,128)} %constant.36.clone.tc_ref) | copy-start | bytes 61444
  2.9 32.6 %copy-start.17 = (f32[40,128]{1,0:T(8,128)S(1)}, f32[40,128]{1,0:T(8,128)}, u32[]{:S(2)}) copy-start(f32[40,128]{1,0:T(8,128)} %constant.37.clone.ts_ref) | copy-start | bytes 61444
  2.9 32.6 %copy-start.18 = (bf16[32,240]{1,0:T(8,128)(2,1)S(1)}, bf16[32,240]{1,0:T(8,128)(2,1)}, u32[]{:S(2)}) copy-start(bf16[32,240]{1,0:T(8,128)(2,1)} %constant.35.clone.li_ref) | copy-start | bytes 46084
  39.6 12.3 %collective-permute-start.1 = (bf16[2,48,2048]{2,1,0:T(8,128)(2,1)S(1)}, bf16[2,48,2048]{2,1,0:T(8,128)(2,1)S(1)}, u32[]{:S(2)}, u32[]{:S(2)}) collective-permute-start(bf16[2,48,2048]{2,1,0:T(8,128)(2,1)S(1)} %get-tuple-element.34.refs_8_.refs_0_), channel_id=1, source_target_pairs={{0,2},{2,4},{4,6},{6,8},{8,10},{10,12},{12,14},{14,0},{1,15},{3,1}... | collective-permute-start | bytes 1179656 | tf_op jit(solution)/shard_map/ppermute | solution.py:232
  40.0 5.1 %collective-permute-start.2 = (bf16[2,48,2048]{2,1,0:T(8,128)(2,1)S(1)}, bf16[2,48,2048]{2,1,0:T(8,128)(2,1)S(1)}, u32[]{:S(2)}, u32[]{:S(2)}) collective-permute-start(bf16[2,48,2048]{2,1,0:T(8,128)(2,1)S(1)} %get-tuple-element.34.refs_8_.refs_0_), channel_id=1, source_target_pairs={{0,1},{1,0},{2,3},{3,2},{4,5},{5,4},{6,7},{7,6},{8,9},{9,8},{10,11... | collective-permute-start | bytes 1179656 | tf_op jit(solution)/shard_map/ppermute | solution.py:236
  43.8 8.0 %collective-permute-start = (bf16[32,32,128]{2,1,0:T(8,128)(2,1)S(1)}, bf16[32,32,128]{2,1,0:T(8,128)(2,1)S(1)}, u32[]{:S(2)}, u32[]{:S(2)}) collective-permute-start(bf16[32,32,128]{2,1,0:T(8,128)(2,1)S(1)} %get-tuple-element.66), channel_id=1, source_target_pairs={{0,16},{16,0},{1,17},{17,1},{2,18},{18,2},{3,19},{19,3},{4,20},{20... | collective-permute-start | bytes 786440 | tf_op jit(solution)/shard_map/ppermute | solution.py:236
  45.1 12.0 %collective-permute-start.4 = (bf16[2,48,2048]{2,1,0:T(8,128)(2,1)S(1)}, bf16[2,48,2048]{2,1,0:T(8,128)(2,1)S(1)}, u32[]{:S(2)}, u32[]{:S(2)}) collective-permute-start(bf16[2,48,2048]{2,1,0:T(8,128)(2,1)S(1)} %collective-permute-done.2), channel_id=1, source_target_pairs={{0,2},{2,4},{4,6},{6,8},{8,10},{10,12},{12,14},{14,0},{1,15},{3,1}... | collective-permute-start | bytes 1179656 | tf_op jit(solution)/shard_map/ppermute | solution.py:232
  51.9 6.0 %collective-permute-start.5 = (bf16[2,32,32,128]{3,2,1,0:T(8,128)(2,1)S(1)}, bf16[2,32,32,128]{3,2,1,0:T(8,128)(2,1)S(1)}, u32[]{:S(2)}, u32[]{:S(2)}) collective-permute-start(bf16[2,32,32,128]{3,2,1,0:T(8,128)(2,1)S(1)} %pad_maximum_fusion.refs_0_), channel_id=1, source_target_pairs={{0,1},{1,0},{2,3},{3,2},{4,5},{5,4},{6,7},{7,6},{8,9},{9,8},{10,11... | collective-permute-start | bytes 1572872 | tf_op jit(solution)/shard_map/ppermute | solution.py:236
  52.8 8.6 %collective-permute-start.3 = (bf16[2,32,32,128]{3,2,1,0:T(8,128)(2,1)S(1)}, bf16[2,32,32,128]{3,2,1,0:T(8,128)(2,1)S(1)}, u32[]{:S(2)}, u32[]{:S(2)}) collective-permute-start(bf16[2,32,32,128]{3,2,1,0:T(8,128)(2,1)S(1)} %pad_maximum_fusion.refs_0_), channel_id=1, source_target_pairs={{0,32},{32,64},{64,96},{96,0},{1,97},{33,1},{65,33},{97,65},{2,34}... | collective-permute-start | bytes 1572872 | tf_op jit(solution)/shard_map/ppermute | solution.py:232
  55.3 9.5 %collective-permute-start.8 = (bf16[2,48,2048]{2,1,0:T(8,128)(2,1)S(1)}, bf16[2,48,2048]{2,1,0:T(8,128)(2,1)S(1)}, u32[]{:S(2)}, u32[]{:S(2)}) collective-permute-start(bf16[2,48,2048]{2,1,0:T(8,128)(2,1)S(1)} %collective-permute-done.1.refs_9_.refs_1_), channel_id=1, source_target_pairs={{0,2},{2,4},{4,6},{6,8},{8,10},{10,12},{12,14},{14,0},{1,15},{3,1}... | collective-permute-start | bytes 1179656 | tf_op jit(solution)/shard_map/ppermute | solution.py:232
  56.4 0.7 copy-start
  57.1 9.3 %collective-permute-start.10 = (bf16[2,48,2048]{2,1,0:T(8,128)(2,1)S(1)}, bf16[2,48,2048]{2,1,0:T(8,128)(2,1)S(1)}, u32[]{:S(2)}, u32[]{:S(2)}) collective-permute-start(bf16[2,48,2048]{2,1,0:T(8,128)(2,1)S(1)} %collective-permute-done.4.refs_10_.refs_2_), channel_id=1, source_target_pairs={{0,2},{2,4},{4,6},{6,8},{8,10},{10,12},{12,14},{14,0},{1,15},{3,1}... | collective-permute-start | bytes 1179656 | tf_op jit(solution)/shard_map/ppermute | solution.py:232
  57.1 0.7 copy-start.2
  57.9 14.8 %collective-permute-start.6 = (bf16[2,32,32,128]{3,2,1,0:T(8,128)(2,1)S(1)}, bf16[2,32,32,128]{3,2,1,0:T(8,128)(2,1)S(1)}, u32[]{:S(2)}, u32[]{:S(2)}) collective-permute-start(bf16[2,32,32,128]{3,2,1,0:T(8,128)(2,1)S(1)} %collective-permute-done.5.refs_4_), channel_id=1, source_target_pairs={{0,32},{32,64},{64,96},{96,0},{1,97},{33,1},{65,33},{97,65},{2,34}... | collective-permute-start | bytes 1572872 | tf_op jit(solution)/shard_map/ppermute | solution.py:232
  61.4 11.3 %collective-permute-start.7 = (bf16[2,32,32,128]{3,2,1,0:T(8,128)(2,1)S(1)}, bf16[2,32,32,128]{3,2,1,0:T(8,128)(2,1)S(1)}, u32[]{:S(2)}, u32[]{:S(2)}) collective-permute-start(bf16[2,32,32,128]{3,2,1,0:T(8,128)(2,1)S(1)} %collective-permute-done.3.refs_1_), channel_id=1, source_target_pairs={{0,32},{32,64},{64,96},{96,0},{1,97},{33,1},{65,33},{97,65},{2,34}... | collective-permute-start | bytes 1572872 | tf_op jit(solution)/shard_map/ppermute | solution.py:232
  64.8 7.0 %collective-permute-start.9 = (bf16[2,48,2048]{2,1,0:T(8,128)(2,1)S(1)}, bf16[2,48,2048]{2,1,0:T(8,128)(2,1)}, u32[]{:S(2)}, u32[]{:S(2)}) collective-permute-start(bf16[2,48,2048]{2,1,0:T(8,128)(2,1)S(1)} %collective-permute-done.8.refs_11_.refs_3_), channel_id=1, source_target_pairs={{0,2},{2,4},{4,6},{6,8},{8,10},{10,12},{12,14},{14,0},{1,15},{3,1}... | collective-permute-start | bytes 1179656 | tf_op jit(solution)/shard_map/ppermute | solution.py:232
  65.6 0.8 copy-start.4
  66.4 9.5 %collective-permute-start.13 = (bf16[2,48,2048]{2,1,0:T(8,128)(2,1)S(1)}, bf16[2,48,2048]{2,1,0:T(8,128)(2,1)S(1)}, u32[]{:S(2)}, u32[]{:S(2)}) collective-permute-start(bf16[2,48,2048]{2,1,0:T(8,128)(2,1)S(1)} %collective-permute-done.10.refs_12_.refs_4_), channel_id=1, source_target_pairs={{0,2},{2,4},{4,6},{6,8},{8,10},{10,12},{12,14},{14,0},{1,15},{3,1}... | collective-permute-start | bytes 1179656 | tf_op jit(solution)/shard_map/ppermute | solution.py:232
  68.7 0.8 copy-start.6
  71.8 11.4 %collective-permute-start.11 = (bf16[2,32,32,128]{3,2,1,0:T(8,128)(2,1)S(1)}, bf16[2,32,32,128]{3,2,1,0:T(8,128)(2,1)S(1)}, u32[]{:S(2)}, u32[]{:S(2)}) collective-permute-start(bf16[2,32,32,128]{3,2,1,0:T(8,128)(2,1)S(1)} %collective-permute-done.3.refs_1_), channel_id=1, source_target_pairs={{0,1},{1,0},{2,3},{3,2},{4,5},{5,4},{6,7},{7,6},{8,9},{9,8},{10,11... | collective-permute-start | bytes 1572872 | tf_op jit(solution)/shard_map/ppermute | solution.py:236
  72.7 11.2 %collective-permute-start.12 = (bf16[2,32,32,128]{3,2,1,0:T(8,128)(2,1)S(1)}, bf16[2,32,32,128]{3,2,1,0:T(8,128)(2,1)}, u32[]{:S(2)}, u32[]{:S(2)}) collective-permute-start(bf16[2,32,32,128]{3,2,1,0:T(8,128)(2,1)S(1)} %collective-permute-done.6.refs_2_), channel_id=1, source_target_pairs={{0,1},{1,0},{2,3},{3,2},{4,5},{5,4},{6,7},{7,6},{8,9},{9,8},{10,11... | collective-permute-start | bytes 1572872 | tf_op jit(solution)/shard_map/ppermute | solution.py:236
  76.0 0.8 copy-start.8
  76.7 8.7 %collective-permute-start.14 = (bf16[2,32,32,128]{3,2,1,0:T(8,128)(2,1)S(1)}, bf16[2,32,32,128]{3,2,1,0:T(8,128)(2,1)}, u32[]{:S(2)}, u32[]{:S(2)}) collective-permute-start(bf16[2,32,32,128]{3,2,1,0:T(8,128)(2,1)S(1)} %collective-permute-done.7.refs_3_), channel_id=1, source_target_pairs={{0,1},{1,0},{2,3},{3,2},{4,5},{5,4},{6,7},{7,6},{8,9},{9,8},{10,11... | collective-permute-start | bytes 1572872 | tf_op jit(solution)/shard_map/ppermute | solution.py:236
  77.5 10.5 %collective-permute-start.21 = (bf16[2,48,2048]{2,1,0:T(8,128)(2,1)}, bf16[2,48,2048]{2,1,0:T(8,128)(2,1)}, u32[]{:S(2)}, u32[]{:S(2)}) collective-permute-start(bf16[2,48,2048]{2,1,0:T(8,128)(2,1)} %collective-permute-done.9.refs_8_), channel_id=1, source_target_pairs={{0,2},{2,4},{4,6},{6,8},{8,10},{10,12},{12,14},{14,0},{1,15},{3,1}... | collective-permute-start | bytes 1179656 | tf_op jit(solution)/shard_map/ppermute | solution.py:232
  78.5 1.0 copy-start.1
  79.5 1.0 copy-start.3
  80.5 1.0 copy-start.5
  81.5 1.0 copy-start.7
  83.1 8.6 %collective-permute-start.18 = (bf16[240,128]{1,0:T(8,128)(2,1)S(1)}, bf16[240,128]{1,0:T(8,128)(2,1)S(1)}, u32[]{:S(2)}, u32[]{:S(2)}) collective-permute-start(bf16[240,128]{1,0:T(8,128)(2,1)S(1)} %get-tuple-element.52), channel_id=1, source_target_pairs={{0,1},{1,0},{2,3},{3,2},{4,5},{5,4},{6,7},{7,6},{8,9},{9,8},{10,11... | collective-permute-start | bytes 184328 | tf_op jit(solution)/shard_map/ppermute | solution.py:236
  83.2 9.0 %collective-permute-start.19 = (bf16[240,128]{1,0:T(8,128)(2,1)S(1)}, bf16[240,128]{1,0:T(8,128)(2,1)S(1)}, u32[]{:S(2)}, u32[]{:S(2)}) collective-permute-start(bf16[240,128]{1,0:T(8,128)(2,1)S(1)} %get-tuple-element.53), channel_id=1, source_target_pairs={{0,16},{16,0},{1,17},{17,1},{2,18},{18,2},{3,19},{19,3},{4,20},{20... | collective-permute-start | bytes 184328 | tf_op jit(solution)/shard_map/ppermute | solution.py:236
  83.9 4.2 %copy-start.9 = (bf16[2,48,2048]{2,1,0:T(8,128)(2,1)S(1)}, bf16[2,48,2048]{2,1,0:T(8,128)(2,1)}, u32[]{:S(2)}) copy-start(bf16[2,48,2048]{2,1,0:T(8,128)(2,1)} %copy-done.8) | copy-start | bytes 1179652
  83.9 9.5 %collective-permute-start.20 = (bf16[240,128]{1,0:T(8,128)(2,1)S(1)}, bf16[240,128]{1,0:T(8,128)(2,1)S(1)}, u32[]{:S(2)}, u32[]{:S(2)}) collective-permute-start(bf16[240,128]{1,0:T(8,128)(2,1)S(1)} %get-tuple-element.54), channel_id=1, source_target_pairs={{0,17},{1,16},{16,1},{17,0},{2,19},{3,18},{18,3},{19,2},{4,21},{5,... | collective-permute-start | bytes 184328 | tf_op jit(solution)/shard_map/ppermute | solution.py:244
  88.0 6.0 %collective-permute-start.15 = (bf16[240,128]{1,0:T(8,128)(2,1)S(1)}, bf16[240,128]{1,0:T(8,128)(2,1)S(1)}, u32[]{:S(2)}, u32[]{:S(2)}) collective-permute-start(bf16[240,128]{1,0:T(8,128)(2,1)S(1)} %get-tuple-element.48), channel_id=1, source_target_pairs={{0,1},{1,0},{2,3},{3,2},{4,5},{5,4},{6,7},{7,6},{8,9},{9,8},{10,11... | collective-permute-start | bytes 184328 | tf_op jit(solution)/shard_map/ppermute | solution.py:236
  91.1 8.8 %collective-permute-start.22 = (bf16[288,128]{1,0:T(8,128)(2,1)S(1)}, bf16[288,128]{1,0:T(8,128)(2,1)S(1)}, u32[]{:S(2)}, u32[]{:S(2)}) collective-permute-start(bf16[288,128]{1,0:T(8,128)(2,1)S(1)} %get-tuple-element.59), channel_id=1, source_target_pairs={{0,1},{1,0},{2,3},{3,2},{4,5},{5,4},{6,7},{7,6},{8,9},{9,8},{10,11... | collective-permute-start | bytes 221192 | tf_op jit(solution)/shard_map/ppermute | solution.py:236
  91.7 8.2 %collective-permute-start.23 = (bf16[288,128]{1,0:T(8,128)(2,1)S(1)}, bf16[288,128]{1,0:T(8,128)(2,1)S(1)}, u32[]{:S(2)}, u32[]{:S(2)}) collective-permute-start(bf16[288,128]{1,0:T(8,128)(2,1)S(1)} %get-tuple-element.60), channel_id=1, source_target_pairs={{0,16},{16,0},{1,17},{17,1},{2,18},{18,2},{3,19},{19,3},{4,20},{20... | collective-permute-start | bytes 221192 | tf_op jit(solution)/shard_map/ppermute | solution.py:236
  92.3 7.7 %collective-permute-start.24 = (bf16[288,128]{1,0:T(8,128)(2,1)S(1)}, bf16[288,128]{1,0:T(8,128)(2,1)S(1)}, u32[]{:S(2)}, u32[]{:S(2)}) collective-permute-start(bf16[288,128]{1,0:T(8,128)(2,1)S(1)} %get-tuple-element.61), channel_id=1, source_target_pairs={{0,17},{1,16},{16,1},{17,0},{2,19},{3,18},{18,3},{19,2},{4,21},{5,... | collective-permute-start | bytes 221192 | tf_op jit(solution)/shard_map/ppermute | solution.py:244
  93.4 5.0 %collective-permute-start.16 = (bf16[240,128]{1,0:T(8,128)(2,1)S(1)}, bf16[240,128]{1,0:T(8,128)(2,1)S(1)}, u32[]{:S(2)}, u32[]{:S(2)}) collective-permute-start(bf16[240,128]{1,0:T(8,128)(2,1)S(1)} %get-tuple-element.49), channel_id=1, source_target_pairs={{0,16},{16,0},{1,17},{17,1},{2,18},{18,2},{3,19},{19,3},{4,20},{20... | collective-permute-start | bytes 184328 | tf_op jit(solution)/shard_map/ppermute | solution.py:236
  94.0 5.9 %collective-permute-start.17 = (bf16[240,128]{1,0:T(8,128)(2,1)S(1)}, bf16[240,128]{1,0:T(8,128)(2,1)S(1)}, u32[]{:S(2)}, u32[]{:S(2)}) collective-permute-start(bf16[240,128]{1,0:T(8,128)(2,1)S(1)} %get-tuple-element.50), channel_id=1, source_target_pairs={{0,17},{1,16},{16,1},{17,0},{2,19},{3,18},{18,3},{19,2},{4,21},{5,... | collective-permute-start | bytes 184328 | tf_op jit(solution)/shard_map/ppermute | solution.py:244

commit v5 on v4

--- a/solution.py
+++ b/solution.py
@@ -169,13 +169,14 @@
     return jnp.concatenate([block[half, :, pl.ds(at, 128)] for block in blocks], 0)
 
 
-def chunk_kernel(place_ref, *refs):
-    blocks, outs = refs[:-4], refs[-4:]
-    for near, out_ref in enumerate(outs):
-        out_ref[...] = chunk(place_ref, blocks, near // 2, near % 2)
-
-
-def product_kernel(with_chunks, place_ref, *refs):
+def stack_kernel(*refs):
+    blocks, out_ref = refs[:-1], refs[-1]
+    count = out_ref.shape[1] // len(blocks)
+    for k, block in enumerate(blocks):
+        out_ref[:, k * count : (k + 1) * count] = block[...]
+
+
+def product_kernel(place_ref, *refs):
     own, first, second, third, other, other_first, other_second, other_third = refs[:8]
     blocks, outs = refs[8:-4], refs[-4:]
     halves = [jnp.concatenate([block[h] for block in blocks], 0) for h in range(2)]
@@ -196,8 +197,7 @@
             u = jnp.concatenate([t[:, :part], t[:, 3 * part :], t[:, 2 * part : 3 * part], t[:, part : 2 * part]], 1)
             out_ref = outs[2 * ry + rc]
             out_ref[:rows] = jnp.where(place_ref[2] == 0, u, t).astype(jnp.bfloat16)
-            if with_chunks:
-                out_ref[rows:] = chunk(place_ref, blocks, ry, rc)
+            out_ref[rows:] = chunk(place_ref, blocks, ry, rc)
 
 
 def finish_kernel(chans, n, slots, place_ref, *refs):
@@ -206,8 +206,7 @@
     for g, slot_list in enumerate(slots):
         rows = 3 * chans * len(slot_list)
         for near in range(4):
-            weights = groups[8 * g + near]
-            chunks, base = (groups[4 + near], 0) if g == 0 else (weights, rows)
+            ref = groups[4 * g + near]
             core = lax.rem(c + near % 2, 2)
             row_y = lax.rem(y + near // 2, 2) * 2 * n
             for m, (hops, turned) in enumerate(slot_list):
@@ -215,8 +214,8 @@
                 at = pl.multiple_of(owner * chans, chans)
                 for s in range(3):
                     row = (3 * m + s) * chans
-                    turned_ref[s, pl.ds(at, chans), :] = weights[row : row + chans, :].astype(jnp.float32)
-                    proj_ref[s, pl.ds(at, chans), :] = chunks[base + row : base + row + chans, :]
+                    turned_ref[s, pl.ds(at, chans), :] = ref[row : row + chans, :].astype(jnp.float32)
+                    proj_ref[s, pl.ds(at, chans), :] = ref[rows + row : rows + row + chans, :]
     n_x = 4
     part = weight_ref.shape[1] // n_x
     for s in range(3):
@@ -268,19 +267,21 @@
     )
     sent = lax.all_to_all(sent, SEQ, split_axis=0, concat_axis=0, tiled=True)
     own_rows = sent[:, 4 * chans :]
-    both_rows = jnp.stack([own_rows, swap(own_rows, "ylo")])
+    sent, own_rows = lax.optimization_barrier((sent, own_rows))
+    y_rows = swap(own_rows, "ylo")
 
     block, filter_grad = spectral(sent, filters)
     a1 = spread(block, "z")
-    turned = after(swap(block, "core"), block)
+    turned = swap(block, "core")
+    turned = after(turned, block)
     b1 = spread(turned, "z")
     a1 = after(a1, turned)
     a2 = spread(a1, "z")
-    both_rows = after(both_rows, a1)
+    b1 = after(b1, a1)
+    b2 = spread(b1, "z")
+    both_rows = jnp.stack([own_rows, after(y_rows, a1)])
     other_rows = swap(both_rows, "core")
     xa1 = spread(both_rows, "x")
-    b1 = after(b1, a1)
-    b2 = spread(b1, "z")
     other_rows = after(other_rows, b1)
     xb1 = spread(other_rows, "x")
     a2 = after(a2, b1)
@@ -289,24 +290,26 @@
     b3 = spread(b2, "z")
     xa1 = after(xa1, b1)
     xa2 = spread(xa1, "x")
+    (first,) = vmem_call(stack_kernel, [((2, 6 * block.shape[1], block.shape[2]), bf16)], block, a1, b1, a2, b2, b3)
     a3 = after(a3, b2)
     a4 = spread(a3, "z")
 
-    slots = (((0, 0), (1, 0), (1, 1), (2, 0), (2, 1)), ((3, 0), (3, 1), (4, 0)))
-    first, last = (block, a1, b1, a2, b2), (a3, b3, a4)
+    slots = (((0, 0), (1, 0), (1, 1), (2, 0), (2, 1), (3, 1)), ((3, 0), (4, 0)))
+    first, last = (first,), (a3, a4)
     size = 3 * chans
-    chunks = trade(vmem_call(chunk_kernel, [((size * len(first), width), bf16)] * 4, *first, place=place))
-    far = [swap(after(xa1, a3), "core"), swap(after(xb1, a3), "core"), swap(after(xa2, b3), "core")]
+    fa1 = swap(after(xa1, a3), "core")
+    fb1 = swap(after(xb1, a3), "core")
+    fa2 = swap(after(xa2, first), "core")
+    far = [fa1, fb1, fa2]
     pieces = (both_rows, xa1, xb1, xa2, other_rows, *far)
-    parts = vmem_call(
-        functools.partial(product_kernel, False), [((size * len(first), width), bf16)] * 4, *pieces, *first, place=place
-    )
-    early = trade(parts)
-    last = lax.optimization_barrier((*last, parts[0]))[:-1]
-    parts = vmem_call(
-        functools.partial(product_kernel, True), [((2 * size * len(last), width), bf16)] * 4, *pieces, *last, place=place
-    )
-    groups = (*early, *chunks, *trade(parts))
+    groups = ()
+    for slot_list, blocks in zip(slots, (first, last)):
+        if groups:
+            blocks = lax.optimization_barrier((*blocks, groups[0]))[:-1]
+        parts = vmem_call(
+            product_kernel, [((2 * size * len(slot_list), width), bf16)] * 4, *pieces, *blocks, place=place
+        )
+        groups += trade(parts)
     proj_grad, weight_grad = vmem_call(
         functools.partial(finish_kernel, chans, n, slots),
         [((3, count, width), bf16), ((3, n_x * rows, count), jnp.float32)],

time: 102 us -> 95.1 us (0.932)
  local copies, waits for them, and re-layouts: 7.88 us -> 0.08 us
  waiting for transfers between devices: 19.9 us -> 21.2 us
  starting transfers between devices: 26.1 us -> 25 us
    unnamed x38 -> x18, local copies, waits for them, and re-layouts: 7.81 us -> 0.06 us
    ppermute x10, waiting for transfers between devices: 8.62 us -> 16.1 us  [spread(): return lax.ppermute(x, (axis, 'core'), perm)]
    ppermute x12 -> x10, waiting for transfers between devices: 9.8 us -> 3.41 us  [swap(): return lax.ppermute(x, axis, [(0, 1), (1, 0)])]
    ppermute x3 -> x2, starting transfers between devices: 3.86 us -> 2.07 us  [trade(): lax.ppermute(parts[3], ('ylo', 'core'), [(0, 3), (1, 2), (2, 1), (3, 0)])]
    ppermute x12 -> x10, starting transfers between devices: 9.14 us -> 10.4 us  [swap(): return lax.ppermute(x, axis, [(0, 1), (1, 0)])]
  transfers between devices with their start and end apart: 25 -> 22, of which waited for: 7 -> 10; matrix products, arithmetic and copies ran while one was open for 0% -> 0% of each run, Pallas kernels for 6% -> 7%
where the time goes in v5:
time: 95.1 us; the launch traced here: 94.9 us
  blocking collectives  32.4 us (34%)
  starting transfers between devices  25 us (26%)
  waiting for transfers between devices  21.2 us (22%)
  Pallas kernels  15.3 us (16%)
    all_to_all x1, blocking collectives, local(): sent = lax.all_to_all(sent, SEQ, split_axis=0, concat_axis=0, tiled=True)  32.4 us
    ppermute x10, waiting for transfers between devices, spread(): return lax.ppermute(x, (axis, 'core'), perm)  16.1 us
    pallas_call x5, Pallas kernels, vmem_call(): pl.pallas_call(body, out_shape=tuple((jax.ShapeDtypeStruct(shape, dtype)...  13.1 us
    ppermute x10, starting transfers between devices, spread(): return lax.ppermute(x, (axis, 'core'), perm)  12.5 us
    ppermute x10, starting transfers between devices, swap(): return lax.ppermute(x, axis, [(0, 1), (1, 0)])  10.4 us
    ppermute x10, waiting for transfers between devices, swap(): return lax.ppermute(x, axis, [(0, 1), (1, 0)])  3.41 us
    pallas_call x1, Pallas kernels, local(): pl.pallas_call(functools.partial(pack_kernel, chans), out_shape=jax.Shape...  2.22 us
    ppermute x2, starting transfers between devices, trade(): lax.ppermute(parts[3], ('ylo', 'core'), [(0, 3), (1, 2), (2, 1), (3, 0)])  2.07 us
  transfers between devices with their start and end apart: 22, of which 10 were waited for; matrix products, arithmetic and copies ran while one was open for 0% of the time, Pallas kernels for 7%

profile of v5, /device:TPU:1, one launch (start us, length us, event | category | flops | bytes accessed | tf_op | source)
XLA Modules:
  0.0 94.9 jit_solution(16194725191716259443)
XLA Ops:
  0.6 0.0 copy-start.5
  0.6 0.0 copy-start.8
  0.7 0.0 copy-start.6
  0.7 0.0 copy-start.7
  0.7 0.0 copy-start.1
  0.7 0.0 copy-start.2
  0.7 0.0 copy-start.3
  0.7 0.0 copy-start.4
  0.7 0.0 copy-start
  0.7 2.2 %shard_map.139 = bf16[32,96,128]{2,1,0:T(8,128)(2,1)} custom-call(bf16[32,4,32,128]{3,2,1,0:T(8,128)(2,1)} %bitcast.10, bf16[3,32,16,128]{3,2,1,0:T(8,128)(2,1)} %bitcast.12, bf16[32,16,128]{2,1,0:T(8,128)(2,1)} %bitcast.14), custom_call_target="tpu_custom_call" | custom-call | tf_op jit(solution)/shard_map/pallas_call | solution.py:257
  3.0 32.4 %all_to_all.5.sent_ref = bf16[32,96,128]{2,1,0:T(8,128)(2,1)S(1)} all-to-all(bf16[32,96,128]{2,1,0:T(8,128)(2,1)} %shard_map.139), channel_id=1, replica_groups=mesh['yhi'=2,'x'=4,'ylo'=2,'z'=8,'core'=2] {'ylo','z','core'}, dimensions={0} | all-to-all | bytes 1572864 | tf_op jit(solution)/shard_map/all_to_all | solution.py:268
  35.4 0.0 copy-done.5
  35.4 0.0 copy-done.8
  35.5 4.2 %shard_map.140 = (bf16[2,48,2048]{2,1,0:T(8,128)(2,1)S(1)}, f32[16,4096]{1,0:T(8,128)}) custom-call(bf16[32,96,128]{2,1,0:T(8,128)(2,1)S(1)} %all_to_all.5.sent_ref, f32[16,4096]{1,0:T(8,128)S(1)} %copy-done, bf16[80,96]{1,0:T(8,128)(2,1)S(1)} %copy-done.5, bf16[32,240]{1,0:T(8,128)(2,1)S(1)} %copy-done.8, f32[40,128]{1,0:T(8,128)S(1)} %copy-done.6, ...), custom_call_target="tpu_custom_call" | custom-call | tf_op jit(solution)/shard_map/pallas_call | solution.py:130
  39.6 2.3 %collective-permute-start.2 = (bf16[2,48,2048]{2,1,0:T(8,128)(2,1)S(1)}, bf16[2,48,2048]{2,1,0:T(8,128)(2,1)S(1)}, u32[]{:S(2)}, u32[]{:S(2)}) collective-permute-start(bf16[2,48,2048]{2,1,0:T(8,128)(2,1)S(1)} %get-tuple-element.33.refs_0_), channel_id=1, source_target_pairs={{0,1},{1,0},{2,3},{3,2},{4,5},{5,4},{6,7},{7,6},{8,9},{9,8},{10,11... | collective-permute-start | bytes 1179656 | tf_op jit(solution)/shard_map/ppermute | solution.py:235
  42.0 0.2 collective-permute-start.1
  42.2 0.5 collective-permute-start
  42.7 0.6 collective-permute-done.2
  43.3 0.5 collective-permute-start.4
  43.8 5.2 %collective-permute-done.1.refs_1_ = bf16[2,48,2048]{2,1,0:T(8,128)(2,1)S(1)} collective-permute-done((bf16[2,48,2048]{2,1,0:T(8,128)(2,1)S(1)}, bf16[2,48,2048]{2,1,0:T(8,128)(2,1)S(1)}, u32[]{:S(2)}, u32[]{:S(2)}) %collective-permute-start.1) | collective-permute-done | bytes 393248 | tf_op jit(solution)/shard_map/ppermute | solution.py:231
  49.0 0.0 collective-permute-done
  49.0 0.1 pad_maximum_fusion.refs_0_
  49.0 2.1 %collective-permute-start.5 = (bf16[2,32,32,128]{3,2,1,0:T(8,128)(2,1)S(1)}, bf16[2,32,32,128]{3,2,1,0:T(8,128)(2,1)S(1)}, u32[]{:S(2)}, u32[]{:S(2)}) collective-permute-start(bf16[2,32,32,128]{3,2,1,0:T(8,128)(2,1)S(1)} %pad_maximum_fusion.refs_0_), channel_id=1, source_target_pairs={{0,1},{1,0},{2,3},{3,2},{4,5},{5,4},{6,7},{7,6},{8,9},{9,8},{10,11... | collective-permute-start | bytes 1572872 | tf_op jit(solution)/shard_map/ppermute | solution.py:235
  51.1 2.5 %collective-permute-start.3 = (bf16[2,32,32,128]{3,2,1,0:T(8,128)(2,1)S(1)}, bf16[2,32,32,128]{3,2,1,0:T(8,128)(2,1)}, u32[]{:S(2)}, u32[]{:S(2)}) collective-permute-start(bf16[2,32,32,128]{3,2,1,0:T(8,128)(2,1)S(1)} %pad_maximum_fusion.refs_0_), channel_id=1, source_target_pairs={{0,32},{32,64},{64,96},{96,0},{1,97},{33,1},{65,33},{97,65},{2,34}... | collective-permute-start | bytes 1572872 | tf_op jit(solution)/shard_map/ppermute | solution.py:231
  53.6 0.6 collective-permute-start.8
  54.2 0.0 collective-permute-done.4.refs_2_
  54.2 0.4 collective-permute-start.10
  54.6 0.0 collective-permute-done.5.refs_4_
  54.6 2.1 %collective-permute-start.6 = (bf16[2,32,32,128]{3,2,1,0:T(8,128)(2,1)S(1)}, bf16[2,32,32,128]{3,2,1,0:T(8,128)(2,1)}, u32[]{:S(2)}, u32[]{:S(2)}) collective-permute-start(bf16[2,32,32,128]{3,2,1,0:T(8,128)(2,1)S(1)} %collective-permute-done.5.refs_4_), channel_id=1, source_target_pairs={{0,32},{32,64},{64,96},{96,0},{1,97},{33,1},{65,33},{97,65},{2,34}... | collective-permute-start | bytes 1572872 | tf_op jit(solution)/shard_map/ppermute | solution.py:231
  56.7 3.0 %collective-permute-done.3.refs_1_ = bf16[2,32,32,128]{3,2,1,0:T(8,128)(2,1)} collective-permute-done((bf16[2,32,32,128]{3,2,1,0:T(8,128)(2,1)S(1)}, bf16[2,32,32,128]{3,2,1,0:T(8,128)(2,1)}, u32[]{:S(2)}, u32[]{:S(2)}) %collective-permute-start.3) | collective-permute-done | bytes 524320 | tf_op jit(solution)/shard_map/ppermute | solution.py:231
  59.7 3.4 %collective-permute-start.7 = (bf16[2,32,32,128]{3,2,1,0:T(8,128)(2,1)}, bf16[2,32,32,128]{3,2,1,0:T(8,128)(2,1)}, u32[]{:S(2)}, u32[]{:S(2)}) collective-permute-start(bf16[2,32,32,128]{3,2,1,0:T(8,128)(2,1)} %collective-permute-done.3.refs_1_), channel_id=1, source_target_pairs={{0,32},{32,64},{64,96},{96,0},{1,97},{33,1},{65,33},{97,65},{2,34}... | collective-permute-start | bytes 1572872 | tf_op jit(solution)/shard_map/ppermute | solution.py:231
  63.1 0.0 collective-permute-done.8.refs_3_
  63.1 0.4 collective-permute-start.9
  63.5 1.3 %collective-permute-done.10.refs_4_ = bf16[2,48,2048]{2,1,0:T(8,128)(2,1)S(1)} collective-permute-done((bf16[2,48,2048]{2,1,0:T(8,128)(2,1)S(1)}, bf16[2,48,2048]{2,1,0:T(8,128)(2,1)S(1)}, u32[]{:S(2)}, u32[]{:S(2)}) %collective-permute-start.10) | collective-permute-done | bytes 393248 | tf_op jit(solution)/shard_map/ppermute | solution.py:231
  64.8 1.8 %collective-permute-start.13 = (bf16[2,48,2048]{2,1,0:T(8,128)(2,1)S(1)}, bf16[2,48,2048]{2,1,0:T(8,128)(2,1)S(1)}, u32[]{:S(2)}, u32[]{:S(2)}) collective-permute-start(bf16[2,48,2048]{2,1,0:T(8,128)(2,1)S(1)} %collective-permute-done.10.refs_4_), channel_id=1, source_target_pairs={{0,2},{2,4},{4,6},{6,8},{8,10},{10,12},{12,14},{14,0},{1,15},{3,1}... | collective-permute-start | bytes 1179656 | tf_op jit(solution)/shard_map/ppermute | solution.py:231
  66.6 3.5 %collective-permute-done.9.refs_8_ = bf16[2,48,2048]{2,1,0:T(8,128)(2,1)} collective-permute-done((bf16[2,48,2048]{2,1,0:T(8,128)(2,1)S(1)}, bf16[2,48,2048]{2,1,0:T(8,128)(2,1)}, u32[]{:S(2)}, u32[]{:S(2)}) %collective-permute-start.9) | collective-permute-done | bytes 393248 | tf_op jit(solution)/shard_map/ppermute | solution.py:231
  70.1 0.9 collective-permute-start.11
  71.1 0.0 collective-permute-done.6.refs_2_
  71.1 0.0 collective-permute-start.12
  71.1 3.2 %collective-permute-done.13.refs_5_ = bf16[2,48,2048]{2,1,0:T(8,128)(2,1)S(1)} collective-permute-done((bf16[2,48,2048]{2,1,0:T(8,128)(2,1)S(1)}, bf16[2,48,2048]{2,1,0:T(8,128)(2,1)S(1)}, u32[]{:S(2)}, u32[]{:S(2)}) %collective-permute-start.13) | collective-permute-done | bytes 393248 | tf_op jit(solution)/shard_map/ppermute | solution.py:231
  74.3 0.2 shard_map.141.refs_8_
  74.4 0.0 collective-permute-done.7.refs_3_
  74.4 1.0 %collective-permute-start.14 = (bf16[2,32,32,128]{3,2,1,0:T(8,128)(2,1)}, bf16[2,32,32,128]{3,2,1,0:T(8,128)(2,1)}, u32[]{:S(2)}, u32[]{:S(2)}) collective-permute-start(bf16[2,32,32,128]{3,2,1,0:T(8,128)(2,1)} %collective-permute-done.7.refs_3_), channel_id=1, source_target_pairs={{0,1},{1,0},{2,3},{3,2},{4,5},{5,4},{6,7},{7,6},{8,9},{9,8},{10,11... | collective-permute-start | bytes 1572872 | tf_op jit(solution)/shard_map/ppermute | solution.py:235
  75.4 0.5 collective-permute-start.18
  75.9 0.1 pad_add_fusion.place_ref
  76.0 0.0 collective-permute-done.11.refs_5_
  76.0 0.0 collective-permute-done.12.refs_6_
  76.0 1.3 %collective-permute-done.14.refs_7_ = bf16[2,32,32,128]{3,2,1,0:T(8,128)(2,1)} collective-permute-done((bf16[2,32,32,128]{3,2,1,0:T(8,128)(2,1)}, bf16[2,32,32,128]{3,2,1,0:T(8,128)(2,1)}, u32[]{:S(2)}, u32[]{:S(2)}) %collective-permute-start.14) | collective-permute-done | bytes 524320 | tf_op jit(solution)/shard_map/ppermute | solution.py:235
  77.3 3.4 %shard_map.142 = (bf16[576,128]{1,0:T(8,128)(2,1)S(1)}, bf16[576,128]{1,0:T(8,128)(2,1)S(1)}, bf16[576,128]{1,0:T(8,128)(2,1)S(1)}, bf16[576,128]{1,0:T(8,128)(2,1)S(1)}) custom-call(s32[4]{0:T(128)S(1)} %pad_add_fusion.place_ref, bf16[2,32,32,128]{3,2,1,0:T(8,128)(2,1)S(1)} %pad_maximum_fusion.refs_0_, ...), custom_call_target="tpu_custom_call" | custom-call | tf_op jit(solution)/shard_map/pallas_call | solution.py:130
  80.7 0.5 collective-permute-start.15
  81.2 0.6 collective-permute-start.16
  81.7 1.2 %collective-permute-start.17 = (bf16[576,128]{1,0:T(8,128)(2,1)S(1)}, bf16[576,128]{1,0:T(8,128)(2,1)S(1)}, u32[]{:S(2)}, u32[]{:S(2)}) collective-permute-start(bf16[576,128]{1,0:T(8,128)(2,1)S(1)} %get-tuple-element.49), channel_id=1, source_target_pairs={{0,17},{1,16},{16,1},{17,0},{2,19},{3,18},{18,3},{19,2},{4,21},{5,... | collective-permute-start | bytes 442376 | tf_op jit(solution)/shard_map/ppermute | solution.py:243
  82.9 0.0 collective-permute-done.18.refs_9_
  83.0 3.5 %shard_map.143 = (bf16[192,128]{1,0:T(8,128)(2,1)S(1)}, bf16[192,128]{1,0:T(8,128)(2,1)S(1)}, bf16[192,128]{1,0:T(8,128)(2,1)S(1)}, bf16[192,128]{1,0:T(8,128)(2,1)S(1)}) custom-call(s32[4]{0:T(128)S(1)} %pad_add_fusion.place_ref, bf16[2,32,32,128]{3,2,1,0:T(8,128)(2,1)S(1)} %pad_maximum_fusion.refs_0_, ...), custom_call_target="tpu_custom_call" | custom-call | tf_op jit(solution)/shard_map/pallas_call | solution.py:130
  86.5 2.0 %collective-permute-start.19 = (bf16[192,128]{1,0:T(8,128)(2,1)S(1)}, bf16[192,128]{1,0:T(8,128)(2,1)S(1)}, u32[]{:S(2)}, u32[]{:S(2)}) collective-permute-start(bf16[192,128]{1,0:T(8,128)(2,1)S(1)} %get-tuple-element.53), channel_id=1, source_target_pairs={{0,1},{1,0},{2,3},{3,2},{4,5},{5,4},{6,7},{7,6},{8,9},{9,8},{10,11... | collective-permute-start | bytes 147464 | tf_op jit(solution)/shard_map/ppermute | solution.py:235
  88.5 0.6 collective-permute-start.20
  89.0 0.3 collective-permute-done.19.refs_5_
  89.3 0.9 collective-permute-start.21
  90.2 1.2 %collective-permute-done.20.refs_6_ = bf16[192,128]{1,0:T(8,128)(2,1)S(1)} collective-permute-done((bf16[192,128]{1,0:T(8,128)(2,1)S(1)}, bf16[192,128]{1,0:T(8,128)(2,1)S(1)}, u32[]{:S(2)}, u32[]{:S(2)}) %collective-permute-start.20) | collective-permute-done | bytes 49184 | tf_op jit(solution)/shard_map/ppermute | solution.py:235
  91.4 1.6 %collective-permute-done.21.refs_7_ = bf16[192,128]{1,0:T(8,128)(2,1)S(1)} collective-permute-done((bf16[192,128]{1,0:T(8,128)(2,1)S(1)}, bf16[192,128]{1,0:T(8,128)(2,1)S(1)}, u32[]{:S(2)}, u32[]{:S(2)}) %collective-permute-start.21) | collective-permute-done | bytes 49184 | tf_op jit(solution)/shard_map/ppermute | solution.py:243
  93.0 0.0 collective-permute-done.15.refs_1_
  93.0 0.0 collective-permute-done.16.refs_2_
  93.0 0.0 collective-permute-done.17.refs_3_
  93.1 1.8 %shard_map.144 = (bf16[3,512,128]{2,1,0:T(8,128)(2,1)}, f32[3,128,512]{2,1,0:T(8,128)}) custom-call(s32[4]{0:T(128)S(1)} %pad_add_fusion.place_ref, bf16[576,128]{1,0:T(8,128)(2,1)S(1)} %get-tuple-element.46.refs_0_, bf16[576,128]{1,0:T(8,128)(2,1)S(1)} %collective-permute-done.15.refs_1_, bf16[576,128]{1,0:T(8,128)(2,1)S(1)} %collective-permute-done.16.refs_2_, ...), custom_call_target="tpu_custom_call" | custom-call | tf_op jit(solution)/shard_map/pallas_call | solution.py:130
  (8 shorter events, 0.0 us)
Async XLA Ops:
  0.6 34.8 %copy-start.5 = (bf16[80,96]{1,0:T(8,128)(2,1)S(1)}, bf16[80,96]{1,0:T(8,128)(2,1)}, u32[]{:S(2)}) copy-start(bf16[80,96]{1,0:T(8,128)(2,1)} %constant.34.clone.lf_ref) | copy-start | bytes 46084
  0.6 34.7 %copy-start.8 = (bf16[32,240]{1,0:T(8,128)(2,1)S(1)}, bf16[32,240]{1,0:T(8,128)(2,1)}, u32[]{:S(2)}) copy-start(bf16[32,240]{1,0:T(8,128)(2,1)} %constant.35.clone.li_ref) | copy-start | bytes 46084
  0.7 34.7 %copy-start.6 = (f32[40,128]{1,0:T(8,128)S(1)}, f32[40,128]{1,0:T(8,128)}, u32[]{:S(2)}) copy-start(f32[40,128]{1,0:T(8,128)} %constant.36.clone.tc_ref) | copy-start | bytes 61444
  0.7 34.7 %copy-start.7 = (f32[40,128]{1,0:T(8,128)S(1)}, f32[40,128]{1,0:T(8,128)}, u32[]{:S(2)}) copy-start(f32[40,128]{1,0:T(8,128)} %constant.37.clone.ts_ref) | copy-start | bytes 61444
  0.7 34.7 %copy-start.1 = (bf16[256,256]{1,0:T(8,128)(2,1)S(1)}, bf16[256,256]{1,0:T(8,128)(2,1)}, u32[]{:S(2)}) copy-start(bf16[256,256]{1,0:T(8,128)(2,1)} %constant.38.clone.th_ref) | copy-start | bytes 393220
  0.7 34.7 %copy-start.2 = (bf16[256,256]{1,0:T(8,128)(2,1)S(1)}, bf16[256,256]{1,0:T(8,128)(2,1)}, u32[]{:S(2)}) copy-start(bf16[256,256]{1,0:T(8,128)(2,1)} %constant.39.clone.tl_ref) | copy-start | bytes 393220
  0.7 34.7 %copy-start.3 = (bf16[256,256]{1,0:T(8,128)(2,1)S(1)}, bf16[256,256]{1,0:T(8,128)(2,1)}, u32[]{:S(2)}) copy-start(bf16[256,256]{1,0:T(8,128)(2,1)} %constant.40.clone.uh_ref) | copy-start | bytes 393220
  0.7 34.7 %copy-start.4 = (bf16[256,256]{1,0:T(8,128)(2,1)S(1)}, bf16[256,256]{1,0:T(8,128)(2,1)}, u32[]{:S(2)}) copy-start(bf16[256,256]{1,0:T(8,128)(2,1)} %constant.41.clone.ul_ref) | copy-start | bytes 393220
  0.7 34.7 %copy-start = (f32[16,4096]{1,0:T(8,128)S(1)}, f32[16,4096]{1,0:T(8,128)}, u32[]{:S(2)}) copy-start(f32[16,4096]{1,0:T(8,128)} %filt_ref.1) | copy-start | bytes 786436
  39.6 3.7 %collective-permute-start.2 = (bf16[2,48,2048]{2,1,0:T(8,128)(2,1)S(1)}, bf16[2,48,2048]{2,1,0:T(8,128)(2,1)S(1)}, u32[]{:S(2)}, u32[]{:S(2)}) collective-permute-start(bf16[2,48,2048]{2,1,0:T(8,128)(2,1)S(1)} %get-tuple-element.33.refs_0_), channel_id=1, source_target_pairs={{0,1},{1,0},{2,3},{3,2},{4,5},{5,4},{6,7},{7,6},{8,9},{9,8},{10,11... | collective-permute-start | bytes 1179656 | tf_op jit(solution)/shard_map/ppermute | solution.py:235
  42.0 7.0 %collective-permute-start.1 = (bf16[2,48,2048]{2,1,0:T(8,128)(2,1)S(1)}, bf16[2,48,2048]{2,1,0:T(8,128)(2,1)S(1)}, u32[]{:S(2)}, u32[]{:S(2)}) collective-permute-start(bf16[2,48,2048]{2,1,0:T(8,128)(2,1)S(1)} %get-tuple-element.33.refs_0_), channel_id=1, source_target_pairs={{0,2},{2,4},{4,6},{6,8},{8,10},{10,12},{12,14},{14,0},{1,15},{3,1}... | collective-permute-start | bytes 1179656 | tf_op jit(solution)/shard_map/ppermute | solution.py:231
  42.2 6.8 %collective-permute-start = (bf16[32,32,128]{2,1,0:T(8,128)(2,1)S(1)}, bf16[32,32,128]{2,1,0:T(8,128)(2,1)S(1)}, u32[]{:S(2)}, u32[]{:S(2)}) collective-permute-start(bf16[32,32,128]{2,1,0:T(8,128)(2,1)S(1)} %slice.4), channel_id=1, source_target_pairs={{0,16},{16,0},{1,17},{17,1},{2,18},{18,2},{3,19},{19,3},{4,20},{20... | collective-permute-start | bytes 786440 | tf_op jit(solution)/shard_map/ppermute | solution.py:235
  43.3 10.9 %collective-permute-start.4 = (bf16[2,48,2048]{2,1,0:T(8,128)(2,1)S(1)}, bf16[2,48,2048]{2,1,0:T(8,128)(2,1)S(1)}, u32[]{:S(2)}, u32[]{:S(2)}) collective-permute-start(bf16[2,48,2048]{2,1,0:T(8,128)(2,1)S(1)} %collective-permute-done.2), channel_id=1, source_target_pairs={{0,2},{2,4},{4,6},{6,8},{8,10},{10,12},{12,14},{14,0},{1,15},{3,1}... | collective-permute-start | bytes 1179656 | tf_op jit(solution)/shard_map/ppermute | solution.py:231
  49.0 5.6 %collective-permute-start.5 = (bf16[2,32,32,128]{3,2,1,0:T(8,128)(2,1)S(1)}, bf16[2,32,32,128]{3,2,1,0:T(8,128)(2,1)S(1)}, u32[]{:S(2)}, u32[]{:S(2)}) collective-permute-start(bf16[2,32,32,128]{3,2,1,0:T(8,128)(2,1)S(1)} %pad_maximum_fusion.refs_0_), channel_id=1, source_target_pairs={{0,1},{1,0},{2,3},{3,2},{4,5},{5,4},{6,7},{7,6},{8,9},{9,8},{10,11... | collective-permute-start | bytes 1572872 | tf_op jit(solution)/shard_map/ppermute | solution.py:235
  51.1 8.6 %collective-permute-start.3 = (bf16[2,32,32,128]{3,2,1,0:T(8,128)(2,1)S(1)}, bf16[2,32,32,128]{3,2,1,0:T(8,128)(2,1)}, u32[]{:S(2)}, u32[]{:S(2)}) collective-permute-start(bf16[2,32,32,128]{3,2,1,0:T(8,128)(2,1)S(1)} %pad_maximum_fusion.refs_0_), channel_id=1, source_target_pairs={{0,32},{32,64},{64,96},{96,0},{1,97},{33,1},{65,33},{97,65},{2,34}... | collective-permute-start | bytes 1572872 | tf_op jit(solution)/shard_map/ppermute | solution.py:231
  53.6 9.5 %collective-permute-start.8 = (bf16[2,48,2048]{2,1,0:T(8,128)(2,1)S(1)}, bf16[2,48,2048]{2,1,0:T(8,128)(2,1)S(1)}, u32[]{:S(2)}, u32[]{:S(2)}) collective-permute-start(bf16[2,48,2048]{2,1,0:T(8,128)(2,1)S(1)} %collective-permute-done.1.refs_1_), channel_id=1, source_target_pairs={{0,2},{2,4},{4,6},{6,8},{8,10},{10,12},{12,14},{14,0},{1,15},{3,1}... | collective-permute-start | bytes 1179656 | tf_op jit(solution)/shard_map/ppermute | solution.py:231
  54.2 10.6 %collective-permute-start.10 = (bf16[2,48,2048]{2,1,0:T(8,128)(2,1)S(1)}, bf16[2,48,2048]{2,1,0:T(8,128)(2,1)S(1)}, u32[]{:S(2)}, u32[]{:S(2)}) collective-permute-start(bf16[2,48,2048]{2,1,0:T(8,128)(2,1)S(1)} %collective-permute-done.4.refs_2_), channel_id=1, source_target_pairs={{0,2},{2,4},{4,6},{6,8},{8,10},{10,12},{12,14},{14,0},{1,15},{3,1}... | collective-permute-start | bytes 1179656 | tf_op jit(solution)/shard_map/ppermute | solution.py:231
  54.6 16.4 %collective-permute-start.6 = (bf16[2,32,32,128]{3,2,1,0:T(8,128)(2,1)S(1)}, bf16[2,32,32,128]{3,2,1,0:T(8,128)(2,1)}, u32[]{:S(2)}, u32[]{:S(2)}) collective-permute-start(bf16[2,32,32,128]{3,2,1,0:T(8,128)(2,1)S(1)} %collective-permute-done.5.refs_4_), channel_id=1, source_target_pairs={{0,32},{32,64},{64,96},{96,0},{1,97},{33,1},{65,33},{97,65},{2,34}... | collective-permute-start | bytes 1572872 | tf_op jit(solution)/shard_map/ppermute | solution.py:231
  59.7 14.7 %collective-permute-start.7 = (bf16[2,32,32,128]{3,2,1,0:T(8,128)(2,1)}, bf16[2,32,32,128]{3,2,1,0:T(8,128)(2,1)}, u32[]{:S(2)}, u32[]{:S(2)}) collective-permute-start(bf16[2,32,32,128]{3,2,1,0:T(8,128)(2,1)} %collective-permute-done.3.refs_1_), channel_id=1, source_target_pairs={{0,32},{32,64},{64,96},{96,0},{1,97},{33,1},{65,33},{97,65},{2,34}... | collective-permute-start | bytes 1572872 | tf_op jit(solution)/shard_map/ppermute | solution.py:231
  63.1 7.0 %collective-permute-start.9 = (bf16[2,48,2048]{2,1,0:T(8,128)(2,1)S(1)}, bf16[2,48,2048]{2,1,0:T(8,128)(2,1)}, u32[]{:S(2)}, u32[]{:S(2)}) collective-permute-start(bf16[2,48,2048]{2,1,0:T(8,128)(2,1)S(1)} %collective-permute-done.8.refs_3_), channel_id=1, source_target_pairs={{0,2},{2,4},{4,6},{6,8},{8,10},{10,12},{12,14},{14,0},{1,15},{3,1}... | collective-permute-start | bytes 1179656 | tf_op jit(solution)/shard_map/ppermute | solution.py:231
  64.8 9.4 %collective-permute-start.13 = (bf16[2,48,2048]{2,1,0:T(8,128)(2,1)S(1)}, bf16[2,48,2048]{2,1,0:T(8,128)(2,1)S(1)}, u32[]{:S(2)}, u32[]{:S(2)}) collective-permute-start(bf16[2,48,2048]{2,1,0:T(8,128)(2,1)S(1)} %collective-permute-done.10.refs_4_), channel_id=1, source_target_pairs={{0,2},{2,4},{4,6},{6,8},{8,10},{10,12},{12,14},{14,0},{1,15},{3,1}... | collective-permute-start | bytes 1179656 | tf_op jit(solution)/shard_map/ppermute | solution.py:231
  70.1 5.9 %collective-permute-start.11 = (bf16[2,32,32,128]{3,2,1,0:T(8,128)(2,1)}, bf16[2,32,32,128]{3,2,1,0:T(8,128)(2,1)}, u32[]{:S(2)}, u32[]{:S(2)}) collective-permute-start(bf16[2,32,32,128]{3,2,1,0:T(8,128)(2,1)} %collective-permute-done.3.refs_1_), channel_id=1, source_target_pairs={{0,1},{1,0},{2,3},{3,2},{4,5},{5,4},{6,7},{7,6},{8,9},{9,8},{10,11... | collective-permute-start | bytes 1572872 | tf_op jit(solution)/shard_map/ppermute | solution.py:235
  71.1 4.9 %collective-permute-start.12 = (bf16[2,32,32,128]{3,2,1,0:T(8,128)(2,1)}, bf16[2,32,32,128]{3,2,1,0:T(8,128)(2,1)}, u32[]{:S(2)}, u32[]{:S(2)}) collective-permute-start(bf16[2,32,32,128]{3,2,1,0:T(8,128)(2,1)} %collective-permute-done.6.refs_2_), channel_id=1, source_target_pairs={{0,1},{1,0},{2,3},{3,2},{4,5},{5,4},{6,7},{7,6},{8,9},{9,8},{10,11... | collective-permute-start | bytes 1572872 | tf_op jit(solution)/shard_map/ppermute | solution.py:235
  74.4 2.9 %collective-permute-start.14 = (bf16[2,32,32,128]{3,2,1,0:T(8,128)(2,1)}, bf16[2,32,32,128]{3,2,1,0:T(8,128)(2,1)}, u32[]{:S(2)}, u32[]{:S(2)}) collective-permute-start(bf16[2,32,32,128]{3,2,1,0:T(8,128)(2,1)} %collective-permute-done.7.refs_3_), channel_id=1, source_target_pairs={{0,1},{1,0},{2,3},{3,2},{4,5},{5,4},{6,7},{7,6},{8,9},{9,8},{10,11... | collective-permute-start | bytes 1572872 | tf_op jit(solution)/shard_map/ppermute | solution.py:235
  75.4 7.5 %collective-permute-start.18 = (bf16[2,48,2048]{2,1,0:T(8,128)(2,1)}, bf16[2,48,2048]{2,1,0:T(8,128)(2,1)}, u32[]{:S(2)}, u32[]{:S(2)}) collective-permute-start(bf16[2,48,2048]{2,1,0:T(8,128)(2,1)} %collective-permute-done.9.refs_8_), channel_id=1, source_target_pairs={{0,2},{2,4},{4,6},{6,8},{8,10},{10,12},{12,14},{14,0},{1,15},{3,1}... | collective-permute-start | bytes 1179656 | tf_op jit(solution)/shard_map/ppermute | solution.py:231
  80.7 12.3 %collective-permute-start.15 = (bf16[576,128]{1,0:T(8,128)(2,1)S(1)}, bf16[576,128]{1,0:T(8,128)(2,1)S(1)}, u32[]{:S(2)}, u32[]{:S(2)}) collective-permute-start(bf16[576,128]{1,0:T(8,128)(2,1)S(1)} %get-tuple-element.47), channel_id=1, source_target_pairs={{0,1},{1,0},{2,3},{3,2},{4,5},{5,4},{6,7},{7,6},{8,9},{9,8},{10,11... | collective-permute-start | bytes 442376 | tf_op jit(solution)/shard_map/ppermute | solution.py:235
  81.2 11.9 %collective-permute-start.16 = (bf16[576,128]{1,0:T(8,128)(2,1)S(1)}, bf16[576,128]{1,0:T(8,128)(2,1)S(1)}, u32[]{:S(2)}, u32[]{:S(2)}) collective-permute-start(bf16[576,128]{1,0:T(8,128)(2,1)S(1)} %get-tuple-element.48), channel_id=1, source_target_pairs={{0,16},{16,0},{1,17},{17,1},{2,18},{18,2},{3,19},{19,3},{4,20},{20... | collective-permute-start | bytes 442376 | tf_op jit(solution)/shard_map/ppermute | solution.py:235
  81.7 11.3 %collective-permute-start.17 = (bf16[576,128]{1,0:T(8,128)(2,1)S(1)}, bf16[576,128]{1,0:T(8,128)(2,1)S(1)}, u32[]{:S(2)}, u32[]{:S(2)}) collective-permute-start(bf16[576,128]{1,0:T(8,128)(2,1)S(1)} %get-tuple-element.49), channel_id=1, source_target_pairs={{0,17},{1,16},{16,1},{17,0},{2,19},{3,18},{18,3},{19,2},{4,21},{5,... | collective-permute-start | bytes 442376 | tf_op jit(solution)/shard_map/ppermute | solution.py:243
  86.5 2.8 %collective-permute-start.19 = (bf16[192,128]{1,0:T(8,128)(2,1)S(1)}, bf16[192,128]{1,0:T(8,128)(2,1)S(1)}, u32[]{:S(2)}, u32[]{:S(2)}) collective-permute-start(bf16[192,128]{1,0:T(8,128)(2,1)S(1)} %get-tuple-element.53), channel_id=1, source_target_pairs={{0,1},{1,0},{2,3},{3,2},{4,5},{5,4},{6,7},{7,6},{8,9},{9,8},{10,11... | collective-permute-start | bytes 147464 | tf_op jit(solution)/shard_map/ppermute | solution.py:235
  88.5 3.0 %collective-permute-start.20 = (bf16[192,128]{1,0:T(8,128)(2,1)S(1)}, bf16[192,128]{1,0:T(8,128)(2,1)S(1)}, u32[]{:S(2)}, u32[]{:S(2)}) collective-permute-start(bf16[192,128]{1,0:T(8,128)(2,1)S(1)} %get-tuple-element.54), channel_id=1, source_target_pairs={{0,16},{16,0},{1,17},{17,1},{2,18},{18,2},{3,19},{19,3},{4,20},{20... | collective-permute-start | bytes 147464 | tf_op jit(solution)/shard_map/ppermute | solution.py:235
  89.3 3.7 %collective-permute-start.21 = (bf16[192,128]{1,0:T(8,128)(2,1)S(1)}, bf16[192,128]{1,0:T(8,128)(2,1)S(1)}, u32[]{:S(2)}, u32[]{:S(2)}) collective-permute-start(bf16[192,128]{1,0:T(8,128)(2,1)S(1)} %get-tuple-element.55), channel_id=1, source_target_pairs={{0,17},{1,16},{16,1},{17,0},{2,19},{3,18},{18,3},{19,2},{4,21},{5,... | collective-permute-start | bytes 147464 | tf_op jit(solution)/shard_map/ppermute | solution.py:243

commit v6 on v5

--- a/solution.py
+++ b/solution.py
@@ -177,27 +177,33 @@
 
 
 def product_kernel(place_ref, *refs):
-    own, first, second, third, other, other_first, other_second, other_third = refs[:8]
-    blocks, outs = refs[8:-4], refs[-4:]
-    halves = [jnp.concatenate([block[h] for block in blocks], 0) for h in range(2)]
-    rows, length = halves[0].shape
-    _, steps, part, width = own.shape
-    size = 4 * part
-    for rc, pieces in enumerate(((own, first, third, other_second), (other, second, other_third, other_first))):
+    if len(refs) == 14:
+        own, first, second, third, other, other_first, other_second, other_third = refs[:8]
+        block, outs, x_ref = refs[8], refs[9:13], refs[13]
+        _, steps, part, width = own.shape
+        for rc, pieces in enumerate(((own, first, third, other_second), (other, second, other_third, other_first))):
+            for ry in range(2):
+                for k, ref in enumerate(pieces):
+                    row = ((2 * rc + ry) * 4 + k) * part
+                    for i in range(steps):
+                        x_ref[row : row + part, i * width : (i + 1) * width] = ref[ry, i]
+    else:
+        x_ref, block, outs = refs[0], refs[1], refs[2:]
+    _, rows, length = block.shape
+    size = x_ref.shape[0] // 4
+    part = size // 4
+    for rc in range(2):
         total = None
         for h in range(2):
-            span = range(h * steps // 2, (h + 1) * steps // 2)
-            x = jnp.concatenate(
-                [jnp.concatenate([ref[y, i] for i in span], 1) for y in range(2) for ref in pieces], 0
-            )
-            got = lax.dot_general(halves[h], x, (((1,), (1,)), ((), ())), preferred_element_type=jnp.float32)
+            x = x_ref[2 * rc * size : 2 * (rc + 1) * size, h * length : (h + 1) * length]
+            got = lax.dot_general(block[h], x, (((1,), (1,)), ((), ())), preferred_element_type=jnp.float32)
             total = got if total is None else total + got
         for ry in range(2):
             t = total[:, ry * size : (ry + 1) * size]
             u = jnp.concatenate([t[:, :part], t[:, 3 * part :], t[:, 2 * part : 3 * part], t[:, part : 2 * part]], 1)
             out_ref = outs[2 * ry + rc]
             out_ref[:rows] = jnp.where(place_ref[2] == 0, u, t).astype(jnp.bfloat16)
-            out_ref[rows:] = chunk(place_ref, blocks, ry, rc)
+            out_ref[rows:] = chunk(place_ref, [block], ry, rc)
 
 
 def finish_kernel(chans, n, slots, place_ref, *refs):
@@ -225,9 +231,12 @@
             weight_ref[s, pl.ds(at, part), :] = rows[k * part : (k + 1) * part]
 
 
-def spread(x, axis):
+def spread(x, axis, crossed=False, hops=1):
     n = lax.axis_size(axis)
-    perm = [(2 * i, 2 * ((i + 1) % n)) for i in range(n)] + [(2 * i + 1, 2 * ((i + n - 1) % n) + 1) for i in range(n)]
+    perm = []
+    for i in range(n):
+        for core, way in ((0, 1), (1, -1)):
+            perm.append((2 * i + (1 - core if crossed else core), 2 * ((i + way * hops) % n) + core))
     return lax.ppermute(x, (axis, "core"), perm)
 
 
@@ -272,44 +281,41 @@
 
     block, filter_grad = spectral(sent, filters)
     a1 = spread(block, "z")
-    turned = swap(block, "core")
-    turned = after(turned, block)
-    b1 = spread(turned, "z")
-    a1 = after(a1, turned)
-    a2 = spread(a1, "z")
+    start, y_rows = lax.optimization_barrier((block, y_rows))
+    b1 = spread(start, "z", True)
+    a2 = spread(after(a1, block), "z")
     b1 = after(b1, a1)
     b2 = spread(b1, "z")
-    both_rows = jnp.stack([own_rows, after(y_rows, a1)])
-    other_rows = swap(both_rows, "core")
+    both_rows = jnp.stack([own_rows, after(y_rows, block)])
+    other_rows = swap(after(both_rows, b1), "core")
     xa1 = spread(both_rows, "x")
-    other_rows = after(other_rows, b1)
-    xb1 = spread(other_rows, "x")
+    xb1 = spread(after(both_rows, a1), "x", True)
     a2 = after(a2, b1)
     a3 = spread(a2, "z")
     b2 = after(b2, a2)
     b3 = spread(b2, "z")
-    xa1 = after(xa1, b1)
+    xa1 = after(xa1, a2)
     xa2 = spread(xa1, "x")
-    (first,) = vmem_call(stack_kernel, [((2, 6 * block.shape[1], block.shape[2]), bf16)], block, a1, b1, a2, b2, b3)
+    (first,) = vmem_call(stack_kernel, [((2, 7 * block.shape[1], block.shape[2]), bf16)], block, a1, b1, a2, b2, a3, b3)
     a3 = after(a3, b2)
     a4 = spread(a3, "z")
 
-    slots = (((0, 0), (1, 0), (1, 1), (2, 0), (2, 1), (3, 1)), ((3, 0), (4, 0)))
-    first, last = (first,), (a3, a4)
-    size = 3 * chans
+    slots = (((0, 0), (1, 0), (1, 1), (2, 0), (2, 1), (3, 0), (3, 1)), ((4, 0),))
     fa1 = swap(after(xa1, a3), "core")
     fb1 = swap(after(xb1, a3), "core")
     fa2 = swap(after(xa2, first), "core")
-    far = [fa1, fb1, fa2]
-    pieces = (both_rows, xa1, xb1, xa2, other_rows, *far)
-    groups = ()
-    for slot_list, blocks in zip(slots, (first, last)):
-        if groups:
-            blocks = lax.optimization_barrier((*blocks, groups[0]))[:-1]
-        parts = vmem_call(
-            product_kernel, [((2 * size * len(slot_list), width), bf16)] * 4, *pieces, *blocks, place=place
-        )
-        groups += trade(parts)
+    pieces = (both_rows, xa1, xb1, xa2, other_rows, fa1, fb1, fa2)
+    *parts, whole = vmem_call(
+        product_kernel,
+        [((2 * first.shape[1], width), bf16)] * 4 + [((4 * n_x * rows, owners * width), bf16)],
+        *pieces,
+        first,
+        place=place,
+    )
+    groups = trade(parts)
+    a4 = after(a4, parts[0])
+    parts = vmem_call(product_kernel, [((2 * a4.shape[1], width), bf16)] * 4, whole, a4, place=place)
+    groups += trade(parts)
     proj_grad, weight_grad = vmem_call(
         functools.partial(finish_kernel, chans, n, slots),
         [((3, count, width), bf16), ((3, n_x * rows, count), jnp.float32)],

time: 95.1 us -> 99.4 us (1.045)
  starting transfers between devices: 25 us -> 40.6 us
  waiting for transfers between devices: 21.2 us -> 9.34 us
    ppermute x10, waiting for transfers between devices: 16.1 us -> 3.76 us  [spread(): return lax.ppermute(x, (axis, 'core'), perm)]
    ppermute x10 -> x9, starting transfers between devices: 10.4 us -> 19.4 us  [swap(): return lax.ppermute(x, axis, [(0, 1), (1, 0)])]
    ppermute x10, starting transfers between devices: 12.5 us -> 19 us  [spread(): return lax.ppermute(x, (axis, 'core'), perm)]
    ppermute x10 -> x9, waiting for transfers between devices: 3.41 us -> 4.46 us  [swap(): return lax.ppermute(x, axis, [(0, 1), (1, 0)])]
  transfers between devices with their start and end apart: 22 -> 21, of which waited for: 10 -> 6; matrix products, arithmetic and copies ran while one was open for 0% -> 0% of each run, Pallas kernels for 7% -> 12%
where the time goes in v6:
time: 99.4 us; the launch traced here: 99.1 us
  starting transfers between devices  40.6 us (41%)
  blocking collectives  32.4 us (33%)
  Pallas kernels  15.7 us (16%)
  waiting for transfers between devices  9.34 us (9%)
    all_to_all x1, blocking collectives, local(): sent = lax.all_to_all(sent, SEQ, split_axis=0, concat_axis=0, tiled=True)  32.4 us
    ppermute x9, starting transfers between devices, swap(): return lax.ppermute(x, axis, [(0, 1), (1, 0)])  19.4 us
    ppermute x10, starting transfers between devices, spread(): return lax.ppermute(x, (axis, 'core'), perm)  19 us
    pallas_call x5, Pallas kernels, vmem_call(): pl.pallas_call(body, out_shape=tuple((jax.ShapeDtypeStruct(shape, dtype)...  13.5 us
    ppermute x9, waiting for transfers between devices, swap(): return lax.ppermute(x, axis, [(0, 1), (1, 0)])  4.46 us
    ppermute x10, waiting for transfers between devices, spread(): return lax.ppermute(x, (axis, 'core'), perm)  3.76 us
    pallas_call x1, Pallas kernels, local(): pl.pallas_call(functools.partial(pack_kernel, chans), out_shape=jax.Shape...  2.28 us
    ppermute x2, starting transfers between devices, trade(): lax.ppermute(parts[3], ('ylo', 'core'), [(0, 3), (1, 2), (2, 1), (3, 0)])  2.15 us
  transfers between devices with their start and end apart: 21, of which 6 were waited for; matrix products, arithmetic and copies ran while one was open for 0% of the time, Pallas kernels for 12%

profile of v6, /device:TPU:1, one launch (start us, length us, event | category | flops | bytes accessed | tf_op | source)
XLA Modules:
  0.0 99.1 jit_solution(14253380322853775345)
XLA Ops:
  0.6 0.0 copy-start.1
  0.6 0.0 copy-start.2
  0.7 0.0 copy-start.3
  0.7 0.0 copy-start.4
  0.7 0.0 copy-start.5
  0.7 0.0 copy-start.6
  0.7 0.0 copy-start.8
  0.7 0.0 copy-start.7
  0.7 0.0 copy-start
  0.7 2.3 %shard_map.139 = bf16[32,96,128]{2,1,0:T(8,128)(2,1)} custom-call(bf16[32,4,32,128]{3,2,1,0:T(8,128)(2,1)} %bitcast.10, bf16[3,32,16,128]{3,2,1,0:T(8,128)(2,1)} %bitcast.12, bf16[32,16,128]{2,1,0:T(8,128)(2,1)} %bitcast.14), custom_call_target="tpu_custom_call" | custom-call | tf_op jit(solution)/shard_map/pallas_call | solution.py:266
  3.0 32.4 %all_to_all.5.sent_ref = bf16[32,96,128]{2,1,0:T(8,128)(2,1)S(1)} all-to-all(bf16[32,96,128]{2,1,0:T(8,128)(2,1)} %shard_map.139), channel_id=1, replica_groups=mesh['yhi'=2,'x'=4,'ylo'=2,'z'=8,'core'=2] {'ylo','z','core'}, dimensions={0} | all-to-all | bytes 1572864 | tf_op jit(solution)/shard_map/all_to_all | solution.py:277
  35.4 1.3 %collective-permute-start = (bf16[32,32,128]{2,1,0:T(8,128)(2,1)S(1)}, bf16[32,32,128]{2,1,0:T(8,128)(2,1)S(1)}, u32[]{:S(2)}, u32[]{:S(2)}) collective-permute-start(bf16[32,32,128]{2,1,0:T(8,128)(2,1)S(1)} %slice.4), channel_id=1, source_target_pairs={{0,16},{16,0},{1,17},{17,1},{2,18},{18,2},{3,19},{19,3},{4,20},{20... | collective-permute-start | bytes 786440 | tf_op jit(solution)/shard_map/ppermute | solution.py:244
  36.7 0.0 copy-done.1
  36.7 0.0 copy-done.2
  36.7 0.0 copy-done.3
  36.7 0.0 copy-done.4
  36.8 4.1 %shard_map.140 = (bf16[2,48,2048]{2,1,0:T(8,128)(2,1)S(1)}, f32[16,4096]{1,0:T(8,128)}) custom-call(bf16[32,96,128]{2,1,0:T(8,128)(2,1)S(1)} %all_to_all.5.sent_ref, f32[16,4096]{1,0:T(8,128)S(1)} %copy-done, bf16[80,96]{1,0:T(8,128)(2,1)S(1)} %copy-done.7, bf16[32,240]{1,0:T(8,128)(2,1)S(1)} %copy-done.8, f32[40,128]{1,0:T(8,128)S(1)} %copy-done.6, ...), custom_call_target="tpu_custom_call" | custom-call | tf_op jit(solution)/shard_map/pallas_call | solution.py:130
  40.9 0.5 collective-permute-start.2
  41.4 0.0 collective-permute-done
  41.4 5.6 %collective-permute-start.4 = (bf16[2,48,2048]{2,1,0:T(8,128)(2,1)S(1)}, bf16[2,48,2048]{2,1,0:T(8,128)(2,1)S(1)}, u32[]{:S(2)}, u32[]{:S(2)}) collective-permute-start(bf16[2,48,2048]{2,1,0:T(8,128)(2,1)S(1)} %get-tuple-element.39.refs_0_), channel_id=1, source_target_pairs={{1,2},{0,15},{3,4},{2,1},{5,6},{4,3},{7,8},{6,5},{9,10},{8,7},{11,... | collective-permute-start | bytes 1179656 | tf_op jit(solution)/shard_map/ppermute | solution.py:240
  47.0 0.1 pad_maximum_fusion.refs_0_
  47.1 2.6 %collective-permute-start.1 = (bf16[2,32,32,128]{3,2,1,0:T(8,128)(2,1)S(1)}, bf16[2,32,32,128]{3,2,1,0:T(8,128)(2,1)}, u32[]{:S(2)}, u32[]{:S(2)}) collective-permute-start(bf16[2,32,32,128]{3,2,1,0:T(8,128)(2,1)S(1)} %pad_maximum_fusion.refs_0_), channel_id=1, source_target_pairs={{0,32},{1,97},{32,64},{33,1},{64,96},{65,33},{96,0},{97,65},{2,34}... | collective-permute-start | bytes 1572872 | tf_op jit(solution)/shard_map/ppermute | solution.py:240
  49.6 0.0 collective-permute-done.2.refs_1_
  49.6 0.7 collective-permute-start.3
  50.3 3.2 %collective-permute-done.4.refs_2_ = bf16[2,48,2048]{2,1,0:T(8,128)(2,1)S(1)} collective-permute-done((bf16[2,48,2048]{2,1,0:T(8,128)(2,1)S(1)}, bf16[2,48,2048]{2,1,0:T(8,128)(2,1)S(1)}, u32[]{:S(2)}, u32[]{:S(2)}) %collective-permute-start.4) | collective-permute-done | bytes 393248 | tf_op jit(solution)/shard_map/ppermute | solution.py:240
  53.5 1.5 %collective-permute-start.9 = (bf16[2,48,2048]{2,1,0:T(8,128)(2,1)S(1)}, bf16[2,48,2048]{2,1,0:T(8,128)(2,1)S(1)}, u32[]{:S(2)}, u32[]{:S(2)}) collective-permute-start(bf16[2,48,2048]{2,1,0:T(8,128)(2,1)S(1)} %collective-permute-done.4.refs_2_), channel_id=1, source_target_pairs={{0,2},{1,15},{2,4},{3,1},{4,6},{5,3},{6,8},{7,5},{8,10},{9,7},{10,... | collective-permute-start | bytes 1179656 | tf_op jit(solution)/shard_map/ppermute | solution.py:240
  54.9 2.5 %collective-permute-start.5 = (bf16[2,32,32,128]{3,2,1,0:T(8,128)(2,1)S(1)}, bf16[2,32,32,128]{3,2,1,0:T(8,128)(2,1)}, u32[]{:S(2)}, u32[]{:S(2)}) collective-permute-start(bf16[2,32,32,128]{3,2,1,0:T(8,128)(2,1)S(1)} %pad_maximum_fusion.refs_0_), channel_id=1, source_target_pairs={{1,32},{0,97},{33,64},{32,1},{65,96},{64,33},{97,0},{96,65},{3,34}... | collective-permute-start | bytes 1572872 | tf_op jit(solution)/shard_map/ppermute | solution.py:240
  57.5 0.0 collective-permute-done.3.refs_3_
  57.5 0.0 collective-permute-done.1.refs_1_
  57.5 1.7 %collective-permute-start.6 = (bf16[2,32,32,128]{3,2,1,0:T(8,128)(2,1)}, bf16[2,32,32,128]{3,2,1,0:T(8,128)(2,1)}, u32[]{:S(2)}, u32[]{:S(2)}) collective-permute-start(bf16[2,32,32,128]{3,2,1,0:T(8,128)(2,1)} %collective-permute-done.1.refs_1_), channel_id=1, source_target_pairs={{0,32},{1,97},{32,64},{33,1},{64,96},{65,33},{96,0},{97,65},{2,34}... | collective-permute-start | bytes 1572872 | tf_op jit(solution)/shard_map/ppermute | solution.py:240
  59.2 2.4 %collective-permute-start.8 = (bf16[2,48,2048]{2,1,0:T(8,128)(2,1)S(1)}, bf16[2,48,2048]{2,1,0:T(8,128)(2,1)}, u32[]{:S(2)}, u32[]{:S(2)}) collective-permute-start(bf16[2,48,2048]{2,1,0:T(8,128)(2,1)S(1)} %collective-permute-done.3.refs_3_), channel_id=1, source_target_pairs={{0,2},{1,15},{2,4},{3,1},{4,6},{5,3},{6,8},{7,5},{8,10},{9,7},{10,... | collective-permute-start | bytes 1179656 | tf_op jit(solution)/shard_map/ppermute | solution.py:240
  61.6 0.0 collective-permute-done.9.refs_4_
  61.6 1.6 %collective-permute-start.12 = (bf16[2,48,2048]{2,1,0:T(8,128)(2,1)S(1)}, bf16[2,48,2048]{2,1,0:T(8,128)(2,1)S(1)}, u32[]{:S(2)}, u32[]{:S(2)}) collective-permute-start(bf16[2,48,2048]{2,1,0:T(8,128)(2,1)S(1)} %collective-permute-done.9.refs_4_), channel_id=1, source_target_pairs={{0,2},{1,15},{2,4},{3,1},{4,6},{5,3},{6,8},{7,5},{8,10},{9,7},{10,... | collective-permute-start | bytes 1179656 | tf_op jit(solution)/shard_map/ppermute | solution.py:240
  63.2 5.2 %collective-permute-start.7 = (bf16[2,32,32,128]{3,2,1,0:T(8,128)(2,1)S(1)}, bf16[2,32,32,128]{3,2,1,0:T(8,128)(2,1)}, u32[]{:S(2)}, u32[]{:S(2)}) collective-permute-start(bf16[2,32,32,128]{3,2,1,0:T(8,128)(2,1)S(1)} %pad_maximum_fusion.refs_0_), channel_id=1, source_target_pairs={{0,1},{1,0},{2,3},{3,2},{4,5},{5,4},{6,7},{7,6},{8,9},{9,8},{10,11... | collective-permute-start | bytes 1572872 | tf_op jit(solution)/shard_map/ppermute | solution.py:244
  68.4 0.0 collective-permute-done.8.refs_5_
  68.4 0.6 collective-permute-done.5.refs_2_
  68.9 5.8 %collective-permute-start.11 = (bf16[2,32,32,128]{3,2,1,0:T(8,128)(2,1)}, bf16[2,32,32,128]{3,2,1,0:T(8,128)(2,1)}, u32[]{:S(2)}, u32[]{:S(2)}) collective-permute-start(bf16[2,32,32,128]{3,2,1,0:T(8,128)(2,1)} %collective-permute-done.5.refs_2_), channel_id=1, source_target_pairs={{0,1},{1,0},{2,3},{3,2},{4,5},{5,4},{6,7},{7,6},{8,9},{9,8},{10,11... | collective-permute-start | bytes 1572872 | tf_op jit(solution)/shard_map/ppermute | solution.py:244
  74.7 0.0 collective-permute-start.10
  74.7 0.0 collective-permute-done.12.refs_6_
  74.7 1.2 %shard_map.141.refs_8_ = bf16[2,336,2048]{2,1,0:T(8,128)(2,1)S(1)} custom-call(bf16[2,48,2048]{2,1,0:T(8,128)(2,1)S(1)} %get-tuple-element.39.refs_0_, bf16[2,48,2048]{2,1,0:T(8,128)(2,1)S(1)} %collective-permute-done.2.refs_1_, bf16[2,48,2048]{2,1,0:T(8,128)(2,1)S(1)} %collective-permute-done.4.refs_2_, ...), custom_call_target="tpu_custom_call" | custom-call | tf_op jit(solution)/shard_map/pallas_call | solution.py:130
  75.9 0.0 collective-permute-done.6.refs_3_
  75.9 4.2 %collective-permute-start.13 = (bf16[2,32,32,128]{3,2,1,0:T(8,128)(2,1)}, bf16[2,32,32,128]{3,2,1,0:T(8,128)(2,1)}, u32[]{:S(2)}, u32[]{:S(2)}) collective-permute-start(bf16[2,32,32,128]{3,2,1,0:T(8,128)(2,1)} %collective-permute-done.6.refs_3_), channel_id=1, source_target_pairs={{0,1},{1,0},{2,3},{3,2},{4,5},{5,4},{6,7},{7,6},{8,9},{9,8},{10,11... | collective-permute-start | bytes 1572872 | tf_op jit(solution)/shard_map/ppermute | solution.py:244
  80.1 0.0 collective-permute-start.17
  80.1 0.1 pad_add_fusion.place_ref
  80.2 0.0 collective-permute-done.7.refs_4_
  80.2 0.0 collective-permute-done.11.refs_6_
  80.2 0.0 collective-permute-done.10.refs_5_
  80.2 1.8 %collective-permute-done.13.refs_7_ = bf16[2,32,32,128]{3,2,1,0:T(8,128)(2,1)} collective-permute-done((bf16[2,32,32,128]{3,2,1,0:T(8,128)(2,1)}, bf16[2,32,32,128]{3,2,1,0:T(8,128)(2,1)}, u32[]{:S(2)}, u32[]{:S(2)}) %collective-permute-start.13) | collective-permute-done | bytes 524320 | tf_op jit(solution)/shard_map/ppermute | solution.py:244
  82.0 3.9 %shard_map.142 = (bf16[672,128]{1,0:T(8,128)(2,1)S(1)}, bf16[672,128]{1,0:T(8,128)(2,1)S(1)}, bf16[672,128]{1,0:T(8,128)(2,1)S(1)}, bf16[672,128]{1,0:T(8,128)(2,1)S(1)}, bf16[512,4096]{1,0:T(8,128)(2,1)S(1)}) custom-call(s32[4]{0:T(128)S(1)} %pad_add_fusion.place_ref, bf16[2,32,32,128]{3,2,1,0:T(8,128)(2,1)S(1)} %pad_maximum_fusion.refs_0_, ...), custom_call_target="tpu_custom_call" | custom-call | tf_op jit(solution)/shard_map/pallas_call | solution.py:130
  85.9 0.5 collective-permute-start.14
  86.4 0.5 collective-permute-start.15
  86.9 1.3 %collective-permute-start.16 = (bf16[672,128]{1,0:T(8,128)(2,1)S(1)}, bf16[672,128]{1,0:T(8,128)(2,1)S(1)}, u32[]{:S(2)}, u32[]{:S(2)}) collective-permute-start(bf16[672,128]{1,0:T(8,128)(2,1)S(1)} %get-tuple-element.53), channel_id=1, source_target_pairs={{0,17},{1,16},{16,1},{17,0},{2,19},{3,18},{18,3},{19,2},{4,21},{5,... | collective-permute-start | bytes 516104 | tf_op jit(solution)/shard_map/ppermute | solution.py:252
  88.2 0.0 collective-permute-done.17.refs_1_
  88.2 2.4 %shard_map.143 = (bf16[96,128]{1,0:T(8,128)(2,1)S(1)}, bf16[96,128]{1,0:T(8,128)(2,1)S(1)}, bf16[96,128]{1,0:T(8,128)(2,1)S(1)}, bf16[96,128]{1,0:T(8,128)(2,1)S(1)}) custom-call(s32[4]{0:T(128)S(1)} %pad_add_fusion.place_ref, bf16[512,4096]{1,0:T(8,128)(2,1)S(1)} %get-tuple-element.54.refs_0_, bf16[2,48,2048]{2,1,0:T(8,128)(2,1)} %collective-permute-done.17.refs_1_), custom_call_target="tpu_custom_call" | custom-call | tf_op jit(solution)/shard_map/pallas_call | solution.py:130
  90.6 1.4 %collective-permute-start.18 = (bf16[96,128]{1,0:T(8,128)(2,1)S(1)}, bf16[96,128]{1,0:T(8,128)(2,1)S(1)}, u32[]{:S(2)}, u32[]{:S(2)}) collective-permute-start(bf16[96,128]{1,0:T(8,128)(2,1)S(1)} %get-tuple-element.57), channel_id=1, source_target_pairs={{0,1},{1,0},{2,3},{3,2},{4,5},{5,4},{6,7},{7,6},{8,9},{9,8},{10,11... | collective-permute-start | bytes 73736 | tf_op jit(solution)/shard_map/ppermute | solution.py:244
  92.0 0.5 collective-permute-start.19
  92.6 0.3 collective-permute-done.18.refs_5_
  92.9 0.9 collective-permute-start.20
  93.8 2.4 %collective-permute-done.19.refs_6_ = bf16[96,128]{1,0:T(8,128)(2,1)S(1)} collective-permute-done((bf16[96,128]{1,0:T(8,128)(2,1)S(1)}, bf16[96,128]{1,0:T(8,128)(2,1)S(1)}, u32[]{:S(2)}, u32[]{:S(2)}) %collective-permute-start.19) | collective-permute-done | bytes 24608 | tf_op jit(solution)/shard_map/ppermute | solution.py:244
  96.1 1.1 %collective-permute-done.20.refs_7_ = bf16[96,128]{1,0:T(8,128)(2,1)S(1)} collective-permute-done((bf16[96,128]{1,0:T(8,128)(2,1)S(1)}, bf16[96,128]{1,0:T(8,128)(2,1)S(1)}, u32[]{:S(2)}, u32[]{:S(2)}) %collective-permute-start.20) | collective-permute-done | bytes 24608 | tf_op jit(solution)/shard_map/ppermute | solution.py:252
  97.2 0.0 collective-permute-done.14.refs_1_
  97.2 0.0 collective-permute-done.15.refs_2_
  97.3 0.0 collective-permute-done.16.refs_3_
  97.3 1.8 %shard_map.144 = (bf16[3,512,128]{2,1,0:T(8,128)(2,1)}, f32[3,128,512]{2,1,0:T(8,128)}) custom-call(s32[4]{0:T(128)S(1)} %pad_add_fusion.place_ref, bf16[672,128]{1,0:T(8,128)(2,1)S(1)} %get-tuple-element.50.refs_0_, bf16[672,128]{1,0:T(8,128)(2,1)S(1)} %collective-permute-done.14.refs_1_, bf16[672,128]{1,0:T(8,128)(2,1)S(1)} %collective-permute-done.15.refs_2_, ...), custom_call_target="tpu_custom_call" | custom-call | tf_op jit(solution)/shard_map/pallas_call | solution.py:130
  (6 shorter events, 0.0 us)
Async XLA Ops:
  0.6 36.1 %copy-start.1 = (bf16[256,256]{1,0:T(8,128)(2,1)S(1)}, bf16[256,256]{1,0:T(8,128)(2,1)}, u32[]{:S(2)}) copy-start(bf16[256,256]{1,0:T(8,128)(2,1)} %constant.41.clone.ul_ref) | copy-start | bytes 393220
  0.6 36.1 %copy-start.2 = (bf16[256,256]{1,0:T(8,128)(2,1)S(1)}, bf16[256,256]{1,0:T(8,128)(2,1)}, u32[]{:S(2)}) copy-start(bf16[256,256]{1,0:T(8,128)(2,1)} %constant.40.clone.uh_ref) | copy-start | bytes 393220
  0.7 36.1 %copy-start.3 = (bf16[256,256]{1,0:T(8,128)(2,1)S(1)}, bf16[256,256]{1,0:T(8,128)(2,1)}, u32[]{:S(2)}) copy-start(bf16[256,256]{1,0:T(8,128)(2,1)} %constant.39.clone.tl_ref) | copy-start | bytes 393220
  0.7 36.1 %copy-start.4 = (bf16[256,256]{1,0:T(8,128)(2,1)S(1)}, bf16[256,256]{1,0:T(8,128)(2,1)}, u32[]{:S(2)}) copy-start(bf16[256,256]{1,0:T(8,128)(2,1)} %constant.38.clone.th_ref) | copy-start | bytes 393220
  0.7 36.0 %copy-start.5 = (f32[40,128]{1,0:T(8,128)S(1)}, f32[40,128]{1,0:T(8,128)}, u32[]{:S(2)}) copy-start(f32[40,128]{1,0:T(8,128)} %constant.37.clone.ts_ref) | copy-start | bytes 61444
  0.7 36.0 %copy-start.6 = (f32[40,128]{1,0:T(8,128)S(1)}, f32[40,128]{1,0:T(8,128)}, u32[]{:S(2)}) copy-start(f32[40,128]{1,0:T(8,128)} %constant.36.clone.tc_ref) | copy-start | bytes 61444
  0.7 36.0 %copy-start.8 = (bf16[32,240]{1,0:T(8,128)(2,1)S(1)}, bf16[32,240]{1,0:T(8,128)(2,1)}, u32[]{:S(2)}) copy-start(bf16[32,240]{1,0:T(8,128)(2,1)} %constant.35.clone.li_ref) | copy-start | bytes 46084
  0.7 36.0 %copy-start.7 = (bf16[80,96]{1,0:T(8,128)(2,1)S(1)}, bf16[80,96]{1,0:T(8,128)(2,1)}, u32[]{:S(2)}) copy-start(bf16[80,96]{1,0:T(8,128)(2,1)} %constant.34.clone.lf_ref) | copy-start | bytes 46084
  0.7 36.0 %copy-start = (f32[16,4096]{1,0:T(8,128)S(1)}, f32[16,4096]{1,0:T(8,128)}, u32[]{:S(2)}) copy-start(f32[16,4096]{1,0:T(8,128)} %filt_ref.1) | copy-start | bytes 786436
  35.4 6.0 %collective-permute-start = (bf16[32,32,128]{2,1,0:T(8,128)(2,1)S(1)}, bf16[32,32,128]{2,1,0:T(8,128)(2,1)S(1)}, u32[]{:S(2)}, u32[]{:S(2)}) collective-permute-start(bf16[32,32,128]{2,1,0:T(8,128)(2,1)S(1)} %slice.4), channel_id=1, source_target_pairs={{0,16},{16,0},{1,17},{17,1},{2,18},{18,2},{3,19},{19,3},{4,20},{20... | collective-permute-start | bytes 786440 | tf_op jit(solution)/shard_map/ppermute | solution.py:244
  40.9 8.7 %collective-permute-start.2 = (bf16[2,48,2048]{2,1,0:T(8,128)(2,1)S(1)}, bf16[2,48,2048]{2,1,0:T(8,128)(2,1)S(1)}, u32[]{:S(2)}, u32[]{:S(2)}) collective-permute-start(bf16[2,48,2048]{2,1,0:T(8,128)(2,1)S(1)} %get-tuple-element.39.refs_0_), channel_id=1, source_target_pairs={{0,2},{1,15},{2,4},{3,1},{4,6},{5,3},{6,8},{7,5},{8,10},{9,7},{10,... | collective-permute-start | bytes 1179656 | tf_op jit(solution)/shard_map/ppermute | solution.py:240
  41.4 12.0 %collective-permute-start.4 = (bf16[2,48,2048]{2,1,0:T(8,128)(2,1)S(1)}, bf16[2,48,2048]{2,1,0:T(8,128)(2,1)S(1)}, u32[]{:S(2)}, u32[]{:S(2)}) collective-permute-start(bf16[2,48,2048]{2,1,0:T(8,128)(2,1)S(1)} %get-tuple-element.39.refs_0_), channel_id=1, source_target_pairs={{1,2},{0,15},{3,4},{2,1},{5,6},{4,3},{7,8},{6,5},{9,10},{8,7},{11,... | collective-permute-start | bytes 1179656 | tf_op jit(solution)/shard_map/ppermute | solution.py:240
  47.1 10.4 %collective-permute-start.1 = (bf16[2,32,32,128]{3,2,1,0:T(8,128)(2,1)S(1)}, bf16[2,32,32,128]{3,2,1,0:T(8,128)(2,1)}, u32[]{:S(2)}, u32[]{:S(2)}) collective-permute-start(bf16[2,32,32,128]{3,2,1,0:T(8,128)(2,1)S(1)} %pad_maximum_fusion.refs_0_), channel_id=1, source_target_pairs={{0,32},{1,97},{32,64},{33,1},{64,96},{65,33},{96,0},{97,65},{2,34}... | collective-permute-start | bytes 1572872 | tf_op jit(solution)/shard_map/ppermute | solution.py:240
  49.6 7.8 %collective-permute-start.3 = (bf16[2,48,2048]{2,1,0:T(8,128)(2,1)S(1)}, bf16[2,48,2048]{2,1,0:T(8,128)(2,1)S(1)}, u32[]{:S(2)}, u32[]{:S(2)}) collective-permute-start(bf16[2,48,2048]{2,1,0:T(8,128)(2,1)S(1)} %collective-permute-done.2.refs_1_), channel_id=1, source_target_pairs={{0,2},{1,15},{2,4},{3,1},{4,6},{5,3},{6,8},{7,5},{8,10},{9,7},{10,... | collective-permute-start | bytes 1179656 | tf_op jit(solution)/shard_map/ppermute | solution.py:240
  53.5 8.1 %collective-permute-start.9 = (bf16[2,48,2048]{2,1,0:T(8,128)(2,1)S(1)}, bf16[2,48,2048]{2,1,0:T(8,128)(2,1)S(1)}, u32[]{:S(2)}, u32[]{:S(2)}) collective-permute-start(bf16[2,48,2048]{2,1,0:T(8,128)(2,1)S(1)} %collective-permute-done.4.refs_2_), channel_id=1, source_target_pairs={{0,2},{1,15},{2,4},{3,1},{4,6},{5,3},{6,8},{7,5},{8,10},{9,7},{10,... | collective-permute-start | bytes 1179656 | tf_op jit(solution)/shard_map/ppermute | solution.py:240
  54.9 14.0 %collective-permute-start.5 = (bf16[2,32,32,128]{3,2,1,0:T(8,128)(2,1)S(1)}, bf16[2,32,32,128]{3,2,1,0:T(8,128)(2,1)}, u32[]{:S(2)}, u32[]{:S(2)}) collective-permute-start(bf16[2,32,32,128]{3,2,1,0:T(8,128)(2,1)S(1)} %pad_maximum_fusion.refs_0_), channel_id=1, source_target_pairs={{1,32},{0,97},{33,64},{32,1},{65,96},{64,33},{97,0},{96,65},{3,34}... | collective-permute-start | bytes 1572872 | tf_op jit(solution)/shard_map/ppermute | solution.py:240
  57.5 18.4 %collective-permute-start.6 = (bf16[2,32,32,128]{3,2,1,0:T(8,128)(2,1)}, bf16[2,32,32,128]{3,2,1,0:T(8,128)(2,1)}, u32[]{:S(2)}, u32[]{:S(2)}) collective-permute-start(bf16[2,32,32,128]{3,2,1,0:T(8,128)(2,1)} %collective-permute-done.1.refs_1_), channel_id=1, source_target_pairs={{0,32},{1,97},{32,64},{33,1},{64,96},{65,33},{96,0},{97,65},{2,34}... | collective-permute-start | bytes 1572872 | tf_op jit(solution)/shard_map/ppermute | solution.py:240
  59.2 9.2 %collective-permute-start.8 = (bf16[2,48,2048]{2,1,0:T(8,128)(2,1)S(1)}, bf16[2,48,2048]{2,1,0:T(8,128)(2,1)}, u32[]{:S(2)}, u32[]{:S(2)}) collective-permute-start(bf16[2,48,2048]{2,1,0:T(8,128)(2,1)S(1)} %collective-permute-done.3.refs_3_), channel_id=1, source_target_pairs={{0,2},{1,15},{2,4},{3,1},{4,6},{5,3},{6,8},{7,5},{8,10},{9,7},{10,... | collective-permute-start | bytes 1179656 | tf_op jit(solution)/shard_map/ppermute | solution.py:240
  61.6 13.1 %collective-permute-start.12 = (bf16[2,48,2048]{2,1,0:T(8,128)(2,1)S(1)}, bf16[2,48,2048]{2,1,0:T(8,128)(2,1)S(1)}, u32[]{:S(2)}, u32[]{:S(2)}) collective-permute-start(bf16[2,48,2048]{2,1,0:T(8,128)(2,1)S(1)} %collective-permute-done.9.refs_4_), channel_id=1, source_target_pairs={{0,2},{1,15},{2,4},{3,1},{4,6},{5,3},{6,8},{7,5},{8,10},{9,7},{10,... | collective-permute-start | bytes 1179656 | tf_op jit(solution)/shard_map/ppermute | solution.py:240
  63.2 17.0 %collective-permute-start.7 = (bf16[2,32,32,128]{3,2,1,0:T(8,128)(2,1)S(1)}, bf16[2,32,32,128]{3,2,1,0:T(8,128)(2,1)}, u32[]{:S(2)}, u32[]{:S(2)}) collective-permute-start(bf16[2,32,32,128]{3,2,1,0:T(8,128)(2,1)S(1)} %pad_maximum_fusion.refs_0_), channel_id=1, source_target_pairs={{0,1},{1,0},{2,3},{3,2},{4,5},{5,4},{6,7},{7,6},{8,9},{9,8},{10,11... | collective-permute-start | bytes 1572872 | tf_op jit(solution)/shard_map/ppermute | solution.py:244
  68.9 11.3 %collective-permute-start.11 = (bf16[2,32,32,128]{3,2,1,0:T(8,128)(2,1)}, bf16[2,32,32,128]{3,2,1,0:T(8,128)(2,1)}, u32[]{:S(2)}, u32[]{:S(2)}) collective-permute-start(bf16[2,32,32,128]{3,2,1,0:T(8,128)(2,1)} %collective-permute-done.5.refs_2_), channel_id=1, source_target_pairs={{0,1},{1,0},{2,3},{3,2},{4,5},{5,4},{6,7},{7,6},{8,9},{9,8},{10,11... | collective-permute-start | bytes 1572872 | tf_op jit(solution)/shard_map/ppermute | solution.py:244
  74.7 5.5 %collective-permute-start.10 = (bf16[2,32,32,128]{3,2,1,0:T(8,128)(2,1)}, bf16[2,32,32,128]{3,2,1,0:T(8,128)(2,1)}, u32[]{:S(2)}, u32[]{:S(2)}) collective-permute-start(bf16[2,32,32,128]{3,2,1,0:T(8,128)(2,1)} %collective-permute-done.1.refs_1_), channel_id=1, source_target_pairs={{0,1},{1,0},{2,3},{3,2},{4,5},{5,4},{6,7},{7,6},{8,9},{9,8},{10,11... | collective-permute-start | bytes 1572872 | tf_op jit(solution)/shard_map/ppermute | solution.py:244
  75.9 6.1 %collective-permute-start.13 = (bf16[2,32,32,128]{3,2,1,0:T(8,128)(2,1)}, bf16[2,32,32,128]{3,2,1,0:T(8,128)(2,1)}, u32[]{:S(2)}, u32[]{:S(2)}) collective-permute-start(bf16[2,32,32,128]{3,2,1,0:T(8,128)(2,1)} %collective-permute-done.6.refs_3_), channel_id=1, source_target_pairs={{0,1},{1,0},{2,3},{3,2},{4,5},{5,4},{6,7},{7,6},{8,9},{9,8},{10,11... | collective-permute-start | bytes 1572872 | tf_op jit(solution)/shard_map/ppermute | solution.py:244
  80.1 8.0 %collective-permute-start.17 = (bf16[2,48,2048]{2,1,0:T(8,128)(2,1)}, bf16[2,48,2048]{2,1,0:T(8,128)(2,1)}, u32[]{:S(2)}, u32[]{:S(2)}) collective-permute-start(bf16[2,48,2048]{2,1,0:T(8,128)(2,1)} %collective-permute-done.8.refs_5_), channel_id=1, source_target_pairs={{0,2},{1,15},{2,4},{3,1},{4,6},{5,3},{6,8},{7,5},{8,10},{9,7},{10,... | collective-permute-start | bytes 1179656 | tf_op jit(solution)/shard_map/ppermute | solution.py:240
  85.9 11.3 %collective-permute-start.14 = (bf16[672,128]{1,0:T(8,128)(2,1)S(1)}, bf16[672,128]{1,0:T(8,128)(2,1)S(1)}, u32[]{:S(2)}, u32[]{:S(2)}) collective-permute-start(bf16[672,128]{1,0:T(8,128)(2,1)S(1)} %get-tuple-element.51), channel_id=1, source_target_pairs={{0,1},{1,0},{2,3},{3,2},{4,5},{5,4},{6,7},{7,6},{8,9},{9,8},{10,11... | collective-permute-start | bytes 516104 | tf_op jit(solution)/shard_map/ppermute | solution.py:244
  86.4 10.9 %collective-permute-start.15 = (bf16[672,128]{1,0:T(8,128)(2,1)S(1)}, bf16[672,128]{1,0:T(8,128)(2,1)S(1)}, u32[]{:S(2)}, u32[]{:S(2)}) collective-permute-start(bf16[672,128]{1,0:T(8,128)(2,1)S(1)} %get-tuple-element.52), channel_id=1, source_target_pairs={{0,16},{16,0},{1,17},{17,1},{2,18},{18,2},{3,19},{19,3},{4,20},{20... | collective-permute-start | bytes 516104 | tf_op jit(solution)/shard_map/ppermute | solution.py:244
  86.9 10.4 %collective-permute-start.16 = (bf16[672,128]{1,0:T(8,128)(2,1)S(1)}, bf16[672,128]{1,0:T(8,128)(2,1)S(1)}, u32[]{:S(2)}, u32[]{:S(2)}) collective-permute-start(bf16[672,128]{1,0:T(8,128)(2,1)S(1)} %get-tuple-element.53), channel_id=1, source_target_pairs={{0,17},{1,16},{16,1},{17,0},{2,19},{3,18},{18,3},{19,2},{4,21},{5,... | collective-permute-start | bytes 516104 | tf_op jit(solution)/shard_map/ppermute | solution.py:252
  90.6 2.3 %collective-permute-start.18 = (bf16[96,128]{1,0:T(8,128)(2,1)S(1)}, bf16[96,128]{1,0:T(8,128)(2,1)S(1)}, u32[]{:S(2)}, u32[]{:S(2)}) collective-permute-start(bf16[96,128]{1,0:T(8,128)(2,1)S(1)} %get-tuple-element.57), channel_id=1, source_target_pairs={{0,1},{1,0},{2,3},{3,2},{4,5},{5,4},{6,7},{7,6},{8,9},{9,8},{10,11... | collective-permute-start | bytes 73736 | tf_op jit(solution)/shard_map/ppermute | solution.py:244
  92.0 4.1 %collective-permute-start.19 = (bf16[96,128]{1,0:T(8,128)(2,1)S(1)}, bf16[96,128]{1,0:T(8,128)(2,1)S(1)}, u32[]{:S(2)}, u32[]{:S(2)}) collective-permute-start(bf16[96,128]{1,0:T(8,128)(2,1)S(1)} %get-tuple-element.58), channel_id=1, source_target_pairs={{0,16},{16,0},{1,17},{17,1},{2,18},{18,2},{3,19},{19,3},{4,20},{20... | collective-permute-start | bytes 73736 | tf_op jit(solution)/shard_map/ppermute | solution.py:244
  92.9 4.3 %collective-permute-start.20 = (bf16[96,128]{1,0:T(8,128)(2,1)S(1)}, bf16[96,128]{1,0:T(8,128)(2,1)S(1)}, u32[]{:S(2)}, u32[]{:S(2)}) collective-permute-start(bf16[96,128]{1,0:T(8,128)(2,1)S(1)} %get-tuple-element.59), channel_id=1, source_target_pairs={{0,17},{1,16},{16,1},{17,0},{2,19},{3,18},{18,3},{19,2},{4,21},{5,... | collective-permute-start | bytes 73736 | tf_op jit(solution)/shard_map/ppermute | solution.py:252

commit v7 on v6

--- a/solution.py
+++ b/solution.py
@@ -60,30 +60,40 @@
     return high, (x - high.astype(jnp.float32)).astype(jnp.bfloat16)
 
 
+def flat(x):
+    return pltpu.einshape("icj->i(cj)", x)
+
+
+def forward(high, low, chans, width, tables):
+    lf, tc, ts, th, tl = tables
+    rows = tc.shape[0]
+    blocks = high.shape[0]
+    if low is None:
+        a = dot(lf[:, : 2 * blocks], jnp.concatenate([high, high], 0))
+    else:
+        a = dot(lf, jnp.concatenate([high, high, low], 0))
+    parts = []
+    for c in range(chans):
+        ar = a[:rows, c * width : (c + 1) * width]
+        ai = a[rows:, c * width : (c + 1) * width]
+        parts.append(jnp.concatenate([ar * tc + ai * ts, ai * tc - ar * ts], 1))
+    high, low = split(jnp.concatenate(parts, 0))
+    return dot(high, th) + dot(low, th) + dot(high, tl)
+
+
+def filter_kernel(chans, width, blocks, filt_ref, lf_ref, tc_ref, ts_ref, th_ref, tl_ref, out_ref):
+    filt = jnp.stack([filt_ref[:, i * width : (i + 1) * width] for i in range(blocks)], 0)
+    tables = tuple(ref[...] for ref in (lf_ref, tc_ref, ts_ref, th_ref, tl_ref))
+    out_ref[...] = forward(*split(flat(filt)), chans, width, tables)
+
+
 def kernel(
-    chans, width, blocks, sent_ref, filt_ref, lf_ref, li_ref, tc_ref, ts_ref, th_ref, tl_ref, uh_ref, ul_ref, out_ref, taps_ref
+    chans, width, blocks, sent_ref, spec_ref, lf_ref, li_ref, tc_ref, ts_ref, th_ref, tl_ref, uh_ref, ul_ref, out_ref, taps_ref
 ):
     rows = tc_ref.shape[0]
     tc, ts = tc_ref[...], ts_ref[...]
     th, tl, uh, ul = th_ref[...], tl_ref[...], uh_ref[...], ul_ref[...]
     lf, li = lf_ref[...], li_ref[...]
-
-    def flat(x):
-        return pltpu.einshape("icj->i(cj)", x)
-
-    def forward(high, low):
-        if low is None:
-            a = dot(lf[:, : 2 * blocks], jnp.concatenate([high, high], 0))
-        else:
-            a = dot(lf, jnp.concatenate([high, high, low], 0))
-        parts = []
-        for c in range(chans):
-            ar = a[:rows, c * width : (c + 1) * width]
-            ai = a[rows:, c * width : (c + 1) * width]
-            parts.append(jnp.concatenate([ar * tc + ai * ts, ai * tc - ar * ts], 1))
-        high, low = split(jnp.concatenate(parts, 0))
-        x = dot(high, th) + dot(low, th) + dot(high, tl)
-        return x[:, :width], x[:, width:]
 
     def inverse(re, im):
         high, low = split(jnp.concatenate([re, im], 1))
@@ -108,10 +118,10 @@
 
     gate = flat((stream(1) * stream(2)).astype(jnp.bfloat16).astype(jnp.float32)).astype(jnp.bfloat16)
     carr = flat((stream(3) * stream(0)).astype(jnp.bfloat16).astype(jnp.float32)).astype(jnp.bfloat16)
-    filt = jnp.stack([filt_ref[:, i * width : (i + 1) * width] for i in range(blocks)], 0)
-    fr, fi = forward(*split(flat(filt)))
-    gr, gi = forward(gate, None)
-    cr, ci = forward(carr, None)
+    fr, fi = spec_ref[:, :width], spec_ref[:, width:]
+    gate, carr = (forward(x, None, chans, width, (lf, tc, ts, th, tl)) for x in (gate, carr))
+    gr, gi = gate[:, :width], gate[:, width:]
+    cr, ci = carr[:, :width], carr[:, width:]
     conv = inverse(fr * gr - fi * gi, fr * gi + fi * gr).astype(jnp.bfloat16).astype(jnp.float32)
     put(0, stream(3) * conv)
     back = inverse(fr * cr + fi * ci, fr * ci - fi * cr).astype(jnp.bfloat16).astype(jnp.float32)
@@ -137,14 +147,30 @@
     )(*args)
 
 
-def spectral(sent, filters):
+def filter_spectrum(filters, blocks):
+    chans, length = filters.shape
+    width = length // blocks
+    lf, _, tc, ts, th, tl, _, _ = tables(blocks, width)
+    (spectrum,) = vmem_call(
+        functools.partial(filter_kernel, chans, width, blocks),
+        [((chans * tc.shape[0], 2 * width), jnp.float32)],
+        filters,
+        lf,
+        tc,
+        ts,
+        th,
+        tl,
+    )
+    return spectrum
+
+
+def spectral(sent, spectrum, chans):
     blocks, _, width = sent.shape
-    chans = filters.shape[0]
     return vmem_call(
         functools.partial(kernel, chans, width, blocks),
-        [((2, 3 * chans, blocks * width // 2), jnp.bfloat16), (filters.shape, jnp.float32)],
+        [((2, 3 * chans, blocks * width // 2), jnp.bfloat16), ((chans, blocks * width), jnp.float32)],
         sent,
-        filters,
+        spectrum,
         *tables(blocks, width),
     )
 
@@ -176,10 +202,15 @@
         out_ref[:, k * count : (k + 1) * count] = block[...]
 
 
+def chunk_kernel(place_ref, *refs):
+    for near in range(4):
+        refs[near - 4][...] = chunk(place_ref, refs[:-4], near // 2, near % 2)
+
+
 def product_kernel(place_ref, *refs):
-    if len(refs) == 14:
+    if len(refs) > 10:
         own, first, second, third, other, other_first, other_second, other_third = refs[:8]
-        block, outs, x_ref = refs[8], refs[9:13], refs[13]
+        blocks, chunked, outs, x_ref = refs[8:9], refs[9:10], refs[-5:-1], refs[-1]
         _, steps, part, width = own.shape
         for rc, pieces in enumerate(((own, first, third, other_second), (other, second, other_third, other_first))):
             for ry in range(2):
@@ -188,40 +219,47 @@
                     for i in range(steps):
                         x_ref[row : row + part, i * width : (i + 1) * width] = ref[ry, i]
     else:
-        x_ref, block, outs = refs[0], refs[1], refs[2:]
-    _, rows, length = block.shape
+        x_ref, blocks, outs = refs[0], refs[1:-4], refs[-4:]
+        chunked = blocks
+    halves = [jnp.concatenate([block[h] for block in blocks], 0) for h in range(2)]
+    rows, length = halves[0].shape
     size = x_ref.shape[0] // 4
     part = size // 4
     for rc in range(2):
         total = None
         for h in range(2):
             x = x_ref[2 * rc * size : 2 * (rc + 1) * size, h * length : (h + 1) * length]
-            got = lax.dot_general(block[h], x, (((1,), (1,)), ((), ())), preferred_element_type=jnp.float32)
+            got = lax.dot_general(halves[h], x, (((1,), (1,)), ((), ())), preferred_element_type=jnp.float32)
             total = got if total is None else total + got
         for ry in range(2):
             t = total[:, ry * size : (ry + 1) * size]
             u = jnp.concatenate([t[:, :part], t[:, 3 * part :], t[:, 2 * part : 3 * part], t[:, part : 2 * part]], 1)
             out_ref = outs[2 * ry + rc]
             out_ref[:rows] = jnp.where(place_ref[2] == 0, u, t).astype(jnp.bfloat16)
-            out_ref[rows:] = chunk(place_ref, [block], ry, rc)
+            out_ref[rows:] = chunk(place_ref, chunked, ry, rc)
 
 
 def finish_kernel(chans, n, slots, place_ref, *refs):
     groups, (proj_ref, weight_ref, turned_ref) = refs[:-3], refs[-3:]
     y, z, c, x = (place_ref[k] for k in range(4))
-    for g, slot_list in enumerate(slots):
-        rows = 3 * chans * len(slot_list)
-        for near in range(4):
-            ref = groups[4 * g + near]
-            core = lax.rem(c + near % 2, 2)
-            row_y = lax.rem(y + near // 2, 2) * 2 * n
-            for m, (hops, turned) in enumerate(slot_list):
-                owner = row_y + 2 * lax.rem(z + n - hops + 2 * hops * core, n) + (1 - core if turned else core)
-                at = pl.multiple_of(owner * chans, chans)
-                for s in range(3):
-                    row = (3 * m + s) * chans
-                    turned_ref[s, pl.ds(at, chans), :] = ref[row : row + chans, :].astype(jnp.float32)
-                    proj_ref[s, pl.ds(at, chans), :] = ref[rows + row : rows + row + chans, :]
+    for near in range(4):
+        core = lax.rem(c + near % 2, 2)
+        row_y = lax.rem(y + near // 2, 2) * 2 * n
+
+        def put(ref, row, slot, chunk):
+            hops, turned = slot
+            owner = row_y + 2 * lax.rem(z + n - hops + 2 * hops * core, n) + (1 - core if turned else core)
+            at = pl.multiple_of(owner * chans, chans)
+            for s in range(3):
+                part = ref[row + s * chans : row + (s + 1) * chans, :]
+                if chunk:
+                    proj_ref[s, pl.ds(at, chans), :] = part
+                else:
+                    turned_ref[s, pl.ds(at, chans), :] = part.astype(jnp.float32)
+
+        for g, (products, chunks) in enumerate(slots):
+            for m, slot in enumerate(products + chunks):
+                put(groups[4 * g + near], 3 * m * chans, slot, m >= len(products))
     n_x = 4
     part = weight_ref.shape[1] // n_x
     for s in range(3):
@@ -231,12 +269,9 @@
             weight_ref[s, pl.ds(at, part), :] = rows[k * part : (k + 1) * part]
 
 
-def spread(x, axis, crossed=False, hops=1):
+def spread(x, axis):
     n = lax.axis_size(axis)
-    perm = []
-    for i in range(n):
-        for core, way in ((0, 1), (1, -1)):
-            perm.append((2 * i + (1 - core if crossed else core), 2 * ((i + way * hops) % n) + core))
+    perm = [(2 * i, 2 * ((i + 1) % n)) for i in range(n)] + [(2 * i + 1, 2 * ((i + n - 1) % n) + 1) for i in range(n)]
     return lax.ppermute(x, (axis, "core"), perm)
 
 
@@ -274,47 +309,48 @@
         projected.reshape(3, owners, chans, width),
         grad_out.reshape(owners, chans, width),
     )
+    spectrum = filter_spectrum(filters, owners)
     sent = lax.all_to_all(sent, SEQ, split_axis=0, concat_axis=0, tiled=True)
     own_rows = sent[:, 4 * chans :]
     sent, own_rows = lax.optimization_barrier((sent, own_rows))
     y_rows = swap(own_rows, "ylo")
 
-    block, filter_grad = spectral(sent, filters)
+    block, filter_grad = spectral(sent, spectrum, chans)
     a1 = spread(block, "z")
-    start, y_rows = lax.optimization_barrier((block, y_rows))
-    b1 = spread(start, "z", True)
-    a2 = spread(after(a1, block), "z")
-    b1 = after(b1, a1)
-    b2 = spread(b1, "z")
-    both_rows = jnp.stack([own_rows, after(y_rows, block)])
-    other_rows = swap(after(both_rows, b1), "core")
+    turned = swap(block, "core")
+    turned = after(turned, block)
+    b1 = spread(turned, "z")
+    a2 = spread(after(a1, turned), "z")
+    b2 = spread(after(b1, a1), "z")
+    both_rows = jnp.stack([own_rows, after(y_rows, a1)])
+    other_rows = swap(both_rows, "core")
     xa1 = spread(both_rows, "x")
-    xb1 = spread(after(both_rows, a1), "x", True)
-    a2 = after(a2, b1)
-    a3 = spread(a2, "z")
-    b2 = after(b2, a2)
-    b3 = spread(b2, "z")
-    xa1 = after(xa1, a2)
-    xa2 = spread(xa1, "x")
-    (first,) = vmem_call(stack_kernel, [((2, 7 * block.shape[1], block.shape[2]), bf16)], block, a1, b1, a2, b2, a3, b3)
-    a3 = after(a3, b2)
-    a4 = spread(a3, "z")
-
-    slots = (((0, 0), (1, 0), (1, 1), (2, 0), (2, 1), (3, 0), (3, 1)), ((4, 0),))
+    xb1 = spread(after(other_rows, b1), "x")
+    a3 = spread(after(a2, b1), "z")
+    b3 = spread(after(b2, a2), "z")
+    xa2 = spread(after(xa1, b1), "x")
+    (first,) = vmem_call(stack_kernel, [((2, 6 * block.shape[1], block.shape[2]), bf16)], block, a1, b1, a2, b2, b3)
+    early = (block, a1, b1, a2, b2)
+    chunks = trade(vmem_call(chunk_kernel, [((len(early) * block.shape[1], width), bf16)] * 4, *early, place=place))
+    a4 = spread(after(a3, b2), "z")
+
+    near_slots, last_slots = ((0, 0), (1, 0), (1, 1), (2, 0), (2, 1)), ((3, 0), (4, 0))
+    slots = (((), near_slots), (near_slots + ((3, 1),), ((3, 1),)), (last_slots, last_slots))
     fa1 = swap(after(xa1, a3), "core")
     fb1 = swap(after(xb1, a3), "core")
-    fa2 = swap(after(xa2, first), "core")
+    fa2 = swap(after(xa2, first, *chunks[1:]), "core")
     pieces = (both_rows, xa1, xb1, xa2, other_rows, fa1, fb1, fa2)
     *parts, whole = vmem_call(
         product_kernel,
-        [((2 * first.shape[1], width), bf16)] * 4 + [((4 * n_x * rows, owners * width), bf16)],
+        [((first.shape[1] + b3.shape[1], width), bf16)] * 4 + [((4 * n_x * rows, owners * width), bf16)],
         *pieces,
         first,
+        b3,
         place=place,
     )
-    groups = trade(parts)
-    a4 = after(a4, parts[0])
-    parts = vmem_call(product_kernel, [((2 * a4.shape[1], width), bf16)] * 4, whole, a4, place=place)
+    groups = (*chunks, *trade(parts))
+    a3, a4 = lax.optimization_barrier((a3, a4, parts[0]))[:2]
+    parts = vmem_call(product_kernel, [((4 * a4.shape[1], width), bf16)] * 4, whole, a3, a4, place=place)
     groups += trade(parts)
     proj_grad, weight_grad = vmem_call(
         functools.partial(finish_kernel, chans, n, slots),

time: 99.4 us -> 98.6 us (level)
  blocking collectives: 32.4 us -> 0 us
  waiting for transfers between devices: 9.34 us -> 38.9 us
  local copies, waits for them, and re-layouts: 0.08 us -> 5.01 us
  starting transfers between devices: 40.6 us -> 38.3 us
    all_to_all x1 -> x0, blocking collectives: 32.4 us -> none  [local(): sent = lax.all_to_all(sent, SEQ, split_axis=0, concat_axis=0, tiled=True)]
    all_to_all x0 -> x1, waiting for transfers between devices: none -> 15.7 us  [local(): sent = lax.all_to_all(sent, SEQ, split_axis=0, concat_axis=0, tiled=True)]
    all_to_all x0 -> x1, starting transfers between devices: none -> 11.1 us  [local(): sent = lax.all_to_all(sent, SEQ, split_axis=0, concat_axis=0, tiled=True)]
    ppermute x9 -> x12, starting transfers between devices: 19.4 us -> 10.9 us  [swap(): return lax.ppermute(x, axis, [(0, 1), (1, 0)])]
    ppermute x10, waiting for transfers between devices: 3.76 us -> 11 us  [spread(): return lax.ppermute(x, (axis, 'core'), perm)]
    ppermute x10, starting transfers between devices: 19 us -> 12.3 us  [spread(): return lax.ppermute(x, (axis, 'core'), perm)]
    ppermute x9 -> x12, waiting for transfers between devices: 4.46 us -> 10.1 us  [swap(): return lax.ppermute(x, axis, [(0, 1), (1, 0)])]
    unnamed x18 -> x28, local copies, waits for them, and re-layouts: 0.06 us -> 4.99 us
  transfers between devices with their start and end apart: 21 -> 26, of which waited for: 6 -> 15; matrix products, arithmetic and copies ran while one was open for 0% -> 0% of each run, Pallas kernels for 12% -> 4%
where the time goes in v7:
time: 98.6 us; the launch traced here: 98.1 us
  waiting for transfers between devices  38.9 us (39%)
  starting transfers between devices  38.3 us (39%)
  Pallas kernels  14.9 us (15%)
  local copies, waits for them, and re-layouts  5.01 us (5%)
    all_to_all x1, waiting for transfers between devices, local(): sent = lax.all_to_all(sent, SEQ, split_axis=0, concat_axis=0, tiled=True)  15.7 us
    pallas_call x7, Pallas kernels, vmem_call(): pl.pallas_call(body, out_shape=tuple((jax.ShapeDtypeStruct(shape, dtype)...  12.6 us
    ppermute x10, starting transfers between devices, spread(): return lax.ppermute(x, (axis, 'core'), perm)  12.3 us
    all_to_all x1, starting transfers between devices, local(): sent = lax.all_to_all(sent, SEQ, split_axis=0, concat_axis=0, tiled=True)  11.1 us
    ppermute x10, waiting for transfers between devices, spread(): return lax.ppermute(x, (axis, 'core'), perm)  11 us
    ppermute x12, starting transfers between devices, swap(): return lax.ppermute(x, axis, [(0, 1), (1, 0)])  10.9 us
    ppermute x12, waiting for transfers between devices, swap(): return lax.ppermute(x, axis, [(0, 1), (1, 0)])  10.1 us
    unnamed x28, local copies, waits for them, and re-layouts  4.99 us
  transfers between devices with their start and end apart: 26, of which 15 were waited for; matrix products, arithmetic and copies ran while one was open for 0% of the time, Pallas kernels for 4%

profile of v7, /device:TPU:1, one launch (start us, length us, event | category | flops | bytes accessed | tf_op | source)
XLA Modules:
  0.0 98.1 jit_solution(8825752054647667946)
XLA Ops:
  0.6 0.0 copy-start.1
  0.6 0.0 copy-start.3
  0.7 0.0 copy-start.10
  0.7 0.0 copy-start.12
  0.7 0.0 copy-start.5
  0.7 0.0 copy-start.6
  0.7 2.3 %shard_map.184 = bf16[32,96,128]{2,1,0:T(8,128)(2,1)} custom-call(bf16[32,4,32,128]{3,2,1,0:T(8,128)(2,1)} %bitcast.10, bf16[3,32,16,128]{3,2,1,0:T(8,128)(2,1)} %bitcast.12, bf16[32,16,128]{2,1,0:T(8,128)(2,1)} %bitcast.14), custom_call_target="tpu_custom_call" | custom-call | tf_op jit(solution)/shard_map/pallas_call | solution.py:301
  3.0 11.1 %all-to-all-start = ((bf16[32,96,128]{2,1,0:T(8,128)(2,1)}), bf16[32,96,128]{2,1,0:T(8,128)(2,1)S(1)}, u32[]{:S(2)}, u32[]{:S(2)}) async-start(bf16[32,96,128]{2,1,0:T(8,128)(2,1)} %shard_map.184), calls=%async_computation | async-start | bytes 1572864 | tf_op jit(solution)/shard_map/all_to_all | solution.py:313
  14.2 0.0 copy-start
  14.2 0.9 copy-done
  15.1 0.9 copy-done.2
  16.0 0.9 copy-done.4
  16.9 0.7 copy-done.7
  17.7 0.7 copy-done.9
  18.4 0.7 copy-done.11
  19.1 0.6 shard_map.185.spec_ref
  19.7 15.7 %all-to-all-done.sent_ref = bf16[32,96,128]{2,1,0:T(8,128)(2,1)S(1)} async-done(((bf16[32,96,128]{2,1,0:T(8,128)(2,1)}), bf16[32,96,128]{2,1,0:T(8,128)(2,1)S(1)}, u32[]{:S(2)}, u32[]{:S(2)}) %all-to-all-start) | async-done | bytes 786464 | tf_op jit(solution)/shard_map/all_to_all | solution.py:313
  35.5 3.9 %shard_map.186 = (bf16[2,48,2048]{2,1,0:T(8,128)(2,1)S(1)}, f32[16,4096]{1,0:T(8,128)}) custom-call(bf16[32,96,128]{2,1,0:T(8,128)(2,1)S(1)} %all-to-all-done.sent_ref, f32[640,256]{1,0:T(8,128)S(1)} %shard_map.185.spec_ref, bf16[80,96]{1,0:T(8,128)(2,1)S(1)} %copy-done.12, bf16[32,240]{1,0:T(8,128)(2,1)S(1)} %copy-done.13, f32[40,128]{1,0:T(8,128)S(1)} %copy-done.10, ...), custom_call_target="tpu_custom_call" | custom-call | tf_op jit(solution)/shard_map/pallas_call | solution.py:140
  39.4 2.3 %collective-permute-start.1 = (bf16[2,48,2048]{2,1,0:T(8,128)(2,1)S(1)}, bf16[2,48,2048]{2,1,0:T(8,128)(2,1)S(1)}, u32[]{:S(2)}, u32[]{:S(2)}) collective-permute-start(bf16[2,48,2048]{2,1,0:T(8,128)(2,1)S(1)} %get-tuple-element.37.refs_0_), channel_id=1, source_target_pairs={{0,1},{1,0},{2,3},{3,2},{4,5},{5,4},{6,7},{7,6},{8,9},{9,8},{10,11... | collective-permute-start | bytes 1179656 | tf_op jit(solution)/shard_map/ppermute | solution.py:279
  41.7 0.2 collective-permute-start
  42.0 0.5 collective-permute-start.8
  42.5 0.6 collective-permute-done.1
  43.1 0.5 collective-permute-start.2
  43.6 4.6 %collective-permute-done.8 = bf16[32,32,128]{2,1,0:T(8,128)(2,1)S(1)} collective-permute-done((bf16[32,32,128]{2,1,0:T(8,128)(2,1)S(1)}, bf16[32,32,128]{2,1,0:T(8,128)(2,1)S(1)}, u32[]{:S(2)}, u32[]{:S(2)}) %collective-permute-start.8) | collective-permute-done | bytes 262176 | tf_op jit(solution)/shard_map/ppermute | solution.py:279
  48.2 0.6 collective-permute-done.refs_1_
  48.8 0.1 pad_maximum_fusion.refs_0_
  48.8 2.1 %collective-permute-start.10 = (bf16[2,32,32,128]{3,2,1,0:T(8,128)(2,1)S(1)}, bf16[2,32,32,128]{3,2,1,0:T(8,128)(2,1)S(1)}, u32[]{:S(2)}, u32[]{:S(2)}) collective-permute-start(bf16[2,32,32,128]{3,2,1,0:T(8,128)(2,1)S(1)} %pad_maximum_fusion.refs_0_), channel_id=1, source_target_pairs={{0,1},{1,0},{2,3},{3,2},{4,5},{5,4},{6,7},{7,6},{8,9},{9,8},{10,11... | collective-permute-start | bytes 1572872 | tf_op jit(solution)/shard_map/ppermute | solution.py:279
  50.9 2.5 %collective-permute-start.9 = (bf16[2,32,32,128]{3,2,1,0:T(8,128)(2,1)S(1)}, bf16[2,32,32,128]{3,2,1,0:T(8,128)(2,1)}, u32[]{:S(2)}, u32[]{:S(2)}) collective-permute-start(bf16[2,32,32,128]{3,2,1,0:T(8,128)(2,1)S(1)} %pad_maximum_fusion.refs_0_), channel_id=1, source_target_pairs={{0,32},{32,64},{64,96},{96,0},{1,97},{33,1},{65,33},{97,65},{2,34}... | collective-permute-start | bytes 1572872 | tf_op jit(solution)/shard_map/ppermute | solution.py:275
  53.4 0.6 collective-permute-start.3
  54.0 0.4 collective-permute-start.4
  54.4 2.1 %collective-permute-start.11 = (bf16[2,32,32,128]{3,2,1,0:T(8,128)(2,1)S(1)}, bf16[2,32,32,128]{3,2,1,0:T(8,128)(2,1)}, u32[]{:S(2)}, u32[]{:S(2)}) collective-permute-start(bf16[2,32,32,128]{3,2,1,0:T(8,128)(2,1)S(1)} %collective-permute-done.10.refs_4_), channel_id=1, source_target_pairs={{0,32},{32,64},{64,96},{96,0},{1,97},{33,1},{65,33},{97,65},{2,34}... | collective-permute-start | bytes 1572872 | tf_op jit(solution)/shard_map/ppermute | solution.py:275
  56.5 3.0 %collective-permute-done.9.refs_1_ = bf16[2,32,32,128]{3,2,1,0:T(8,128)(2,1)} collective-permute-done((bf16[2,32,32,128]{3,2,1,0:T(8,128)(2,1)S(1)}, bf16[2,32,32,128]{3,2,1,0:T(8,128)(2,1)}, u32[]{:S(2)}, u32[]{:S(2)}) %collective-permute-start.9) | collective-permute-done | bytes 524320 | tf_op jit(solution)/shard_map/ppermute | solution.py:275
  59.5 3.4 %collective-permute-start.12 = (bf16[2,32,32,128]{3,2,1,0:T(8,128)(2,1)}, bf16[2,32,32,128]{3,2,1,0:T(8,128)(2,1)}, u32[]{:S(2)}, u32[]{:S(2)}) collective-permute-start(bf16[2,32,32,128]{3,2,1,0:T(8,128)(2,1)} %collective-permute-done.9.refs_1_), channel_id=1, source_target_pairs={{0,32},{32,64},{64,96},{96,0},{1,97},{33,1},{65,33},{97,65},{2,34}... | collective-permute-start | bytes 1572872 | tf_op jit(solution)/shard_map/ppermute | solution.py:275
  62.9 0.4 collective-permute-start.13
  63.3 1.3 %collective-permute-done.4.refs_4_ = bf16[2,48,2048]{2,1,0:T(8,128)(2,1)S(1)} collective-permute-done((bf16[2,48,2048]{2,1,0:T(8,128)(2,1)S(1)}, bf16[2,48,2048]{2,1,0:T(8,128)(2,1)S(1)}, u32[]{:S(2)}, u32[]{:S(2)}) %collective-permute-start.4) | collective-permute-done | bytes 393248 | tf_op jit(solution)/shard_map/ppermute | solution.py:275
  64.6 1.8 %collective-permute-start.16 = (bf16[2,48,2048]{2,1,0:T(8,128)(2,1)S(1)}, bf16[2,48,2048]{2,1,0:T(8,128)(2,1)S(1)}, u32[]{:S(2)}, u32[]{:S(2)}) collective-permute-start(bf16[2,48,2048]{2,1,0:T(8,128)(2,1)S(1)} %collective-permute-done.4.refs_4_), channel_id=1, source_target_pairs={{0,2},{2,4},{4,6},{6,8},{8,10},{10,12},{12,14},{14,0},{1,15},{3,1}... | collective-permute-start | bytes 1179656 | tf_op jit(solution)/shard_map/ppermute | solution.py:275
  66.4 0.1 pad_add_fusion.place_ref
  66.5 0.6 shard_map.187
  67.1 0.1 collective-permute-start.5
  67.2 2.7 %collective-permute-done.13.refs_1_ = bf16[2,48,2048]{2,1,0:T(8,128)(2,1)} collective-permute-done((bf16[2,48,2048]{2,1,0:T(8,128)(2,1)S(1)}, bf16[2,48,2048]{2,1,0:T(8,128)(2,1)}, u32[]{:S(2)}, u32[]{:S(2)}) %collective-permute-start.13) | collective-permute-done | bytes 393248 | tf_op jit(solution)/shard_map/ppermute | solution.py:275
  69.9 0.6 collective-permute-start.6
  70.5 2.0 %collective-permute-start.7 = (bf16[240,128]{1,0:T(8,128)(2,1)S(1)}, bf16[240,128]{1,0:T(8,128)(2,1)S(1)}, u32[]{:S(2)}, u32[]{:S(2)}) collective-permute-start(bf16[240,128]{1,0:T(8,128)(2,1)S(1)} %get-tuple-element.44), channel_id=1, source_target_pairs={{0,17},{1,16},{16,1},{17,0},{2,19},{3,18},{18,3},{19,2},{4,21},{5,... | collective-permute-start | bytes 184328 | tf_op jit(solution)/shard_map/ppermute | solution.py:287
  72.5 1.6 %collective-permute-done.16.refs_5_.refs_9_ = bf16[2,48,2048]{2,1,0:T(8,128)(2,1)S(1)} collective-permute-done((bf16[2,48,2048]{2,1,0:T(8,128)(2,1)S(1)}, bf16[2,48,2048]{2,1,0:T(8,128)(2,1)S(1)}, u32[]{:S(2)}, u32[]{:S(2)}) %collective-permute-start.16) | collective-permute-done | bytes 393248 | tf_op jit(solution)/shard_map/ppermute | solution.py:275
  74.0 0.9 collective-permute-start.14
  74.9 0.2 shard_map.188.refs_8_
  75.1 0.1 collective-permute-start.15
  75.2 0.5 collective-permute-done.7.refs_3_
  75.7 0.3 collective-permute-start.17
  76.0 0.3 collective-permute-start.21
  76.3 0.4 collective-permute-done.14.refs_5_
  76.7 0.7 collective-permute-done.15.refs_6_
  77.4 0.7 collective-permute-done.17.refs_7_
  78.2 3.1 %shard_map.189 = (bf16[336,128]{1,0:T(8,128)(2,1)S(1)}, bf16[336,128]{1,0:T(8,128)(2,1)S(1)}, bf16[336,128]{1,0:T(8,128)(2,1)S(1)}, bf16[336,128]{1,0:T(8,128)(2,1)S(1)}, bf16[512,4096]{1,0:T(8,128)(2,1)S(1)}) custom-call(s32[4]{0:T(128)S(1)} %pad_add_fusion.place_ref, bf16[2,32,32,128]{3,2,1,0:T(8,128)(2,1)S(1)} %pad_maximum_fusion.refs_0_, ...), custom_call_target="tpu_custom_call" | custom-call | tf_op jit(solution)/shard_map/pallas_call | solution.py:140
  81.3 1.9 %collective-permute-done.21.refs_2_ = bf16[2,48,2048]{2,1,0:T(8,128)(2,1)S(1)} collective-permute-done((bf16[2,48,2048]{2,1,0:T(8,128)(2,1)}, bf16[2,48,2048]{2,1,0:T(8,128)(2,1)S(1)}, u32[]{:S(2)}, u32[]{:S(2)}) %collective-permute-start.21) | collective-permute-done | bytes 393248 | tf_op jit(solution)/shard_map/ppermute | solution.py:275
  83.1 2.5 %shard_map.190 = (bf16[192,128]{1,0:T(8,128)(2,1)S(1)}, bf16[192,128]{1,0:T(8,128)(2,1)S(1)}, bf16[192,128]{1,0:T(8,128)(2,1)S(1)}, bf16[192,128]{1,0:T(8,128)(2,1)S(1)}) custom-call(s32[4]{0:T(128)S(1)} %pad_add_fusion.place_ref, bf16[512,4096]{1,0:T(8,128)(2,1)S(1)} %get-tuple-element.58.refs_0_, bf16[2,48,2048]{2,1,0:T(8,128)(2,1)} %collective-permute-done.13.refs_1_, ...), custom_call_target="tpu_custom_call" | custom-call | tf_op jit(solution)/shard_map/pallas_call | solution.py:140
  85.6 2.4 %collective-permute-start.22 = (bf16[192,128]{1,0:T(8,128)(2,1)S(1)}, bf16[192,128]{1,0:T(8,128)(2,1)S(1)}, u32[]{:S(2)}, u32[]{:S(2)}) collective-permute-start(bf16[192,128]{1,0:T(8,128)(2,1)S(1)} %get-tuple-element.63), channel_id=1, source_target_pairs={{0,1},{1,0},{2,3},{3,2},{4,5},{5,4},{6,7},{7,6},{8,9},{9,8},{10,11... | collective-permute-start | bytes 147464 | tf_op jit(solution)/shard_map/ppermute | solution.py:279
  88.0 0.1 collective-permute-start.18
  88.1 0.8 collective-permute-start.19
  88.8 1.3 %collective-permute-start.20 = (bf16[336,128]{1,0:T(8,128)(2,1)S(1)}, bf16[336,128]{1,0:T(8,128)(2,1)S(1)}, u32[]{:S(2)}, u32[]{:S(2)}) collective-permute-start(bf16[336,128]{1,0:T(8,128)(2,1)S(1)} %get-tuple-element.57), channel_id=1, source_target_pairs={{0,17},{1,16},{16,1},{17,0},{2,19},{3,18},{18,3},{19,2},{4,21},{5,... | collective-permute-start | bytes 258056 | tf_op jit(solution)/shard_map/ppermute | solution.py:287
  90.1 0.8 collective-permute-start.23
  90.9 0.7 collective-permute-start.24
  91.6 3.1 %collective-permute-done.23.refs_10_ = bf16[192,128]{1,0:T(8,128)(2,1)S(1)} collective-permute-done((bf16[192,128]{1,0:T(8,128)(2,1)S(1)}, bf16[192,128]{1,0:T(8,128)(2,1)S(1)}, u32[]{:S(2)}, u32[]{:S(2)}) %collective-permute-start.23) | collective-permute-done | bytes 49184 | tf_op jit(solution)/shard_map/ppermute | solution.py:279
  94.6 1.6 %collective-permute-done.24.refs_11_ = bf16[192,128]{1,0:T(8,128)(2,1)S(1)} collective-permute-done((bf16[192,128]{1,0:T(8,128)(2,1)S(1)}, bf16[192,128]{1,0:T(8,128)(2,1)S(1)}, u32[]{:S(2)}, u32[]{:S(2)}) %collective-permute-start.24) | collective-permute-done | bytes 49184 | tf_op jit(solution)/shard_map/ppermute | solution.py:287
  96.3 1.8 %shard_map.191 = (bf16[3,512,128]{2,1,0:T(8,128)(2,1)}, f32[3,128,512]{2,1,0:T(8,128)}) custom-call(s32[4]{0:T(128)S(1)} %pad_add_fusion.place_ref, bf16[240,128]{1,0:T(8,128)(2,1)S(1)} %get-tuple-element.41.refs_0_, bf16[240,128]{1,0:T(8,128)(2,1)S(1)} %collective-permute-done.5.refs_1_, bf16[240,128]{1,0:T(8,128)(2,1)S(1)} %collective-permute-done.6.refs_2_, ...), custom_call_target="tpu_custom_call" | custom-call | tf_op jit(solution)/shard_map/pallas_call | solution.py:140
  (27 shorter events, 0.1 us)
Async XLA Ops:
  0.6 34.8 %copy-start.1 = (bf16[256,256]{1,0:T(8,128)(2,1)S(1)}, bf16[256,256]{1,0:T(8,128)(2,1)}, u32[]{:S(2)}) copy-start(bf16[256,256]{1,0:T(8,128)(2,1)} %constant.38.clone.tl_ref) | copy-start | bytes 393220
  0.6 34.8 %copy-start.3 = (bf16[256,256]{1,0:T(8,128)(2,1)S(1)}, bf16[256,256]{1,0:T(8,128)(2,1)}, u32[]{:S(2)}) copy-start(bf16[256,256]{1,0:T(8,128)(2,1)} %constant.37.clone.th_ref) | copy-start | bytes 393220
  0.7 34.8 %copy-start.8 = (f32[40,128]{1,0:T(8,128)S(1)}, f32[40,128]{1,0:T(8,128)}, u32[]{:S(2)}) copy-start(f32[40,128]{1,0:T(8,128)} %constant.36.clone.ts_ref) | copy-start | bytes 61444
  0.7 34.8 %copy-start.10 = (f32[40,128]{1,0:T(8,128)S(1)}, f32[40,128]{1,0:T(8,128)}, u32[]{:S(2)}) copy-start(f32[40,128]{1,0:T(8,128)} %constant.35.clone.tc_ref) | copy-start | bytes 61444
  0.7 34.8 %copy-start.12 = (bf16[80,96]{1,0:T(8,128)(2,1)S(1)}, bf16[80,96]{1,0:T(8,128)(2,1)}, u32[]{:S(2)}) copy-start(bf16[80,96]{1,0:T(8,128)(2,1)} %constant.34.clone.lf_ref) | copy-start | bytes 46084
  0.7 34.8 %copy-start.5 = (bf16[256,256]{1,0:T(8,128)(2,1)S(1)}, bf16[256,256]{1,0:T(8,128)(2,1)}, u32[]{:S(2)}) copy-start(bf16[256,256]{1,0:T(8,128)(2,1)} %constant.41.clone.ul_ref) | copy-start | bytes 393220
  0.7 34.8 %copy-start.6 = (bf16[256,256]{1,0:T(8,128)(2,1)S(1)}, bf16[256,256]{1,0:T(8,128)(2,1)}, u32[]{:S(2)}) copy-start(bf16[256,256]{1,0:T(8,128)(2,1)} %constant.40.clone.uh_ref) | copy-start | bytes 393220
  0.7 34.8 %copy-start.13 = (bf16[32,240]{1,0:T(8,128)(2,1)S(1)}, bf16[32,240]{1,0:T(8,128)(2,1)}, u32[]{:S(2)}) copy-start(bf16[32,240]{1,0:T(8,128)(2,1)} %constant.39.clone.li_ref) | copy-start | bytes 46084
  3.0 32.4 %all-to-all-start = ((bf16[32,96,128]{2,1,0:T(8,128)(2,1)}), bf16[32,96,128]{2,1,0:T(8,128)(2,1)S(1)}, u32[]{:S(2)}, u32[]{:S(2)}) async-start(bf16[32,96,128]{2,1,0:T(8,128)(2,1)} %shard_map.184), calls=%async_computation | async-start | bytes 1572864 | tf_op jit(solution)/shard_map/all_to_all | solution.py:313
  14.2 0.9 copy-start
  15.1 0.9 copy-start.2
  16.0 0.9 copy-start.4
  16.9 0.7 copy-start.7
  17.7 0.7 copy-start.9
  18.4 0.7 copy-start.11
  39.4 3.7 %collective-permute-start.1 = (bf16[2,48,2048]{2,1,0:T(8,128)(2,1)S(1)}, bf16[2,48,2048]{2,1,0:T(8,128)(2,1)S(1)}, u32[]{:S(2)}, u32[]{:S(2)}) collective-permute-start(bf16[2,48,2048]{2,1,0:T(8,128)(2,1)S(1)} %get-tuple-element.37.refs_0_), channel_id=1, source_target_pairs={{0,1},{1,0},{2,3},{3,2},{4,5},{5,4},{6,7},{7,6},{8,9},{9,8},{10,11... | collective-permute-start | bytes 1179656 | tf_op jit(solution)/shard_map/ppermute | solution.py:279
  41.7 7.0 %collective-permute-start = (bf16[2,48,2048]{2,1,0:T(8,128)(2,1)S(1)}, bf16[2,48,2048]{2,1,0:T(8,128)(2,1)S(1)}, u32[]{:S(2)}, u32[]{:S(2)}) collective-permute-start(bf16[2,48,2048]{2,1,0:T(8,128)(2,1)S(1)} %get-tuple-element.37.refs_0_), channel_id=1, source_target_pairs={{0,2},{2,4},{4,6},{6,8},{8,10},{10,12},{12,14},{14,0},{1,15},{3,1}... | collective-permute-start | bytes 1179656 | tf_op jit(solution)/shard_map/ppermute | solution.py:275
  42.0 6.2 %collective-permute-start.8 = (bf16[32,32,128]{2,1,0:T(8,128)(2,1)S(1)}, bf16[32,32,128]{2,1,0:T(8,128)(2,1)S(1)}, u32[]{:S(2)}, u32[]{:S(2)}) collective-permute-start(bf16[32,32,128]{2,1,0:T(8,128)(2,1)S(1)} %slice.4), channel_id=1, source_target_pairs={{0,16},{16,0},{1,17},{17,1},{2,18},{18,2},{3,19},{19,3},{4,20},{20... | collective-permute-start | bytes 786440 | tf_op jit(solution)/shard_map/ppermute | solution.py:279
  43.1 10.9 %collective-permute-start.2 = (bf16[2,48,2048]{2,1,0:T(8,128)(2,1)S(1)}, bf16[2,48,2048]{2,1,0:T(8,128)(2,1)S(1)}, u32[]{:S(2)}, u32[]{:S(2)}) collective-permute-start(bf16[2,48,2048]{2,1,0:T(8,128)(2,1)S(1)} %collective-permute-done.1), channel_id=1, source_target_pairs={{0,2},{2,4},{4,6},{6,8},{8,10},{10,12},{12,14},{14,0},{1,15},{3,1}... | collective-permute-start | bytes 1179656 | tf_op jit(solution)/shard_map/ppermute | solution.py:275
  48.8 5.6 %collective-permute-start.10 = (bf16[2,32,32,128]{3,2,1,0:T(8,128)(2,1)S(1)}, bf16[2,32,32,128]{3,2,1,0:T(8,128)(2,1)S(1)}, u32[]{:S(2)}, u32[]{:S(2)}) collective-permute-start(bf16[2,32,32,128]{3,2,1,0:T(8,128)(2,1)S(1)} %pad_maximum_fusion.refs_0_), channel_id=1, source_target_pairs={{0,1},{1,0},{2,3},{3,2},{4,5},{5,4},{6,7},{7,6},{8,9},{9,8},{10,11... | collective-permute-start | bytes 1572872 | tf_op jit(solution)/shard_map/ppermute | solution.py:279
  50.9 8.6 %collective-permute-start.9 = (bf16[2,32,32,128]{3,2,1,0:T(8,128)(2,1)S(1)}, bf16[2,32,32,128]{3,2,1,0:T(8,128)(2,1)}, u32[]{:S(2)}, u32[]{:S(2)}) collective-permute-start(bf16[2,32,32,128]{3,2,1,0:T(8,128)(2,1)S(1)} %pad_maximum_fusion.refs_0_), channel_id=1, source_target_pairs={{0,32},{32,64},{64,96},{96,0},{1,97},{33,1},{65,33},{97,65},{2,34}... | collective-permute-start | bytes 1572872 | tf_op jit(solution)/shard_map/ppermute | solution.py:275
  53.4 9.5 %collective-permute-start.3 = (bf16[2,48,2048]{2,1,0:T(8,128)(2,1)S(1)}, bf16[2,48,2048]{2,1,0:T(8,128)(2,1)S(1)}, u32[]{:S(2)}, u32[]{:S(2)}) collective-permute-start(bf16[2,48,2048]{2,1,0:T(8,128)(2,1)S(1)} %collective-permute-done.refs_1_), channel_id=1, source_target_pairs={{0,2},{2,4},{4,6},{6,8},{8,10},{10,12},{12,14},{14,0},{1,15},{3,1}... | collective-permute-start | bytes 1179656 | tf_op jit(solution)/shard_map/ppermute | solution.py:275
  54.0 10.6 %collective-permute-start.4 = (bf16[2,48,2048]{2,1,0:T(8,128)(2,1)S(1)}, bf16[2,48,2048]{2,1,0:T(8,128)(2,1)S(1)}, u32[]{:S(2)}, u32[]{:S(2)}) collective-permute-start(bf16[2,48,2048]{2,1,0:T(8,128)(2,1)S(1)} %collective-permute-done.2.refs_2_), channel_id=1, source_target_pairs={{0,2},{2,4},{4,6},{6,8},{8,10},{10,12},{12,14},{14,0},{1,15},{3,1}... | collective-permute-start | bytes 1179656 | tf_op jit(solution)/shard_map/ppermute | solution.py:275
  54.4 16.1 %collective-permute-start.11 = (bf16[2,32,32,128]{3,2,1,0:T(8,128)(2,1)S(1)}, bf16[2,32,32,128]{3,2,1,0:T(8,128)(2,1)}, u32[]{:S(2)}, u32[]{:S(2)}) collective-permute-start(bf16[2,32,32,128]{3,2,1,0:T(8,128)(2,1)S(1)} %collective-permute-done.10.refs_4_), channel_id=1, source_target_pairs={{0,32},{32,64},{64,96},{96,0},{1,97},{33,1},{65,33},{97,65},{2,34}... | collective-permute-start | bytes 1572872 | tf_op jit(solution)/shard_map/ppermute | solution.py:275
  59.5 16.2 %collective-permute-start.12 = (bf16[2,32,32,128]{3,2,1,0:T(8,128)(2,1)}, bf16[2,32,32,128]{3,2,1,0:T(8,128)(2,1)}, u32[]{:S(2)}, u32[]{:S(2)}) collective-permute-start(bf16[2,32,32,128]{3,2,1,0:T(8,128)(2,1)} %collective-permute-done.9.refs_1_), channel_id=1, source_target_pairs={{0,32},{32,64},{64,96},{96,0},{1,97},{33,1},{65,33},{97,65},{2,34}... | collective-permute-start | bytes 1572872 | tf_op jit(solution)/shard_map/ppermute | solution.py:275
  62.9 7.0 %collective-permute-start.13 = (bf16[2,48,2048]{2,1,0:T(8,128)(2,1)S(1)}, bf16[2,48,2048]{2,1,0:T(8,128)(2,1)}, u32[]{:S(2)}, u32[]{:S(2)}) collective-permute-start(bf16[2,48,2048]{2,1,0:T(8,128)(2,1)S(1)} %collective-permute-done.3.refs_3_), channel_id=1, source_target_pairs={{0,2},{2,4},{4,6},{6,8},{8,10},{10,12},{12,14},{14,0},{1,15},{3,1}... | collective-permute-start | bytes 1179656 | tf_op jit(solution)/shard_map/ppermute | solution.py:275
  64.6 9.4 %collective-permute-start.16 = (bf16[2,48,2048]{2,1,0:T(8,128)(2,1)S(1)}, bf16[2,48,2048]{2,1,0:T(8,128)(2,1)S(1)}, u32[]{:S(2)}, u32[]{:S(2)}) collective-permute-start(bf16[2,48,2048]{2,1,0:T(8,128)(2,1)S(1)} %collective-permute-done.4.refs_4_), channel_id=1, source_target_pairs={{0,2},{2,4},{4,6},{6,8},{8,10},{10,12},{12,14},{14,0},{1,15},{3,1}... | collective-permute-start | bytes 1179656 | tf_op jit(solution)/shard_map/ppermute | solution.py:275
  67.1 8.0 %collective-permute-start.5 = (bf16[240,128]{1,0:T(8,128)(2,1)S(1)}, bf16[240,128]{1,0:T(8,128)(2,1)S(1)}, u32[]{:S(2)}, u32[]{:S(2)}) collective-permute-start(bf16[240,128]{1,0:T(8,128)(2,1)S(1)} %get-tuple-element.42), channel_id=1, source_target_pairs={{0,1},{1,0},{2,3},{3,2},{4,5},{5,4},{6,7},{7,6},{8,9},{9,8},{10,11... | collective-permute-start | bytes 184328 | tf_op jit(solution)/shard_map/ppermute | solution.py:279
  69.9 5.3 %collective-permute-start.6 = (bf16[240,128]{1,0:T(8,128)(2,1)S(1)}, bf16[240,128]{1,0:T(8,128)(2,1)S(1)}, u32[]{:S(2)}, u32[]{:S(2)}) collective-permute-start(bf16[240,128]{1,0:T(8,128)(2,1)S(1)} %get-tuple-element.43), channel_id=1, source_target_pairs={{0,16},{16,0},{1,17},{17,1},{2,18},{18,2},{3,19},{19,3},{4,20},{20... | collective-permute-start | bytes 184328 | tf_op jit(solution)/shard_map/ppermute | solution.py:279
  70.5 5.2 %collective-permute-start.7 = (bf16[240,128]{1,0:T(8,128)(2,1)S(1)}, bf16[240,128]{1,0:T(8,128)(2,1)S(1)}, u32[]{:S(2)}, u32[]{:S(2)}) collective-permute-start(bf16[240,128]{1,0:T(8,128)(2,1)S(1)} %get-tuple-element.44), channel_id=1, source_target_pairs={{0,17},{1,16},{16,1},{17,0},{2,19},{3,18},{18,3},{19,2},{4,21},{5,... | collective-permute-start | bytes 184328 | tf_op jit(solution)/shard_map/ppermute | solution.py:287
  74.0 2.7 %collective-permute-start.14 = (bf16[2,32,32,128]{3,2,1,0:T(8,128)(2,1)}, bf16[2,32,32,128]{3,2,1,0:T(8,128)(2,1)S(1)}, u32[]{:S(2)}, u32[]{:S(2)}) collective-permute-start(bf16[2,32,32,128]{3,2,1,0:T(8,128)(2,1)} %collective-permute-done.9.refs_1_), channel_id=1, source_target_pairs={{0,1},{1,0},{2,3},{3,2},{4,5},{5,4},{6,7},{7,6},{8,9},{9,8},{10,11... | collective-permute-start | bytes 1572872 | tf_op jit(solution)/shard_map/ppermute | solution.py:279
  75.1 2.3 %collective-permute-start.15 = (bf16[2,32,32,128]{3,2,1,0:T(8,128)(2,1)}, bf16[2,32,32,128]{3,2,1,0:T(8,128)(2,1)S(1)}, u32[]{:S(2)}, u32[]{:S(2)}) collective-permute-start(bf16[2,32,32,128]{3,2,1,0:T(8,128)(2,1)} %collective-permute-done.11.refs_2_), channel_id=1, source_target_pairs={{0,1},{1,0},{2,3},{3,2},{4,5},{5,4},{6,7},{7,6},{8,9},{9,8},{10,11... | collective-permute-start | bytes 1572872 | tf_op jit(solution)/shard_map/ppermute | solution.py:279
  75.7 2.5 %collective-permute-start.17 = (bf16[2,32,32,128]{3,2,1,0:T(8,128)(2,1)}, bf16[2,32,32,128]{3,2,1,0:T(8,128)(2,1)S(1)}, u32[]{:S(2)}, u32[]{:S(2)}) collective-permute-start(bf16[2,32,32,128]{3,2,1,0:T(8,128)(2,1)} %collective-permute-done.12.refs_3_), channel_id=1, source_target_pairs={{0,1},{1,0},{2,3},{3,2},{4,5},{5,4},{6,7},{7,6},{8,9},{9,8},{10,11... | collective-permute-start | bytes 1572872 | tf_op jit(solution)/shard_map/ppermute | solution.py:279
  76.0 7.1 %collective-permute-start.21 = (bf16[2,48,2048]{2,1,0:T(8,128)(2,1)}, bf16[2,48,2048]{2,1,0:T(8,128)(2,1)S(1)}, u32[]{:S(2)}, u32[]{:S(2)}) collective-permute-start(bf16[2,48,2048]{2,1,0:T(8,128)(2,1)} %collective-permute-done.13.refs_1_), channel_id=1, source_target_pairs={{0,2},{2,4},{4,6},{6,8},{8,10},{10,12},{12,14},{14,0},{1,15},{3,1}... | collective-permute-start | bytes 1179656 | tf_op jit(solution)/shard_map/ppermute | solution.py:275
  85.6 5.3 %collective-permute-start.22 = (bf16[192,128]{1,0:T(8,128)(2,1)S(1)}, bf16[192,128]{1,0:T(8,128)(2,1)S(1)}, u32[]{:S(2)}, u32[]{:S(2)}) collective-permute-start(bf16[192,128]{1,0:T(8,128)(2,1)S(1)} %get-tuple-element.63), channel_id=1, source_target_pairs={{0,1},{1,0},{2,3},{3,2},{4,5},{5,4},{6,7},{7,6},{8,9},{9,8},{10,11... | collective-permute-start | bytes 147464 | tf_op jit(solution)/shard_map/ppermute | solution.py:279
  88.0 8.3 %collective-permute-start.18 = (bf16[336,128]{1,0:T(8,128)(2,1)S(1)}, bf16[336,128]{1,0:T(8,128)(2,1)S(1)}, u32[]{:S(2)}, u32[]{:S(2)}) collective-permute-start(bf16[336,128]{1,0:T(8,128)(2,1)S(1)} %get-tuple-element.55), channel_id=1, source_target_pairs={{0,1},{1,0},{2,3},{3,2},{4,5},{5,4},{6,7},{7,6},{8,9},{9,8},{10,11... | collective-permute-start | bytes 258056 | tf_op jit(solution)/shard_map/ppermute | solution.py:279
  88.1 8.2 %collective-permute-start.19 = (bf16[336,128]{1,0:T(8,128)(2,1)S(1)}, bf16[336,128]{1,0:T(8,128)(2,1)S(1)}, u32[]{:S(2)}, u32[]{:S(2)}) collective-permute-start(bf16[336,128]{1,0:T(8,128)(2,1)S(1)} %get-tuple-element.56), channel_id=1, source_target_pairs={{0,16},{16,0},{1,17},{17,1},{2,18},{18,2},{3,19},{19,3},{4,20},{20... | collective-permute-start | bytes 258056 | tf_op jit(solution)/shard_map/ppermute | solution.py:279
  88.8 7.5 %collective-permute-start.20 = (bf16[336,128]{1,0:T(8,128)(2,1)S(1)}, bf16[336,128]{1,0:T(8,128)(2,1)S(1)}, u32[]{:S(2)}, u32[]{:S(2)}) collective-permute-start(bf16[336,128]{1,0:T(8,128)(2,1)S(1)} %get-tuple-element.57), channel_id=1, source_target_pairs={{0,17},{1,16},{16,1},{17,0},{2,19},{3,18},{18,3},{19,2},{4,21},{5,... | collective-permute-start | bytes 258056 | tf_op jit(solution)/shard_map/ppermute | solution.py:287
  90.1 4.5 %collective-permute-start.23 = (bf16[192,128]{1,0:T(8,128)(2,1)S(1)}, bf16[192,128]{1,0:T(8,128)(2,1)S(1)}, u32[]{:S(2)}, u32[]{:S(2)}) collective-permute-start(bf16[192,128]{1,0:T(8,128)(2,1)S(1)} %get-tuple-element.64), channel_id=1, source_target_pairs={{0,16},{16,0},{1,17},{17,1},{2,18},{18,2},{3,19},{19,3},{4,20},{20... | collective-permute-start | bytes 147464 | tf_op jit(solution)/shard_map/ppermute | solution.py:279
  90.9 5.4 %collective-permute-start.24 = (bf16[192,128]{1,0:T(8,128)(2,1)S(1)}, bf16[192,128]{1,0:T(8,128)(2,1)S(1)}, u32[]{:S(2)}, u32[]{:S(2)}) collective-permute-start(bf16[192,128]{1,0:T(8,128)(2,1)S(1)} %get-tuple-element.65), channel_id=1, source_target_pairs={{0,17},{1,16},{16,1},{17,0},{2,19},{3,18},{18,3},{19,2},{4,21},{5,... | collective-permute-start | bytes 147464 | tf_op jit(solution)/shard_map/ppermute | solution.py:287

commit v8 on v6

--- a/solution.py
+++ b/solution.py
@@ -61,7 +61,7 @@
 
 
 def kernel(
-    chans, width, blocks, sent_ref, filt_ref, lf_ref, li_ref, tc_ref, ts_ref, th_ref, tl_ref, uh_ref, ul_ref, out_ref, taps_ref
+    chans, width, blocks, sent_ref, filt_ref, lf_ref, li_ref, tc_ref, ts_ref, th_ref, tl_ref, uh_ref, ul_ref, out_ref, taps_ref, held_ref, sem
 ):
     rows = tc_ref.shape[0]
     tc, ts = tc_ref[...], ts_ref[...]
@@ -112,17 +112,20 @@
     fr, fi = forward(*split(flat(filt)))
     gr, gi = forward(gate, None)
     cr, ci = forward(carr, None)
+    taps = inverse(cr * gr + ci * gi, ci * gr - cr * gi)
+    for i in range(blocks):
+        held_ref[:, i * width : (i + 1) * width] = taps[i]
+    copy = pltpu.make_async_copy(held_ref, taps_ref, sem)
+    copy.start()
     conv = inverse(fr * gr - fi * gi, fr * gi + fi * gr).astype(jnp.bfloat16).astype(jnp.float32)
     put(0, stream(3) * conv)
     back = inverse(fr * cr + fi * ci, fr * ci - fi * cr).astype(jnp.bfloat16).astype(jnp.float32)
     put(1, back * stream(2))
     put(2, back * stream(1))
-    taps = inverse(cr * gr + ci * gi, ci * gr - cr * gi)
-    for i in range(blocks):
-        taps_ref[:, i * width : (i + 1) * width] = taps[i]
-
-
-def vmem_call(body, outs, *args, scratch=(), place=None):
+    copy.wait()
+
+
+def vmem_call(body, outs, *args, scratch=(), place=None, away=(), micros=None):
     specs = [pl.BlockSpec(memory_space=pltpu.VMEM)] * len(args)
     if place is not None:
         specs = [pl.BlockSpec(memory_space=pltpu.SMEM)] + specs
@@ -131,8 +134,10 @@
         body,
         out_shape=tuple(jax.ShapeDtypeStruct(shape, dtype) for shape, dtype in outs),
         in_specs=specs,
-        out_specs=tuple(pl.BlockSpec(memory_space=pltpu.VMEM) for _ in outs),
+        out_specs=tuple(pl.BlockSpec(memory_space=pl.ANY if k in away else pltpu.VMEM) for k in range(len(outs))),
         scratch_shapes=scratch,
+        cost_estimate=micros
+        and pl.CostEstimate(flops=int(micros * 1.15e9), bytes_accessed=int(micros * 3.6e6), transcendentals=0),
         compiler_params=pltpu.CompilerParams(vmem_limit_bytes=24 * 1024 * 1024),
     )(*args)
 
@@ -146,16 +151,22 @@
         sent,
         filters,
         *tables(blocks, width),
-    )
-
-
-def pack_kernel(chans, inputs_ref, projected_ref, grad_ref, out_ref, sems):
-    copies = [
-        pltpu.make_async_copy(projected_ref.at[s], out_ref.at[:, s * chans : (s + 1) * chans], sems.at[s])
-        for s in range(3)
-    ]
-    copies.append(pltpu.make_async_copy(grad_ref, out_ref.at[:, 3 * chans : 4 * chans], sems.at[3]))
-    copies.append(pltpu.make_async_copy(inputs_ref.at[:, lax.axis_index("x")], out_ref.at[:, 4 * chans :], sems.at[4]))
+        scratch=[pltpu.VMEM(filters.shape, jnp.float32), pltpu.SemaphoreType.DMA],
+        away=(1,),
+    )
+
+
+def pack_kernel(chans, parts, inputs_ref, projected_ref, grad_ref, out_ref, sems):
+    owners = inputs_ref.shape[0]
+    step = owners // parts
+    copies = []
+    for k in range(parts):
+        here = pl.ds(k * step, step)
+        sources = [projected_ref.at[s, here] for s in range(3)] + [grad_ref.at[here]]
+        sources.append(inputs_ref.at[here, lax.axis_index("x")])
+        for s, source in enumerate(sources):
+            rows = pl.ds(s * chans, source.shape[1])
+            copies.append(pltpu.make_async_copy(source, out_ref.at[here, rows], sems.at[k, s]))
     for copy in copies:
         copy.start()
     for copy in copies:
@@ -177,9 +188,9 @@
 
 
 def product_kernel(place_ref, *refs):
-    if len(refs) == 14:
+    if len(refs) > 10:
         own, first, second, third, other, other_first, other_second, other_third = refs[:8]
-        block, outs, x_ref = refs[8], refs[9:13], refs[13]
+        blocks, outs, x_ref = refs[8:-5], refs[-5:-1], refs[-1]
         _, steps, part, width = own.shape
         for rc, pieces in enumerate(((own, first, third, other_second), (other, second, other_third, other_first))):
             for ry in range(2):
@@ -188,26 +199,27 @@
                     for i in range(steps):
                         x_ref[row : row + part, i * width : (i + 1) * width] = ref[ry, i]
     else:
-        x_ref, block, outs = refs[0], refs[1], refs[2:]
-    _, rows, length = block.shape
+        x_ref, blocks, outs = refs[0], refs[1:-4], refs[-4:]
+    halves = [jnp.concatenate([block[h] for block in blocks], 0) for h in range(2)]
+    rows, length = halves[0].shape
     size = x_ref.shape[0] // 4
     part = size // 4
     for rc in range(2):
         total = None
         for h in range(2):
             x = x_ref[2 * rc * size : 2 * (rc + 1) * size, h * length : (h + 1) * length]
-            got = lax.dot_general(block[h], x, (((1,), (1,)), ((), ())), preferred_element_type=jnp.float32)
+            got = lax.dot_general(halves[h], x, (((1,), (1,)), ((), ())), preferred_element_type=jnp.float32)
             total = got if total is None else total + got
         for ry in range(2):
             t = total[:, ry * size : (ry + 1) * size]
             u = jnp.concatenate([t[:, :part], t[:, 3 * part :], t[:, 2 * part : 3 * part], t[:, part : 2 * part]], 1)
             out_ref = outs[2 * ry + rc]
             out_ref[:rows] = jnp.where(place_ref[2] == 0, u, t).astype(jnp.bfloat16)
-            out_ref[rows:] = chunk(place_ref, [block], ry, rc)
+            out_ref[rows:] = chunk(place_ref, blocks, ry, rc)
 
 
 def finish_kernel(chans, n, slots, place_ref, *refs):
-    groups, (proj_ref, weight_ref, turned_ref) = refs[:-3], refs[-3:]
+    groups, (proj_out, weight_out, proj_ref, weight_ref, turned_ref, sems) = refs[:-6], refs[-6:]
     y, z, c, x = (place_ref[k] for k in range(4))
     for g, slot_list in enumerate(slots):
         rows = 3 * chans * len(slot_list)
@@ -222,6 +234,8 @@
                     row = (3 * m + s) * chans
                     turned_ref[s, pl.ds(at, chans), :] = ref[row : row + chans, :].astype(jnp.float32)
                     proj_ref[s, pl.ds(at, chans), :] = ref[rows + row : rows + row + chans, :]
+    copies = [pltpu.make_async_copy(proj_ref, proj_out, sems.at[3])]
+    copies[0].start()
     n_x = 4
     part = weight_ref.shape[1] // n_x
     for s in range(3):
@@ -229,14 +243,15 @@
         for k in range(n_x):
             at = pl.multiple_of(lax.rem(x + k, n_x) * part, part)
             weight_ref[s, pl.ds(at, part), :] = rows[k * part : (k + 1) * part]
-
-
-def spread(x, axis, crossed=False, hops=1):
+        copies.append(pltpu.make_async_copy(weight_ref.at[s], weight_out.at[s], sems.at[s]))
+        copies[-1].start()
+    for copy in copies:
+        copy.wait()
+
+
+def spread(x, axis):
     n = lax.axis_size(axis)
-    perm = []
-    for i in range(n):
-        for core, way in ((0, 1), (1, -1)):
-            perm.append((2 * i + (1 - core if crossed else core), 2 * ((i + way * hops) % n) + core))
+    perm = [(2 * i, 2 * ((i + 1) % n)) for i in range(n)] + [(2 * i + 1, 2 * ((i + n - 1) % n) + 1) for i in range(n)]
     return lax.ppermute(x, (axis, "core"), perm)
 
 
@@ -264,11 +279,11 @@
     rows = inputs.shape[0] // (owners * n_x)
 
     sent = pl.pallas_call(
-        functools.partial(pack_kernel, chans),
+        functools.partial(pack_kernel, chans, 4),
         out_shape=jax.ShapeDtypeStruct((owners, 4 * chans + rows, width), bf16),
         in_specs=[pl.BlockSpec(memory_space=pl.ANY)] * 3,
         out_specs=pl.BlockSpec(memory_space=pltpu.VMEM),
-        scratch_shapes=[pltpu.SemaphoreType.DMA((5,))],
+        scratch_shapes=[pltpu.SemaphoreType.DMA((4, 5))],
     )(
         inputs.reshape(owners, n_x, rows, width),
         projected.reshape(3, owners, chans, width),
@@ -281,26 +296,22 @@
 
     block, filter_grad = spectral(sent, filters)
     a1 = spread(block, "z")
-    start, y_rows = lax.optimization_barrier((block, y_rows))
-    b1 = spread(start, "z", True)
-    a2 = spread(after(a1, block), "z")
-    b1 = after(b1, a1)
-    b2 = spread(b1, "z")
-    both_rows = jnp.stack([own_rows, after(y_rows, block)])
-    other_rows = swap(after(both_rows, b1), "core")
+    turned = swap(block, "core")
+    turned = after(turned, block)
+    b1 = spread(turned, "z")
+    a2 = spread(after(a1, turned), "z")
+    b2 = spread(after(b1, a1), "z")
+    both_rows = jnp.stack([own_rows, after(y_rows, a1)])
+    other_rows = swap(both_rows, "core")
     xa1 = spread(both_rows, "x")
-    xb1 = spread(after(both_rows, a1), "x", True)
-    a2 = after(a2, b1)
-    a3 = spread(a2, "z")
-    b2 = after(b2, a2)
-    b3 = spread(b2, "z")
-    xa1 = after(xa1, a2)
-    xa2 = spread(xa1, "x")
-    (first,) = vmem_call(stack_kernel, [((2, 7 * block.shape[1], block.shape[2]), bf16)], block, a1, b1, a2, b2, a3, b3)
-    a3 = after(a3, b2)
-    a4 = spread(a3, "z")
-
-    slots = (((0, 0), (1, 0), (1, 1), (2, 0), (2, 1), (3, 0), (3, 1)), ((4, 0),))
+    xb1 = spread(after(other_rows, b1), "x")
+    a3 = spread(after(a2, b1), "z")
+    b3 = spread(after(b2, a2), "z")
+    xa2 = spread(after(xa1, b1), "x")
+    (first,) = vmem_call(stack_kernel, [((2, 6 * block.shape[1], block.shape[2]), bf16)], block, a1, b1, a2, b2, b3, micros=5)
+    a4 = spread(after(a3, b2), "z")
+
+    slots = (((0, 0), (1, 0), (1, 1), (2, 0), (2, 1), (3, 1)), ((3, 0), (4, 0)))
     fa1 = swap(after(xa1, a3), "core")
     fb1 = swap(after(xb1, a3), "core")
     fa2 = swap(after(xa2, first), "core")
@@ -313,14 +324,20 @@
         place=place,
     )
     groups = trade(parts)
-    a4 = after(a4, parts[0])
-    parts = vmem_call(product_kernel, [((2 * a4.shape[1], width), bf16)] * 4, whole, a4, place=place)
+    a3, a4 = lax.optimization_barrier((a3, a4, parts[0]))[:2]
+    parts = vmem_call(product_kernel, [((4 * a4.shape[1], width), bf16)] * 4, whole, a3, a4, place=place)
     groups += trade(parts)
     proj_grad, weight_grad = vmem_call(
         functools.partial(finish_kernel, chans, n, slots),
         [((3, count, width), bf16), ((3, n_x * rows, count), jnp.float32)],
         *groups,
-        scratch=[pltpu.VMEM((3, count, width), jnp.float32)],
+        scratch=[
+            pltpu.VMEM((3, count, width), bf16),
+            pltpu.VMEM((3, n_x * rows, count), jnp.float32),
+            pltpu.VMEM((3, count, width), jnp.float32),
+            pltpu.SemaphoreType.DMA((4,)),
+        ],
+        away=(0, 1),
         place=place,
     )
     return proj_grad, weight_grad.transpose(1, 0, 2), filter_grad

time: 99.4 us -> 96.5 us (0.971)
  starting transfers between devices: 40.6 us -> 31.5 us
  waiting for transfers between devices: 9.34 us -> 17 us
  Pallas kernels: 15.7 us -> 14.1 us
    ppermute x10, starting transfers between devices: 19 us -> 13.2 us  [spread(): return lax.ppermute(x, (axis, 'core'), perm)]
    ppermute x10, waiting for transfers between devices: 3.76 us -> 8.05 us  [spread(): return lax.ppermute(x, (axis, 'core'), perm)]
    ppermute x9 -> x10, waiting for transfers between devices: 4.46 us -> 7.81 us  [swap(): return lax.ppermute(x, axis, [(0, 1), (1, 0)])]
    ppermute x9 -> x10, starting transfers between devices: 19.4 us -> 16 us  [swap(): return lax.ppermute(x, axis, [(0, 1), (1, 0)])]
    pallas_call x5, Pallas kernels: 13.5 us -> 11.8 us  [vmem_call(): pl.pallas_call(body, out_shape=tuple((jax.ShapeDtypeStruct(shape, dtype)...]
  transfers between devices with their start and end apart: 21 -> 22, of which waited for: 6 -> 11; matrix products, arithmetic and copies ran while one was open for 0% -> 0% of each run, Pallas kernels for 12% -> 7%
where the time goes in v8:
time: 96.5 us; the launch traced here: 96.3 us
  blocking collectives  32.4 us (34%)
  starting transfers between devices  31.5 us (33%)
  waiting for transfers between devices  17 us (18%)
  Pallas kernels  14.1 us (15%)
  between operations  1.01 us (1%)
    all_to_all x1, blocking collectives, local(): sent = lax.all_to_all(sent, SEQ, split_axis=0, concat_axis=0, tiled=True)  32.4 us
    ppermute x10, starting transfers between devices, swap(): return lax.ppermute(x, axis, [(0, 1), (1, 0)])  16 us
    ppermute x10, starting transfers between devices, spread(): return lax.ppermute(x, (axis, 'core'), perm)  13.2 us
    pallas_call x5, Pallas kernels, vmem_call(): pl.pallas_call(body, out_shape=tuple((jax.ShapeDtypeStruct(shape, dtype)...  11.8 us
    ppermute x10, waiting for transfers between devices, spread(): return lax.ppermute(x, (axis, 'core'), perm)  8.05 us
    ppermute x10, waiting for transfers between devices, swap(): return lax.ppermute(x, axis, [(0, 1), (1, 0)])  7.81 us
    pallas_call x1, Pallas kernels, local(): pl.pallas_call(functools.partial(pack_kernel, chans, 4), out_shape=jax.Sh...  2.36 us
    ppermute x2, starting transfers between devices, trade(): lax.ppermute(parts[3], ('ylo', 'core'), [(0, 3), (1, 2), (2, 1), (3, 0)])  2.33 us
  transfers between devices with their start and end apart: 22, of which 11 were waited for; matrix products, arithmetic and copies ran while one was open for 0% of the time, Pallas kernels for 7%

profile of v8, /device:TPU:1, one launch (start us, length us, event | category | flops | bytes accessed | tf_op | source)
XLA Modules:
  0.0 96.3 jit_solution(8612409459981427388)
XLA Ops:
  0.6 0.0 copy-start.1
  0.6 0.0 copy-start.2
  0.7 0.0 copy-start.3
  0.7 0.0 copy-start.4
  0.7 0.0 copy-start.5
  0.7 0.0 copy-start.6
  0.7 0.0 copy-start.8
  0.7 0.0 copy-start.7
  0.7 0.0 copy-start
  0.7 2.4 %shard_map.139 = bf16[32,96,128]{2,1,0:T(8,128)(2,1)} custom-call(bf16[32,4,32,128]{3,2,1,0:T(8,128)(2,1)} %bitcast.10, bf16[3,32,16,128]{3,2,1,0:T(8,128)(2,1)} %bitcast.12, bf16[32,16,128]{2,1,0:T(8,128)(2,1)} %bitcast.14), custom_call_target="tpu_custom_call" | custom-call | tf_op jit(solution)/shard_map/pallas_call | solution.py:281
  3.1 32.4 %all_to_all.5.sent_ref = bf16[32,96,128]{2,1,0:T(8,128)(2,1)S(1)} all-to-all(bf16[32,96,128]{2,1,0:T(8,128)(2,1)} %shard_map.139), channel_id=1, replica_groups=mesh['yhi'=2,'x'=4,'ylo'=2,'z'=8,'core'=2] {'ylo','z','core'}, dimensions={0} | all-to-all | bytes 1572864 | tf_op jit(solution)/shard_map/all_to_all | solution.py:292
  35.5 0.0 copy-done.1
  35.5 0.0 copy-done.2
  35.6 3.7 %shard_map.140 = (bf16[2,48,2048]{2,1,0:T(8,128)(2,1)S(1)}, f32[16,4096]{1,0:T(8,128)}) custom-call(bf16[32,96,128]{2,1,0:T(8,128)(2,1)S(1)} %all_to_all.5.sent_ref, f32[16,4096]{1,0:T(8,128)S(1)} %copy-done, bf16[80,96]{1,0:T(8,128)(2,1)S(1)} %copy-done.7, bf16[32,240]{1,0:T(8,128)(2,1)S(1)} %copy-done.8, f32[40,128]{1,0:T(8,128)S(1)} %copy-done.6, ...), custom_call_target="tpu_custom_call" | custom-call | tf_op jit(solution)/shard_map/pallas_call | solution.py:133
  39.4 2.4 %collective-permute-start.4 = (bf16[2,48,2048]{2,1,0:T(8,128)(2,1)S(1)}, bf16[2,48,2048]{2,1,0:T(8,128)(2,1)S(1)}, u32[]{:S(2)}, u32[]{:S(2)}) collective-permute-start(bf16[2,48,2048]{2,1,0:T(8,128)(2,1)S(1)} %get-tuple-element.34.refs_0_), channel_id=1, source_target_pairs={{0,1},{1,0},{2,3},{3,2},{4,5},{5,4},{6,7},{7,6},{8,9},{9,8},{10,11... | collective-permute-start | bytes 1179656 | tf_op jit(solution)/shard_map/ppermute | solution.py:259
  41.8 0.2 collective-permute-start.1
  42.0 0.5 collective-permute-start
  42.5 0.6 collective-permute-done.4
  43.1 0.5 collective-permute-start.5
  43.6 4.5 %collective-permute-done = bf16[32,32,128]{2,1,0:T(8,128)(2,1)S(1)} collective-permute-done((bf16[32,32,128]{2,1,0:T(8,128)(2,1)S(1)}, bf16[32,32,128]{2,1,0:T(8,128)(2,1)S(1)}, u32[]{:S(2)}, u32[]{:S(2)}) %collective-permute-start) | collective-permute-done | bytes 262176 | tf_op jit(solution)/shard_map/ppermute | solution.py:259
  48.1 0.7 collective-permute-done.1.refs_1_
  48.8 0.1 pad_maximum_fusion.refs_0_
  48.8 2.1 %collective-permute-start.3 = (bf16[2,32,32,128]{3,2,1,0:T(8,128)(2,1)S(1)}, bf16[2,32,32,128]{3,2,1,0:T(8,128)(2,1)S(1)}, u32[]{:S(2)}, u32[]{:S(2)}) collective-permute-start(bf16[2,32,32,128]{3,2,1,0:T(8,128)(2,1)S(1)} %pad_maximum_fusion.refs_0_), channel_id=1, source_target_pairs={{0,1},{1,0},{2,3},{3,2},{4,5},{5,4},{6,7},{7,6},{8,9},{9,8},{10,11... | collective-permute-start | bytes 1572872 | tf_op jit(solution)/shard_map/ppermute | solution.py:259
  51.0 0.6 collective-permute-start.8
  51.6 1.4 %collective-permute-done.5.refs_2_ = bf16[2,48,2048]{2,1,0:T(8,128)(2,1)S(1)} collective-permute-done((bf16[2,48,2048]{2,1,0:T(8,128)(2,1)S(1)}, bf16[2,48,2048]{2,1,0:T(8,128)(2,1)S(1)}, u32[]{:S(2)}, u32[]{:S(2)}) %collective-permute-start.5) | collective-permute-done | bytes 393248 | tf_op jit(solution)/shard_map/ppermute | solution.py:255
  53.0 1.0 %collective-permute-start.12 = (bf16[2,48,2048]{2,1,0:T(8,128)(2,1)S(1)}, bf16[2,48,2048]{2,1,0:T(8,128)(2,1)S(1)}, u32[]{:S(2)}, u32[]{:S(2)}) collective-permute-start(bf16[2,48,2048]{2,1,0:T(8,128)(2,1)S(1)} %collective-permute-done.5.refs_2_), channel_id=1, source_target_pairs={{0,2},{2,4},{4,6},{6,8},{8,10},{10,12},{12,14},{14,0},{1,15},{3,1}... | collective-permute-start | bytes 1179656 | tf_op jit(solution)/shard_map/ppermute | solution.py:255
  54.0 2.5 %collective-permute-start.2 = (bf16[2,32,32,128]{3,2,1,0:T(8,128)(2,1)S(1)}, bf16[2,32,32,128]{3,2,1,0:T(8,128)(2,1)}, u32[]{:S(2)}, u32[]{:S(2)}) collective-permute-start(bf16[2,32,32,128]{3,2,1,0:T(8,128)(2,1)S(1)} %pad_maximum_fusion.refs_0_), channel_id=1, source_target_pairs={{0,32},{32,64},{64,96},{96,0},{1,97},{33,1},{65,33},{97,65},{2,34}... | collective-permute-start | bytes 1572872 | tf_op jit(solution)/shard_map/ppermute | solution.py:255
  56.5 0.0 collective-permute-done.3.refs_4_
  56.5 0.5 collective-permute-start.6
  57.1 0.8 collective-permute-done.8.refs_3_
  57.9 1.5 %collective-permute-start.9 = (bf16[2,48,2048]{2,1,0:T(8,128)(2,1)S(1)}, bf16[2,48,2048]{2,1,0:T(8,128)(2,1)}, u32[]{:S(2)}, u32[]{:S(2)}) collective-permute-start(bf16[2,48,2048]{2,1,0:T(8,128)(2,1)S(1)} %collective-permute-done.8.refs_3_), channel_id=1, source_target_pairs={{0,2},{2,4},{4,6},{6,8},{8,10},{10,12},{12,14},{14,0},{1,15},{3,1}... | collective-permute-start | bytes 1179656 | tf_op jit(solution)/shard_map/ppermute | solution.py:255
  59.4 2.8 %collective-permute-done.12.refs_4_ = bf16[2,48,2048]{2,1,0:T(8,128)(2,1)S(1)} collective-permute-done((bf16[2,48,2048]{2,1,0:T(8,128)(2,1)S(1)}, bf16[2,48,2048]{2,1,0:T(8,128)(2,1)S(1)}, u32[]{:S(2)}, u32[]{:S(2)}) %collective-permute-start.12) | collective-permute-done | bytes 393248 | tf_op jit(solution)/shard_map/ppermute | solution.py:255
  62.2 1.8 %collective-permute-start.13 = (bf16[2,48,2048]{2,1,0:T(8,128)(2,1)S(1)}, bf16[2,48,2048]{2,1,0:T(8,128)(2,1)S(1)}, u32[]{:S(2)}, u32[]{:S(2)}) collective-permute-start(bf16[2,48,2048]{2,1,0:T(8,128)(2,1)S(1)} %collective-permute-done.12.refs_4_), channel_id=1, source_target_pairs={{0,2},{2,4},{4,6},{6,8},{8,10},{10,12},{12,14},{14,0},{1,15},{3,1}... | collective-permute-start | bytes 1179656 | tf_op jit(solution)/shard_map/ppermute | solution.py:255
  64.0 0.0 collective-permute-done.2.refs_1_
  64.0 2.1 %collective-permute-start.7 = (bf16[2,32,32,128]{3,2,1,0:T(8,128)(2,1)}, bf16[2,32,32,128]{3,2,1,0:T(8,128)(2,1)}, u32[]{:S(2)}, u32[]{:S(2)}) collective-permute-start(bf16[2,32,32,128]{3,2,1,0:T(8,128)(2,1)} %collective-permute-done.2.refs_1_), channel_id=1, source_target_pairs={{0,32},{32,64},{64,96},{96,0},{1,97},{33,1},{65,33},{97,65},{2,34}... | collective-permute-start | bytes 1572872 | tf_op jit(solution)/shard_map/ppermute | solution.py:255
  66.1 0.3 collective-permute-done.9.refs_1_
  66.4 2.7 %collective-permute-start.10 = (bf16[2,32,32,128]{3,2,1,0:T(8,128)(2,1)}, bf16[2,32,32,128]{3,2,1,0:T(8,128)(2,1)}, u32[]{:S(2)}, u32[]{:S(2)}) collective-permute-start(bf16[2,32,32,128]{3,2,1,0:T(8,128)(2,1)} %collective-permute-done.2.refs_1_), channel_id=1, source_target_pairs={{0,1},{1,0},{2,3},{3,2},{4,5},{5,4},{6,7},{7,6},{8,9},{9,8},{10,11... | collective-permute-start | bytes 1572872 | tf_op jit(solution)/shard_map/ppermute | solution.py:259
  69.1 0.0 collective-permute-done.6.refs_2_
  69.2 2.6 %collective-permute-start.11 = (bf16[2,32,32,128]{3,2,1,0:T(8,128)(2,1)}, bf16[2,32,32,128]{3,2,1,0:T(8,128)(2,1)}, u32[]{:S(2)}, u32[]{:S(2)}) collective-permute-start(bf16[2,32,32,128]{3,2,1,0:T(8,128)(2,1)} %collective-permute-done.6.refs_2_), channel_id=1, source_target_pairs={{0,1},{1,0},{2,3},{3,2},{4,5},{5,4},{6,7},{7,6},{8,9},{9,8},{10,11... | collective-permute-start | bytes 1572872 | tf_op jit(solution)/shard_map/ppermute | solution.py:259
  71.8 0.0 collective-permute-done.13.refs_5_
  71.8 0.2 shard_map.141.refs_8_
  72.0 2.0 %collective-permute-done.7.refs_3_ = bf16[2,32,32,128]{3,2,1,0:T(8,128)(2,1)} collective-permute-done((bf16[2,32,32,128]{3,2,1,0:T(8,128)(2,1)}, bf16[2,32,32,128]{3,2,1,0:T(8,128)(2,1)}, u32[]{:S(2)}, u32[]{:S(2)}) %collective-permute-start.7) | collective-permute-done | bytes 524320 | tf_op jit(solution)/shard_map/ppermute | solution.py:255
  74.0 3.4 %collective-permute-start.14 = (bf16[2,32,32,128]{3,2,1,0:T(8,128)(2,1)}, bf16[2,32,32,128]{3,2,1,0:T(8,128)(2,1)}, u32[]{:S(2)}, u32[]{:S(2)}) collective-permute-start(bf16[2,32,32,128]{3,2,1,0:T(8,128)(2,1)} %collective-permute-done.7.refs_3_), channel_id=1, source_target_pairs={{0,1},{1,0},{2,3},{3,2},{4,5},{5,4},{6,7},{7,6},{8,9},{9,8},{10,11... | collective-permute-start | bytes 1572872 | tf_op jit(solution)/shard_map/ppermute | solution.py:259
  77.4 2.3 %collective-permute-start.18 = (bf16[2,48,2048]{2,1,0:T(8,128)(2,1)}, bf16[2,48,2048]{2,1,0:T(8,128)(2,1)}, u32[]{:S(2)}, u32[]{:S(2)}) collective-permute-start(bf16[2,48,2048]{2,1,0:T(8,128)(2,1)} %collective-permute-done.9.refs_1_), channel_id=1, source_target_pairs={{0,2},{2,4},{4,6},{6,8},{8,10},{10,12},{12,14},{14,0},{1,15},{3,1}... | collective-permute-start | bytes 1179656 | tf_op jit(solution)/shard_map/ppermute | solution.py:255
  79.7 0.1 pad_add_fusion.place_ref
  79.8 0.0 collective-permute-done.10.refs_5_
  79.8 0.0 collective-permute-done.11.refs_6_
  79.8 0.0 collective-permute-done.14.refs_7_
  79.8 3.6 %shard_map.142 = (bf16[576,128]{1,0:T(8,128)(2,1)S(1)}, bf16[576,128]{1,0:T(8,128)(2,1)S(1)}, bf16[576,128]{1,0:T(8,128)(2,1)S(1)}, bf16[576,128]{1,0:T(8,128)(2,1)S(1)}, bf16[512,4096]{1,0:T(8,128)(2,1)S(1)}) custom-call(s32[4]{0:T(128)S(1)} %pad_add_fusion.place_ref, bf16[2,32,32,128]{3,2,1,0:T(8,128)(2,1)S(1)} %pad_maximum_fusion.refs_0_, ...), custom_call_target="tpu_custom_call" | custom-call | tf_op jit(solution)/shard_map/pallas_call | solution.py:133
  83.4 0.1 collective-permute-start.15
  83.5 0.7 collective-permute-start.16
  84.2 1.5 %collective-permute-start.17 = (bf16[576,128]{1,0:T(8,128)(2,1)S(1)}, bf16[576,128]{1,0:T(8,128)(2,1)S(1)}, u32[]{:S(2)}, u32[]{:S(2)}) collective-permute-start(bf16[576,128]{1,0:T(8,128)(2,1)S(1)} %get-tuple-element.49), channel_id=1, source_target_pairs={{0,17},{1,16},{16,1},{17,0},{2,19},{3,18},{18,3},{19,2},{4,21},{5,... | collective-permute-start | bytes 442376 | tf_op jit(solution)/shard_map/ppermute | solution.py:267
  85.6 0.0 collective-permute-done.18.refs_2_
  85.6 2.6 %shard_map.143 = (bf16[192,128]{1,0:T(8,128)(2,1)S(1)}, bf16[192,128]{1,0:T(8,128)(2,1)S(1)}, bf16[192,128]{1,0:T(8,128)(2,1)S(1)}, bf16[192,128]{1,0:T(8,128)(2,1)S(1)}) custom-call(s32[4]{0:T(128)S(1)} %pad_add_fusion.place_ref, bf16[512,4096]{1,0:T(8,128)(2,1)S(1)} %get-tuple-element.50.refs_0_, bf16[2,48,2048]{2,1,0:T(8,128)(2,1)} %collective-permute-done.9.refs_1_, ...), custom_call_target="tpu_custom_call" | custom-call | tf_op jit(solution)/shard_map/pallas_call | solution.py:133
  88.2 1.2 %collective-permute-start.19 = (bf16[192,128]{1,0:T(8,128)(2,1)S(1)}, bf16[192,128]{1,0:T(8,128)(2,1)S(1)}, u32[]{:S(2)}, u32[]{:S(2)}) collective-permute-start(bf16[192,128]{1,0:T(8,128)(2,1)S(1)} %get-tuple-element.55), channel_id=1, source_target_pairs={{0,1},{1,0},{2,3},{3,2},{4,5},{5,4},{6,7},{7,6},{8,9},{9,8},{10,11... | collective-permute-start | bytes 147464 | tf_op jit(solution)/shard_map/ppermute | solution.py:259
  89.4 0.3 collective-permute-start.20
  89.7 0.6 collective-permute-done.19.refs_5_
  90.3 0.9 collective-permute-start.21
  91.2 2.1 %collective-permute-done.20.refs_6_ = bf16[192,128]{1,0:T(8,128)(2,1)S(1)} collective-permute-done((bf16[192,128]{1,0:T(8,128)(2,1)S(1)}, bf16[192,128]{1,0:T(8,128)(2,1)S(1)}, u32[]{:S(2)}, u32[]{:S(2)}) %collective-permute-start.20) | collective-permute-done | bytes 49184 | tf_op jit(solution)/shard_map/ppermute | solution.py:259
  93.3 1.2 %collective-permute-done.21.refs_7_ = bf16[192,128]{1,0:T(8,128)(2,1)S(1)} collective-permute-done((bf16[192,128]{1,0:T(8,128)(2,1)S(1)}, bf16[192,128]{1,0:T(8,128)(2,1)S(1)}, u32[]{:S(2)}, u32[]{:S(2)}) %collective-permute-start.21) | collective-permute-done | bytes 49184 | tf_op jit(solution)/shard_map/ppermute | solution.py:267
  94.4 0.0 collective-permute-done.15.refs_1_
  94.4 0.0 collective-permute-done.16.refs_2_
  94.4 0.0 collective-permute-done.17.refs_3_
  94.4 1.7 %shard_map.144 = (bf16[3,512,128]{2,1,0:T(8,128)(2,1)}, f32[3,128,512]{2,1,0:T(8,128)}) custom-call(s32[4]{0:T(128)S(1)} %pad_add_fusion.place_ref, bf16[576,128]{1,0:T(8,128)(2,1)S(1)} %get-tuple-element.46.refs_0_, bf16[576,128]{1,0:T(8,128)(2,1)S(1)} %collective-permute-done.15.refs_1_, bf16[576,128]{1,0:T(8,128)(2,1)S(1)} %collective-permute-done.16.refs_2_, ...), custom_call_target="tpu_custom_call" | custom-call | tf_op jit(solution)/shard_map/pallas_call | solution.py:133
  (8 shorter events, 0.0 us)
Async XLA Ops:
  0.6 34.9 %copy-start.1 = (bf16[256,256]{1,0:T(8,128)(2,1)S(1)}, bf16[256,256]{1,0:T(8,128)(2,1)}, u32[]{:S(2)}) copy-start(bf16[256,256]{1,0:T(8,128)(2,1)} %constant.41.clone.ul_ref) | copy-start | bytes 393220
  0.6 34.9 %copy-start.2 = (bf16[256,256]{1,0:T(8,128)(2,1)S(1)}, bf16[256,256]{1,0:T(8,128)(2,1)}, u32[]{:S(2)}) copy-start(bf16[256,256]{1,0:T(8,128)(2,1)} %constant.40.clone.uh_ref) | copy-start | bytes 393220
  0.7 34.9 %copy-start.3 = (bf16[256,256]{1,0:T(8,128)(2,1)S(1)}, bf16[256,256]{1,0:T(8,128)(2,1)}, u32[]{:S(2)}) copy-start(bf16[256,256]{1,0:T(8,128)(2,1)} %constant.39.clone.tl_ref) | copy-start | bytes 393220
  0.7 34.9 %copy-start.4 = (bf16[256,256]{1,0:T(8,128)(2,1)S(1)}, bf16[256,256]{1,0:T(8,128)(2,1)}, u32[]{:S(2)}) copy-start(bf16[256,256]{1,0:T(8,128)(2,1)} %constant.38.clone.th_ref) | copy-start | bytes 393220
  0.7 34.9 %copy-start.5 = (f32[40,128]{1,0:T(8,128)S(1)}, f32[40,128]{1,0:T(8,128)}, u32[]{:S(2)}) copy-start(f32[40,128]{1,0:T(8,128)} %constant.37.clone.ts_ref) | copy-start | bytes 61444
  0.7 34.9 %copy-start.6 = (f32[40,128]{1,0:T(8,128)S(1)}, f32[40,128]{1,0:T(8,128)}, u32[]{:S(2)}) copy-start(f32[40,128]{1,0:T(8,128)} %constant.36.clone.tc_ref) | copy-start | bytes 61444
  0.7 34.9 %copy-start.8 = (bf16[32,240]{1,0:T(8,128)(2,1)S(1)}, bf16[32,240]{1,0:T(8,128)(2,1)}, u32[]{:S(2)}) copy-start(bf16[32,240]{1,0:T(8,128)(2,1)} %constant.35.clone.li_ref) | copy-start | bytes 46084
  0.7 34.9 %copy-start.7 = (bf16[80,96]{1,0:T(8,128)(2,1)S(1)}, bf16[80,96]{1,0:T(8,128)(2,1)}, u32[]{:S(2)}) copy-start(bf16[80,96]{1,0:T(8,128)(2,1)} %constant.34.clone.lf_ref) | copy-start | bytes 46084
  0.7 34.9 %copy-start = (f32[16,4096]{1,0:T(8,128)S(1)}, f32[16,4096]{1,0:T(8,128)}, u32[]{:S(2)}) copy-start(f32[16,4096]{1,0:T(8,128)} %filt_ref.1) | copy-start | bytes 786436
  39.4 3.8 %collective-permute-start.4 = (bf16[2,48,2048]{2,1,0:T(8,128)(2,1)S(1)}, bf16[2,48,2048]{2,1,0:T(8,128)(2,1)S(1)}, u32[]{:S(2)}, u32[]{:S(2)}) collective-permute-start(bf16[2,48,2048]{2,1,0:T(8,128)(2,1)S(1)} %get-tuple-element.34.refs_0_), channel_id=1, source_target_pairs={{0,1},{1,0},{2,3},{3,2},{4,5},{5,4},{6,7},{7,6},{8,9},{9,8},{10,11... | collective-permute-start | bytes 1179656 | tf_op jit(solution)/shard_map/ppermute | solution.py:259
  41.8 7.0 %collective-permute-start.1 = (bf16[2,48,2048]{2,1,0:T(8,128)(2,1)S(1)}, bf16[2,48,2048]{2,1,0:T(8,128)(2,1)S(1)}, u32[]{:S(2)}, u32[]{:S(2)}) collective-permute-start(bf16[2,48,2048]{2,1,0:T(8,128)(2,1)S(1)} %get-tuple-element.34.refs_0_), channel_id=1, source_target_pairs={{0,2},{2,4},{4,6},{6,8},{8,10},{10,12},{12,14},{14,0},{1,15},{3,1}... | collective-permute-start | bytes 1179656 | tf_op jit(solution)/shard_map/ppermute | solution.py:255
  42.0 6.1 %collective-permute-start = (bf16[32,32,128]{2,1,0:T(8,128)(2,1)S(1)}, bf16[32,32,128]{2,1,0:T(8,128)(2,1)S(1)}, u32[]{:S(2)}, u32[]{:S(2)}) collective-permute-start(bf16[32,32,128]{2,1,0:T(8,128)(2,1)S(1)} %slice.4), channel_id=1, source_target_pairs={{0,16},{16,0},{1,17},{17,1},{2,18},{18,2},{3,19},{19,3},{4,20},{20... | collective-permute-start | bytes 786440 | tf_op jit(solution)/shard_map/ppermute | solution.py:259
  43.1 9.9 %collective-permute-start.5 = (bf16[2,48,2048]{2,1,0:T(8,128)(2,1)S(1)}, bf16[2,48,2048]{2,1,0:T(8,128)(2,1)S(1)}, u32[]{:S(2)}, u32[]{:S(2)}) collective-permute-start(bf16[2,48,2048]{2,1,0:T(8,128)(2,1)S(1)} %collective-permute-done.4), channel_id=1, source_target_pairs={{0,2},{2,4},{4,6},{6,8},{8,10},{10,12},{12,14},{14,0},{1,15},{3,1}... | collective-permute-start | bytes 1179656 | tf_op jit(solution)/shard_map/ppermute | solution.py:255
  48.8 7.7 %collective-permute-start.3 = (bf16[2,32,32,128]{3,2,1,0:T(8,128)(2,1)S(1)}, bf16[2,32,32,128]{3,2,1,0:T(8,128)(2,1)S(1)}, u32[]{:S(2)}, u32[]{:S(2)}) collective-permute-start(bf16[2,32,32,128]{3,2,1,0:T(8,128)(2,1)S(1)} %pad_maximum_fusion.refs_0_), channel_id=1, source_target_pairs={{0,1},{1,0},{2,3},{3,2},{4,5},{5,4},{6,7},{7,6},{8,9},{9,8},{10,11... | collective-permute-start | bytes 1572872 | tf_op jit(solution)/shard_map/ppermute | solution.py:259
  51.0 6.9 %collective-permute-start.8 = (bf16[2,48,2048]{2,1,0:T(8,128)(2,1)S(1)}, bf16[2,48,2048]{2,1,0:T(8,128)(2,1)S(1)}, u32[]{:S(2)}, u32[]{:S(2)}) collective-permute-start(bf16[2,48,2048]{2,1,0:T(8,128)(2,1)S(1)} %collective-permute-done.1.refs_1_), channel_id=1, source_target_pairs={{0,2},{2,4},{4,6},{6,8},{8,10},{10,12},{12,14},{14,0},{1,15},{3,1}... | collective-permute-start | bytes 1179656 | tf_op jit(solution)/shard_map/ppermute | solution.py:255
  53.0 9.2 %collective-permute-start.12 = (bf16[2,48,2048]{2,1,0:T(8,128)(2,1)S(1)}, bf16[2,48,2048]{2,1,0:T(8,128)(2,1)S(1)}, u32[]{:S(2)}, u32[]{:S(2)}) collective-permute-start(bf16[2,48,2048]{2,1,0:T(8,128)(2,1)S(1)} %collective-permute-done.5.refs_2_), channel_id=1, source_target_pairs={{0,2},{2,4},{4,6},{6,8},{8,10},{10,12},{12,14},{14,0},{1,15},{3,1}... | collective-permute-start | bytes 1179656 | tf_op jit(solution)/shard_map/ppermute | solution.py:255
  54.0 10.0 %collective-permute-start.2 = (bf16[2,32,32,128]{3,2,1,0:T(8,128)(2,1)S(1)}, bf16[2,32,32,128]{3,2,1,0:T(8,128)(2,1)}, u32[]{:S(2)}, u32[]{:S(2)}) collective-permute-start(bf16[2,32,32,128]{3,2,1,0:T(8,128)(2,1)S(1)} %pad_maximum_fusion.refs_0_), channel_id=1, source_target_pairs={{0,32},{32,64},{64,96},{96,0},{1,97},{33,1},{65,33},{97,65},{2,34}... | collective-permute-start | bytes 1572872 | tf_op jit(solution)/shard_map/ppermute | solution.py:255
  56.5 12.6 %collective-permute-start.6 = (bf16[2,32,32,128]{3,2,1,0:T(8,128)(2,1)S(1)}, bf16[2,32,32,128]{3,2,1,0:T(8,128)(2,1)}, u32[]{:S(2)}, u32[]{:S(2)}) collective-permute-start(bf16[2,32,32,128]{3,2,1,0:T(8,128)(2,1)S(1)} %collective-permute-done.3.refs_4_), channel_id=1, source_target_pairs={{0,32},{32,64},{64,96},{96,0},{1,97},{33,1},{65,33},{97,65},{2,34}... | collective-permute-start | bytes 1572872 | tf_op jit(solution)/shard_map/ppermute | solution.py:255
  57.9 8.5 %collective-permute-start.9 = (bf16[2,48,2048]{2,1,0:T(8,128)(2,1)S(1)}, bf16[2,48,2048]{2,1,0:T(8,128)(2,1)}, u32[]{:S(2)}, u32[]{:S(2)}) collective-permute-start(bf16[2,48,2048]{2,1,0:T(8,128)(2,1)S(1)} %collective-permute-done.8.refs_3_), channel_id=1, source_target_pairs={{0,2},{2,4},{4,6},{6,8},{8,10},{10,12},{12,14},{14,0},{1,15},{3,1}... | collective-permute-start | bytes 1179656 | tf_op jit(solution)/shard_map/ppermute | solution.py:255
  62.2 9.6 %collective-permute-start.13 = (bf16[2,48,2048]{2,1,0:T(8,128)(2,1)S(1)}, bf16[2,48,2048]{2,1,0:T(8,128)(2,1)S(1)}, u32[]{:S(2)}, u32[]{:S(2)}) collective-permute-start(bf16[2,48,2048]{2,1,0:T(8,128)(2,1)S(1)} %collective-permute-done.12.refs_4_), channel_id=1, source_target_pairs={{0,2},{2,4},{4,6},{6,8},{8,10},{10,12},{12,14},{14,0},{1,15},{3,1}... | collective-permute-start | bytes 1179656 | tf_op jit(solution)/shard_map/ppermute | solution.py:255
  64.0 9.9 %collective-permute-start.7 = (bf16[2,32,32,128]{3,2,1,0:T(8,128)(2,1)}, bf16[2,32,32,128]{3,2,1,0:T(8,128)(2,1)}, u32[]{:S(2)}, u32[]{:S(2)}) collective-permute-start(bf16[2,32,32,128]{3,2,1,0:T(8,128)(2,1)} %collective-permute-done.2.refs_1_), channel_id=1, source_target_pairs={{0,32},{32,64},{64,96},{96,0},{1,97},{33,1},{65,33},{97,65},{2,34}... | collective-permute-start | bytes 1572872 | tf_op jit(solution)/shard_map/ppermute | solution.py:255
  66.4 13.4 %collective-permute-start.10 = (bf16[2,32,32,128]{3,2,1,0:T(8,128)(2,1)}, bf16[2,32,32,128]{3,2,1,0:T(8,128)(2,1)}, u32[]{:S(2)}, u32[]{:S(2)}) collective-permute-start(bf16[2,32,32,128]{3,2,1,0:T(8,128)(2,1)} %collective-permute-done.2.refs_1_), channel_id=1, source_target_pairs={{0,1},{1,0},{2,3},{3,2},{4,5},{5,4},{6,7},{7,6},{8,9},{9,8},{10,11... | collective-permute-start | bytes 1572872 | tf_op jit(solution)/shard_map/ppermute | solution.py:259
  69.2 10.7 %collective-permute-start.11 = (bf16[2,32,32,128]{3,2,1,0:T(8,128)(2,1)}, bf16[2,32,32,128]{3,2,1,0:T(8,128)(2,1)}, u32[]{:S(2)}, u32[]{:S(2)}) collective-permute-start(bf16[2,32,32,128]{3,2,1,0:T(8,128)(2,1)} %collective-permute-done.6.refs_2_), channel_id=1, source_target_pairs={{0,1},{1,0},{2,3},{3,2},{4,5},{5,4},{6,7},{7,6},{8,9},{9,8},{10,11... | collective-permute-start | bytes 1572872 | tf_op jit(solution)/shard_map/ppermute | solution.py:259
  74.0 5.8 %collective-permute-start.14 = (bf16[2,32,32,128]{3,2,1,0:T(8,128)(2,1)}, bf16[2,32,32,128]{3,2,1,0:T(8,128)(2,1)}, u32[]{:S(2)}, u32[]{:S(2)}) collective-permute-start(bf16[2,32,32,128]{3,2,1,0:T(8,128)(2,1)} %collective-permute-done.7.refs_3_), channel_id=1, source_target_pairs={{0,1},{1,0},{2,3},{3,2},{4,5},{5,4},{6,7},{7,6},{8,9},{9,8},{10,11... | collective-permute-start | bytes 1572872 | tf_op jit(solution)/shard_map/ppermute | solution.py:259
  77.4 8.2 %collective-permute-start.18 = (bf16[2,48,2048]{2,1,0:T(8,128)(2,1)}, bf16[2,48,2048]{2,1,0:T(8,128)(2,1)}, u32[]{:S(2)}, u32[]{:S(2)}) collective-permute-start(bf16[2,48,2048]{2,1,0:T(8,128)(2,1)} %collective-permute-done.9.refs_1_), channel_id=1, source_target_pairs={{0,2},{2,4},{4,6},{6,8},{8,10},{10,12},{12,14},{14,0},{1,15},{3,1}... | collective-permute-start | bytes 1179656 | tf_op jit(solution)/shard_map/ppermute | solution.py:255
  83.4 11.0 %collective-permute-start.15 = (bf16[576,128]{1,0:T(8,128)(2,1)S(1)}, bf16[576,128]{1,0:T(8,128)(2,1)S(1)}, u32[]{:S(2)}, u32[]{:S(2)}) collective-permute-start(bf16[576,128]{1,0:T(8,128)(2,1)S(1)} %get-tuple-element.47), channel_id=1, source_target_pairs={{0,1},{1,0},{2,3},{3,2},{4,5},{5,4},{6,7},{7,6},{8,9},{9,8},{10,11... | collective-permute-start | bytes 442376 | tf_op jit(solution)/shard_map/ppermute | solution.py:259
  83.5 10.9 %collective-permute-start.16 = (bf16[576,128]{1,0:T(8,128)(2,1)S(1)}, bf16[576,128]{1,0:T(8,128)(2,1)S(1)}, u32[]{:S(2)}, u32[]{:S(2)}) collective-permute-start(bf16[576,128]{1,0:T(8,128)(2,1)S(1)} %get-tuple-element.48), channel_id=1, source_target_pairs={{0,16},{16,0},{1,17},{17,1},{2,18},{18,2},{3,19},{19,3},{4,20},{20... | collective-permute-start | bytes 442376 | tf_op jit(solution)/shard_map/ppermute | solution.py:259
  84.2 10.3 %collective-permute-start.17 = (bf16[576,128]{1,0:T(8,128)(2,1)S(1)}, bf16[576,128]{1,0:T(8,128)(2,1)S(1)}, u32[]{:S(2)}, u32[]{:S(2)}) collective-permute-start(bf16[576,128]{1,0:T(8,128)(2,1)S(1)} %get-tuple-element.49), channel_id=1, source_target_pairs={{0,17},{1,16},{16,1},{17,0},{2,19},{3,18},{18,3},{19,2},{4,21},{5,... | collective-permute-start | bytes 442376 | tf_op jit(solution)/shard_map/ppermute | solution.py:267
  88.2 2.1 %collective-permute-start.19 = (bf16[192,128]{1,0:T(8,128)(2,1)S(1)}, bf16[192,128]{1,0:T(8,128)(2,1)S(1)}, u32[]{:S(2)}, u32[]{:S(2)}) collective-permute-start(bf16[192,128]{1,0:T(8,128)(2,1)S(1)} %get-tuple-element.55), channel_id=1, source_target_pairs={{0,1},{1,0},{2,3},{3,2},{4,5},{5,4},{6,7},{7,6},{8,9},{9,8},{10,11... | collective-permute-start | bytes 147464 | tf_op jit(solution)/shard_map/ppermute | solution.py:259
  89.4 3.8 %collective-permute-start.20 = (bf16[192,128]{1,0:T(8,128)(2,1)S(1)}, bf16[192,128]{1,0:T(8,128)(2,1)S(1)}, u32[]{:S(2)}, u32[]{:S(2)}) collective-permute-start(bf16[192,128]{1,0:T(8,128)(2,1)S(1)} %get-tuple-element.56), channel_id=1, source_target_pairs={{0,16},{16,0},{1,17},{17,1},{2,18},{18,2},{3,19},{19,3},{4,20},{20... | collective-permute-start | bytes 147464 | tf_op jit(solution)/shard_map/ppermute | solution.py:259
  90.3 4.1 %collective-permute-start.21 = (bf16[192,128]{1,0:T(8,128)(2,1)S(1)}, bf16[192,128]{1,0:T(8,128)(2,1)S(1)}, u32[]{:S(2)}, u32[]{:S(2)}) collective-permute-start(bf16[192,128]{1,0:T(8,128)(2,1)S(1)} %get-tuple-element.57), channel_id=1, source_target_pairs={{0,17},{1,16},{16,1},{17,0},{2,19},{3,18},{18,3},{19,2},{4,21},{5,... | collective-permute-start | bytes 147464 | tf_op jit(solution)/shard_map/ppermute | solution.py:267

commit v9 on v8

--- a/solution.py
+++ b/solution.py
@@ -125,7 +125,7 @@
     copy.wait()
 
 
-def vmem_call(body, outs, *args, scratch=(), place=None, away=(), micros=None):
+def vmem_call(body, outs, *args, scratch=(), place=None, away=()):
     specs = [pl.BlockSpec(memory_space=pltpu.VMEM)] * len(args)
     if place is not None:
         specs = [pl.BlockSpec(memory_space=pltpu.SMEM)] + specs
@@ -136,8 +136,6 @@
         in_specs=specs,
         out_specs=tuple(pl.BlockSpec(memory_space=pl.ANY if k in away else pltpu.VMEM) for k in range(len(outs))),
         scratch_shapes=scratch,
-        cost_estimate=micros
-        and pl.CostEstimate(flops=int(micros * 1.15e9), bytes_accessed=int(micros * 3.6e6), transcendentals=0),
         compiler_params=pltpu.CompilerParams(vmem_limit_bytes=24 * 1024 * 1024),
     )(*args)
 
@@ -156,17 +154,13 @@
     )
 
 
-def pack_kernel(chans, parts, inputs_ref, projected_ref, grad_ref, out_ref, sems):
-    owners = inputs_ref.shape[0]
-    step = owners // parts
-    copies = []
-    for k in range(parts):
-        here = pl.ds(k * step, step)
-        sources = [projected_ref.at[s, here] for s in range(3)] + [grad_ref.at[here]]
-        sources.append(inputs_ref.at[here, lax.axis_index("x")])
-        for s, source in enumerate(sources):
-            rows = pl.ds(s * chans, source.shape[1])
-            copies.append(pltpu.make_async_copy(source, out_ref.at[here, rows], sems.at[k, s]))
+def pack_kernel(chans, inputs_ref, projected_ref, grad_ref, out_ref, sems):
+    copies = [
+        pltpu.make_async_copy(projected_ref.at[s], out_ref.at[:, s * chans : (s + 1) * chans], sems.at[s])
+        for s in range(3)
+    ]
+    copies.append(pltpu.make_async_copy(grad_ref, out_ref.at[:, 3 * chans : 4 * chans], sems.at[3]))
+    copies.append(pltpu.make_async_copy(inputs_ref.at[:, lax.axis_index("x")], out_ref.at[:, 4 * chans :], sems.at[4]))
     for copy in copies:
         copy.start()
     for copy in copies:
@@ -279,11 +273,11 @@
     rows = inputs.shape[0] // (owners * n_x)
 
     sent = pl.pallas_call(
-        functools.partial(pack_kernel, chans, 4),
+        functools.partial(pack_kernel, chans),
         out_shape=jax.ShapeDtypeStruct((owners, 4 * chans + rows, width), bf16),
         in_specs=[pl.BlockSpec(memory_space=pl.ANY)] * 3,
         out_specs=pl.BlockSpec(memory_space=pltpu.VMEM),
-        scratch_shapes=[pltpu.SemaphoreType.DMA((4, 5))],
+        scratch_shapes=[pltpu.SemaphoreType.DMA((5,))],
     )(
         inputs.reshape(owners, n_x, rows, width),
         projected.reshape(3, owners, chans, width),
@@ -308,7 +302,7 @@
     a3 = spread(after(a2, b1), "z")
     b3 = spread(after(b2, a2), "z")
     xa2 = spread(after(xa1, b1), "x")
-    (first,) = vmem_call(stack_kernel, [((2, 6 * block.shape[1], block.shape[2]), bf16)], block, a1, b1, a2, b2, b3, micros=5)
+    (first,) = vmem_call(stack_kernel, [((2, 6 * block.shape[1], block.shape[2]), bf16)], block, a1, b1, a2, b2, b3)
     a4 = spread(after(a3, b2), "z")
 
     slots = (((0, 0), (1, 0), (1, 1), (2, 0), (2, 1), (3, 1)), ((3, 0), (4, 0)))

time: 96.5 us -> 94.1 us (0.975)
  starting transfers between devices: 31.5 us -> 24.9 us
  waiting for transfers between devices: 17 us -> 21.3 us
    ppermute x10, starting transfers between devices: 16 us -> 10.4 us  [swap(): return lax.ppermute(x, axis, [(0, 1), (1, 0)])]
    ppermute x10, waiting for transfers between devices: 8.05 us -> 11.7 us  [spread(): return lax.ppermute(x, (axis, 'core'), perm)]
where the time goes in v9:
time: 94.1 us; the launch traced here: 93.9 us
  blocking collectives  32.4 us (34%)
  starting transfers between devices  24.9 us (26%)
  waiting for transfers between devices  21.3 us (23%)
  Pallas kernels  14 us (15%)
  between operations  1.01 us (1%)
    all_to_all x1, blocking collectives, local(): sent = lax.all_to_all(sent, SEQ, split_axis=0, concat_axis=0, tiled=True)  32.4 us
    ppermute x10, starting transfers between devices, spread(): return lax.ppermute(x, (axis, 'core'), perm)  12.4 us
    pallas_call x5, Pallas kernels, vmem_call(): pl.pallas_call(body, out_shape=tuple((jax.ShapeDtypeStruct(shape, dtype)...  11.8 us
    ppermute x10, waiting for transfers between devices, spread(): return lax.ppermute(x, (axis, 'core'), perm)  11.7 us
    ppermute x10, starting transfers between devices, swap(): return lax.ppermute(x, axis, [(0, 1), (1, 0)])  10.4 us
    ppermute x10, waiting for transfers between devices, swap(): return lax.ppermute(x, axis, [(0, 1), (1, 0)])  8.44 us
    pallas_call x1, Pallas kernels, local(): pl.pallas_call(functools.partial(pack_kernel, chans), out_shape=jax.Shape...  2.28 us
    ppermute x2, starting transfers between devices, trade(): lax.ppermute(parts[3], ('ylo', 'core'), [(0, 3), (1, 2), (2, 1), (3, 0)])  2.07 us
  transfers between devices with their start and end apart: 22, of which 11 were waited for; matrix products, arithmetic and copies ran while one was open for 0% of the time, Pallas kernels for 7%

profile of v9, /device:TPU:1, one launch (start us, length us, event | category | flops | bytes accessed | tf_op | source)
XLA Modules:
  0.0 93.9 jit_solution(11183169133643393358)
XLA Ops:
  0.6 0.0 copy-start.1
  0.6 0.0 copy-start.2
  0.7 0.0 copy-start.3
  0.7 0.0 copy-start.4
  0.7 0.0 copy-start.5
  0.7 0.0 copy-start.6
  0.7 0.0 copy-start.8
  0.7 0.0 copy-start.7
  0.7 2.3 %shard_map.139 = bf16[32,96,128]{2,1,0:T(8,128)(2,1)} custom-call(bf16[32,4,32,128]{3,2,1,0:T(8,128)(2,1)} %bitcast.10, bf16[3,32,16,128]{3,2,1,0:T(8,128)(2,1)} %bitcast.12, bf16[32,16,128]{2,1,0:T(8,128)(2,1)} %bitcast.14), custom_call_target="tpu_custom_call" | custom-call | tf_op jit(solution)/shard_map/pallas_call | solution.py:275
  3.0 32.4 %all_to_all.5.sent_ref = bf16[32,96,128]{2,1,0:T(8,128)(2,1)S(1)} all-to-all(bf16[32,96,128]{2,1,0:T(8,128)(2,1)} %shard_map.139), channel_id=1, replica_groups=mesh['yhi'=2,'x'=4,'ylo'=2,'z'=8,'core'=2] {'ylo','z','core'}, dimensions={0} | all-to-all | bytes 1572864 | tf_op jit(solution)/shard_map/all_to_all | solution.py:286
  35.4 0.0 copy-done.1
  35.4 0.0 copy-done.2
  35.5 0.0 copy-done.3
  35.5 3.7 %shard_map.140 = (bf16[2,48,2048]{2,1,0:T(8,128)(2,1)S(1)}, f32[16,4096]{1,0:T(8,128)}) custom-call(bf16[32,96,128]{2,1,0:T(8,128)(2,1)S(1)} %all_to_all.5.sent_ref, f32[16,4096]{1,0:T(8,128)S(1)} %copy-done, bf16[80,96]{1,0:T(8,128)(2,1)S(1)} %copy-done.7, bf16[32,240]{1,0:T(8,128)(2,1)S(1)} %copy-done.8, f32[40,128]{1,0:T(8,128)S(1)} %copy-done.6, ...), custom_call_target="tpu_custom_call" | custom-call | tf_op jit(solution)/shard_map/pallas_call | solution.py:133
  39.3 2.4 %collective-permute-start.4 = (bf16[2,48,2048]{2,1,0:T(8,128)(2,1)S(1)}, bf16[2,48,2048]{2,1,0:T(8,128)(2,1)S(1)}, u32[]{:S(2)}, u32[]{:S(2)}) collective-permute-start(bf16[2,48,2048]{2,1,0:T(8,128)(2,1)S(1)} %get-tuple-element.34.refs_0_), channel_id=1, source_target_pairs={{0,1},{1,0},{2,3},{3,2},{4,5},{5,4},{6,7},{7,6},{8,9},{9,8},{10,11... | collective-permute-start | bytes 1179656 | tf_op jit(solution)/shard_map/ppermute | solution.py:253
  41.7 0.2 collective-permute-start.1
  41.9 0.5 collective-permute-start
  42.5 0.6 collective-permute-done.4
  43.0 0.5 collective-permute-start.5
  43.5 4.5 %collective-permute-done = bf16[32,32,128]{2,1,0:T(8,128)(2,1)S(1)} collective-permute-done((bf16[32,32,128]{2,1,0:T(8,128)(2,1)S(1)}, bf16[32,32,128]{2,1,0:T(8,128)(2,1)S(1)}, u32[]{:S(2)}, u32[]{:S(2)}) %collective-permute-start) | collective-permute-done | bytes 262176 | tf_op jit(solution)/shard_map/ppermute | solution.py:253
  48.0 0.7 collective-permute-done.1.refs_1_
  48.7 0.1 pad_maximum_fusion.refs_0_
  48.8 2.1 %collective-permute-start.3 = (bf16[2,32,32,128]{3,2,1,0:T(8,128)(2,1)S(1)}, bf16[2,32,32,128]{3,2,1,0:T(8,128)(2,1)S(1)}, u32[]{:S(2)}, u32[]{:S(2)}) collective-permute-start(bf16[2,32,32,128]{3,2,1,0:T(8,128)(2,1)S(1)} %pad_maximum_fusion.refs_0_), channel_id=1, source_target_pairs={{0,1},{1,0},{2,3},{3,2},{4,5},{5,4},{6,7},{7,6},{8,9},{9,8},{10,11... | collective-permute-start | bytes 1572872 | tf_op jit(solution)/shard_map/ppermute | solution.py:253
  50.9 2.5 %collective-permute-start.2 = (bf16[2,32,32,128]{3,2,1,0:T(8,128)(2,1)S(1)}, bf16[2,32,32,128]{3,2,1,0:T(8,128)(2,1)}, u32[]{:S(2)}, u32[]{:S(2)}) collective-permute-start(bf16[2,32,32,128]{3,2,1,0:T(8,128)(2,1)S(1)} %pad_maximum_fusion.refs_0_), channel_id=1, source_target_pairs={{0,32},{32,64},{64,96},{96,0},{1,97},{33,1},{65,33},{97,65},{2,34}... | collective-permute-start | bytes 1572872 | tf_op jit(solution)/shard_map/ppermute | solution.py:249
  53.4 0.6 collective-permute-start.8
  54.0 0.0 collective-permute-done.5.refs_2_
  54.0 0.4 collective-permute-start.12
  54.4 0.0 collective-permute-done.3.refs_4_
  54.4 2.1 %collective-permute-start.6 = (bf16[2,32,32,128]{3,2,1,0:T(8,128)(2,1)S(1)}, bf16[2,32,32,128]{3,2,1,0:T(8,128)(2,1)}, u32[]{:S(2)}, u32[]{:S(2)}) collective-permute-start(bf16[2,32,32,128]{3,2,1,0:T(8,128)(2,1)S(1)} %collective-permute-done.3.refs_4_), channel_id=1, source_target_pairs={{0,32},{32,64},{64,96},{96,0},{1,97},{33,1},{65,33},{97,65},{2,34}... | collective-permute-start | bytes 1572872 | tf_op jit(solution)/shard_map/ppermute | solution.py:249
  56.4 3.1 %collective-permute-done.2.refs_1_ = bf16[2,32,32,128]{3,2,1,0:T(8,128)(2,1)} collective-permute-done((bf16[2,32,32,128]{3,2,1,0:T(8,128)(2,1)S(1)}, bf16[2,32,32,128]{3,2,1,0:T(8,128)(2,1)}, u32[]{:S(2)}, u32[]{:S(2)}) %collective-permute-start.2) | collective-permute-done | bytes 524320 | tf_op jit(solution)/shard_map/ppermute | solution.py:249
  59.5 3.4 %collective-permute-start.7 = (bf16[2,32,32,128]{3,2,1,0:T(8,128)(2,1)}, bf16[2,32,32,128]{3,2,1,0:T(8,128)(2,1)}, u32[]{:S(2)}, u32[]{:S(2)}) collective-permute-start(bf16[2,32,32,128]{3,2,1,0:T(8,128)(2,1)} %collective-permute-done.2.refs_1_), channel_id=1, source_target_pairs={{0,32},{32,64},{64,96},{96,0},{1,97},{33,1},{65,33},{97,65},{2,34}... | collective-permute-start | bytes 1572872 | tf_op jit(solution)/shard_map/ppermute | solution.py:249
  62.9 0.0 collective-permute-done.8.refs_3_
  62.9 0.4 collective-permute-start.9
  63.3 1.3 %collective-permute-done.12.refs_4_ = bf16[2,48,2048]{2,1,0:T(8,128)(2,1)S(1)} collective-permute-done((bf16[2,48,2048]{2,1,0:T(8,128)(2,1)S(1)}, bf16[2,48,2048]{2,1,0:T(8,128)(2,1)S(1)}, u32[]{:S(2)}, u32[]{:S(2)}) %collective-permute-start.12) | collective-permute-done | bytes 393248 | tf_op jit(solution)/shard_map/ppermute | solution.py:249
  64.6 1.8 %collective-permute-start.13 = (bf16[2,48,2048]{2,1,0:T(8,128)(2,1)S(1)}, bf16[2,48,2048]{2,1,0:T(8,128)(2,1)S(1)}, u32[]{:S(2)}, u32[]{:S(2)}) collective-permute-start(bf16[2,48,2048]{2,1,0:T(8,128)(2,1)S(1)} %collective-permute-done.12.refs_4_), channel_id=1, source_target_pairs={{0,2},{2,4},{4,6},{6,8},{8,10},{10,12},{12,14},{14,0},{1,15},{3,1}... | collective-permute-start | bytes 1179656 | tf_op jit(solution)/shard_map/ppermute | solution.py:249
  66.4 3.5 %collective-permute-done.9.refs_1_ = bf16[2,48,2048]{2,1,0:T(8,128)(2,1)} collective-permute-done((bf16[2,48,2048]{2,1,0:T(8,128)(2,1)S(1)}, bf16[2,48,2048]{2,1,0:T(8,128)(2,1)}, u32[]{:S(2)}, u32[]{:S(2)}) %collective-permute-start.9) | collective-permute-done | bytes 393248 | tf_op jit(solution)/shard_map/ppermute | solution.py:249
  69.9 0.9 collective-permute-start.10
  70.9 0.0 collective-permute-done.6.refs_2_
  70.9 0.0 collective-permute-start.11
  70.9 3.2 %collective-permute-done.13.refs_5_ = bf16[2,48,2048]{2,1,0:T(8,128)(2,1)S(1)} collective-permute-done((bf16[2,48,2048]{2,1,0:T(8,128)(2,1)S(1)}, bf16[2,48,2048]{2,1,0:T(8,128)(2,1)S(1)}, u32[]{:S(2)}, u32[]{:S(2)}) %collective-permute-start.13) | collective-permute-done | bytes 393248 | tf_op jit(solution)/shard_map/ppermute | solution.py:249
  74.1 0.2 shard_map.141.refs_8_
  74.2 0.0 collective-permute-done.7.refs_3_
  74.2 1.0 %collective-permute-start.14 = (bf16[2,32,32,128]{3,2,1,0:T(8,128)(2,1)}, bf16[2,32,32,128]{3,2,1,0:T(8,128)(2,1)}, u32[]{:S(2)}, u32[]{:S(2)}) collective-permute-start(bf16[2,32,32,128]{3,2,1,0:T(8,128)(2,1)} %collective-permute-done.7.refs_3_), channel_id=1, source_target_pairs={{0,1},{1,0},{2,3},{3,2},{4,5},{5,4},{6,7},{7,6},{8,9},{9,8},{10,11... | collective-permute-start | bytes 1572872 | tf_op jit(solution)/shard_map/ppermute | solution.py:253
  75.2 0.5 collective-permute-start.18
  75.7 0.1 pad_add_fusion.place_ref
  75.8 0.0 collective-permute-done.10.refs_5_
  75.8 0.0 collective-permute-done.11.refs_6_
  75.8 1.3 %collective-permute-done.14.refs_7_ = bf16[2,32,32,128]{3,2,1,0:T(8,128)(2,1)} collective-permute-done((bf16[2,32,32,128]{3,2,1,0:T(8,128)(2,1)}, bf16[2,32,32,128]{3,2,1,0:T(8,128)(2,1)}, u32[]{:S(2)}, u32[]{:S(2)}) %collective-permute-start.14) | collective-permute-done | bytes 524320 | tf_op jit(solution)/shard_map/ppermute | solution.py:253
  77.1 3.6 %shard_map.142 = (bf16[576,128]{1,0:T(8,128)(2,1)S(1)}, bf16[576,128]{1,0:T(8,128)(2,1)S(1)}, bf16[576,128]{1,0:T(8,128)(2,1)S(1)}, bf16[576,128]{1,0:T(8,128)(2,1)S(1)}, bf16[512,4096]{1,0:T(8,128)(2,1)S(1)}) custom-call(s32[4]{0:T(128)S(1)} %pad_add_fusion.place_ref, bf16[2,32,32,128]{3,2,1,0:T(8,128)(2,1)S(1)} %pad_maximum_fusion.refs_0_, ...), custom_call_target="tpu_custom_call" | custom-call | tf_op jit(solution)/shard_map/pallas_call | solution.py:133
  80.7 0.5 collective-permute-start.15
  81.1 0.6 collective-permute-start.16
  81.7 1.2 %collective-permute-start.17 = (bf16[576,128]{1,0:T(8,128)(2,1)S(1)}, bf16[576,128]{1,0:T(8,128)(2,1)S(1)}, u32[]{:S(2)}, u32[]{:S(2)}) collective-permute-start(bf16[576,128]{1,0:T(8,128)(2,1)S(1)} %get-tuple-element.49), channel_id=1, source_target_pairs={{0,17},{1,16},{16,1},{17,0},{2,19},{3,18},{18,3},{19,2},{4,21},{5,... | collective-permute-start | bytes 442376 | tf_op jit(solution)/shard_map/ppermute | solution.py:261
  82.9 0.0 collective-permute-done.18.refs_2_
  82.9 2.6 %shard_map.143 = (bf16[192,128]{1,0:T(8,128)(2,1)S(1)}, bf16[192,128]{1,0:T(8,128)(2,1)S(1)}, bf16[192,128]{1,0:T(8,128)(2,1)S(1)}, bf16[192,128]{1,0:T(8,128)(2,1)S(1)}) custom-call(s32[4]{0:T(128)S(1)} %pad_add_fusion.place_ref, bf16[512,4096]{1,0:T(8,128)(2,1)S(1)} %get-tuple-element.50.refs_0_, bf16[2,48,2048]{2,1,0:T(8,128)(2,1)} %collective-permute-done.9.refs_1_, ...), custom_call_target="tpu_custom_call" | custom-call | tf_op jit(solution)/shard_map/pallas_call | solution.py:133
  85.5 1.8 %collective-permute-start.19 = (bf16[192,128]{1,0:T(8,128)(2,1)S(1)}, bf16[192,128]{1,0:T(8,128)(2,1)S(1)}, u32[]{:S(2)}, u32[]{:S(2)}) collective-permute-start(bf16[192,128]{1,0:T(8,128)(2,1)S(1)} %get-tuple-element.55), channel_id=1, source_target_pairs={{0,1},{1,0},{2,3},{3,2},{4,5},{5,4},{6,7},{7,6},{8,9},{9,8},{10,11... | collective-permute-start | bytes 147464 | tf_op jit(solution)/shard_map/ppermute | solution.py:253
  87.3 0.6 collective-permute-start.20
  87.9 0.3 collective-permute-done.19.refs_5_
  88.2 0.9 collective-permute-start.21
  89.1 1.8 %collective-permute-done.20.refs_6_ = bf16[192,128]{1,0:T(8,128)(2,1)S(1)} collective-permute-done((bf16[192,128]{1,0:T(8,128)(2,1)S(1)}, bf16[192,128]{1,0:T(8,128)(2,1)S(1)}, u32[]{:S(2)}, u32[]{:S(2)}) %collective-permute-start.20) | collective-permute-done | bytes 49184 | tf_op jit(solution)/shard_map/ppermute | solution.py:253
  90.8 1.1 %collective-permute-done.21.refs_7_ = bf16[192,128]{1,0:T(8,128)(2,1)S(1)} collective-permute-done((bf16[192,128]{1,0:T(8,128)(2,1)S(1)}, bf16[192,128]{1,0:T(8,128)(2,1)S(1)}, u32[]{:S(2)}, u32[]{:S(2)}) %collective-permute-start.21) | collective-permute-done | bytes 49184 | tf_op jit(solution)/shard_map/ppermute | solution.py:261
  92.0 0.0 collective-permute-done.15.refs_1_
  92.0 0.0 collective-permute-done.16.refs_2_
  92.0 0.0 collective-permute-done.17.refs_3_
  92.0 1.7 %shard_map.144 = (bf16[3,512,128]{2,1,0:T(8,128)(2,1)}, f32[3,128,512]{2,1,0:T(8,128)}) custom-call(s32[4]{0:T(128)S(1)} %pad_add_fusion.place_ref, bf16[576,128]{1,0:T(8,128)(2,1)S(1)} %get-tuple-element.46.refs_0_, bf16[576,128]{1,0:T(8,128)(2,1)S(1)} %collective-permute-done.15.refs_1_, bf16[576,128]{1,0:T(8,128)(2,1)S(1)} %collective-permute-done.16.refs_2_, ...), custom_call_target="tpu_custom_call" | custom-call | tf_op jit(solution)/shard_map/pallas_call | solution.py:133
  (8 shorter events, 0.0 us)
Async XLA Ops:
  0.6 34.8 %copy-start.1 = (bf16[256,256]{1,0:T(8,128)(2,1)S(1)}, bf16[256,256]{1,0:T(8,128)(2,1)}, u32[]{:S(2)}) copy-start(bf16[256,256]{1,0:T(8,128)(2,1)} %constant.41.clone.ul_ref) | copy-start | bytes 393220
  0.6 34.8 %copy-start.2 = (bf16[256,256]{1,0:T(8,128)(2,1)S(1)}, bf16[256,256]{1,0:T(8,128)(2,1)}, u32[]{:S(2)}) copy-start(bf16[256,256]{1,0:T(8,128)(2,1)} %constant.40.clone.uh_ref) | copy-start | bytes 393220
  0.7 34.8 %copy-start.3 = (bf16[256,256]{1,0:T(8,128)(2,1)S(1)}, bf16[256,256]{1,0:T(8,128)(2,1)}, u32[]{:S(2)}) copy-start(bf16[256,256]{1,0:T(8,128)(2,1)} %constant.39.clone.tl_ref) | copy-start | bytes 393220
  0.7 34.8 %copy-start.4 = (bf16[256,256]{1,0:T(8,128)(2,1)S(1)}, bf16[256,256]{1,0:T(8,128)(2,1)}, u32[]{:S(2)}) copy-start(bf16[256,256]{1,0:T(8,128)(2,1)} %constant.38.clone.th_ref) | copy-start | bytes 393220
  0.7 34.8 %copy-start.5 = (f32[40,128]{1,0:T(8,128)S(1)}, f32[40,128]{1,0:T(8,128)}, u32[]{:S(2)}) copy-start(f32[40,128]{1,0:T(8,128)} %constant.37.clone.ts_ref) | copy-start | bytes 61444
  0.7 34.8 %copy-start.6 = (f32[40,128]{1,0:T(8,128)S(1)}, f32[40,128]{1,0:T(8,128)}, u32[]{:S(2)}) copy-start(f32[40,128]{1,0:T(8,128)} %constant.36.clone.tc_ref) | copy-start | bytes 61444
  0.7 34.8 %copy-start.8 = (bf16[32,240]{1,0:T(8,128)(2,1)S(1)}, bf16[32,240]{1,0:T(8,128)(2,1)}, u32[]{:S(2)}) copy-start(bf16[32,240]{1,0:T(8,128)(2,1)} %constant.35.clone.li_ref) | copy-start | bytes 46084
  0.7 34.8 %copy-start.7 = (bf16[80,96]{1,0:T(8,128)(2,1)S(1)}, bf16[80,96]{1,0:T(8,128)(2,1)}, u32[]{:S(2)}) copy-start(bf16[80,96]{1,0:T(8,128)(2,1)} %constant.34.clone.lf_ref) | copy-start | bytes 46084
  0.7 34.8 %copy-start = (f32[16,4096]{1,0:T(8,128)S(1)}, f32[16,4096]{1,0:T(8,128)}, u32[]{:S(2)}) copy-start(f32[16,4096]{1,0:T(8,128)} %filt_ref.1) | copy-start | bytes 786436
  39.3 3.8 %collective-permute-start.4 = (bf16[2,48,2048]{2,1,0:T(8,128)(2,1)S(1)}, bf16[2,48,2048]{2,1,0:T(8,128)(2,1)S(1)}, u32[]{:S(2)}, u32[]{:S(2)}) collective-permute-start(bf16[2,48,2048]{2,1,0:T(8,128)(2,1)S(1)} %get-tuple-element.34.refs_0_), channel_id=1, source_target_pairs={{0,1},{1,0},{2,3},{3,2},{4,5},{5,4},{6,7},{7,6},{8,9},{9,8},{10,11... | collective-permute-start | bytes 1179656 | tf_op jit(solution)/shard_map/ppermute | solution.py:253
  41.7 7.0 %collective-permute-start.1 = (bf16[2,48,2048]{2,1,0:T(8,128)(2,1)S(1)}, bf16[2,48,2048]{2,1,0:T(8,128)(2,1)S(1)}, u32[]{:S(2)}, u32[]{:S(2)}) collective-permute-start(bf16[2,48,2048]{2,1,0:T(8,128)(2,1)S(1)} %get-tuple-element.34.refs_0_), channel_id=1, source_target_pairs={{0,2},{2,4},{4,6},{6,8},{8,10},{10,12},{12,14},{14,0},{1,15},{3,1}... | collective-permute-start | bytes 1179656 | tf_op jit(solution)/shard_map/ppermute | solution.py:249
  41.9 6.1 %collective-permute-start = (bf16[32,32,128]{2,1,0:T(8,128)(2,1)S(1)}, bf16[32,32,128]{2,1,0:T(8,128)(2,1)S(1)}, u32[]{:S(2)}, u32[]{:S(2)}) collective-permute-start(bf16[32,32,128]{2,1,0:T(8,128)(2,1)S(1)} %slice.4), channel_id=1, source_target_pairs={{0,16},{16,0},{1,17},{17,1},{2,18},{18,2},{3,19},{19,3},{4,20},{20... | collective-permute-start | bytes 786440 | tf_op jit(solution)/shard_map/ppermute | solution.py:253
  43.0 11.0 %collective-permute-start.5 = (bf16[2,48,2048]{2,1,0:T(8,128)(2,1)S(1)}, bf16[2,48,2048]{2,1,0:T(8,128)(2,1)S(1)}, u32[]{:S(2)}, u32[]{:S(2)}) collective-permute-start(bf16[2,48,2048]{2,1,0:T(8,128)(2,1)S(1)} %collective-permute-done.4), channel_id=1, source_target_pairs={{0,2},{2,4},{4,6},{6,8},{8,10},{10,12},{12,14},{14,0},{1,15},{3,1}... | collective-permute-start | bytes 1179656 | tf_op jit(solution)/shard_map/ppermute | solution.py:249
  48.8 5.6 %collective-permute-start.3 = (bf16[2,32,32,128]{3,2,1,0:T(8,128)(2,1)S(1)}, bf16[2,32,32,128]{3,2,1,0:T(8,128)(2,1)S(1)}, u32[]{:S(2)}, u32[]{:S(2)}) collective-permute-start(bf16[2,32,32,128]{3,2,1,0:T(8,128)(2,1)S(1)} %pad_maximum_fusion.refs_0_), channel_id=1, source_target_pairs={{0,1},{1,0},{2,3},{3,2},{4,5},{5,4},{6,7},{7,6},{8,9},{9,8},{10,11... | collective-permute-start | bytes 1572872 | tf_op jit(solution)/shard_map/ppermute | solution.py:253
  50.9 8.6 %collective-permute-start.2 = (bf16[2,32,32,128]{3,2,1,0:T(8,128)(2,1)S(1)}, bf16[2,32,32,128]{3,2,1,0:T(8,128)(2,1)}, u32[]{:S(2)}, u32[]{:S(2)}) collective-permute-start(bf16[2,32,32,128]{3,2,1,0:T(8,128)(2,1)S(1)} %pad_maximum_fusion.refs_0_), channel_id=1, source_target_pairs={{0,32},{32,64},{64,96},{96,0},{1,97},{33,1},{65,33},{97,65},{2,34}... | collective-permute-start | bytes 1572872 | tf_op jit(solution)/shard_map/ppermute | solution.py:249
  53.4 9.5 %collective-permute-start.8 = (bf16[2,48,2048]{2,1,0:T(8,128)(2,1)S(1)}, bf16[2,48,2048]{2,1,0:T(8,128)(2,1)S(1)}, u32[]{:S(2)}, u32[]{:S(2)}) collective-permute-start(bf16[2,48,2048]{2,1,0:T(8,128)(2,1)S(1)} %collective-permute-done.1.refs_1_), channel_id=1, source_target_pairs={{0,2},{2,4},{4,6},{6,8},{8,10},{10,12},{12,14},{14,0},{1,15},{3,1}... | collective-permute-start | bytes 1179656 | tf_op jit(solution)/shard_map/ppermute | solution.py:249
  54.0 10.6 %collective-permute-start.12 = (bf16[2,48,2048]{2,1,0:T(8,128)(2,1)S(1)}, bf16[2,48,2048]{2,1,0:T(8,128)(2,1)S(1)}, u32[]{:S(2)}, u32[]{:S(2)}) collective-permute-start(bf16[2,48,2048]{2,1,0:T(8,128)(2,1)S(1)} %collective-permute-done.5.refs_2_), channel_id=1, source_target_pairs={{0,2},{2,4},{4,6},{6,8},{8,10},{10,12},{12,14},{14,0},{1,15},{3,1}... | collective-permute-start | bytes 1179656 | tf_op jit(solution)/shard_map/ppermute | solution.py:249
  54.4 16.5 %collective-permute-start.6 = (bf16[2,32,32,128]{3,2,1,0:T(8,128)(2,1)S(1)}, bf16[2,32,32,128]{3,2,1,0:T(8,128)(2,1)}, u32[]{:S(2)}, u32[]{:S(2)}) collective-permute-start(bf16[2,32,32,128]{3,2,1,0:T(8,128)(2,1)S(1)} %collective-permute-done.3.refs_4_), channel_id=1, source_target_pairs={{0,32},{32,64},{64,96},{96,0},{1,97},{33,1},{65,33},{97,65},{2,34}... | collective-permute-start | bytes 1572872 | tf_op jit(solution)/shard_map/ppermute | solution.py:249
  59.5 14.7 %collective-permute-start.7 = (bf16[2,32,32,128]{3,2,1,0:T(8,128)(2,1)}, bf16[2,32,32,128]{3,2,1,0:T(8,128)(2,1)}, u32[]{:S(2)}, u32[]{:S(2)}) collective-permute-start(bf16[2,32,32,128]{3,2,1,0:T(8,128)(2,1)} %collective-permute-done.2.refs_1_), channel_id=1, source_target_pairs={{0,32},{32,64},{64,96},{96,0},{1,97},{33,1},{65,33},{97,65},{2,34}... | collective-permute-start | bytes 1572872 | tf_op jit(solution)/shard_map/ppermute | solution.py:249
  62.9 7.0 %collective-permute-start.9 = (bf16[2,48,2048]{2,1,0:T(8,128)(2,1)S(1)}, bf16[2,48,2048]{2,1,0:T(8,128)(2,1)}, u32[]{:S(2)}, u32[]{:S(2)}) collective-permute-start(bf16[2,48,2048]{2,1,0:T(8,128)(2,1)S(1)} %collective-permute-done.8.refs_3_), channel_id=1, source_target_pairs={{0,2},{2,4},{4,6},{6,8},{8,10},{10,12},{12,14},{14,0},{1,15},{3,1}... | collective-permute-start | bytes 1179656 | tf_op jit(solution)/shard_map/ppermute | solution.py:249
  64.6 9.4 %collective-permute-start.13 = (bf16[2,48,2048]{2,1,0:T(8,128)(2,1)S(1)}, bf16[2,48,2048]{2,1,0:T(8,128)(2,1)S(1)}, u32[]{:S(2)}, u32[]{:S(2)}) collective-permute-start(bf16[2,48,2048]{2,1,0:T(8,128)(2,1)S(1)} %collective-permute-done.12.refs_4_), channel_id=1, source_target_pairs={{0,2},{2,4},{4,6},{6,8},{8,10},{10,12},{12,14},{14,0},{1,15},{3,1}... | collective-permute-start | bytes 1179656 | tf_op jit(solution)/shard_map/ppermute | solution.py:249
  69.9 5.9 %collective-permute-start.10 = (bf16[2,32,32,128]{3,2,1,0:T(8,128)(2,1)}, bf16[2,32,32,128]{3,2,1,0:T(8,128)(2,1)}, u32[]{:S(2)}, u32[]{:S(2)}) collective-permute-start(bf16[2,32,32,128]{3,2,1,0:T(8,128)(2,1)} %collective-permute-done.2.refs_1_), channel_id=1, source_target_pairs={{0,1},{1,0},{2,3},{3,2},{4,5},{5,4},{6,7},{7,6},{8,9},{9,8},{10,11... | collective-permute-start | bytes 1572872 | tf_op jit(solution)/shard_map/ppermute | solution.py:253
  70.9 5.0 %collective-permute-start.11 = (bf16[2,32,32,128]{3,2,1,0:T(8,128)(2,1)}, bf16[2,32,32,128]{3,2,1,0:T(8,128)(2,1)}, u32[]{:S(2)}, u32[]{:S(2)}) collective-permute-start(bf16[2,32,32,128]{3,2,1,0:T(8,128)(2,1)} %collective-permute-done.6.refs_2_), channel_id=1, source_target_pairs={{0,1},{1,0},{2,3},{3,2},{4,5},{5,4},{6,7},{7,6},{8,9},{9,8},{10,11... | collective-permute-start | bytes 1572872 | tf_op jit(solution)/shard_map/ppermute | solution.py:253
  74.2 2.9 %collective-permute-start.14 = (bf16[2,32,32,128]{3,2,1,0:T(8,128)(2,1)}, bf16[2,32,32,128]{3,2,1,0:T(8,128)(2,1)}, u32[]{:S(2)}, u32[]{:S(2)}) collective-permute-start(bf16[2,32,32,128]{3,2,1,0:T(8,128)(2,1)} %collective-permute-done.7.refs_3_), channel_id=1, source_target_pairs={{0,1},{1,0},{2,3},{3,2},{4,5},{5,4},{6,7},{7,6},{8,9},{9,8},{10,11... | collective-permute-start | bytes 1572872 | tf_op jit(solution)/shard_map/ppermute | solution.py:253
  75.2 7.7 %collective-permute-start.18 = (bf16[2,48,2048]{2,1,0:T(8,128)(2,1)}, bf16[2,48,2048]{2,1,0:T(8,128)(2,1)}, u32[]{:S(2)}, u32[]{:S(2)}) collective-permute-start(bf16[2,48,2048]{2,1,0:T(8,128)(2,1)} %collective-permute-done.9.refs_1_), channel_id=1, source_target_pairs={{0,2},{2,4},{4,6},{6,8},{8,10},{10,12},{12,14},{14,0},{1,15},{3,1}... | collective-permute-start | bytes 1179656 | tf_op jit(solution)/shard_map/ppermute | solution.py:249
  80.7 11.3 %collective-permute-start.15 = (bf16[576,128]{1,0:T(8,128)(2,1)S(1)}, bf16[576,128]{1,0:T(8,128)(2,1)S(1)}, u32[]{:S(2)}, u32[]{:S(2)}) collective-permute-start(bf16[576,128]{1,0:T(8,128)(2,1)S(1)} %get-tuple-element.47), channel_id=1, source_target_pairs={{0,1},{1,0},{2,3},{3,2},{4,5},{5,4},{6,7},{7,6},{8,9},{9,8},{10,11... | collective-permute-start | bytes 442376 | tf_op jit(solution)/shard_map/ppermute | solution.py:253
  81.1 10.9 %collective-permute-start.16 = (bf16[576,128]{1,0:T(8,128)(2,1)S(1)}, bf16[576,128]{1,0:T(8,128)(2,1)S(1)}, u32[]{:S(2)}, u32[]{:S(2)}) collective-permute-start(bf16[576,128]{1,0:T(8,128)(2,1)S(1)} %get-tuple-element.48), channel_id=1, source_target_pairs={{0,16},{16,0},{1,17},{17,1},{2,18},{18,2},{3,19},{19,3},{4,20},{20... | collective-permute-start | bytes 442376 | tf_op jit(solution)/shard_map/ppermute | solution.py:253
  81.7 10.3 %collective-permute-start.17 = (bf16[576,128]{1,0:T(8,128)(2,1)S(1)}, bf16[576,128]{1,0:T(8,128)(2,1)S(1)}, u32[]{:S(2)}, u32[]{:S(2)}) collective-permute-start(bf16[576,128]{1,0:T(8,128)(2,1)S(1)} %get-tuple-element.49), channel_id=1, source_target_pairs={{0,17},{1,16},{16,1},{17,0},{2,19},{3,18},{18,3},{19,2},{4,21},{5,... | collective-permute-start | bytes 442376 | tf_op jit(solution)/shard_map/ppermute | solution.py:261
  85.5 2.7 %collective-permute-start.19 = (bf16[192,128]{1,0:T(8,128)(2,1)S(1)}, bf16[192,128]{1,0:T(8,128)(2,1)S(1)}, u32[]{:S(2)}, u32[]{:S(2)}) collective-permute-start(bf16[192,128]{1,0:T(8,128)(2,1)S(1)} %get-tuple-element.55), channel_id=1, source_target_pairs={{0,1},{1,0},{2,3},{3,2},{4,5},{5,4},{6,7},{7,6},{8,9},{9,8},{10,11... | collective-permute-start | bytes 147464 | tf_op jit(solution)/shard_map/ppermute | solution.py:253
  87.3 3.5 %collective-permute-start.20 = (bf16[192,128]{1,0:T(8,128)(2,1)S(1)}, bf16[192,128]{1,0:T(8,128)(2,1)S(1)}, u32[]{:S(2)}, u32[]{:S(2)}) collective-permute-start(bf16[192,128]{1,0:T(8,128)(2,1)S(1)} %get-tuple-element.56), channel_id=1, source_target_pairs={{0,16},{16,0},{1,17},{17,1},{2,18},{18,2},{3,19},{19,3},{4,20},{20... | collective-permute-start | bytes 147464 | tf_op jit(solution)/shard_map/ppermute | solution.py:253
  88.2 3.8 %collective-permute-start.21 = (bf16[192,128]{1,0:T(8,128)(2,1)S(1)}, bf16[192,128]{1,0:T(8,128)(2,1)S(1)}, u32[]{:S(2)}, u32[]{:S(2)}) collective-permute-start(bf16[192,128]{1,0:T(8,128)(2,1)S(1)} %get-tuple-element.57), channel_id=1, source_target_pairs={{0,17},{1,16},{16,1},{17,0},{2,19},{3,18},{18,3},{19,2},{4,21},{5,... | collective-permute-start | bytes 147464 | tf_op jit(solution)/shard_map/ppermute | solution.py:261

commit v10 on v9

--- a/solution.py
+++ b/solution.py
@@ -290,12 +290,12 @@
 
     block, filter_grad = spectral(sent, filters)
     a1 = spread(block, "z")
-    turned = swap(block, "core")
-    turned = after(turned, block)
+    start, y_rows = lax.optimization_barrier((block, y_rows))
+    turned = swap(start, "core")
     b1 = spread(turned, "z")
     a2 = spread(after(a1, turned), "z")
     b2 = spread(after(b1, a1), "z")
-    both_rows = jnp.stack([own_rows, after(y_rows, a1)])
+    both_rows = jnp.stack([own_rows, after(y_rows, block)])
     other_rows = swap(both_rows, "core")
     xa1 = spread(both_rows, "x")
     xb1 = spread(after(other_rows, b1), "x")

time: 94.1 us -> 94.8 us (level)
  starting transfers between devices: 24.9 us -> 28 us
  waiting for transfers between devices: 21.3 us -> 19 us
    ppermute x10, waiting for transfers between devices: 8.44 us -> 3.71 us  [swap(): return lax.ppermute(x, axis, [(0, 1), (1, 0)])]
    ppermute x10, starting transfers between devices: 10.4 us -> 14.7 us  [swap(): return lax.ppermute(x, axis, [(0, 1), (1, 0)])]
    ppermute x10, waiting for transfers between devices: 11.7 us -> 14 us  [spread(): return lax.ppermute(x, (axis, 'core'), perm)]
    ppermute x10, starting transfers between devices: 12.4 us -> 11.4 us  [spread(): return lax.ppermute(x, (axis, 'core'), perm)]
  transfers between devices with their start and end apart: 22 -> 22, of which waited for: 11 -> 10; matrix products, arithmetic and copies ran while one was open for 0% -> 0% of each run, Pallas kernels for 7% -> 11%
where the time goes in v10:
time: 94.8 us; the launch traced here: 94.6 us
  blocking collectives  32.4 us (34%)
  starting transfers between devices  28 us (30%)
  waiting for transfers between devices  19 us (20%)
  Pallas kernels  14 us (15%)
  between operations  0.98 us (1%)
    all_to_all x1, blocking collectives, local(): sent = lax.all_to_all(sent, SEQ, split_axis=0, concat_axis=0, tiled=True)  32.4 us
    ppermute x10, starting transfers between devices, swap(): return lax.ppermute(x, axis, [(0, 1), (1, 0)])  14.7 us
    ppermute x10, waiting for transfers between devices, spread(): return lax.ppermute(x, (axis, 'core'), perm)  14 us
    pallas_call x5, Pallas kernels, vmem_call(): pl.pallas_call(body, out_shape=tuple((jax.ShapeDtypeStruct(shape, dtype)...  11.8 us
    ppermute x10, starting transfers between devices, spread(): return lax.ppermute(x, (axis, 'core'), perm)  11.4 us
    ppermute x10, waiting for transfers between devices, swap(): return lax.ppermute(x, axis, [(0, 1), (1, 0)])  3.71 us
    pallas_call x1, Pallas kernels, local(): pl.pallas_call(functools.partial(pack_kernel, chans), out_shape=jax.Shape...  2.28 us
  transfers between devices with their start and end apart: 22, of which 10 were waited for; matrix products, arithmetic and copies ran while one was open for 0% of the time, Pallas kernels for 11%

profile of v10, /device:TPU:1, one launch (start us, length us, event | category | flops | bytes accessed | tf_op | source)
XLA Modules:
  0.0 94.6 jit_solution(167516991429653061)
XLA Ops:
  0.6 0.0 copy-start.1
  0.6 0.0 copy-start.2
  0.7 0.0 copy-start.3
  0.7 0.0 copy-start.4
  0.7 0.0 copy-start.5
  0.7 0.0 copy-start.6
  0.7 0.0 copy-start.8
  0.7 0.0 copy-start.7
  0.7 0.0 copy-start
  0.7 2.3 %shard_map.139 = bf16[32,96,128]{2,1,0:T(8,128)(2,1)} custom-call(bf16[32,4,32,128]{3,2,1,0:T(8,128)(2,1)} %bitcast.10, bf16[3,32,16,128]{3,2,1,0:T(8,128)(2,1)} %bitcast.12, bf16[32,16,128]{2,1,0:T(8,128)(2,1)} %bitcast.14), custom_call_target="tpu_custom_call" | custom-call | tf_op jit(solution)/shard_map/pallas_call | solution.py:275
  3.0 32.4 %all_to_all.5.sent_ref = bf16[32,96,128]{2,1,0:T(8,128)(2,1)S(1)} all-to-all(bf16[32,96,128]{2,1,0:T(8,128)(2,1)} %shard_map.139), channel_id=1, replica_groups=mesh['yhi'=2,'x'=4,'ylo'=2,'z'=8,'core'=2] {'ylo','z','core'}, dimensions={0} | all-to-all | bytes 1572864 | tf_op jit(solution)/shard_map/all_to_all | solution.py:286
  35.4 1.3 %collective-permute-start = (bf16[32,32,128]{2,1,0:T(8,128)(2,1)S(1)}, bf16[32,32,128]{2,1,0:T(8,128)(2,1)S(1)}, u32[]{:S(2)}, u32[]{:S(2)}) collective-permute-start(bf16[32,32,128]{2,1,0:T(8,128)(2,1)S(1)} %slice.4), channel_id=1, source_target_pairs={{0,16},{16,0},{1,17},{17,1},{2,18},{18,2},{3,19},{19,3},{4,20},{20... | collective-permute-start | bytes 786440 | tf_op jit(solution)/shard_map/ppermute | solution.py:253
  36.7 0.0 copy-done.1
  36.7 0.0 copy-done.2
  36.8 3.7 %shard_map.140 = (bf16[2,48,2048]{2,1,0:T(8,128)(2,1)S(1)}, f32[16,4096]{1,0:T(8,128)}) custom-call(bf16[32,96,128]{2,1,0:T(8,128)(2,1)S(1)} %all_to_all.5.sent_ref, f32[16,4096]{1,0:T(8,128)S(1)} %copy-done, bf16[80,96]{1,0:T(8,128)(2,1)S(1)} %copy-done.7, bf16[32,240]{1,0:T(8,128)(2,1)S(1)} %copy-done.8, f32[40,128]{1,0:T(8,128)S(1)} %copy-done.6, ...), custom_call_target="tpu_custom_call" | custom-call | tf_op jit(solution)/shard_map/pallas_call | solution.py:133
  40.5 0.2 collective-permute-done
  40.7 3.5 %collective-permute-start.3 = (bf16[2,48,2048]{2,1,0:T(8,128)(2,1)S(1)}, bf16[2,48,2048]{2,1,0:T(8,128)(2,1)S(1)}, u32[]{:S(2)}, u32[]{:S(2)}) collective-permute-start(bf16[2,48,2048]{2,1,0:T(8,128)(2,1)S(1)} %get-tuple-element.38.refs_0_), channel_id=1, source_target_pairs={{0,1},{1,0},{2,3},{3,2},{4,5},{5,4},{6,7},{7,6},{8,9},{9,8},{10,11... | collective-permute-start | bytes 1179656 | tf_op jit(solution)/shard_map/ppermute | solution.py:253
  44.2 0.4 collective-permute-start.7
  44.6 1.0 %collective-permute-done.3 = bf16[2,48,2048]{2,1,0:T(8,128)(2,1)S(1)} collective-permute-done((bf16[2,48,2048]{2,1,0:T(8,128)(2,1)S(1)}, bf16[2,48,2048]{2,1,0:T(8,128)(2,1)S(1)}, u32[]{:S(2)}, u32[]{:S(2)}) %collective-permute-start.3) | collective-permute-done | bytes 393248 | tf_op jit(solution)/shard_map/ppermute | solution.py:253
  45.6 1.8 %collective-permute-start.4 = (bf16[2,48,2048]{2,1,0:T(8,128)(2,1)S(1)}, bf16[2,48,2048]{2,1,0:T(8,128)(2,1)S(1)}, u32[]{:S(2)}, u32[]{:S(2)}) collective-permute-start(bf16[2,48,2048]{2,1,0:T(8,128)(2,1)S(1)} %collective-permute-done.3), channel_id=1, source_target_pairs={{0,2},{2,4},{4,6},{6,8},{8,10},{10,12},{12,14},{14,0},{1,15},{3,1}... | collective-permute-start | bytes 1179656 | tf_op jit(solution)/shard_map/ppermute | solution.py:249
  47.4 0.1 pad_maximum_fusion.refs_0_
  47.5 1.8 %collective-permute-start.2 = (bf16[2,32,32,128]{3,2,1,0:T(8,128)(2,1)S(1)}, bf16[2,32,32,128]{3,2,1,0:T(8,128)(2,1)S(1)}, u32[]{:S(2)}, u32[]{:S(2)}) collective-permute-start(bf16[2,32,32,128]{3,2,1,0:T(8,128)(2,1)S(1)} %pad_maximum_fusion.refs_0_), channel_id=1, source_target_pairs={{0,1},{1,0},{2,3},{3,2},{4,5},{5,4},{6,7},{7,6},{8,9},{9,8},{10,11... | collective-permute-start | bytes 1572872 | tf_op jit(solution)/shard_map/ppermute | solution.py:253
  49.3 2.5 %collective-permute-start.1 = (bf16[2,32,32,128]{3,2,1,0:T(8,128)(2,1)S(1)}, bf16[2,32,32,128]{3,2,1,0:T(8,128)(2,1)}, u32[]{:S(2)}, u32[]{:S(2)}) collective-permute-start(bf16[2,32,32,128]{3,2,1,0:T(8,128)(2,1)S(1)} %pad_maximum_fusion.refs_0_), channel_id=1, source_target_pairs={{0,32},{32,64},{64,96},{96,0},{1,97},{33,1},{65,33},{97,65},{2,34}... | collective-permute-start | bytes 1572872 | tf_op jit(solution)/shard_map/ppermute | solution.py:249
  51.7 0.8 collective-permute-done.7.refs_1_
  52.6 0.4 collective-permute-start.8
  53.0 3.9 %collective-permute-done.4.refs_2_ = bf16[2,48,2048]{2,1,0:T(8,128)(2,1)S(1)} collective-permute-done((bf16[2,48,2048]{2,1,0:T(8,128)(2,1)S(1)}, bf16[2,48,2048]{2,1,0:T(8,128)(2,1)S(1)}, u32[]{:S(2)}, u32[]{:S(2)}) %collective-permute-start.4) | collective-permute-done | bytes 393248 | tf_op jit(solution)/shard_map/ppermute | solution.py:249
  56.9 0.2 collective-permute-start.12
  57.1 0.0 collective-permute-done.2.refs_4_
  57.1 2.3 %collective-permute-start.5 = (bf16[2,32,32,128]{3,2,1,0:T(8,128)(2,1)S(1)}, bf16[2,32,32,128]{3,2,1,0:T(8,128)(2,1)}, u32[]{:S(2)}, u32[]{:S(2)}) collective-permute-start(bf16[2,32,32,128]{3,2,1,0:T(8,128)(2,1)S(1)} %collective-permute-done.2.refs_4_), channel_id=1, source_target_pairs={{0,32},{32,64},{64,96},{96,0},{1,97},{33,1},{65,33},{97,65},{2,34}... | collective-permute-start | bytes 1572872 | tf_op jit(solution)/shard_map/ppermute | solution.py:249
  59.4 0.0 collective-permute-done.1.refs_1_
  59.4 1.9 %collective-permute-start.6 = (bf16[2,32,32,128]{3,2,1,0:T(8,128)(2,1)}, bf16[2,32,32,128]{3,2,1,0:T(8,128)(2,1)}, u32[]{:S(2)}, u32[]{:S(2)}) collective-permute-start(bf16[2,32,32,128]{3,2,1,0:T(8,128)(2,1)} %collective-permute-done.1.refs_1_), channel_id=1, source_target_pairs={{0,32},{32,64},{64,96},{96,0},{1,97},{33,1},{65,33},{97,65},{2,34}... | collective-permute-start | bytes 1572872 | tf_op jit(solution)/shard_map/ppermute | solution.py:249
  61.3 0.0 collective-permute-done.8.refs_3_
  61.3 1.1 %collective-permute-start.9 = (bf16[2,48,2048]{2,1,0:T(8,128)(2,1)S(1)}, bf16[2,48,2048]{2,1,0:T(8,128)(2,1)}, u32[]{:S(2)}, u32[]{:S(2)}) collective-permute-start(bf16[2,48,2048]{2,1,0:T(8,128)(2,1)S(1)} %collective-permute-done.8.refs_3_), channel_id=1, source_target_pairs={{0,2},{2,4},{4,6},{6,8},{8,10},{10,12},{12,14},{14,0},{1,15},{3,1}... | collective-permute-start | bytes 1179656 | tf_op jit(solution)/shard_map/ppermute | solution.py:249
  62.3 3.0 %collective-permute-done.12.refs_4_ = bf16[2,48,2048]{2,1,0:T(8,128)(2,1)S(1)} collective-permute-done((bf16[2,48,2048]{2,1,0:T(8,128)(2,1)S(1)}, bf16[2,48,2048]{2,1,0:T(8,128)(2,1)S(1)}, u32[]{:S(2)}, u32[]{:S(2)}) %collective-permute-start.12) | collective-permute-done | bytes 393248 | tf_op jit(solution)/shard_map/ppermute | solution.py:249
  65.3 0.2 collective-permute-start.13
  65.5 4.0 %collective-permute-done.9.refs_1_ = bf16[2,48,2048]{2,1,0:T(8,128)(2,1)} collective-permute-done((bf16[2,48,2048]{2,1,0:T(8,128)(2,1)S(1)}, bf16[2,48,2048]{2,1,0:T(8,128)(2,1)}, u32[]{:S(2)}, u32[]{:S(2)}) %collective-permute-start.9) | collective-permute-done | bytes 393248 | tf_op jit(solution)/shard_map/ppermute | solution.py:249
  69.5 1.9 %collective-permute-start.10 = (bf16[2,32,32,128]{3,2,1,0:T(8,128)(2,1)}, bf16[2,32,32,128]{3,2,1,0:T(8,128)(2,1)}, u32[]{:S(2)}, u32[]{:S(2)}) collective-permute-start(bf16[2,32,32,128]{3,2,1,0:T(8,128)(2,1)} %collective-permute-done.1.refs_1_), channel_id=1, source_target_pairs={{0,1},{1,0},{2,3},{3,2},{4,5},{5,4},{6,7},{7,6},{8,9},{9,8},{10,11... | collective-permute-start | bytes 1572872 | tf_op jit(solution)/shard_map/ppermute | solution.py:253
  71.5 0.0 collective-permute-done.5.refs_2_
  71.5 0.0 collective-permute-start.11
  71.5 2.3 %collective-permute-done.13.refs_5_ = bf16[2,48,2048]{2,1,0:T(8,128)(2,1)S(1)} collective-permute-done((bf16[2,48,2048]{2,1,0:T(8,128)(2,1)S(1)}, bf16[2,48,2048]{2,1,0:T(8,128)(2,1)S(1)}, u32[]{:S(2)}, u32[]{:S(2)}) %collective-permute-start.13) | collective-permute-done | bytes 393248 | tf_op jit(solution)/shard_map/ppermute | solution.py:249
  73.8 0.2 shard_map.141.refs_8_
  73.9 0.0 collective-permute-done.6.refs_3_
  73.9 1.9 %collective-permute-start.14 = (bf16[2,32,32,128]{3,2,1,0:T(8,128)(2,1)}, bf16[2,32,32,128]{3,2,1,0:T(8,128)(2,1)}, u32[]{:S(2)}, u32[]{:S(2)}) collective-permute-start(bf16[2,32,32,128]{3,2,1,0:T(8,128)(2,1)} %collective-permute-done.6.refs_3_), channel_id=1, source_target_pairs={{0,1},{1,0},{2,3},{3,2},{4,5},{5,4},{6,7},{7,6},{8,9},{9,8},{10,11... | collective-permute-start | bytes 1572872 | tf_op jit(solution)/shard_map/ppermute | solution.py:253
  75.8 0.7 collective-permute-start.18
  76.5 0.1 pad_add_fusion.place_ref
  76.6 0.0 collective-permute-done.10.refs_5_
  76.6 0.0 collective-permute-done.11.refs_6_
  76.6 1.1 %collective-permute-done.14.refs_7_ = bf16[2,32,32,128]{3,2,1,0:T(8,128)(2,1)} collective-permute-done((bf16[2,32,32,128]{3,2,1,0:T(8,128)(2,1)}, bf16[2,32,32,128]{3,2,1,0:T(8,128)(2,1)}, u32[]{:S(2)}, u32[]{:S(2)}) %collective-permute-start.14) | collective-permute-done | bytes 524320 | tf_op jit(solution)/shard_map/ppermute | solution.py:253
  77.7 3.6 %shard_map.142 = (bf16[576,128]{1,0:T(8,128)(2,1)S(1)}, bf16[576,128]{1,0:T(8,128)(2,1)S(1)}, bf16[576,128]{1,0:T(8,128)(2,1)S(1)}, bf16[576,128]{1,0:T(8,128)(2,1)S(1)}, bf16[512,4096]{1,0:T(8,128)(2,1)S(1)}) custom-call(s32[4]{0:T(128)S(1)} %pad_add_fusion.place_ref, bf16[2,32,32,128]{3,2,1,0:T(8,128)(2,1)S(1)} %pad_maximum_fusion.refs_0_, ...), custom_call_target="tpu_custom_call" | custom-call | tf_op jit(solution)/shard_map/pallas_call | solution.py:133
  81.3 0.5 collective-permute-start.15
  81.8 1.0 %collective-permute-start.16 = (bf16[576,128]{1,0:T(8,128)(2,1)S(1)}, bf16[576,128]{1,0:T(8,128)(2,1)S(1)}, u32[]{:S(2)}, u32[]{:S(2)}) collective-permute-start(bf16[576,128]{1,0:T(8,128)(2,1)S(1)} %get-tuple-element.50), channel_id=1, source_target_pairs={{0,16},{16,0},{1,17},{17,1},{2,18},{18,2},{3,19},{19,3},{4,20},{20... | collective-permute-start | bytes 442376 | tf_op jit(solution)/shard_map/ppermute | solution.py:253
  82.8 0.8 collective-permute-start.17
  83.5 0.0 collective-permute-done.18.refs_2_
  83.5 2.6 %shard_map.143 = (bf16[192,128]{1,0:T(8,128)(2,1)S(1)}, bf16[192,128]{1,0:T(8,128)(2,1)S(1)}, bf16[192,128]{1,0:T(8,128)(2,1)S(1)}, bf16[192,128]{1,0:T(8,128)(2,1)S(1)}) custom-call(s32[4]{0:T(128)S(1)} %pad_add_fusion.place_ref, bf16[512,4096]{1,0:T(8,128)(2,1)S(1)} %get-tuple-element.52.refs_0_, bf16[2,48,2048]{2,1,0:T(8,128)(2,1)} %collective-permute-done.9.refs_1_, ...), custom_call_target="tpu_custom_call" | custom-call | tf_op jit(solution)/shard_map/pallas_call | solution.py:133
  86.2 1.8 %collective-permute-start.19 = (bf16[192,128]{1,0:T(8,128)(2,1)S(1)}, bf16[192,128]{1,0:T(8,128)(2,1)S(1)}, u32[]{:S(2)}, u32[]{:S(2)}) collective-permute-start(bf16[192,128]{1,0:T(8,128)(2,1)S(1)} %get-tuple-element.57), channel_id=1, source_target_pairs={{0,1},{1,0},{2,3},{3,2},{4,5},{5,4},{6,7},{7,6},{8,9},{9,8},{10,11... | collective-permute-start | bytes 147464 | tf_op jit(solution)/shard_map/ppermute | solution.py:253
  87.9 1.0 %collective-permute-start.20 = (bf16[192,128]{1,0:T(8,128)(2,1)S(1)}, bf16[192,128]{1,0:T(8,128)(2,1)S(1)}, u32[]{:S(2)}, u32[]{:S(2)}) collective-permute-start(bf16[192,128]{1,0:T(8,128)(2,1)S(1)} %get-tuple-element.58), channel_id=1, source_target_pairs={{0,16},{16,0},{1,17},{17,1},{2,18},{18,2},{3,19},{19,3},{4,20},{20... | collective-permute-start | bytes 147464 | tf_op jit(solution)/shard_map/ppermute | solution.py:253
  89.0 0.0 collective-permute-done.19.refs_5_
  89.0 1.1 %collective-permute-start.21 = (bf16[192,128]{1,0:T(8,128)(2,1)S(1)}, bf16[192,128]{1,0:T(8,128)(2,1)S(1)}, u32[]{:S(2)}, u32[]{:S(2)}) collective-permute-start(bf16[192,128]{1,0:T(8,128)(2,1)S(1)} %get-tuple-element.59), channel_id=1, source_target_pairs={{0,17},{1,16},{16,1},{17,0},{2,19},{3,18},{18,3},{19,2},{4,21},{5,... | collective-permute-start | bytes 147464 | tf_op jit(solution)/shard_map/ppermute | solution.py:261
  90.1 1.4 %collective-permute-done.20.refs_6_ = bf16[192,128]{1,0:T(8,128)(2,1)S(1)} collective-permute-done((bf16[192,128]{1,0:T(8,128)(2,1)S(1)}, bf16[192,128]{1,0:T(8,128)(2,1)S(1)}, u32[]{:S(2)}, u32[]{:S(2)}) %collective-permute-start.20) | collective-permute-done | bytes 49184 | tf_op jit(solution)/shard_map/ppermute | solution.py:253
  91.5 1.2 %collective-permute-done.21.refs_7_ = bf16[192,128]{1,0:T(8,128)(2,1)S(1)} collective-permute-done((bf16[192,128]{1,0:T(8,128)(2,1)S(1)}, bf16[192,128]{1,0:T(8,128)(2,1)S(1)}, u32[]{:S(2)}, u32[]{:S(2)}) %collective-permute-start.21) | collective-permute-done | bytes 49184 | tf_op jit(solution)/shard_map/ppermute | solution.py:261
  92.7 0.0 collective-permute-done.15.refs_1_
  92.7 0.0 collective-permute-done.16.refs_2_
  92.7 0.0 collective-permute-done.17.refs_3_
  92.7 1.7 %shard_map.144 = (bf16[3,512,128]{2,1,0:T(8,128)(2,1)}, f32[3,128,512]{2,1,0:T(8,128)}) custom-call(s32[4]{0:T(128)S(1)} %pad_add_fusion.place_ref, bf16[576,128]{1,0:T(8,128)(2,1)S(1)} %get-tuple-element.48.refs_0_, bf16[576,128]{1,0:T(8,128)(2,1)S(1)} %collective-permute-done.15.refs_1_, bf16[576,128]{1,0:T(8,128)(2,1)S(1)} %collective-permute-done.16.refs_2_, ...), custom_call_target="tpu_custom_call" | custom-call | tf_op jit(solution)/shard_map/pallas_call | solution.py:133
  (8 shorter events, 0.0 us)
Async XLA Ops:
  0.6 36.1 %copy-start.1 = (bf16[256,256]{1,0:T(8,128)(2,1)S(1)}, bf16[256,256]{1,0:T(8,128)(2,1)}, u32[]{:S(2)}) copy-start(bf16[256,256]{1,0:T(8,128)(2,1)} %constant.41.clone.ul_ref) | copy-start | bytes 393220
  0.6 36.1 %copy-start.2 = (bf16[256,256]{1,0:T(8,128)(2,1)S(1)}, bf16[256,256]{1,0:T(8,128)(2,1)}, u32[]{:S(2)}) copy-start(bf16[256,256]{1,0:T(8,128)(2,1)} %constant.40.clone.uh_ref) | copy-start | bytes 393220
  0.7 36.1 %copy-start.3 = (bf16[256,256]{1,0:T(8,128)(2,1)S(1)}, bf16[256,256]{1,0:T(8,128)(2,1)}, u32[]{:S(2)}) copy-start(bf16[256,256]{1,0:T(8,128)(2,1)} %constant.39.clone.tl_ref) | copy-start | bytes 393220
  0.7 36.1 %copy-start.4 = (bf16[256,256]{1,0:T(8,128)(2,1)S(1)}, bf16[256,256]{1,0:T(8,128)(2,1)}, u32[]{:S(2)}) copy-start(bf16[256,256]{1,0:T(8,128)(2,1)} %constant.38.clone.th_ref) | copy-start | bytes 393220
  0.7 36.0 %copy-start.5 = (f32[40,128]{1,0:T(8,128)S(1)}, f32[40,128]{1,0:T(8,128)}, u32[]{:S(2)}) copy-start(f32[40,128]{1,0:T(8,128)} %constant.37.clone.ts_ref) | copy-start | bytes 61444
  0.7 36.0 %copy-start.6 = (f32[40,128]{1,0:T(8,128)S(1)}, f32[40,128]{1,0:T(8,128)}, u32[]{:S(2)}) copy-start(f32[40,128]{1,0:T(8,128)} %constant.36.clone.tc_ref) | copy-start | bytes 61444
  0.7 36.0 %copy-start.8 = (bf16[32,240]{1,0:T(8,128)(2,1)S(1)}, bf16[32,240]{1,0:T(8,128)(2,1)}, u32[]{:S(2)}) copy-start(bf16[32,240]{1,0:T(8,128)(2,1)} %constant.35.clone.li_ref) | copy-start | bytes 46084
  0.7 36.0 %copy-start.7 = (bf16[80,96]{1,0:T(8,128)(2,1)S(1)}, bf16[80,96]{1,0:T(8,128)(2,1)}, u32[]{:S(2)}) copy-start(bf16[80,96]{1,0:T(8,128)(2,1)} %constant.34.clone.lf_ref) | copy-start | bytes 46084
  0.7 36.0 %copy-start = (f32[16,4096]{1,0:T(8,128)S(1)}, f32[16,4096]{1,0:T(8,128)}, u32[]{:S(2)}) copy-start(f32[16,4096]{1,0:T(8,128)} %filt_ref.1) | copy-start | bytes 786436
  35.4 5.3 %collective-permute-start = (bf16[32,32,128]{2,1,0:T(8,128)(2,1)S(1)}, bf16[32,32,128]{2,1,0:T(8,128)(2,1)S(1)}, u32[]{:S(2)}, u32[]{:S(2)}) collective-permute-start(bf16[32,32,128]{2,1,0:T(8,128)(2,1)S(1)} %slice.4), channel_id=1, source_target_pairs={{0,16},{16,0},{1,17},{17,1},{2,18},{18,2},{3,19},{19,3},{4,20},{20... | collective-permute-start | bytes 786440 | tf_op jit(solution)/shard_map/ppermute | solution.py:253
  40.7 4.8 %collective-permute-start.3 = (bf16[2,48,2048]{2,1,0:T(8,128)(2,1)S(1)}, bf16[2,48,2048]{2,1,0:T(8,128)(2,1)S(1)}, u32[]{:S(2)}, u32[]{:S(2)}) collective-permute-start(bf16[2,48,2048]{2,1,0:T(8,128)(2,1)S(1)} %get-tuple-element.38.refs_0_), channel_id=1, source_target_pairs={{0,1},{1,0},{2,3},{3,2},{4,5},{5,4},{6,7},{7,6},{8,9},{9,8},{10,11... | collective-permute-start | bytes 1179656 | tf_op jit(solution)/shard_map/ppermute | solution.py:253
  44.2 8.3 %collective-permute-start.7 = (bf16[2,48,2048]{2,1,0:T(8,128)(2,1)S(1)}, bf16[2,48,2048]{2,1,0:T(8,128)(2,1)S(1)}, u32[]{:S(2)}, u32[]{:S(2)}) collective-permute-start(bf16[2,48,2048]{2,1,0:T(8,128)(2,1)S(1)} %get-tuple-element.38.refs_0_), channel_id=1, source_target_pairs={{0,2},{2,4},{4,6},{6,8},{8,10},{10,12},{12,14},{14,0},{1,15},{3,1}... | collective-permute-start | bytes 1179656 | tf_op jit(solution)/shard_map/ppermute | solution.py:249
  45.6 11.3 %collective-permute-start.4 = (bf16[2,48,2048]{2,1,0:T(8,128)(2,1)S(1)}, bf16[2,48,2048]{2,1,0:T(8,128)(2,1)S(1)}, u32[]{:S(2)}, u32[]{:S(2)}) collective-permute-start(bf16[2,48,2048]{2,1,0:T(8,128)(2,1)S(1)} %collective-permute-done.3), channel_id=1, source_target_pairs={{0,2},{2,4},{4,6},{6,8},{8,10},{10,12},{12,14},{14,0},{1,15},{3,1}... | collective-permute-start | bytes 1179656 | tf_op jit(solution)/shard_map/ppermute | solution.py:249
  47.5 9.6 %collective-permute-start.2 = (bf16[2,32,32,128]{3,2,1,0:T(8,128)(2,1)S(1)}, bf16[2,32,32,128]{3,2,1,0:T(8,128)(2,1)S(1)}, u32[]{:S(2)}, u32[]{:S(2)}) collective-permute-start(bf16[2,32,32,128]{3,2,1,0:T(8,128)(2,1)S(1)} %pad_maximum_fusion.refs_0_), channel_id=1, source_target_pairs={{0,1},{1,0},{2,3},{3,2},{4,5},{5,4},{6,7},{7,6},{8,9},{9,8},{10,11... | collective-permute-start | bytes 1572872 | tf_op jit(solution)/shard_map/ppermute | solution.py:253
  49.3 10.1 %collective-permute-start.1 = (bf16[2,32,32,128]{3,2,1,0:T(8,128)(2,1)S(1)}, bf16[2,32,32,128]{3,2,1,0:T(8,128)(2,1)}, u32[]{:S(2)}, u32[]{:S(2)}) collective-permute-start(bf16[2,32,32,128]{3,2,1,0:T(8,128)(2,1)S(1)} %pad_maximum_fusion.refs_0_), channel_id=1, source_target_pairs={{0,32},{32,64},{64,96},{96,0},{1,97},{33,1},{65,33},{97,65},{2,34}... | collective-permute-start | bytes 1572872 | tf_op jit(solution)/shard_map/ppermute | solution.py:249
  52.6 8.7 %collective-permute-start.8 = (bf16[2,48,2048]{2,1,0:T(8,128)(2,1)S(1)}, bf16[2,48,2048]{2,1,0:T(8,128)(2,1)S(1)}, u32[]{:S(2)}, u32[]{:S(2)}) collective-permute-start(bf16[2,48,2048]{2,1,0:T(8,128)(2,1)S(1)} %collective-permute-done.7.refs_1_), channel_id=1, source_target_pairs={{0,2},{2,4},{4,6},{6,8},{8,10},{10,12},{12,14},{14,0},{1,15},{3,1}... | collective-permute-start | bytes 1179656 | tf_op jit(solution)/shard_map/ppermute | solution.py:249
  56.9 8.4 %collective-permute-start.12 = (bf16[2,48,2048]{2,1,0:T(8,128)(2,1)S(1)}, bf16[2,48,2048]{2,1,0:T(8,128)(2,1)S(1)}, u32[]{:S(2)}, u32[]{:S(2)}) collective-permute-start(bf16[2,48,2048]{2,1,0:T(8,128)(2,1)S(1)} %collective-permute-done.4.refs_2_), channel_id=1, source_target_pairs={{0,2},{2,4},{4,6},{6,8},{8,10},{10,12},{12,14},{14,0},{1,15},{3,1}... | collective-permute-start | bytes 1179656 | tf_op jit(solution)/shard_map/ppermute | solution.py:249
  57.1 14.4 %collective-permute-start.5 = (bf16[2,32,32,128]{3,2,1,0:T(8,128)(2,1)S(1)}, bf16[2,32,32,128]{3,2,1,0:T(8,128)(2,1)}, u32[]{:S(2)}, u32[]{:S(2)}) collective-permute-start(bf16[2,32,32,128]{3,2,1,0:T(8,128)(2,1)S(1)} %collective-permute-done.2.refs_4_), channel_id=1, source_target_pairs={{0,32},{32,64},{64,96},{96,0},{1,97},{33,1},{65,33},{97,65},{2,34}... | collective-permute-start | bytes 1572872 | tf_op jit(solution)/shard_map/ppermute | solution.py:249
  59.4 14.5 %collective-permute-start.6 = (bf16[2,32,32,128]{3,2,1,0:T(8,128)(2,1)}, bf16[2,32,32,128]{3,2,1,0:T(8,128)(2,1)}, u32[]{:S(2)}, u32[]{:S(2)}) collective-permute-start(bf16[2,32,32,128]{3,2,1,0:T(8,128)(2,1)} %collective-permute-done.1.refs_1_), channel_id=1, source_target_pairs={{0,32},{32,64},{64,96},{96,0},{1,97},{33,1},{65,33},{97,65},{2,34}... | collective-permute-start | bytes 1572872 | tf_op jit(solution)/shard_map/ppermute | solution.py:249
  61.3 8.3 %collective-permute-start.9 = (bf16[2,48,2048]{2,1,0:T(8,128)(2,1)S(1)}, bf16[2,48,2048]{2,1,0:T(8,128)(2,1)}, u32[]{:S(2)}, u32[]{:S(2)}) collective-permute-start(bf16[2,48,2048]{2,1,0:T(8,128)(2,1)S(1)} %collective-permute-done.8.refs_3_), channel_id=1, source_target_pairs={{0,2},{2,4},{4,6},{6,8},{8,10},{10,12},{12,14},{14,0},{1,15},{3,1}... | collective-permute-start | bytes 1179656 | tf_op jit(solution)/shard_map/ppermute | solution.py:249
  65.3 8.4 %collective-permute-start.13 = (bf16[2,48,2048]{2,1,0:T(8,128)(2,1)S(1)}, bf16[2,48,2048]{2,1,0:T(8,128)(2,1)S(1)}, u32[]{:S(2)}, u32[]{:S(2)}) collective-permute-start(bf16[2,48,2048]{2,1,0:T(8,128)(2,1)S(1)} %collective-permute-done.12.refs_4_), channel_id=1, source_target_pairs={{0,2},{2,4},{4,6},{6,8},{8,10},{10,12},{12,14},{14,0},{1,15},{3,1}... | collective-permute-start | bytes 1179656 | tf_op jit(solution)/shard_map/ppermute | solution.py:249
  69.5 7.1 %collective-permute-start.10 = (bf16[2,32,32,128]{3,2,1,0:T(8,128)(2,1)}, bf16[2,32,32,128]{3,2,1,0:T(8,128)(2,1)}, u32[]{:S(2)}, u32[]{:S(2)}) collective-permute-start(bf16[2,32,32,128]{3,2,1,0:T(8,128)(2,1)} %collective-permute-done.1.refs_1_), channel_id=1, source_target_pairs={{0,1},{1,0},{2,3},{3,2},{4,5},{5,4},{6,7},{7,6},{8,9},{9,8},{10,11... | collective-permute-start | bytes 1572872 | tf_op jit(solution)/shard_map/ppermute | solution.py:253
  71.5 5.1 %collective-permute-start.11 = (bf16[2,32,32,128]{3,2,1,0:T(8,128)(2,1)}, bf16[2,32,32,128]{3,2,1,0:T(8,128)(2,1)}, u32[]{:S(2)}, u32[]{:S(2)}) collective-permute-start(bf16[2,32,32,128]{3,2,1,0:T(8,128)(2,1)} %collective-permute-done.5.refs_2_), channel_id=1, source_target_pairs={{0,1},{1,0},{2,3},{3,2},{4,5},{5,4},{6,7},{7,6},{8,9},{9,8},{10,11... | collective-permute-start | bytes 1572872 | tf_op jit(solution)/shard_map/ppermute | solution.py:253
  73.9 3.8 %collective-permute-start.14 = (bf16[2,32,32,128]{3,2,1,0:T(8,128)(2,1)}, bf16[2,32,32,128]{3,2,1,0:T(8,128)(2,1)}, u32[]{:S(2)}, u32[]{:S(2)}) collective-permute-start(bf16[2,32,32,128]{3,2,1,0:T(8,128)(2,1)} %collective-permute-done.6.refs_3_), channel_id=1, source_target_pairs={{0,1},{1,0},{2,3},{3,2},{4,5},{5,4},{6,7},{7,6},{8,9},{9,8},{10,11... | collective-permute-start | bytes 1572872 | tf_op jit(solution)/shard_map/ppermute | solution.py:253
  75.8 7.7 %collective-permute-start.18 = (bf16[2,48,2048]{2,1,0:T(8,128)(2,1)}, bf16[2,48,2048]{2,1,0:T(8,128)(2,1)}, u32[]{:S(2)}, u32[]{:S(2)}) collective-permute-start(bf16[2,48,2048]{2,1,0:T(8,128)(2,1)} %collective-permute-done.9.refs_1_), channel_id=1, source_target_pairs={{0,2},{2,4},{4,6},{6,8},{8,10},{10,12},{12,14},{14,0},{1,15},{3,1}... | collective-permute-start | bytes 1179656 | tf_op jit(solution)/shard_map/ppermute | solution.py:249
  81.3 11.4 %collective-permute-start.15 = (bf16[576,128]{1,0:T(8,128)(2,1)S(1)}, bf16[576,128]{1,0:T(8,128)(2,1)S(1)}, u32[]{:S(2)}, u32[]{:S(2)}) collective-permute-start(bf16[576,128]{1,0:T(8,128)(2,1)S(1)} %get-tuple-element.49), channel_id=1, source_target_pairs={{0,1},{1,0},{2,3},{3,2},{4,5},{5,4},{6,7},{7,6},{8,9},{9,8},{10,11... | collective-permute-start | bytes 442376 | tf_op jit(solution)/shard_map/ppermute | solution.py:253
  81.8 11.0 %collective-permute-start.16 = (bf16[576,128]{1,0:T(8,128)(2,1)S(1)}, bf16[576,128]{1,0:T(8,128)(2,1)S(1)}, u32[]{:S(2)}, u32[]{:S(2)}) collective-permute-start(bf16[576,128]{1,0:T(8,128)(2,1)S(1)} %get-tuple-element.50), channel_id=1, source_target_pairs={{0,16},{16,0},{1,17},{17,1},{2,18},{18,2},{3,19},{19,3},{4,20},{20... | collective-permute-start | bytes 442376 | tf_op jit(solution)/shard_map/ppermute | solution.py:253
  82.8 9.9 %collective-permute-start.17 = (bf16[576,128]{1,0:T(8,128)(2,1)S(1)}, bf16[576,128]{1,0:T(8,128)(2,1)S(1)}, u32[]{:S(2)}, u32[]{:S(2)}) collective-permute-start(bf16[576,128]{1,0:T(8,128)(2,1)S(1)} %get-tuple-element.51), channel_id=1, source_target_pairs={{0,17},{1,16},{16,1},{17,0},{2,19},{3,18},{18,3},{19,2},{4,21},{5,... | collective-permute-start | bytes 442376 | tf_op jit(solution)/shard_map/ppermute | solution.py:261
  86.2 2.8 %collective-permute-start.19 = (bf16[192,128]{1,0:T(8,128)(2,1)S(1)}, bf16[192,128]{1,0:T(8,128)(2,1)S(1)}, u32[]{:S(2)}, u32[]{:S(2)}) collective-permute-start(bf16[192,128]{1,0:T(8,128)(2,1)S(1)} %get-tuple-element.57), channel_id=1, source_target_pairs={{0,1},{1,0},{2,3},{3,2},{4,5},{5,4},{6,7},{7,6},{8,9},{9,8},{10,11... | collective-permute-start | bytes 147464 | tf_op jit(solution)/shard_map/ppermute | solution.py:253
  87.9 3.5 %collective-permute-start.20 = (bf16[192,128]{1,0:T(8,128)(2,1)S(1)}, bf16[192,128]{1,0:T(8,128)(2,1)S(1)}, u32[]{:S(2)}, u32[]{:S(2)}) collective-permute-start(bf16[192,128]{1,0:T(8,128)(2,1)S(1)} %get-tuple-element.58), channel_id=1, source_target_pairs={{0,16},{16,0},{1,17},{17,1},{2,18},{18,2},{3,19},{19,3},{4,20},{20... | collective-permute-start | bytes 147464 | tf_op jit(solution)/shard_map/ppermute | solution.py:253
  89.0 3.7 %collective-permute-start.21 = (bf16[192,128]{1,0:T(8,128)(2,1)S(1)}, bf16[192,128]{1,0:T(8,128)(2,1)S(1)}, u32[]{:S(2)}, u32[]{:S(2)}) collective-permute-start(bf16[192,128]{1,0:T(8,128)(2,1)S(1)} %get-tuple-element.59), channel_id=1, source_target_pairs={{0,17},{1,16},{16,1},{17,0},{2,19},{3,18},{18,3},{19,2},{4,21},{5,... | collective-permute-start | bytes 147464 | tf_op jit(solution)/shard_map/ppermute | solution.py:261

commit v11 on v9

--- a/solution.py
+++ b/solution.py
@@ -60,8 +60,32 @@
     return high, (x - high.astype(jnp.float32)).astype(jnp.bfloat16)
 
 
+def inverse(re, im, chans, width, tables):
+    li, tc, ts, uh, ul = tables
+    rows = tc.shape[0]
+    high, low = split(jnp.concatenate([re, im], 1))
+    b = dot(high, uh) + dot(low, uh) + dot(high, ul)
+    parts = []
+    for c in range(chans):
+        br = b[c * rows : (c + 1) * rows, :width]
+        bi = b[c * rows : (c + 1) * rows, width:]
+        parts.append(jnp.concatenate([br * tc - bi * ts, br * ts + bi * tc], 0))
+    high, low = split(jnp.concatenate(parts, 1))
+    y = dot(li, jnp.concatenate([high, high, low], 0))
+    return pltpu.einshape("i(cj)->icj", y, c=chans)
+
+
+def taps_kernel(chans, width, blocks, gate_ref, carr_ref, li_ref, tc_ref, ts_ref, uh_ref, ul_ref, taps_ref):
+    gr, gi = gate_ref[:, :width], gate_ref[:, width:]
+    cr, ci = carr_ref[:, :width], carr_ref[:, width:]
+    tables = tuple(ref[...] for ref in (li_ref, tc_ref, ts_ref, uh_ref, ul_ref))
+    taps = inverse(cr * gr + ci * gi, ci * gr - cr * gi, chans, width, tables)
+    for i in range(blocks):
+        taps_ref[:, i * width : (i + 1) * width] = taps[i]
+
+
 def kernel(
-    chans, width, blocks, sent_ref, filt_ref, lf_ref, li_ref, tc_ref, ts_ref, th_ref, tl_ref, uh_ref, ul_ref, out_ref, taps_ref, held_ref, sem
+    chans, width, blocks, sent_ref, filt_ref, lf_ref, li_ref, tc_ref, ts_ref, th_ref, tl_ref, uh_ref, ul_ref, out_ref, gate_ref, carr_ref
 ):
     rows = tc_ref.shape[0]
     tc, ts = tc_ref[...], ts_ref[...]
@@ -85,18 +109,6 @@
         x = dot(high, th) + dot(low, th) + dot(high, tl)
         return x[:, :width], x[:, width:]
 
-    def inverse(re, im):
-        high, low = split(jnp.concatenate([re, im], 1))
-        b = dot(high, uh) + dot(low, uh) + dot(high, ul)
-        parts = []
-        for c in range(chans):
-            br = b[c * rows : (c + 1) * rows, :width]
-            bi = b[c * rows : (c + 1) * rows, width:]
-            parts.append(jnp.concatenate([br * tc - bi * ts, br * ts + bi * tc], 0))
-        high, low = split(jnp.concatenate(parts, 1))
-        y = dot(li, jnp.concatenate([high, high, low], 0))
-        return pltpu.einshape("i(cj)->icj", y, c=chans)
-
     def stream(s):
         return sent_ref[:, s * chans : (s + 1) * chans].astype(jnp.float32)
 
@@ -112,17 +124,15 @@
     fr, fi = forward(*split(flat(filt)))
     gr, gi = forward(gate, None)
     cr, ci = forward(carr, None)
-    taps = inverse(cr * gr + ci * gi, ci * gr - cr * gi)
-    for i in range(blocks):
-        held_ref[:, i * width : (i + 1) * width] = taps[i]
-    copy = pltpu.make_async_copy(held_ref, taps_ref, sem)
-    copy.start()
-    conv = inverse(fr * gr - fi * gi, fr * gi + fi * gr).astype(jnp.bfloat16).astype(jnp.float32)
+    for ref, parts in ((gate_ref, (gr, gi)), (carr_ref, (cr, ci))):
+        ref[:, :width] = parts[0]
+        ref[:, width:] = parts[1]
+    tables = (li, tc, ts, uh, ul)
+    conv = inverse(fr * gr - fi * gi, fr * gi + fi * gr, chans, width, tables).astype(jnp.bfloat16).astype(jnp.float32)
     put(0, stream(3) * conv)
-    back = inverse(fr * cr + fi * ci, fr * ci - fi * cr).astype(jnp.bfloat16).astype(jnp.float32)
+    back = inverse(fr * cr + fi * ci, fr * ci - fi * cr, chans, width, tables).astype(jnp.bfloat16).astype(jnp.float32)
     put(1, back * stream(2))
     put(2, back * stream(1))
-    copy.wait()
 
 
 def vmem_call(body, outs, *args, scratch=(), place=None, away=()):
@@ -143,15 +153,31 @@
 def spectral(sent, filters):
     blocks, _, width = sent.shape
     chans = filters.shape[0]
+    values = tables(blocks, width)
+    spectrum = ((chans * values[2].shape[0], 2 * width), jnp.float32)
     return vmem_call(
         functools.partial(kernel, chans, width, blocks),
-        [((2, 3 * chans, blocks * width // 2), jnp.bfloat16), (filters.shape, jnp.float32)],
+        [((2, 3 * chans, blocks * width // 2), jnp.bfloat16), spectrum, spectrum],
         sent,
         filters,
-        *tables(blocks, width),
-        scratch=[pltpu.VMEM(filters.shape, jnp.float32), pltpu.SemaphoreType.DMA],
-        away=(1,),
-    )
+        *values,
+    )
+
+
+def filter_taps(gate, carr, chans, blocks):
+    width = gate.shape[1] // 2
+    _, li, tc, ts, _, _, uh, ul = tables(blocks, width)
+    return vmem_call(
+        functools.partial(taps_kernel, chans, width, blocks),
+        [((chans, blocks * width), jnp.float32)],
+        gate,
+        carr,
+        li,
+        tc,
+        ts,
+        uh,
+        ul,
+    )[0]
 
 
 def pack_kernel(chans, inputs_ref, projected_ref, grad_ref, out_ref, sems):
@@ -288,7 +314,8 @@
     sent, own_rows = lax.optimization_barrier((sent, own_rows))
     y_rows = swap(own_rows, "ylo")
 
-    block, filter_grad = spectral(sent, filters)
+    block, gate, carr = spectral(sent, filters)
+    filter_grad = filter_taps(gate, carr, chans, owners)
     a1 = spread(block, "z")
     turned = swap(block, "core")
     turned = after(turned, block)

time: 94.1 us -> 94.4 us (level)
  local copies, waits for them, and re-layouts: 0.08 us -> 1.93 us
  starting transfers between devices: 24.9 us -> 23.7 us
  waiting for transfers between devices: 21.3 us -> 20.2 us
    unnamed x18 -> x34, local copies, waits for them, and re-layouts: 0.06 us -> 1.91 us
    ppermute x10, starting transfers between devices: 10.4 us -> 9.22 us  [swap(): return lax.ppermute(x, axis, [(0, 1), (1, 0)])]
    pallas_call x5 -> x6, Pallas kernels: 11.8 us -> 12.4 us  [vmem_call(): pl.pallas_call(body, out_shape=tuple((jax.ShapeDtypeStruct(shape, dtype)...]
  transfers between devices with their start and end apart: 22 -> 22, of which waited for: 11 -> 11; matrix products, arithmetic and copies ran while one was open for 0% -> 0% of each run, Pallas kernels for 7% -> 8%
where the time goes in v11:
time: 94.4 us; the launch traced here: 94.1 us
  blocking collectives  32.4 us (34%)
  starting transfers between devices  23.7 us (25%)
  waiting for transfers between devices  20.2 us (21%)
  Pallas kernels  14.7 us (16%)
  local copies, waits for them, and re-layouts  1.93 us (2%)
  between operations  1.04 us (1%)
    all_to_all x1, blocking collectives, local(): sent = lax.all_to_all(sent, SEQ, split_axis=0, concat_axis=0, tiled=True)  32.4 us
    ppermute x10, starting transfers between devices, spread(): return lax.ppermute(x, (axis, 'core'), perm)  12.4 us
    pallas_call x6, Pallas kernels, vmem_call(): pl.pallas_call(body, out_shape=tuple((jax.ShapeDtypeStruct(shape, dtype)...  12.4 us
    ppermute x10, waiting for transfers between devices, spread(): return lax.ppermute(x, (axis, 'core'), perm)  10.9 us
    ppermute x10, starting transfers between devices, swap(): return lax.ppermute(x, axis, [(0, 1), (1, 0)])  9.22 us
    ppermute x10, waiting for transfers between devices, swap(): return lax.ppermute(x, axis, [(0, 1), (1, 0)])  7.62 us
    pallas_call x1, Pallas kernels, local(): pl.pallas_call(functools.partial(pack_kernel, chans), out_shape=jax.Shape...  2.29 us
    ppermute x2, starting transfers between devices, trade(): lax.ppermute(parts[3], ('ylo', 'core'), [(0, 3), (1, 2), (2, 1), (3, 0)])  2.07 us
  transfers between devices with their start and end apart: 22, of which 11 were waited for; matrix products, arithmetic and copies ran while one was open for 0% of the time, Pallas kernels for 8%

profile of v11, /device:TPU:1, one launch (start us, length us, event | category | flops | bytes accessed | tf_op | source)
XLA Modules:
  0.0 94.1 jit_solution(14155946908411853574)
XLA Ops:
  0.6 0.0 copy-start.4
  0.6 0.0 copy-start.6
  0.7 0.0 copy-start.11
  0.7 0.0 copy-start.13
  0.7 0.0 copy-start.15
  0.7 0.0 copy-start.9
  0.7 0.0 copy-start.10
  0.7 0.0 copy-start.16
  0.7 2.3 %shard_map.184 = bf16[32,96,128]{2,1,0:T(8,128)(2,1)} custom-call(bf16[32,4,32,128]{3,2,1,0:T(8,128)(2,1)} %bitcast.10, bf16[3,32,16,128]{3,2,1,0:T(8,128)(2,1)} %bitcast.12, bf16[32,16,128]{2,1,0:T(8,128)(2,1)} %bitcast.14), custom_call_target="tpu_custom_call" | custom-call | tf_op jit(solution)/shard_map/pallas_call | solution.py:301
  3.0 32.4 %all_to_all.5.sent_ref = bf16[32,96,128]{2,1,0:T(8,128)(2,1)S(1)} all-to-all(bf16[32,96,128]{2,1,0:T(8,128)(2,1)} %shard_map.184), channel_id=1, replica_groups=mesh['yhi'=2,'x'=4,'ylo'=2,'z'=8,'core'=2] {'ylo','z','core'}, dimensions={0} | all-to-all | bytes 1572864 | tf_op jit(solution)/shard_map/all_to_all | solution.py:312
  35.5 2.8 %shard_map.185 = (bf16[2,48,2048]{2,1,0:T(8,128)(2,1)S(1)}, f32[640,256]{1,0:T(8,128)S(1)}, f32[640,256]{1,0:T(8,128)S(1)}) custom-call(bf16[32,96,128]{2,1,0:T(8,128)(2,1)S(1)} %all_to_all.5.sent_ref, f32[16,4096]{1,0:T(8,128)S(1)} %copy-done.8, bf16[80,96]{1,0:T(8,128)(2,1)S(1)} %copy-done.16, bf16[32,240]{1,0:T(8,128)(2,1)S(1)} %copy-done.15, ...), custom_call_target="tpu_custom_call" | custom-call | tf_op jit(solution)/shard_map/pallas_call | solution.py:143
  38.3 0.0 copy-start
  38.3 2.4 %collective-permute-start.4 = (bf16[2,48,2048]{2,1,0:T(8,128)(2,1)S(1)}, bf16[2,48,2048]{2,1,0:T(8,128)(2,1)S(1)}, u32[]{:S(2)}, u32[]{:S(2)}) collective-permute-start(bf16[2,48,2048]{2,1,0:T(8,128)(2,1)S(1)} %get-tuple-element.35.refs_0_), channel_id=1, source_target_pairs={{0,1},{1,0},{2,3},{3,2},{4,5},{5,4},{6,7},{7,6},{8,9},{9,8},{10,11... | collective-permute-start | bytes 1179656 | tf_op jit(solution)/shard_map/ppermute | solution.py:279
  40.7 0.2 collective-permute-start.1
  41.0 0.5 collective-permute-start
  41.5 0.6 collective-permute-done.4
  42.1 0.5 collective-permute-start.5
  42.6 4.5 %collective-permute-done = bf16[32,32,128]{2,1,0:T(8,128)(2,1)S(1)} collective-permute-done((bf16[32,32,128]{2,1,0:T(8,128)(2,1)S(1)}, bf16[32,32,128]{2,1,0:T(8,128)(2,1)S(1)}, u32[]{:S(2)}, u32[]{:S(2)}) %collective-permute-start) | collective-permute-done | bytes 262176 | tf_op jit(solution)/shard_map/ppermute | solution.py:279
  47.1 0.7 collective-permute-done.1.refs_1_
  47.8 0.1 pad_maximum_fusion.refs_0_
  47.8 2.1 %collective-permute-start.3 = (bf16[2,32,32,128]{3,2,1,0:T(8,128)(2,1)S(1)}, bf16[2,32,32,128]{3,2,1,0:T(8,128)(2,1)S(1)}, u32[]{:S(2)}, u32[]{:S(2)}) collective-permute-start(bf16[2,32,32,128]{3,2,1,0:T(8,128)(2,1)S(1)} %pad_maximum_fusion.refs_0_), channel_id=1, source_target_pairs={{0,1},{1,0},{2,3},{3,2},{4,5},{5,4},{6,7},{7,6},{8,9},{9,8},{10,11... | collective-permute-start | bytes 1572872 | tf_op jit(solution)/shard_map/ppermute | solution.py:279
  50.0 2.5 %collective-permute-start.2 = (bf16[2,32,32,128]{3,2,1,0:T(8,128)(2,1)S(1)}, bf16[2,32,32,128]{3,2,1,0:T(8,128)(2,1)}, u32[]{:S(2)}, u32[]{:S(2)}) collective-permute-start(bf16[2,32,32,128]{3,2,1,0:T(8,128)(2,1)S(1)} %pad_maximum_fusion.refs_0_), channel_id=1, source_target_pairs={{0,32},{32,64},{64,96},{96,0},{1,97},{33,1},{65,33},{97,65},{2,34}... | collective-permute-start | bytes 1572872 | tf_op jit(solution)/shard_map/ppermute | solution.py:275
  52.4 0.6 collective-permute-start.8
  53.1 0.0 collective-permute-done.5.refs_2_
  53.1 0.4 collective-permute-start.12
  53.4 0.0 collective-permute-done.3.refs_4_
  53.4 2.1 %collective-permute-start.6 = (bf16[2,32,32,128]{3,2,1,0:T(8,128)(2,1)S(1)}, bf16[2,32,32,128]{3,2,1,0:T(8,128)(2,1)}, u32[]{:S(2)}, u32[]{:S(2)}) collective-permute-start(bf16[2,32,32,128]{3,2,1,0:T(8,128)(2,1)S(1)} %collective-permute-done.3.refs_4_), channel_id=1, source_target_pairs={{0,32},{32,64},{64,96},{96,0},{1,97},{33,1},{65,33},{97,65},{2,34}... | collective-permute-start | bytes 1572872 | tf_op jit(solution)/shard_map/ppermute | solution.py:275
  55.5 0.8 copy-done.2
  56.3 2.3 %collective-permute-done.2.refs_1_ = bf16[2,32,32,128]{3,2,1,0:T(8,128)(2,1)} collective-permute-done((bf16[2,32,32,128]{3,2,1,0:T(8,128)(2,1)S(1)}, bf16[2,32,32,128]{3,2,1,0:T(8,128)(2,1)}, u32[]{:S(2)}, u32[]{:S(2)}) %collective-permute-start.2) | collective-permute-done | bytes 524320 | tf_op jit(solution)/shard_map/ppermute | solution.py:275
  58.6 3.4 %collective-permute-start.7 = (bf16[2,32,32,128]{3,2,1,0:T(8,128)(2,1)}, bf16[2,32,32,128]{3,2,1,0:T(8,128)(2,1)}, u32[]{:S(2)}, u32[]{:S(2)}) collective-permute-start(bf16[2,32,32,128]{3,2,1,0:T(8,128)(2,1)} %collective-permute-done.2.refs_1_), channel_id=1, source_target_pairs={{0,32},{32,64},{64,96},{96,0},{1,97},{33,1},{65,33},{97,65},{2,34}... | collective-permute-start | bytes 1572872 | tf_op jit(solution)/shard_map/ppermute | solution.py:275
  62.0 0.0 collective-permute-done.8.refs_3_
  62.0 0.4 collective-permute-start.9
  62.4 1.3 %collective-permute-done.12.refs_4_ = bf16[2,48,2048]{2,1,0:T(8,128)(2,1)S(1)} collective-permute-done((bf16[2,48,2048]{2,1,0:T(8,128)(2,1)S(1)}, bf16[2,48,2048]{2,1,0:T(8,128)(2,1)S(1)}, u32[]{:S(2)}, u32[]{:S(2)}) %collective-permute-start.12) | collective-permute-done | bytes 393248 | tf_op jit(solution)/shard_map/ppermute | solution.py:275
  63.7 1.8 %collective-permute-start.13 = (bf16[2,48,2048]{2,1,0:T(8,128)(2,1)S(1)}, bf16[2,48,2048]{2,1,0:T(8,128)(2,1)S(1)}, u32[]{:S(2)}, u32[]{:S(2)}) collective-permute-start(bf16[2,48,2048]{2,1,0:T(8,128)(2,1)S(1)} %collective-permute-done.12.refs_4_), channel_id=1, source_target_pairs={{0,2},{2,4},{4,6},{6,8},{8,10},{10,12},{12,14},{14,0},{1,15},{3,1}... | collective-permute-start | bytes 1179656 | tf_op jit(solution)/shard_map/ppermute | solution.py:275
  65.5 3.5 %collective-permute-done.9.refs_1_ = bf16[2,48,2048]{2,1,0:T(8,128)(2,1)} collective-permute-done((bf16[2,48,2048]{2,1,0:T(8,128)(2,1)S(1)}, bf16[2,48,2048]{2,1,0:T(8,128)(2,1)}, u32[]{:S(2)}, u32[]{:S(2)}) %collective-permute-start.9) | collective-permute-done | bytes 393248 | tf_op jit(solution)/shard_map/ppermute | solution.py:275
  69.0 0.9 collective-permute-start.10
  69.9 0.0 collective-permute-done.6.refs_2_
  69.9 0.0 collective-permute-start.11
  69.9 3.2 %collective-permute-done.13.refs_5_ = bf16[2,48,2048]{2,1,0:T(8,128)(2,1)S(1)} collective-permute-done((bf16[2,48,2048]{2,1,0:T(8,128)(2,1)S(1)}, bf16[2,48,2048]{2,1,0:T(8,128)(2,1)S(1)}, u32[]{:S(2)}, u32[]{:S(2)}) %collective-permute-start.13) | collective-permute-done | bytes 393248 | tf_op jit(solution)/shard_map/ppermute | solution.py:275
  73.1 0.2 shard_map.186.refs_8_
  73.3 0.0 collective-permute-done.7.refs_3_
  73.3 1.0 %collective-permute-start.14 = (bf16[2,32,32,128]{3,2,1,0:T(8,128)(2,1)}, bf16[2,32,32,128]{3,2,1,0:T(8,128)(2,1)}, u32[]{:S(2)}, u32[]{:S(2)}) collective-permute-start(bf16[2,32,32,128]{3,2,1,0:T(8,128)(2,1)} %collective-permute-done.7.refs_3_), channel_id=1, source_target_pairs={{0,1},{1,0},{2,3},{3,2},{4,5},{5,4},{6,7},{7,6},{8,9},{9,8},{10,11... | collective-permute-start | bytes 1572872 | tf_op jit(solution)/shard_map/ppermute | solution.py:279
  74.3 0.5 collective-permute-start.18
  74.8 0.1 pad_add_fusion.place_ref
  74.9 0.0 collective-permute-done.10.refs_5_
  74.9 1.3 %collective-permute-done.14.refs_7_ = bf16[2,32,32,128]{3,2,1,0:T(8,128)(2,1)} collective-permute-done((bf16[2,32,32,128]{3,2,1,0:T(8,128)(2,1)}, bf16[2,32,32,128]{3,2,1,0:T(8,128)(2,1)}, u32[]{:S(2)}, u32[]{:S(2)}) %collective-permute-start.14) | collective-permute-done | bytes 524320 | tf_op jit(solution)/shard_map/ppermute | solution.py:279
  76.2 1.0 %copy-done.3 = bf16[2,32,32,128]{3,2,1,0:T(8,128)(2,1)S(1)} copy-done((bf16[2,32,32,128]{3,2,1,0:T(8,128)(2,1)S(1)}, bf16[2,32,32,128]{3,2,1,0:T(8,128)(2,1)}, u32[]{:S(2)}) %copy-start.3) | copy-done | bytes 524312
  77.2 3.7 %shard_map.187 = (bf16[576,128]{1,0:T(8,128)(2,1)S(1)}, bf16[576,128]{1,0:T(8,128)(2,1)S(1)}, bf16[576,128]{1,0:T(8,128)(2,1)S(1)}, bf16[576,128]{1,0:T(8,128)(2,1)S(1)}, bf16[512,4096]{1,0:T(8,128)(2,1)S(1)}) custom-call(s32[4]{0:T(128)S(1)} %pad_add_fusion.place_ref, bf16[2,32,32,128]{3,2,1,0:T(8,128)(2,1)S(1)} %pad_maximum_fusion.refs_0_, ...), custom_call_target="tpu_custom_call" | custom-call | tf_op jit(solution)/shard_map/pallas_call | solution.py:143
  80.9 0.5 collective-permute-start.15
  81.4 0.6 collective-permute-start.16
  82.0 1.2 %collective-permute-start.17 = (bf16[576,128]{1,0:T(8,128)(2,1)S(1)}, bf16[576,128]{1,0:T(8,128)(2,1)S(1)}, u32[]{:S(2)}, u32[]{:S(2)}) collective-permute-start(bf16[576,128]{1,0:T(8,128)(2,1)S(1)} %get-tuple-element.50), channel_id=1, source_target_pairs={{0,17},{1,16},{16,1},{17,0},{2,19},{3,18},{18,3},{19,2},{4,21},{5,... | collective-permute-start | bytes 442376 | tf_op jit(solution)/shard_map/ppermute | solution.py:287
  83.2 0.0 collective-permute-done.18.refs_2_
  83.2 2.6 %shard_map.188 = (bf16[192,128]{1,0:T(8,128)(2,1)S(1)}, bf16[192,128]{1,0:T(8,128)(2,1)S(1)}, bf16[192,128]{1,0:T(8,128)(2,1)S(1)}, bf16[192,128]{1,0:T(8,128)(2,1)S(1)}) custom-call(s32[4]{0:T(128)S(1)} %pad_add_fusion.place_ref, bf16[512,4096]{1,0:T(8,128)(2,1)S(1)} %get-tuple-element.51.refs_0_, bf16[2,48,2048]{2,1,0:T(8,128)(2,1)} %collective-permute-done.9.refs_1_, ...), custom_call_target="tpu_custom_call" | custom-call | tf_op jit(solution)/shard_map/pallas_call | solution.py:143
  85.8 0.6 collective-permute-start.19
  86.4 0.6 collective-permute-start.20
  87.0 0.3 collective-permute-done.19.refs_5_
  87.3 0.9 collective-permute-start.21
  88.1 1.5 %shard_map.190 = f32[16,4096]{1,0:T(8,128)} custom-call(f32[640,256]{1,0:T(8,128)S(1)} %get-tuple-element.61.gate_ref, f32[640,256]{1,0:T(8,128)S(1)} %copy-done.1, bf16[32,240]{1,0:T(8,128)(2,1)S(1)} %copy-done.15, f32[40,128]{1,0:T(8,128)S(1)} %copy-done.14, f32[40,128]{1,0:T(8,128)S(1)} %copy-done.12, bf16[256,256]{1,0:T(8,128)(2,1)S(1)} %copy-done.7, ...), custom_call_target="tpu_custom_call" | custom-call | tf_op jit(solution)/shard_map/pallas_call | solution.py:143
  89.6 1.0 %collective-permute-done.20.refs_6_ = bf16[192,128]{1,0:T(8,128)(2,1)S(1)} collective-permute-done((bf16[192,128]{1,0:T(8,128)(2,1)S(1)}, bf16[192,128]{1,0:T(8,128)(2,1)S(1)}, u32[]{:S(2)}, u32[]{:S(2)}) %collective-permute-start.20) | collective-permute-done | bytes 49184 | tf_op jit(solution)/shard_map/ppermute | solution.py:279
  90.6 1.6 %collective-permute-done.21.refs_7_ = bf16[192,128]{1,0:T(8,128)(2,1)S(1)} collective-permute-done((bf16[192,128]{1,0:T(8,128)(2,1)S(1)}, bf16[192,128]{1,0:T(8,128)(2,1)S(1)}, u32[]{:S(2)}, u32[]{:S(2)}) %collective-permute-start.21) | collective-permute-done | bytes 49184 | tf_op jit(solution)/shard_map/ppermute | solution.py:287
  92.2 0.0 collective-permute-done.15.refs_1_
  92.2 0.0 collective-permute-done.16.refs_2_
  92.2 0.0 collective-permute-done.17.refs_3_
  92.2 1.7 %shard_map.189 = (bf16[3,512,128]{2,1,0:T(8,128)(2,1)}, f32[3,128,512]{2,1,0:T(8,128)}) custom-call(s32[4]{0:T(128)S(1)} %pad_add_fusion.place_ref, bf16[576,128]{1,0:T(8,128)(2,1)S(1)} %get-tuple-element.47.refs_0_, bf16[576,128]{1,0:T(8,128)(2,1)S(1)} %collective-permute-done.15.refs_1_, bf16[576,128]{1,0:T(8,128)(2,1)S(1)} %collective-permute-done.16.refs_2_, ...), custom_call_target="tpu_custom_call" | custom-call | tf_op jit(solution)/shard_map/pallas_call | solution.py:143
  (25 shorter events, 0.1 us)
Async XLA Ops:
  0.6 34.8 %copy-start.4 = (bf16[256,256]{1,0:T(8,128)(2,1)S(1)}, bf16[256,256]{1,0:T(8,128)(2,1)}, u32[]{:S(2)}) copy-start(bf16[256,256]{1,0:T(8,128)(2,1)} %constant.41.clone.ul_ref) | copy-start | bytes 393220
  0.6 34.8 %copy-start.6 = (bf16[256,256]{1,0:T(8,128)(2,1)S(1)}, bf16[256,256]{1,0:T(8,128)(2,1)}, u32[]{:S(2)}) copy-start(bf16[256,256]{1,0:T(8,128)(2,1)} %constant.40.clone.uh_ref) | copy-start | bytes 393220
  0.7 34.8 %copy-start.11 = (f32[40,128]{1,0:T(8,128)S(1)}, f32[40,128]{1,0:T(8,128)}, u32[]{:S(2)}) copy-start(f32[40,128]{1,0:T(8,128)} %constant.37.clone.ts_ref) | copy-start | bytes 61444
  0.7 34.8 %copy-start.13 = (f32[40,128]{1,0:T(8,128)S(1)}, f32[40,128]{1,0:T(8,128)}, u32[]{:S(2)}) copy-start(f32[40,128]{1,0:T(8,128)} %constant.36.clone.tc_ref) | copy-start | bytes 61444
  0.7 34.8 %copy-start.15 = (bf16[32,240]{1,0:T(8,128)(2,1)S(1)}, bf16[32,240]{1,0:T(8,128)(2,1)}, u32[]{:S(2)}) copy-start(bf16[32,240]{1,0:T(8,128)(2,1)} %constant.35.clone.li_ref) | copy-start | bytes 46084
  0.7 34.8 %copy-start.9 = (bf16[256,256]{1,0:T(8,128)(2,1)S(1)}, bf16[256,256]{1,0:T(8,128)(2,1)}, u32[]{:S(2)}) copy-start(bf16[256,256]{1,0:T(8,128)(2,1)} %constant.39.clone.tl_ref) | copy-start | bytes 393220
  0.7 34.8 %copy-start.10 = (bf16[256,256]{1,0:T(8,128)(2,1)S(1)}, bf16[256,256]{1,0:T(8,128)(2,1)}, u32[]{:S(2)}) copy-start(bf16[256,256]{1,0:T(8,128)(2,1)} %constant.38.clone.th_ref) | copy-start | bytes 393220
  0.7 34.8 %copy-start.16 = (bf16[80,96]{1,0:T(8,128)(2,1)S(1)}, bf16[80,96]{1,0:T(8,128)(2,1)}, u32[]{:S(2)}) copy-start(bf16[80,96]{1,0:T(8,128)(2,1)} %constant.34.clone.lf_ref) | copy-start | bytes 46084
  0.7 34.8 %copy-start.8 = (f32[16,4096]{1,0:T(8,128)S(1)}, f32[16,4096]{1,0:T(8,128)}, u32[]{:S(2)}) copy-start(f32[16,4096]{1,0:T(8,128)} %filt_ref.1) | copy-start | bytes 786436
  38.3 31.6 %copy-start = (f32[640,256]{1,0:T(8,128)}, f32[640,256]{1,0:T(8,128)S(1)}, u32[]{:S(2)}) copy-start(f32[640,256]{1,0:T(8,128)S(1)} %get-tuple-element.62.carr_ref) | copy-start | bytes 1966084
  38.3 3.8 %collective-permute-start.4 = (bf16[2,48,2048]{2,1,0:T(8,128)(2,1)S(1)}, bf16[2,48,2048]{2,1,0:T(8,128)(2,1)S(1)}, u32[]{:S(2)}, u32[]{:S(2)}) collective-permute-start(bf16[2,48,2048]{2,1,0:T(8,128)(2,1)S(1)} %get-tuple-element.35.refs_0_), channel_id=1, source_target_pairs={{0,1},{1,0},{2,3},{3,2},{4,5},{5,4},{6,7},{7,6},{8,9},{9,8},{10,11... | collective-permute-start | bytes 1179656 | tf_op jit(solution)/shard_map/ppermute | solution.py:279
  40.7 7.0 %collective-permute-start.1 = (bf16[2,48,2048]{2,1,0:T(8,128)(2,1)S(1)}, bf16[2,48,2048]{2,1,0:T(8,128)(2,1)S(1)}, u32[]{:S(2)}, u32[]{:S(2)}) collective-permute-start(bf16[2,48,2048]{2,1,0:T(8,128)(2,1)S(1)} %get-tuple-element.35.refs_0_), channel_id=1, source_target_pairs={{0,2},{2,4},{4,6},{6,8},{8,10},{10,12},{12,14},{14,0},{1,15},{3,1}... | collective-permute-start | bytes 1179656 | tf_op jit(solution)/shard_map/ppermute | solution.py:275
  41.0 6.1 %collective-permute-start = (bf16[32,32,128]{2,1,0:T(8,128)(2,1)S(1)}, bf16[32,32,128]{2,1,0:T(8,128)(2,1)S(1)}, u32[]{:S(2)}, u32[]{:S(2)}) collective-permute-start(bf16[32,32,128]{2,1,0:T(8,128)(2,1)S(1)} %slice.4), channel_id=1, source_target_pairs={{0,16},{16,0},{1,17},{17,1},{2,18},{18,2},{3,19},{19,3},{4,20},{20... | collective-permute-start | bytes 786440 | tf_op jit(solution)/shard_map/ppermute | solution.py:279
  42.1 11.0 %collective-permute-start.5 = (bf16[2,48,2048]{2,1,0:T(8,128)(2,1)S(1)}, bf16[2,48,2048]{2,1,0:T(8,128)(2,1)S(1)}, u32[]{:S(2)}, u32[]{:S(2)}) collective-permute-start(bf16[2,48,2048]{2,1,0:T(8,128)(2,1)S(1)} %collective-permute-done.4), channel_id=1, source_target_pairs={{0,2},{2,4},{4,6},{6,8},{8,10},{10,12},{12,14},{14,0},{1,15},{3,1}... | collective-permute-start | bytes 1179656 | tf_op jit(solution)/shard_map/ppermute | solution.py:275
  47.8 5.6 %collective-permute-start.3 = (bf16[2,32,32,128]{3,2,1,0:T(8,128)(2,1)S(1)}, bf16[2,32,32,128]{3,2,1,0:T(8,128)(2,1)S(1)}, u32[]{:S(2)}, u32[]{:S(2)}) collective-permute-start(bf16[2,32,32,128]{3,2,1,0:T(8,128)(2,1)S(1)} %pad_maximum_fusion.refs_0_), channel_id=1, source_target_pairs={{0,1},{1,0},{2,3},{3,2},{4,5},{5,4},{6,7},{7,6},{8,9},{9,8},{10,11... | collective-permute-start | bytes 1572872 | tf_op jit(solution)/shard_map/ppermute | solution.py:279
  50.0 8.6 %collective-permute-start.2 = (bf16[2,32,32,128]{3,2,1,0:T(8,128)(2,1)S(1)}, bf16[2,32,32,128]{3,2,1,0:T(8,128)(2,1)}, u32[]{:S(2)}, u32[]{:S(2)}) collective-permute-start(bf16[2,32,32,128]{3,2,1,0:T(8,128)(2,1)S(1)} %pad_maximum_fusion.refs_0_), channel_id=1, source_target_pairs={{0,32},{32,64},{64,96},{96,0},{1,97},{33,1},{65,33},{97,65},{2,34}... | collective-permute-start | bytes 1572872 | tf_op jit(solution)/shard_map/ppermute | solution.py:275
  52.4 9.5 %collective-permute-start.8 = (bf16[2,48,2048]{2,1,0:T(8,128)(2,1)S(1)}, bf16[2,48,2048]{2,1,0:T(8,128)(2,1)S(1)}, u32[]{:S(2)}, u32[]{:S(2)}) collective-permute-start(bf16[2,48,2048]{2,1,0:T(8,128)(2,1)S(1)} %collective-permute-done.1.refs_1_), channel_id=1, source_target_pairs={{0,2},{2,4},{4,6},{6,8},{8,10},{10,12},{12,14},{14,0},{1,15},{3,1}... | collective-permute-start | bytes 1179656 | tf_op jit(solution)/shard_map/ppermute | solution.py:275
  53.1 10.6 %collective-permute-start.12 = (bf16[2,48,2048]{2,1,0:T(8,128)(2,1)S(1)}, bf16[2,48,2048]{2,1,0:T(8,128)(2,1)S(1)}, u32[]{:S(2)}, u32[]{:S(2)}) collective-permute-start(bf16[2,48,2048]{2,1,0:T(8,128)(2,1)S(1)} %collective-permute-done.5.refs_2_), channel_id=1, source_target_pairs={{0,2},{2,4},{4,6},{6,8},{8,10},{10,12},{12,14},{14,0},{1,15},{3,1}... | collective-permute-start | bytes 1179656 | tf_op jit(solution)/shard_map/ppermute | solution.py:275
  53.4 16.5 %collective-permute-start.6 = (bf16[2,32,32,128]{3,2,1,0:T(8,128)(2,1)S(1)}, bf16[2,32,32,128]{3,2,1,0:T(8,128)(2,1)}, u32[]{:S(2)}, u32[]{:S(2)}) collective-permute-start(bf16[2,32,32,128]{3,2,1,0:T(8,128)(2,1)S(1)} %collective-permute-done.3.refs_4_), channel_id=1, source_target_pairs={{0,32},{32,64},{64,96},{96,0},{1,97},{33,1},{65,33},{97,65},{2,34}... | collective-permute-start | bytes 1572872 | tf_op jit(solution)/shard_map/ppermute | solution.py:275
  55.5 0.8 copy-start.2
  58.6 14.7 %collective-permute-start.7 = (bf16[2,32,32,128]{3,2,1,0:T(8,128)(2,1)}, bf16[2,32,32,128]{3,2,1,0:T(8,128)(2,1)}, u32[]{:S(2)}, u32[]{:S(2)}) collective-permute-start(bf16[2,32,32,128]{3,2,1,0:T(8,128)(2,1)} %collective-permute-done.2.refs_1_), channel_id=1, source_target_pairs={{0,32},{32,64},{64,96},{96,0},{1,97},{33,1},{65,33},{97,65},{2,34}... | collective-permute-start | bytes 1572872 | tf_op jit(solution)/shard_map/ppermute | solution.py:275
  62.0 7.0 %collective-permute-start.9 = (bf16[2,48,2048]{2,1,0:T(8,128)(2,1)S(1)}, bf16[2,48,2048]{2,1,0:T(8,128)(2,1)}, u32[]{:S(2)}, u32[]{:S(2)}) collective-permute-start(bf16[2,48,2048]{2,1,0:T(8,128)(2,1)S(1)} %collective-permute-done.8.refs_3_), channel_id=1, source_target_pairs={{0,2},{2,4},{4,6},{6,8},{8,10},{10,12},{12,14},{14,0},{1,15},{3,1}... | collective-permute-start | bytes 1179656 | tf_op jit(solution)/shard_map/ppermute | solution.py:275
  63.7 9.4 %collective-permute-start.13 = (bf16[2,48,2048]{2,1,0:T(8,128)(2,1)S(1)}, bf16[2,48,2048]{2,1,0:T(8,128)(2,1)S(1)}, u32[]{:S(2)}, u32[]{:S(2)}) collective-permute-start(bf16[2,48,2048]{2,1,0:T(8,128)(2,1)S(1)} %collective-permute-done.12.refs_4_), channel_id=1, source_target_pairs={{0,2},{2,4},{4,6},{6,8},{8,10},{10,12},{12,14},{14,0},{1,15},{3,1}... | collective-permute-start | bytes 1179656 | tf_op jit(solution)/shard_map/ppermute | solution.py:275
  69.0 5.9 %collective-permute-start.10 = (bf16[2,32,32,128]{3,2,1,0:T(8,128)(2,1)}, bf16[2,32,32,128]{3,2,1,0:T(8,128)(2,1)}, u32[]{:S(2)}, u32[]{:S(2)}) collective-permute-start(bf16[2,32,32,128]{3,2,1,0:T(8,128)(2,1)} %collective-permute-done.2.refs_1_), channel_id=1, source_target_pairs={{0,1},{1,0},{2,3},{3,2},{4,5},{5,4},{6,7},{7,6},{8,9},{9,8},{10,11... | collective-permute-start | bytes 1572872 | tf_op jit(solution)/shard_map/ppermute | solution.py:279
  69.9 5.0 %collective-permute-start.11 = (bf16[2,32,32,128]{3,2,1,0:T(8,128)(2,1)}, bf16[2,32,32,128]{3,2,1,0:T(8,128)(2,1)}, u32[]{:S(2)}, u32[]{:S(2)}) collective-permute-start(bf16[2,32,32,128]{3,2,1,0:T(8,128)(2,1)} %collective-permute-done.6.refs_2_), channel_id=1, source_target_pairs={{0,1},{1,0},{2,3},{3,2},{4,5},{5,4},{6,7},{7,6},{8,9},{9,8},{10,11... | collective-permute-start | bytes 1572872 | tf_op jit(solution)/shard_map/ppermute | solution.py:279
  73.3 2.9 %collective-permute-start.14 = (bf16[2,32,32,128]{3,2,1,0:T(8,128)(2,1)}, bf16[2,32,32,128]{3,2,1,0:T(8,128)(2,1)}, u32[]{:S(2)}, u32[]{:S(2)}) collective-permute-start(bf16[2,32,32,128]{3,2,1,0:T(8,128)(2,1)} %collective-permute-done.7.refs_3_), channel_id=1, source_target_pairs={{0,1},{1,0},{2,3},{3,2},{4,5},{5,4},{6,7},{7,6},{8,9},{9,8},{10,11... | collective-permute-start | bytes 1572872 | tf_op jit(solution)/shard_map/ppermute | solution.py:279
  74.3 8.9 %collective-permute-start.18 = (bf16[2,48,2048]{2,1,0:T(8,128)(2,1)}, bf16[2,48,2048]{2,1,0:T(8,128)(2,1)}, u32[]{:S(2)}, u32[]{:S(2)}) collective-permute-start(bf16[2,48,2048]{2,1,0:T(8,128)(2,1)} %collective-permute-done.9.refs_1_), channel_id=1, source_target_pairs={{0,2},{2,4},{4,6},{6,8},{8,10},{10,12},{12,14},{14,0},{1,15},{3,1}... | collective-permute-start | bytes 1179656 | tf_op jit(solution)/shard_map/ppermute | solution.py:275
  74.9 13.2 %copy-start.1 = (f32[640,256]{1,0:T(8,128)S(1)}, f32[640,256]{1,0:T(8,128)}, u32[]{:S(2)}) copy-start(f32[640,256]{1,0:T(8,128)} %copy-done) | copy-start | bytes 1966084
  76.2 1.0 %copy-start.3 = (bf16[2,32,32,128]{3,2,1,0:T(8,128)(2,1)S(1)}, bf16[2,32,32,128]{3,2,1,0:T(8,128)(2,1)}, u32[]{:S(2)}) copy-start(bf16[2,32,32,128]{3,2,1,0:T(8,128)(2,1)} %copy-done.2) | copy-start | bytes 1572868
  77.2 10.9 %copy-start.5 = (bf16[256,256]{1,0:T(8,128)(2,1)S(1)}, bf16[256,256]{1,0:T(8,128)(2,1)}, u32[]{:S(2)}) copy-start(bf16[256,256]{1,0:T(8,128)(2,1)} %constant.41.clone.ul_ref) | copy-start | bytes 393220
  77.2 10.9 %copy-start.7 = (bf16[256,256]{1,0:T(8,128)(2,1)S(1)}, bf16[256,256]{1,0:T(8,128)(2,1)}, u32[]{:S(2)}) copy-start(bf16[256,256]{1,0:T(8,128)(2,1)} %constant.40.clone.uh_ref) | copy-start | bytes 393220
  77.2 10.9 %copy-start.12 = (f32[40,128]{1,0:T(8,128)S(1)}, f32[40,128]{1,0:T(8,128)}, u32[]{:S(2)}) copy-start(f32[40,128]{1,0:T(8,128)} %constant.37.clone.ts_ref) | copy-start | bytes 61444
  77.2 10.9 %copy-start.14 = (f32[40,128]{1,0:T(8,128)S(1)}, f32[40,128]{1,0:T(8,128)}, u32[]{:S(2)}) copy-start(f32[40,128]{1,0:T(8,128)} %constant.36.clone.tc_ref) | copy-start | bytes 61444
  80.9 11.3 %collective-permute-start.15 = (bf16[576,128]{1,0:T(8,128)(2,1)S(1)}, bf16[576,128]{1,0:T(8,128)(2,1)S(1)}, u32[]{:S(2)}, u32[]{:S(2)}) collective-permute-start(bf16[576,128]{1,0:T(8,128)(2,1)S(1)} %get-tuple-element.48), channel_id=1, source_target_pairs={{0,1},{1,0},{2,3},{3,2},{4,5},{5,4},{6,7},{7,6},{8,9},{9,8},{10,11... | collective-permute-start | bytes 442376 | tf_op jit(solution)/shard_map/ppermute | solution.py:279
  81.4 10.8 %collective-permute-start.16 = (bf16[576,128]{1,0:T(8,128)(2,1)S(1)}, bf16[576,128]{1,0:T(8,128)(2,1)S(1)}, u32[]{:S(2)}, u32[]{:S(2)}) collective-permute-start(bf16[576,128]{1,0:T(8,128)(2,1)S(1)} %get-tuple-element.49), channel_id=1, source_target_pairs={{0,16},{16,0},{1,17},{17,1},{2,18},{18,2},{3,19},{19,3},{4,20},{20... | collective-permute-start | bytes 442376 | tf_op jit(solution)/shard_map/ppermute | solution.py:279
  82.0 10.3 %collective-permute-start.17 = (bf16[576,128]{1,0:T(8,128)(2,1)S(1)}, bf16[576,128]{1,0:T(8,128)(2,1)S(1)}, u32[]{:S(2)}, u32[]{:S(2)}) collective-permute-start(bf16[576,128]{1,0:T(8,128)(2,1)S(1)} %get-tuple-element.50), channel_id=1, source_target_pairs={{0,17},{1,16},{16,1},{17,0},{2,19},{3,18},{18,3},{19,2},{4,21},{5,... | collective-permute-start | bytes 442376 | tf_op jit(solution)/shard_map/ppermute | solution.py:287
  85.8 1.5 %collective-permute-start.19 = (bf16[192,128]{1,0:T(8,128)(2,1)S(1)}, bf16[192,128]{1,0:T(8,128)(2,1)S(1)}, u32[]{:S(2)}, u32[]{:S(2)}) collective-permute-start(bf16[192,128]{1,0:T(8,128)(2,1)S(1)} %get-tuple-element.56), channel_id=1, source_target_pairs={{0,1},{1,0},{2,3},{3,2},{4,5},{5,4},{6,7},{7,6},{8,9},{9,8},{10,11... | collective-permute-start | bytes 147464 | tf_op jit(solution)/shard_map/ppermute | solution.py:279
  86.4 4.2 %collective-permute-start.20 = (bf16[192,128]{1,0:T(8,128)(2,1)S(1)}, bf16[192,128]{1,0:T(8,128)(2,1)S(1)}, u32[]{:S(2)}, u32[]{:S(2)}) collective-permute-start(bf16[192,128]{1,0:T(8,128)(2,1)S(1)} %get-tuple-element.57), channel_id=1, source_target_pairs={{0,16},{16,0},{1,17},{17,1},{2,18},{18,2},{3,19},{19,3},{4,20},{20... | collective-permute-start | bytes 147464 | tf_op jit(solution)/shard_map/ppermute | solution.py:279
  87.3 5.0 %collective-permute-start.21 = (bf16[192,128]{1,0:T(8,128)(2,1)S(1)}, bf16[192,128]{1,0:T(8,128)(2,1)S(1)}, u32[]{:S(2)}, u32[]{:S(2)}) collective-permute-start(bf16[192,128]{1,0:T(8,128)(2,1)S(1)} %get-tuple-element.58), channel_id=1, source_target_pairs={{0,17},{1,16},{16,1},{17,0},{2,19},{3,18},{18,3},{19,2},{4,21},{5,... | collective-permute-start | bytes 147464 | tf_op jit(solution)/shard_map/ppermute | solution.py:287
